TPU v7x, 512 devices: a whole 4x8x8 slice. The times are simulated.
512 devices in a mesh: frame: 16 (over y_hi, x, core), expert: 32 (over y_lo, z).
Axes of the slice: x: 4, y: 8 (y_hi: 2, y_lo: 4; y = y_hi * 4 + y_lo), z: 8, core: 2. Of those that a mesh axis runs over, the one named last changes fastest.
Arguments:
- video: bfloat16 [32, 128, 64, 128], P('frame', 'expert'), may hold values from -6 to 6
- conv_weight: bfloat16 [3, 3, 3, 128, 128], replicated, may hold values from -0.109375 to 0.109375
- latent_weight: bfloat16 [128, 16], replicated, may hold values from -0.5 to 0.5
- embed_weight: bfloat16 [128, 1536], P(None, 'frame'), may hold values from -0.5 to 0.5
- context: bfloat16 [32768, 1536], P(('frame', 'expert')), may hold values from -6 to 6
- router_weight: bfloat16 [2, 1536, 32], P(None, None, 'expert'), may hold values from -0.15625 to 0.15625
- gate_weight: bfloat16 [32, 1536, 3072], P('expert', None, 'frame'), may hold values from -0.15625 to 0.15625
- up_weight: bfloat16 [32, 1536, 3072], P('expert', None, 'frame'), may hold values from -0.15625 to 0.15625
- down_weight: bfloat16 [32, 3072, 1536], P('expert', 'frame'), may hold values from -0.15625 to 0.15625
- routes: int32 [32768, 2], P(('frame', 'expert')), may hold values from 0 to 63, all different within a row
Outputs:
- moe_out: bfloat16 [32768, 1536], P(('frame', 'expert'))
Inputs may be any that keep to these rules, and one draw needn't show every extreme that they name: `routes`: the two experts of a token differ.
All inputs are finite; a program needn't handle non-finite values.
Results may differ from a plain program's by a relative error of at most 0.024.
Values may be sent and summed in bfloat16 or wider, within the bound.
No kernel may reach another device: no remote copies, remote signals or barrier semaphores. Data moves between devices by JAX's collectives and lax.ppermute only.
A program may use at most 64 MiB of HBM per device.

v0:
```python
import jax
import jax.numpy as jnp
from jax import lax
from jax.sharding import PartitionSpec as P


def from_behind(value, axis, steps):
    count = lax.axis_size(axis)
    leading, last = (max(0, -steps), min(count, count - steps))
    return lax.ppermute(value, axis, [(source, source + steps) for source in range(leading, last)])


def with_halo(block, sides, width):
    for axis, dim in sides:
        count = lax.axis_size(axis)
        forward = [(i, i + 1) for i in range(count - 1)]
        backward = [(target, source) for source, target in forward]
        low = lax.ppermute(
            lax.slice_in_dim(block, block.shape[dim] - width, None, axis=dim), axis, forward
        )
        high = lax.ppermute(lax.slice_in_dim(block, 0, width, axis=dim), axis, backward)
        block = jnp.concatenate([low, block, high], axis=dim)
    return block


def local(
    video,
    conv_weight,
    latent_weight,
    embed_weight,
    context,
    router_weight,
    gate_weight,
    up_weight,
    down_weight,
    routes,
):
    frames, rows, cols, chans = video.shape
    past = from_behind(video, "frame", 1)
    stacked = jnp.concatenate([past, video], axis=0)
    rimmed = with_halo(stacked, (("expert", 1),), 1)
    padded = jnp.pad(rimmed, ((0, 0), (0, 0), (1, 1), (0, 0)))
    taps = [
        padded[a : a + frames, b : b + rows, q : q + cols, :]
        for a in range(3)
        for b in range(3)
        for q in range(3)
    ]
    window = jnp.concatenate(taps, axis=-1).reshape(frames * rows * cols, 27 * chans)
    mixed = jnp.dot(
        window, conv_weight.reshape(27 * chans, chans), preferred_element_type=jnp.float32
    )
    feature = (video.reshape(-1, chans).astype(jnp.float32) + jax.nn.silu(mixed)).astype(
        jnp.bfloat16
    )
    latent = jnp.dot(feature, latent_weight, preferred_element_type=jnp.float32).astype(
        jnp.bfloat16
    )
    lat_width = latent.shape[1]
    blocks = latent.reshape(2, rows // 2, 2, cols // 2, 2, lat_width)
    patches = blocks.transpose(1, 3, 0, 2, 4, 5).reshape(-1, 8 * lat_width)
    tok = patches.shape[0]
    embedded = jnp.dot(
        patches,
        lax.all_gather(embed_weight, "frame", axis=1, tiled=True),
        preferred_element_type=jnp.float32,
    ).astype(jnp.bfloat16)
    resid_sum = embedded.astype(jnp.float32) + context.astype(jnp.float32)
    meansq = jnp.mean(resid_sum * resid_sum, axis=1, keepdims=True)
    tokens = (resid_sum * lax.rsqrt(meansq + 1e-06)).astype(jnp.bfloat16)
    width = tokens.shape[1]
    pairs = lax.axis_size("expert")
    experts = 2 * pairs
    capacity = max(2, 2 * tok // experts)
    flat_routes = routes.reshape(-1)
    labels = jnp.arange(experts, dtype=jnp.int32)
    chosen = (flat_routes[:, None] == labels[None, :]).astype(jnp.int32)
    earlier = jnp.cumsum(chosen, axis=0) - chosen
    slot_rank = jnp.sum(earlier * chosen, axis=1)
    place = jnp.where(slot_rank < capacity, flat_routes * capacity + slot_rank, -1)
    table = (place[:, None] == jnp.arange(experts * capacity, dtype=jnp.int32)[None, :]).astype(
        jnp.bfloat16
    )
    doubled = jnp.repeat(tokens, 2, axis=0)
    outgoing = jnp.einsum("as,ad->sd", table, doubled, preferred_element_type=jnp.float32)
    outgoing = outgoing.astype(jnp.bfloat16).reshape(2, pairs, capacity, width)
    arrived = lax.all_to_all(outgoing, "expert", split_axis=1, concat_axis=1, tiled=True)
    groups = lax.axis_size("frame") // 2
    own_half = lax.axis_index("frame") // groups
    router_pair = lax.dynamic_index_in_dim(router_weight, own_half, 0, keepdims=False)
    fanned = jnp.repeat(arrived, groups, axis=0)

    def source_rows(block):
        shape = block.shape
        rows_in = block.reshape(-1, shape[-1])
        score = jax.nn.sigmoid(jnp.dot(rows_in, router_pair, preferred_element_type=jnp.float32))
        gate = jnp.dot(rows_in, gate_weight[0], preferred_element_type=jnp.float32)
        up = jnp.dot(rows_in, up_weight[0], preferred_element_type=jnp.float32)
        hidden = (jax.nn.silu(gate) * up).astype(jnp.bfloat16)
        product = jnp.dot(hidden, down_weight[0], preferred_element_type=jnp.float32)
        return (score * product).astype(jnp.bfloat16).reshape(shape)

    partial_value = lax.map(
        source_rows, lax.all_to_all(fanned, "frame", split_axis=0, concat_axis=0, tiled=True)
    )
    returned = lax.all_to_all(partial_value, "frame", split_axis=0, concat_axis=0, tiled=True)
    summed = (
        returned.reshape(2, groups, pairs, capacity, width)
        .astype(jnp.float32)
        .sum(axis=1)
        .astype(jnp.bfloat16)
    )
    homeward = lax.all_to_all(summed, "expert", split_axis=1, concat_axis=1, tiled=True)
    flat_results = homeward.reshape(experts * capacity, width)
    picked = jnp.dot(table, flat_results, preferred_element_type=jnp.float32).reshape(tok, 2, width)
    return jnp.sum(picked, axis=1).astype(jnp.bfloat16)


def solution(mesh):
    return jax.shard_map(
        local,
        mesh=mesh,
        in_specs=(
            P("frame", "expert", None, None),
            P(),
            P(),
            P(None, "frame"),
            P(("frame", "expert"), None),
            P(None, None, "expert"),
            P("expert", None, "frame"),
            P("expert", None, "frame"),
            P("expert", "frame", None),
            P(("frame", "expert"), None),
        ),
        out_specs=P(("frame", "expert"), None),
        check_vma=False,
    )
```

profile of v0, /device:TPU:6, one launch (start us, length us, event | category | flops | bytes accessed | tf_op | source)
XLA Modules:
  0.0 324.7 jit_solution(12551237331224987751)
XLA Ops:
  0.0 2.0 collective-permute-start
  3.4 3.2 collective-permute-done
  7.6 4.3 %collective-permute-start.1 = (bf16[4,1,64,128]{3,2,1,0:T(8,128)(2,1)S(1)}, bf16[4,1,64,128]{3,2,1,0:T(8,128)(2,1)S(1)}, u32[]{:S(2)}, u32[]{:S(2)}) collective-permute-start(bf16[4,1,64,128]{3,2,1,0:T(8,128)(2,1)S(1)} %get-tuple-element.57), channel_id=1, source_target_pairs={{0,1},{1,2},{2,3},{3,4},{4,5},{5,6},{6,7},{7,8},{8,9},{9,10},{10,1... | collective-permute-start | bytes 196616 | tf_op jit(solution)/shard_map/ppermute | solution.py:18
  11.9 1.3 collective-permute-start.2
  13.2 30.9 %all_gather.3 = bf16[128,1536]{0,1:T(8,128)(2,1)S(1)} all-gather(bf16[128,96]{0,1:T(8,128)(2,1)} %param.15), channel_id=1, replica_groups=mesh['frame'=16,'expert'=32] {'frame'}, dimensions={1}, use_global_device_ids=true | all-gather | bytes 417792 | tf_op jit(solution)/shard_map/all_gather | solution.py:65
  45.5 1.1 fusion.26
  48.9 28.0 %all_to_all.20 = bf16[2,32,2,1536]{3,2,0,1:T(2,128)(2,1)S(1)} all-to-all(bf16[2,32,2,1536]{3,2,0,1:T(2,128)(2,1)S(1)} %copy.36), channel_id=1, replica_groups=mesh['frame'=16,'expert'=32] {'expert'}, dimensions={1} | all-to-all | bytes 786432 | tf_op jit(solution)/shard_map/all_to_all | solution.py:87
  77.1 4.1 %broadcast_in_dim.27 = bf16[2,8,32,2,1536]{4,3,2,1,0:T(2,128)(2,1)} broadcast(bf16[2,32,2,1536]{3,2,1,0:T(2,128)(2,1)S(1)} %copy.37), dimensions={0,2,3,4} | broadcast | bytes 3538944 | tf_op jit(solution)/shard_map/broadcast_in_dim | solution.py:91
  81.3 9.5 %all-to-all-start.1 = ((bf16[16,32,2,1536]{3,2,1,0:T(2,128)(2,1)}), bf16[16,32,2,1536]{3,2,1,0:T(2,128)(2,1)}, u32[]{:S(2)}, u32[]{:S(2)}) async-start(bf16[16,32,2,1536]{3,2,1,0:T(2,128)(2,1)} %bitcast.67), calls=%async_computation.1 | async-start | bytes 6291456 | tf_op jit(solution)/shard_map/all_to_all | solution.py:104
  90.8 45.5 %all-to-all-done.1 = bf16[16,32,2,1536]{3,2,1,0:T(2,128)(2,1)} async-done(((bf16[16,32,2,1536]{3,2,1,0:T(2,128)(2,1)}), bf16[16,32,2,1536]{3,2,1,0:T(2,128)(2,1)}, u32[]{:S(2)}, u32[]{:S(2)}) %all-to-all-start.1) | async-done | bytes 3145760 | tf_op jit(solution)/shard_map/all_to_all | solution.py:104
  136.3 50.9 %while.10 = (s32[]{:T(128)}, bf16[16,32,2,1536]{3,2,1,0:T(2,128)(2,1)}, bf16[16,32,2,1536]{3,2,1,0:T(2,128)(2,1)}, bf16[1536,1]{0,1:T(2,128)(2,1)S(1)}, bf16[1,1...) while((s32[]{:T(128)}, ...), condition=%wide.region_4.5_spmd, body=%wide.region_3.4_spmd.sunk | while | flops 113713344 | bytes 4231257 | solution.py:103
  136.3 1.1 constant_dynamic-slice_fusion.2
  139.5 1.1 constant_dynamic-slice_fusion.2
  142.7 1.1 constant_dynamic-slice_fusion.2
  145.9 1.1 constant_dynamic-slice_fusion.2
  149.0 1.1 constant_dynamic-slice_fusion.2
  161.8 1.1 constant_dynamic-slice_fusion.2
  168.1 1.1 constant_dynamic-slice_fusion.2
  174.5 1.1 constant_dynamic-slice_fusion.2
  177.7 1.1 constant_dynamic-slice_fusion.2
  187.2 46.5 %all_to_all.21 = bf16[16,32,2,1536]{3,2,1,0:T(2,128)(2,1)S(1)} all-to-all(bf16[16,32,2,1536]{3,2,1,0:T(2,128)(2,1)} %get-tuple-element.42), channel_id=1, replica_groups=mesh['frame'=16,'expert'=32] {'frame'}, dimensions={0} | all-to-all | bytes 6291456 | tf_op jit(solution)/shard_map/all_to_all | solution.py:106
  233.7 2.8 bitcast_reduce_fusion
  237.5 70.9 %all-to-all-start.3 = ((bf16[2,32,2,1536]{3,2,0,1:T(2,128)(2,1)}), bf16[2,32,2,1536]{3,2,0,1:T(2,128)(2,1)S(1)}, u32[]{:S(2)}, u32[]{:S(2)}) async-start(bf16[2,32,2,1536]{3,2,0,1:T(2,128)(2,1)} %copy.38), calls=%async_computation.3 | async-start | bytes 786432 | tf_op jit(solution)/shard_map/all_to_all | solution.py:113
  308.8 14.5 %all-to-all-done.3 = bf16[2,32,2,1536]{3,2,0,1:T(2,128)(2,1)S(1)} async-done(((bf16[2,32,2,1536]{3,2,0,1:T(2,128)(2,1)}), bf16[2,32,2,1536]{3,2,0,1:T(2,128)(2,1)S(1)}, u32[]{:S(2)}, u32[]{:S(2)}) %all-to-all-start.3) | async-done | bytes 393248 | tf_op jit(solution)/shard_map/all_to_all | solution.py:113
  (184 shorter events, 49.6 us)
Async XLA Ops:
  0.0 45.5 %copy-start = (bf16[3,3,3,128,128]{4,3,2,1,0:T(8,128)(2,1)S(1)}, bf16[3,3,3,128,128]{4,3,2,1,0:T(8,128)(2,1)}, u32[]{:S(2)}) copy-start(bf16[3,3,3,128,128]{4,3,2,1,0:T(8,128)(2,1)} %param.13) | copy-start | bytes 2654212
  0.0 6.6 %collective-permute-start = (bf16[2,4,64,128]{3,2,1,0:T(8,128)(2,1)}, bf16[2,4,64,128]{3,2,1,0:T(8,128)(2,1)S(1)}, u32[]{:S(2)}, u32[]{:S(2)}) collective-permute-start(bf16[2,4,64,128]{3,2,1,0:T(8,128)(2,1)} %param.12), channel_id=1, source_target_pairs={{0,32},{32,64},{64,96},{96,128},{128,160},{160,192},{192,224},{224... | collective-permute-start | bytes 393224 | tf_op jit(solution)/shard_map/ppermute | solution.py:10
  7.6 36.5 %collective-permute-start.1 = (bf16[4,1,64,128]{3,2,1,0:T(8,128)(2,1)S(1)}, bf16[4,1,64,128]{3,2,1,0:T(8,128)(2,1)S(1)}, u32[]{:S(2)}, u32[]{:S(2)}) collective-permute-start(bf16[4,1,64,128]{3,2,1,0:T(8,128)(2,1)S(1)} %get-tuple-element.57), channel_id=1, source_target_pairs={{0,1},{1,2},{2,3},{3,4},{4,5},{5,6},{6,7},{7,8},{8,9},{9,10},{10,1... | collective-permute-start | bytes 196616 | tf_op jit(solution)/shard_map/ppermute | solution.py:18
  11.9 32.2 %collective-permute-start.2 = (bf16[4,1,64,128]{3,2,1,0:T(8,128)(2,1)S(1)}, bf16[4,1,64,128]{3,2,1,0:T(8,128)(2,1)S(1)}, u32[]{:S(2)}, u32[]{:S(2)}) collective-permute-start(bf16[4,1,64,128]{3,2,1,0:T(8,128)(2,1)S(1)} %get-tuple-element.58), channel_id=1, source_target_pairs={{1,0},{2,1},{3,2},{4,3},{5,4},{6,5},{7,6},{8,7},{9,8},{10,9},{11,1... | collective-permute-start | bytes 196616 | tf_op jit(solution)/shard_map/ppermute | solution.py:21
  44.2 1.1 copy-start.4
  45.3 1.4 copy-start.7
  45.4 1.8 copy-start.5
  81.2 9.5 %copy-start.6 = (bf16[2,1536,1]{1,0,2:T(2,128)(2,1)S(1)}, bf16[2,1536,1]{1,0,2:T(2,128)(2,1)}, u32[]{:S(2)}) copy-start(bf16[2,1536,1]{1,0,2:T(2,128)(2,1)} %param.17) | copy-start | bytes 18436
  81.3 55.0 %copy-start.1 = (bf16[1,1536,192]{1,2,0:T(8,128)(2,1)S(1)}, bf16[1,1536,192]{1,2,0:T(8,128)(2,1)}, u32[]{:S(2)}) copy-start(bf16[1,1536,192]{1,2,0:T(8,128)(2,1)} %param.19) | copy-start | bytes 1769476
  81.3 55.0 %copy-start.2 = (bf16[1,192,1536]{2,1,0:T(8,128)(2,1)S(1)}, bf16[1,192,1536]{2,1,0:T(8,128)(2,1)}, u32[]{:S(2)}) copy-start(bf16[1,192,1536]{2,1,0:T(8,128)(2,1)} %param.20) | copy-start | bytes 1769476
  81.3 55.0 %copy-start.3 = (bf16[1,1536,192]{1,2,0:T(8,128)(2,1)S(1)}, bf16[1,1536,192]{1,2,0:T(8,128)(2,1)}, u32[]{:S(2)}) copy-start(bf16[1,1536,192]{1,2,0:T(8,128)(2,1)} %param.18) | copy-start | bytes 1769476
  81.3 55.0 %all-to-all-start.1 = ((bf16[16,32,2,1536]{3,2,1,0:T(2,128)(2,1)}), bf16[16,32,2,1536]{3,2,1,0:T(2,128)(2,1)}, u32[]{:S(2)}, u32[]{:S(2)}) async-start(bf16[16,32,2,1536]{3,2,1,0:T(2,128)(2,1)} %bitcast.67), calls=%async_computation.1 | async-start | bytes 6291456 | tf_op jit(solution)/shard_map/all_to_all | solution.py:104
  233.7 74.9 %copy-start.8 = (s32[64,2]{0,1:T(2,128)S(1)}, s32[64,2]{0,1:T(2,128)}, u32[]{:S(2)}) copy-start(s32[64,2]{0,1:T(2,128)} %param.21) | copy-start | bytes 1540
  237.5 85.8 %all-to-all-start.3 = ((bf16[2,32,2,1536]{3,2,0,1:T(2,128)(2,1)}), bf16[2,32,2,1536]{3,2,0,1:T(2,128)(2,1)S(1)}, u32[]{:S(2)}, u32[]{:S(2)}) async-start(bf16[2,32,2,1536]{3,2,0,1:T(2,128)(2,1)} %copy.38), calls=%async_computation.3 | async-start | bytes 786432 | tf_op jit(solution)/shard_map/all_to_all | solution.py:113
where the time goes:
time: 327 us; the launch traced here: 325 us
  blocking collectives  105 us (32%)
  starting transfers between devices  88 us (27%)
  waiting for transfers between devices  63.2 us (19%)
  local copies, waits for them, and re-layouts  42.7 us (13%)
  matrix products  20.8 us (6%)
  other arithmetic  3.7 us (1%)
    all_to_all x1, starting transfers between devices, local(): lax.all_to_all(summed, 'expert', split_axis=1, concat_axis=1, tiled=True)  70.9 us
    all_to_all x1, blocking collectives, local(): lax.all_to_all(partial_value, 'frame', split_axis=0, concat_axis=0, tiled...  46.5 us
    all_to_all x1, waiting for transfers between devices, local(): lax.all_to_all(fanned, 'frame', split_axis=0, concat_axis=0, tiled=True)  45.5 us
    all_gather x1, blocking collectives, local(): lax.all_gather(embed_weight, 'frame', axis=1, tiled=True)  30.9 us
    all_to_all x1, blocking collectives, local(): lax.all_to_all(outgoing, 'expert', split_axis=1, concat_axis=1, tiled=True)  28 us
    dynamic_slice x16, local copies, waits for them, and re-layouts, local(): lax.map(source_rows, lax.all_to_all(fanned, 'frame', split_axis=0, concat...  17 us
    all_to_all x1, waiting for transfers between devices, local(): lax.all_to_all(summed, 'expert', split_axis=1, concat_axis=1, tiled=True)  14.5 us
    dynamic_update_slice x16, local copies, waits for them, and re-layouts, local(): lax.map(source_rows, lax.all_to_all(fanned, 'frame', split_axis=0, concat...  13.1 us
  transfers between devices with their start and end apart: 5, of which 3 were waited for; matrix products, arithmetic and copies ran while one was open for 1% of the time, Pallas kernels for 0%

commit v1 on v0

v1 whole, which is shorter than its diff:
```python
import jax
import jax.numpy as jnp
from jax import lax
from jax.sharding import Mesh, PartitionSpec as P

FRAME = ("yh", "x", "c")
EXPERT = ("yl", "z")
SOURCES = ("yh", "yl", "z")
SIZES = (2, 4, 2, 4, 8)
NAMES = ("yh", "x", "c", "yl", "z")
BF = jnp.bfloat16
F32 = jnp.float32


def dot(a, b, dims=((1,), (0,))):
    return lax.dot_general(a, b, (dims, ((), ())), preferred_element_type=F32)


def shifted(value, axes, step):
    count = lax.axis_size(axes)
    pairs = [(i, i + step) for i in range(count) if 0 <= i + step < count]
    return lax.ppermute(value, axes, pairs)


def encode(video, conv_weight, latent_weight):
    frames, rows, cols, chans = video.shape
    above = shifted(video[:, rows - 1 :], EXPERT, 1)
    below = shifted(video[:, :1], EXPERT, -1)
    tall = jnp.concatenate([above, video, below], axis=1)
    past = shifted(tall, FRAME, 1)

    def windows(block):
        wide = jnp.pad(block, ((0, 0), (0, 0), (1, 1), (0, 0)))
        taps = [wide[:, b : b + rows, q : q + cols] for b in range(3) for q in range(3)]
        return jnp.concatenate(taps, axis=-1).reshape(block.shape[0], rows * cols, 9 * chans)

    kernel = conv_weight.reshape(3, 9 * chans, chans)
    own, old = windows(tall), windows(past)
    first = dot(own[0], kernel[2]) + dot(old[0], kernel[0]) + dot(old[1], kernel[1])
    second = dot(own[1], kernel[2]) + dot(own[0], kernel[1]) + dot(old[1], kernel[0])
    mixed = jnp.concatenate([first, second], axis=0)
    feature = (video.reshape(-1, chans).astype(F32) + jax.nn.silu(mixed)).astype(BF)
    return dot(feature, latent_weight).astype(BF)


def place_table(routes, experts, capacity):
    tok = routes.shape[0]
    flat = routes.reshape(-1)
    count = flat.shape[0]
    chosen = (flat[:, None] == jnp.arange(experts, dtype=jnp.int32)[None, :]).astype(BF)
    at = jnp.arange(count, dtype=jnp.int32)
    before = (at[:, None] > at[None, :]).astype(BF)
    rank = jnp.sum(dot(before, chosen) * chosen.astype(F32), axis=1).astype(jnp.int32)
    place = jnp.where(rank < capacity, flat * capacity + rank, -1).reshape(tok, 2)
    slots = jnp.arange(experts * capacity, dtype=jnp.int32)[None, :]
    hit = (place[:, :1] == slots) | (place[:, 1:] == slots)
    return hit.astype(BF)


def local(
    video,
    conv_weight,
    latent_weight,
    embed_weight,
    context,
    router_weight,
    gate_weight,
    up_weight,
    down_weight,
    routes,
):
    rows, cols = video.shape[1:3]
    tok, width = context.shape
    experts, capacity = 64, 2
    share = down_weight.shape[1]

    held = jnp.concatenate([gate_weight[0].T, up_weight[0].T, down_weight[0]], axis=0)
    held = lax.all_gather(held, "x", axis=0, tiled=False)

    part = embed_weight.T
    spread = lax.all_gather(jnp.concatenate([part] * 3, axis=0), FRAME, axis=0, tiled=False)
    embed = spread[:, : part.shape[0]].reshape(width, part.shape[1])

    table = place_table(routes, experts, capacity)
    latent = encode(video, conv_weight, latent_weight)
    lat = latent.shape[1]
    blocks = latent.reshape(2, rows // 2, 2, cols // 2, 2, lat)
    patches = blocks.transpose(1, 3, 0, 2, 4, 5).reshape(tok, 8 * lat)
    embedded = dot(patches, embed, ((1,), (1,))).astype(BF)
    total = embedded.astype(F32) + context.astype(F32)
    meansq = jnp.mean(total * total, axis=1, keepdims=True)
    tokens = (total * lax.rsqrt(meansq + 1e-06)).astype(BF)

    outgoing = dot(table, tokens, ((0,), (0,))).astype(BF).reshape(experts, capacity, width)
    arrived = lax.all_to_all(outgoing, SOURCES, split_axis=0, concat_axis=0, tiled=True)
    mine = arrived.reshape(experts * capacity, width)
    swap = [(0, 1), (1, 0)]
    theirs = lax.ppermute(mine, "c", swap)
    inputs = jnp.concatenate([theirs, mine], axis=0)
    router = lax.dynamic_index_in_dim(router_weight, lax.axis_index("yh"), 0, keepdims=False)
    score = jax.nn.sigmoid(dot(inputs, router))
    result = jnp.zeros((2 * experts * capacity, width), F32)
    for chunk in range(held.shape[0]):
        gate = dot(inputs, held[chunk, :share], ((1,), (1,)))
        up = dot(inputs, held[chunk, share : 2 * share], ((1,), (1,)))
        hidden = (jax.nn.silu(gate) * up).astype(BF)
        result = result + dot(hidden, held[chunk, 2 * share :])
    result = (score * result).astype(BF)
    other, own = result[: experts * capacity], result[experts * capacity :]
    back = lax.ppermute(other, "c", swap)
    summed = (back.astype(F32) + own.astype(F32)).astype(BF).reshape(experts, capacity, width)
    homeward = lax.all_to_all(summed, SOURCES, split_axis=0, concat_axis=0, tiled=True)
    return dot(table, homeward.reshape(experts * capacity, width)).astype(BF)


def solution(mesh):
    fine = Mesh(mesh.devices.reshape(SIZES), NAMES)
    return jax.shard_map(
        local,
        mesh=fine,
        in_specs=(
            P(FRAME, EXPERT, None, None),
            P(),
            P(),
            P(None, FRAME),
            P((*FRAME, *EXPERT), None),
            P(None, None, EXPERT),
            P(EXPERT, None, FRAME),
            P(EXPERT, None, FRAME),
            P(EXPERT, FRAME, None),
            P((*FRAME, *EXPERT), None),
        ),
        out_specs=P((*FRAME, *EXPERT), None),
        check_vma=False,
    )
```

time: 327 us -> 215 us (0.66)
  starting transfers between devices: 88 us -> 12 us
  blocking collectives: 105 us -> 58.9 us
  local copies, waits for them, and re-layouts: 42.7 us -> 4.68 us
  waiting for transfers between devices: 63.2 us -> 97.1 us
  between operations: 0.48 us -> 13.8 us
    all_gather x0 -> x2, waiting for transfers between devices: none -> 89.5 us  [the longest x1 47.1 us: local(): lax.all_gather(jnp.concatenate([part] * 3, axis=0), FRAME, axis=0, tiled=...]
    all_to_all x2 -> x0, starting transfers between devices: 80.4 us -> none  [the longest x1 70.9 us: local(): lax.all_to_all(summed, 'expert', split_axis=1, concat_axis=1, tiled=True)]
    all_to_all x2 -> x0, waiting for transfers between devices: 60 us -> none  [the longest x1 45.5 us: local(): lax.all_to_all(fanned, 'frame', split_axis=0, concat_axis=0, tiled=True)]
    all_gather x1 -> x0, blocking collectives: 30.9 us -> none  [local(): lax.all_gather(embed_weight, 'frame', axis=1, tiled=True)]
    dynamic_slice x16 -> x0, local copies, waits for them, and re-layouts: 17 us -> none  [local(): lax.map(source_rows, lax.all_to_all(fanned, 'frame', split_axis=0, concat...]
    all_to_all x2, blocking collectives: 74.5 us -> 58.9 us  [the longest x1 30.5 us: local(): lax.all_to_all(summed, SOURCES, split_axis=0, concat_axis=0, tiled=True)]
    dynamic_update_slice x16 -> x0, local copies, waits for them, and re-layouts: 13.1 us -> none  [local(): lax.map(source_rows, lax.all_to_all(fanned, 'frame', split_axis=0, concat...]
    broadcast_in_dim x18 -> x0, local copies, waits for them, and re-layouts: 5.56 us -> none  [the longest x1 4.12 us: local(): fanned = jnp.repeat(arrived, groups, axis=0)]
  transfers between devices with their start and end apart: 5 -> 7, of which waited for: 3 -> 6; matrix products, arithmetic and copies ran while one was open for 1% -> 5% of each run, Pallas kernels for 0% -> 0%
where the time goes in v1:
time: 215 us; the launch traced here: 213 us
  waiting for transfers between devices  97.1 us (45%)
  blocking collectives  58.9 us (27%)
  matrix products  21.4 us (10%)
  between operations  13.8 us (6%)
  starting transfers between devices  12 us (6%)
  other arithmetic  5.22 us (2%)
  local copies, waits for them, and re-layouts  4.68 us (2%)
    all_gather x1, waiting for transfers between devices, local(): lax.all_gather(jnp.concatenate([part] * 3, axis=0), FRAME, axis=0, tiled=...  47.1 us
    all_gather x1, waiting for transfers between devices, local(): held = lax.all_gather(held, 'x', axis=0, tiled=False)  42.4 us
    all_to_all x1, blocking collectives, local(): lax.all_to_all(summed, SOURCES, split_axis=0, concat_axis=0, tiled=True)  30.5 us
    all_to_all x1, blocking collectives, local(): lax.all_to_all(outgoing, SOURCES, split_axis=0, concat_axis=0, tiled=True)  28.4 us
    dot_general x20, matrix products, dot(): return lax.dot_general(a, b, (dims, ((), ())), preferred_element_type=F32)  21.4 us
    ppermute x3, starting transfers between devices, shifted(): return lax.ppermute(value, axes, pairs)  8.11 us
  transfers between devices with their start and end apart: 7, of which 6 were waited for; matrix products, arithmetic and copies ran while one was open for 5% of the time, Pallas kernels for 0%

profile of v1, /device:TPU:6, one launch (start us, length us, event | category | flops | bytes accessed | tf_op | source)
XLA Modules:
  0.0 213.1 jit_solution(7102191334460435983)
XLA Ops:
  6.5 1.5 pad_maximum_fusion.4
  8.1 2.8 %pad_maximum_fusion = bf16[576,1536]{1,0:T(8,128)(2,1)} fusion(bf16[192,1536]{1,0:T(8,128)(2,1)} %bitcast.129, bf16[192,1536]{1,0:T(8,128)(2,1)} %bitcast.130, bf16[192,1536]{1,0:T(8,128)(2,1)} %bitcast.131), kind=kLoop, calls=%fused_computation.10 | loop fusion | flops 5308416 | bytes 3538944 | tf_op jit(solution)/shard_map/concatenate | solution.py:77
  11.9 1.3 collective-permute-start.1
  13.1 4.9 %collective-permute-start = (bf16[2,1,64,128]{3,2,1,0:T(8,128)(2,1)S(1)}, bf16[2,1,64,128]{3,2,1,0:T(8,128)(2,1)S(1)}, u32[]{:S(2)}, u32[]{:S(2)}) collective-permute-start(bf16[2,1,64,128]{3,2,1,0:T(8,128)(2,1)S(1)} %get-tuple-element.15), channel_id=1, source_target_pairs={{0,1},{1,2},{2,3},{3,4},{4,5},{5,6},{6,7},{7,8},{8,9},{9,10},{10,1... | collective-permute-start | bytes 98312 | tf_op jit(solution)/shard_map/ppermute | solution.py:22
  19.7 1.9 collective-permute-start.2
  23.1 3.6 %collective-permute-done.2 = bf16[2,6,64,128]{3,2,1,0:T(8,128)(2,1)S(1)} collective-permute-done((bf16[2,6,64,128]{3,2,1,0:T(8,128)(2,1)S(1)}, bf16[2,6,64,128]{3,2,1,0:T(8,128)(2,1)S(1)}, u32[]{:S(2)}, u32[]{:S(2)}) %collective-permute-start.2) | collective-permute-done | bytes 196640 | tf_op jit(solution)/shard_map/ppermute | solution.py:22
  28.8 47.1 %all-gather.5.cloned.1.call-done = bf16[4608,128]{1,0:T(8,128)(2,1)} async-done(((bf16[288,128]{1,0:T(8,128)(2,1)}), bf16[4608,128]{1,0:T(8,128)(2,1)}) %all-gather.5.cloned.1.call-update) | async-done | bytes 1179664 | tf_op jit(solution)/shard_map/all_gather | solution.py:81
  75.9 1.0 slice.202
  77.9 28.4 %all_to_all.10 = bf16[64,2,1536]{2,1,0:T(2,128)(2,1)S(1)} all-to-all(bf16[64,2,1536]{2,1,0:T(2,128)(2,1)S(1)} %reshape.67), channel_id=1, replica_groups=mesh['yh'=2,'x'=4,'c'=2,'yl'=4,'z'=8] {'yh','yl','z'}, dimensions={0} | all-to-all | bytes 786432 | tf_op jit(solution)/shard_map/all_to_all | solution.py:95
  106.5 1.9 collective-permute-start.3
  108.4 1.7 collective-permute-done.3
  111.0 42.4 %all-gather.7.cloned.1.call-done = bf16[2304,1536]{1,0:T(8,128)(2,1)} async-done(((bf16[576,1536]{1,0:T(8,128)(2,1)}), bf16[2304,1536]{1,0:T(8,128)(2,1)}) %all-gather.7.cloned.1.call-update) | async-done | bytes 7077904 | tf_op jit(solution)/shard_map/all_gather | solution.py:78
  153.4 1.5 fusion.7
  154.9 1.5 fusion.9
  156.4 1.5 fusion.5
  157.9 1.5 fusion.12
  159.3 2.4 %fusion.11 = f32[256,1536]{1,0:T(8,128)S(1)} fusion(bf16[4,576,1536]{2,1,0:T(8,128)(2,1)} %bitcast.116, f32[256,192]{0,1:T(8,128)S(1)} %fusion.12, bf16[256,1536]{1,0:T(8,128)(2,1)S(1)} %constant_dynamic-update-slice_fusion.4), kind=kOutput, calls=%fused_computation.35 | convolution fusion | flops 302284800 | bytes 3735552 | tf_op jit(solution)/shard_map/dot_general | solution.py:16
  161.8 3.7 %convolution_add_fusion.2 = f32[256,1536]{1,0:T(8,128)} fusion(f32[256,1536]{1,0:T(8,128)S(1)} %fusion.11, bf16[4,576,1536]{2,1,0:T(8,128)(2,1)} %bitcast.117, f32[256,192]{0,1:T(8,128)S(1)} %fusion.9, bf16[256,1536]{1,0:T(8,128)(2,1)S(1)} %constant_dynamic-update-slice_fusion.4), kind=kOutput, calls=%fused_computation.3 | convolution fusion | flops 302678016 | bytes 5308416 | tf_op jit(solution)/shard_map/dot_general | solution.py:16
  165.4 2.9 %convolution_add_fusion.1 = f32[256,1536]{1,0:T(8,128)S(1)} fusion(f32[256,1536]{1,0:T(8,128)} %convolution_add_fusion.2, bf16[4,576,1536]{2,1,0:T(8,128)(2,1)} %bitcast.118, f32[256,192]{0,1:T(8,128)S(1)} %fusion.7, bf16[256,1536]{1,0:T(8,128)(2,1)S(1)} %constant_dynamic-update-slice_fusion.4), kind=kOutput, calls=%fused_computation.2 | convolution fusion | flops 302678016 | bytes 5308416 | tf_op jit(solution)/shard_map/dot_general | solution.py:16
  168.4 2.4 %fusion.1 = bf16[256,1536]{1,0:T(8,128)(2,1)S(1)} fusion(f32[256,1536]{1,0:T(8,128)S(1)} %convolution_add_fusion.1, f32[256]{0:T(256)} %add_divide_fusion, bf16[4,576,1536]{2,1,0:T(8,128)(2,1)} %bitcast.119, f32[256,192]{0,1:T(8,128)S(1)} %fusion.5, bf16[256,1536]{1,0:T(8,128)(2,1)S(1)} %constant_dynamic-update-slice_fusion.4), kind=kOutput, calls=%fused_computation.4 | convolution fusion | flops 303464448 | bytes 4523008 | tf_op jit(solution)/shard_map/dot_general | solution.py:16
  170.8 1.9 collective-permute-start.4
  172.7 1.7 collective-permute-done.4
  174.7 30.5 %all_to_all.11 = bf16[64,2,1536]{2,1,0:T(2,128)(2,1)S(1)} all-to-all(bf16[64,2,1536]{2,1,0:T(2,128)(2,1)S(1)} %reshape.70), channel_id=1, replica_groups=mesh['yh'=2,'x'=4,'c'=2,'yl'=4,'z'=8] {'yh','yl','z'}, dimensions={0} | all-to-all | bytes 786432 | tf_op jit(solution)/shard_map/all_to_all | solution.py:112
  205.3 0.9 convolution_convert_fusion.1
  (76 shorter events, 8.4 us)
Async XLA Ops:
  6.5 103.6 %copy-start = (bf16[2,1536,1]{1,0,2:T(2,128)(2,1)S(1)}, bf16[2,1536,1]{1,0,2:T(2,128)(2,1)}, u32[]{:S(2)}) copy-start(bf16[2,1536,1]{1,0,2:T(2,128)(2,1)} %param.15) | copy-start | bytes 18436
  6.5 69.4 %all-gather.5.cloned.1.call-start = ((), (), s32[]{:S(2)}) async-start(), calls=%async_computation.2 | async-start | bytes 1253376 | tf_op jit(solution)/shard_map/all_gather | solution.py:81
  8.0 145.4 %all-gather.7.cloned.1.call-start = ((), (), s32[]{:S(2)}) async-start(), calls=%async_computation.3 | async-start | bytes 8847360 | tf_op jit(solution)/shard_map/all_gather | solution.py:78
  10.9 0.9 copy-start.1
  10.9 7.1 %copy-start.5 = (s32[64,2]{0,1:T(2,128)S(1)}, s32[64,2]{0,1:T(2,128)}, u32[]{:S(2)}) copy-start(s32[64,2]{0,1:T(2,128)} %param.19) | copy-start | bytes 1540
  10.9 7.8 %copy-start.2 = (bf16[3,3,3,128,128]{4,3,2,1,0:T(8,128)(2,1)S(1)}, bf16[3,3,3,128,128]{4,3,2,1,0:T(8,128)(2,1)}, u32[]{:S(2)}) copy-start(bf16[3,3,3,128,128]{4,3,2,1,0:T(8,128)(2,1)} %param.11) | copy-start | bytes 2654212
  11.9 7.8 %collective-permute-start.1 = (bf16[2,1,64,128]{3,2,1,0:T(8,128)(2,1)S(1)}, bf16[2,1,64,128]{3,2,1,0:T(8,128)(2,1)S(1)}, u32[]{:S(2)}, u32[]{:S(2)}) collective-permute-start(bf16[2,1,64,128]{3,2,1,0:T(8,128)(2,1)S(1)} %get-tuple-element.14), channel_id=1, source_target_pairs={{1,0},{2,1},{3,2},{4,3},{5,4},{6,5},{7,6},{8,7},{9,8},{10,9},{11,1... | collective-permute-start | bytes 98312 | tf_op jit(solution)/shard_map/ppermute | solution.py:22
  13.1 6.5 %collective-permute-start = (bf16[2,1,64,128]{3,2,1,0:T(8,128)(2,1)S(1)}, bf16[2,1,64,128]{3,2,1,0:T(8,128)(2,1)S(1)}, u32[]{:S(2)}, u32[]{:S(2)}) collective-permute-start(bf16[2,1,64,128]{3,2,1,0:T(8,128)(2,1)S(1)} %get-tuple-element.15), channel_id=1, source_target_pairs={{0,1},{1,2},{2,3},{3,4},{4,5},{5,6},{6,7},{7,8},{8,9},{9,10},{10,1... | collective-permute-start | bytes 98312 | tf_op jit(solution)/shard_map/ppermute | solution.py:22
  19.7 7.0 %collective-permute-start.2 = (bf16[2,6,64,128]{3,2,1,0:T(8,128)(2,1)S(1)}, bf16[2,6,64,128]{3,2,1,0:T(8,128)(2,1)S(1)}, u32[]{:S(2)}, u32[]{:S(2)}) collective-permute-start(bf16[2,6,64,128]{3,2,1,0:T(8,128)(2,1)S(1)} %constant_dynamic-update-slice_fusion), channel_id=1, source_target_pairs={{0,32},{32,64},{64,96},{96,128},{128,160},{160,192},{192,224},{224... | collective-permute-start | bytes 589832 | tf_op jit(solution)/shard_map/ppermute | solution.py:22
  27.6 0.7 copy-start.4
  28.2 48.8 %copy-start.3 = (bf16[64,1536]{1,0:T(8,128)(2,1)S(1)}, bf16[64,1536]{1,0:T(8,128)(2,1)}, u32[]{:S(2)}) copy-start(bf16[64,1536]{1,0:T(8,128)(2,1)} %param.14) | copy-start | bytes 589828
  106.5 3.6 %collective-permute-start.3 = (bf16[128,1536]{1,0:T(8,128)(2,1)S(1)}, bf16[128,1536]{1,0:T(8,128)(2,1)S(1)}, u32[]{:S(2)}, u32[]{:S(2)}) collective-permute-start(bf16[128,1536]{1,0:T(8,128)(2,1)S(1)} %reshape.68), channel_id=1, source_target_pairs={{0,32},{32,0},{1,33},{33,1},{2,34},{34,2},{3,35},{35,3},{4,36},{36... | collective-permute-start | bytes 1179656 | tf_op jit(solution)/shard_map/ppermute | solution.py:98
  170.8 3.6 %collective-permute-start.4 = (bf16[128,1536]{1,0:T(8,128)(2,1)S(1)}, bf16[128,1536]{1,0:T(8,128)(2,1)S(1)}, u32[]{:S(2)}, u32[]{:S(2)}) collective-permute-start(bf16[128,1536]{1,0:T(8,128)(2,1)S(1)} %slice.215), channel_id=1, source_target_pairs={{0,32},{32,0},{1,33},{33,1},{2,34},{34,2},{3,35},{35,3},{4,36},{36... | collective-permute-start | bytes 1179656 | tf_op jit(solution)/shard_map/ppermute | solution.py:110
Sparse Core Ops, SparseCore 0:
  10.7 65.2 all-gather.4
  78.0 75.3 all-gather.6

commit v2 on v1

--- a/solution.py
+++ b/solution.py
@@ -1,6 +1,10 @@
+import functools
+
 import jax
 import jax.numpy as jnp
 from jax import lax
+from jax.experimental import pallas as pl
+from jax.experimental.pallas import tpu as pltpu
 from jax.sharding import Mesh, PartitionSpec as P
 
 FRAME = ("yh", "x", "c")
@@ -10,6 +14,8 @@
 NAMES = ("yh", "x", "c", "yl", "z")
 BF = jnp.bfloat16
 F32 = jnp.float32
+SWAP = [(0, 1), (1, 0)]
+VMEM_BYTES = 40 * 1024 * 1024
 
 
 def dot(a, b, dims=((1,), (0,))):
@@ -20,6 +26,10 @@
     count = lax.axis_size(axes)
     pairs = [(i, i + step) for i in range(count) if 0 <= i + step < count]
     return lax.ppermute(value, axes, pairs)
+
+
+def ring(value, step):
+    return lax.ppermute(value, "x", [(i, (i - step) % 4) for i in range(4)])
 
 
 def encode(video, conv_weight, latent_weight):
@@ -55,6 +65,46 @@
     slots = jnp.arange(experts * capacity, dtype=jnp.int32)[None, :]
     hit = (place[:, :1] == slots) | (place[:, 1:] == slots)
     return hit.astype(BF)
+
+
+def dispatch_kernel(at_ref, own_ref, other_ref, patches_ref, context_ref, table_ref, out_ref, embed_ref):
+    yh, x, c = at_ref[0], at_ref[1], at_ref[2]
+    for shard in range(16):
+        away = jnp.abs(shard // 8 - yh)
+        turn = lax.rem(shard // 2 % 4 - x + 4, 4)
+        near = own_ref[away, turn]
+        far = other_ref[away, turn]
+        embed_ref[shard] = jnp.where(shard % 2 == c, near, far)
+    width = context_ref.shape[1]
+    embed = embed_ref[...].reshape(width, embed_ref.shape[2])
+    embedded = dot(patches_ref[...], embed, ((1,), (1,))).astype(BF)
+    total = embedded.astype(F32) + context_ref[...].astype(F32)
+    meansq = jnp.mean(total * total, axis=1, keepdims=True)
+    tokens = (total * lax.rsqrt(meansq + 1e-06)).astype(BF)
+    out_ref[...] = dot(table_ref[...], tokens, ((0,), (0,))).astype(BF)
+
+
+def expert_kernel(at_ref, inputs_ref, score_ref, held_ref, d0_ref, d1_ref, d2_ref, d3_ref, other_ref, own_ref, hidden_ref):
+    step = pl.program_id(0)
+    share = d0_ref.shape[0]
+    both = dot(held_ref[0], inputs_ref[...])
+    gate, up = both[:share], both[share:]
+    hidden_ref[step] = (gate / (1.0 + jnp.exp(-gate)) * up).astype(BF).T
+
+    @pl.when(step == pl.num_programs(0) - 1)
+    def _():
+        rows, width = other_ref.shape
+        tile = 512
+        score = score_ref[...]
+        for at in range(0, width, tile):
+            part = slice(at, at + tile)
+            total = dot(hidden_ref[0], d0_ref[:, part])
+            total += dot(hidden_ref[1], d1_ref[:, part])
+            total += dot(hidden_ref[2], d2_ref[:, part])
+            total += dot(hidden_ref[3], d3_ref[:, part])
+            total = (total * score).astype(BF)
+            other_ref[:, part] = total[:rows]
+            own_ref[:, part] = total[rows:]
 
 
 def local(
@@ -72,45 +122,73 @@
     rows, cols = video.shape[1:3]
     tok, width = context.shape
     experts, capacity = 64, 2
+    slots = experts * capacity
     share = down_weight.shape[1]
-
-    held = jnp.concatenate([gate_weight[0].T, up_weight[0].T, down_weight[0]], axis=0)
+    yh, x, c = lax.axis_index("yh"), lax.axis_index("x"), lax.axis_index("c")
+
+    held = jnp.concatenate([gate_weight[0].T, up_weight[0].T], axis=0)
     held = lax.all_gather(held, "x", axis=0, tiled=False)
 
     part = embed_weight.T
-    spread = lax.all_gather(jnp.concatenate([part] * 3, axis=0), FRAME, axis=0, tiled=False)
-    embed = spread[:, : part.shape[0]].reshape(width, part.shape[1])
+    around = jnp.stack([part, ring(part, 1), ring(part, 2), ring(part, 3)])
+    near = jnp.stack([around, lax.ppermute(around, "yh", SWAP)])
+    far = lax.ppermute(near, "c", SWAP)
+
+    d0 = down_weight[0]
+    behind, ahead = ring(d0, -1), ring(d0, 1)
+    opposite = jnp.concatenate([ring(behind[: share // 2], -1), ring(ahead[share // 2 :], 1)], axis=0)
 
     table = place_table(routes, experts, capacity)
     latent = encode(video, conv_weight, latent_weight)
     lat = latent.shape[1]
     blocks = latent.reshape(2, rows // 2, 2, cols // 2, 2, lat)
     patches = blocks.transpose(1, 3, 0, 2, 4, 5).reshape(tok, 8 * lat)
-    embedded = dot(patches, embed, ((1,), (1,))).astype(BF)
-    total = embedded.astype(F32) + context.astype(F32)
-    meansq = jnp.mean(total * total, axis=1, keepdims=True)
-    tokens = (total * lax.rsqrt(meansq + 1e-06)).astype(BF)
-
-    outgoing = dot(table, tokens, ((0,), (0,))).astype(BF).reshape(experts, capacity, width)
-    arrived = lax.all_to_all(outgoing, SOURCES, split_axis=0, concat_axis=0, tiled=True)
-    mine = arrived.reshape(experts * capacity, width)
-    swap = [(0, 1), (1, 0)]
-    theirs = lax.ppermute(mine, "c", swap)
+
+    vmem = pl.BlockSpec(memory_space=pltpu.VMEM)
+    outgoing = pl.pallas_call(
+        dispatch_kernel,
+        out_shape=jax.ShapeDtypeStruct((slots, width), BF),
+        in_specs=[pl.BlockSpec(memory_space=pltpu.SMEM)] + [vmem] * 5,
+        out_specs=vmem,
+        scratch_shapes=[pltpu.VMEM((16, *part.shape), BF)],
+        compiler_params=pltpu.CompilerParams(vmem_limit_bytes=VMEM_BYTES),
+    )(jnp.stack([yh, x, c]).astype(jnp.int32), near, far, patches, context, table)
+
+    arrived = lax.all_to_all(outgoing.reshape(experts, capacity, width), SOURCES, split_axis=0, concat_axis=0, tiled=True)
+    mine = arrived.reshape(slots, width)
+    theirs = lax.ppermute(mine, "c", SWAP)
     inputs = jnp.concatenate([theirs, mine], axis=0)
-    router = lax.dynamic_index_in_dim(router_weight, lax.axis_index("yh"), 0, keepdims=False)
+    router = lax.dynamic_index_in_dim(router_weight, yh, 0, keepdims=False)
     score = jax.nn.sigmoid(dot(inputs, router))
-    result = jnp.zeros((2 * experts * capacity, width), F32)
-    for chunk in range(held.shape[0]):
-        gate = dot(inputs, held[chunk, :share], ((1,), (1,)))
-        up = dot(inputs, held[chunk, share : 2 * share], ((1,), (1,)))
-        hidden = (jax.nn.silu(gate) * up).astype(BF)
-        result = result + dot(hidden, held[chunk, 2 * share :])
-    result = (score * result).astype(BF)
-    other, own = result[: experts * capacity], result[experts * capacity :]
-    back = lax.ppermute(other, "c", swap)
+
+    order = jnp.stack([x, x + 3, x + 2, x + 1]).astype(jnp.int32) % 4
+    down = pl.BlockSpec((share, width), lambda i, at: (0, 0))
+    half = pl.BlockSpec((slots, width), lambda i, at: (0, 0))
+    other, own = pl.pallas_call(
+        expert_kernel,
+        out_shape=[jax.ShapeDtypeStruct((slots, width), BF)] * 2,
+        grid_spec=pltpu.PrefetchScalarGridSpec(
+            num_scalar_prefetch=1,
+            grid=(4,),
+            in_specs=[
+                pl.BlockSpec((width, 2 * slots), lambda i, at: (0, 0)),
+                pl.BlockSpec((2 * slots, 1), lambda i, at: (0, 0)),
+                pl.BlockSpec((1, 2 * share, width), lambda i, at: (at[i], 0, 0)),
+                down,
+                down,
+                down,
+                down,
+            ],
+            out_specs=[half, half],
+            scratch_shapes=[pltpu.VMEM((4, 2 * slots, share), BF)],
+        ),
+        compiler_params=pltpu.CompilerParams(vmem_limit_bytes=VMEM_BYTES),
+    )(order, inputs.T, score, held, d0, behind, opposite, ahead)
+
+    back = lax.ppermute(other, "c", SWAP)
     summed = (back.astype(F32) + own.astype(F32)).astype(BF).reshape(experts, capacity, width)
     homeward = lax.all_to_all(summed, SOURCES, split_axis=0, concat_axis=0, tiled=True)
-    return dot(table, homeward.reshape(experts * capacity, width)).astype(BF)
+    return dot(table, homeward.reshape(slots, width)).astype(BF)
 
 
 def solution(mesh):

time: 215 us -> 164 us (0.76)
  the two profiles are of different devices: /device:TPU:6 before, /device:TPU:16 now
where the time goes in v2:
time: 164 us; the launch traced here: 163 us
  starting transfers between devices  65.5 us (40%)
  waiting for transfers between devices  30.7 us (19%)
  blocking collectives  29.4 us (18%)
  between operations  14 us (9%)
  local copies, waits for them, and re-layouts  10 us (6%)
  other arithmetic  5.24 us (3%)
  Pallas kernels  4.85 us (3%)
  matrix products  3.3 us (2%)
    all_to_all x1, blocking collectives, local(): lax.all_to_all(summed, SOURCES, split_axis=0, concat_axis=0, tiled=True)  29.4 us
    ppermute x7, waiting for transfers between devices, ring(): return lax.ppermute(value, 'x', [(i, (i - step) % 4) for i in range(4)])  28.3 us
    ppermute x7, starting transfers between devices, ring(): return lax.ppermute(value, 'x', [(i, (i - step) % 4) for i in range(4)])  23.2 us
    all_to_all x1, starting transfers between devices, local(): lax.all_to_all(outgoing.reshape(experts, capacity, width), SOURCES, split...  15.1 us
    ppermute x3, starting transfers between devices, shifted(): return lax.ppermute(value, axes, pairs)  14 us
    ppermute x1, starting transfers between devices, local(): near = jnp.stack([around, lax.ppermute(around, 'yh', SWAP)])  6.83 us
    unnamed x39, local copies, waits for them, and re-layouts  4.71 us
    pallas_call x1, Pallas kernels, local(): pl.pallas_call(expert_kernel, out_shape=[jax.ShapeDtypeStruct((slots, wid...  3.69 us
  transfers between devices with their start and end apart: 16, of which 4 were waited for; matrix products, arithmetic and copies ran while one was open for 8% of the time, Pallas kernels for 1%

profile of v2, /device:TPU:16, one launch (start us, length us, event | category | flops | bytes accessed | tf_op | source)
XLA Modules:
  0.0 163.1 jit_solution(11723209701393042389)
XLA Ops:
  6.5 3.5 %collective-permute-start.2 = (bf16[96,128]{1,0:T(8,128)(2,1)}, bf16[96,128]{1,0:T(8,128)(2,1)S(1)}, u32[]{:S(2)}, u32[]{:S(2)}) collective-permute-start(bf16[96,128]{1,0:T(8,128)(2,1)} %bitcast.80), channel_id=1, source_target_pairs={{0,64},{64,128},{128,192},{192,0},{1,65},{65,129},{129,193},{193,1... | collective-permute-start | bytes 73736 | tf_op jit(solution)/shard_map/ppermute | solution.py:32
  10.1 4.6 %collective-permute-start.1 = (bf16[96,128]{1,0:T(8,128)(2,1)}, bf16[96,128]{1,0:T(8,128)(2,1)S(1)}, u32[]{:S(2)}, u32[]{:S(2)}) collective-permute-start(bf16[96,128]{1,0:T(8,128)(2,1)} %bitcast.81), channel_id=1, source_target_pairs={{0,128},{64,192},{128,0},{192,64},{1,129},{65,193},{129,1},{193,65... | collective-permute-start | bytes 73736 | tf_op jit(solution)/shard_map/ppermute | solution.py:32
  14.7 3.3 %collective-permute-start = (bf16[96,128]{1,0:T(8,128)(2,1)}, bf16[96,128]{1,0:T(8,128)(2,1)S(1)}, u32[]{:S(2)}, u32[]{:S(2)}) collective-permute-start(bf16[96,128]{1,0:T(8,128)(2,1)} %bitcast.82), channel_id=1, source_target_pairs={{0,192},{64,0},{128,64},{192,128},{1,193},{65,1},{129,65},{193,129... | collective-permute-start | bytes 73736 | tf_op jit(solution)/shard_map/ppermute | solution.py:32
  18.9 4.3 %collective-permute-start.5 = (bf16[2,1,64,128]{3,2,1,0:T(8,128)(2,1)S(1)}, bf16[2,1,64,128]{3,2,1,0:T(8,128)(2,1)S(1)}, u32[]{:S(2)}, u32[]{:S(2)}) collective-permute-start(bf16[2,1,64,128]{3,2,1,0:T(8,128)(2,1)S(1)} %get-tuple-element.19), channel_id=1, source_target_pairs={{0,1},{1,2},{2,3},{3,4},{4,5},{5,6},{6,7},{7,8},{8,9},{9,10},{10,1... | collective-permute-start | bytes 98312 | tf_op jit(solution)/shard_map/ppermute | solution.py:28
  23.1 8.5 %collective-permute-start.6 = (bf16[2,1,64,128]{3,2,1,0:T(8,128)(2,1)S(1)}, bf16[2,1,64,128]{3,2,1,0:T(8,128)(2,1)S(1)}, u32[]{:S(2)}, u32[]{:S(2)}) collective-permute-start(bf16[2,1,64,128]{3,2,1,0:T(8,128)(2,1)S(1)} %get-tuple-element.18), channel_id=1, source_target_pairs={{1,0},{2,1},{3,2},{4,3},{5,4},{6,5},{7,6},{8,7},{9,8},{10,9},{11,1... | collective-permute-start | bytes 98312 | tf_op jit(solution)/shard_map/ppermute | solution.py:28
  31.6 2.4 %pad_maximum_fusion = bf16[384,1536]{1,0:T(8,128)(2,1)} fusion(bf16[192,1536]{1,0:T(8,128)(2,1)} %bitcast.76, bf16[192,1536]{1,0:T(8,128)(2,1)} %bitcast.77), kind=kLoop, calls=%fused_computation.1 | loop fusion | flops 2359296 | bytes 2359296 | tf_op jit(solution)/shard_map/concatenate | solution.py:129
  36.2 6.8 %collective-permute-start.3 = (bf16[4,96,128]{2,1,0:T(8,128)(2,1)S(1)}, bf16[4,96,128]{2,1,0:T(8,128)(2,1)S(1)}, u32[]{:S(2)}, u32[]{:S(2)}) collective-permute-start(bf16[4,96,128]{2,1,0:T(8,128)(2,1)S(1)} %get-tuple-element.21), channel_id=1, source_target_pairs={{0,256},{256,0},{1,257},{257,1},{2,258},{258,2},{3,259},{259,3},{4... | collective-permute-start | bytes 294920 | tf_op jit(solution)/shard_map/ppermute | solution.py:134
  43.2 1.3 collective-permute-start.7
  46.7 2.6 %collective-permute-start.4 = (bf16[2,4,96,128]{3,2,1,0:T(8,128)(2,1)S(1)}, bf16[2,4,96,128]{3,2,1,0:T(8,128)(2,1)S(1)}, u32[]{:S(2)}, u32[]{:S(2)}) collective-permute-start(bf16[2,4,96,128]{3,2,1,0:T(8,128)(2,1)S(1)} %pad_maximum_fusion.5.own_ref), channel_id=1, source_target_pairs={{0,32},{32,0},{1,33},{33,1},{2,34},{34,2},{3,35},{35,3},{4,36},{36... | collective-permute-start | bytes 589832 | tf_op jit(solution)/shard_map/ppermute | solution.py:135
  51.6 1.2 shard_map.100
  53.6 15.1 %all-to-all-start = ((bf16[64,2,1536]{2,1,0:T(2,128)(2,1)}), bf16[64,2,1536]{2,1,0:T(2,128)(2,1)S(1)}, u32[]{:S(2)}, u32[]{:S(2)}) async-start(bf16[64,2,1536]{2,1,0:T(2,128)(2,1)} %reshape.54), calls=%async_computation | async-start | bytes 786432 | tf_op jit(solution)/shard_map/all_to_all | solution.py:157
  68.7 1.9 %collective-permute-start.11 = (bf16[192,1536]{1,0:T(8,128)(2,1)S(1)}, bf16[192,1536]{1,0:T(8,128)(2,1)S(1)}, u32[]{:S(2)}, u32[]{:S(2)}) collective-permute-start(bf16[192,1536]{1,0:T(8,128)(2,1)S(1)} %bitcast.61), channel_id=1, source_target_pairs={{0,192},{64,0},{128,64},{192,128},{1,193},{65,1},{129,65},{193,129... | collective-permute-start | bytes 1769480 | tf_op jit(solution)/shard_map/ppermute | solution.py:32
  70.7 3.9 %collective-permute-start.9 = (bf16[192,1536]{1,0:T(8,128)(2,1)S(1)}, bf16[192,1536]{1,0:T(8,128)(2,1)S(1)}, u32[]{:S(2)}, u32[]{:S(2)}) collective-permute-start(bf16[192,1536]{1,0:T(8,128)(2,1)S(1)} %bitcast.62), channel_id=1, source_target_pairs={{0,64},{64,128},{128,192},{192,0},{1,65},{65,129},{129,193},{193,1... | collective-permute-start | bytes 1769480 | tf_op jit(solution)/shard_map/ppermute | solution.py:32
  74.6 23.2 %collective-permute-done.11.d3_ref = bf16[192,1536]{1,0:T(8,128)(2,1)S(1)} collective-permute-done((bf16[192,1536]{1,0:T(8,128)(2,1)S(1)}, bf16[192,1536]{1,0:T(8,128)(2,1)S(1)}, u32[]{:S(2)}, u32[]{:S(2)}) %collective-permute-start.11) | collective-permute-done | bytes 589856 | tf_op jit(solution)/shard_map/ppermute | solution.py:32
  98.5 3.2 %collective-permute-start.12 = (bf16[96,1536]{1,0:T(8,128)(2,1)}, bf16[96,1536]{1,0:T(8,128)(2,1)}, u32[]{:S(2)}, u32[]{:S(2)}) collective-permute-start(bf16[96,1536]{1,0:T(8,128)(2,1)} %slice.151), channel_id=1, source_target_pairs={{0,192},{64,0},{128,64},{192,128},{1,193},{65,1},{129,65},{193,129... | collective-permute-start | bytes 884744 | tf_op jit(solution)/shard_map/ppermute | solution.py:32
  102.5 2.6 %collective-permute-start.10 = (bf16[96,1536]{1,0:T(8,128)(2,1)}, bf16[96,1536]{1,0:T(8,128)(2,1)}, u32[]{:S(2)}, u32[]{:S(2)}) collective-permute-start(bf16[96,1536]{1,0:T(8,128)(2,1)} %slice.150), channel_id=1, source_target_pairs={{0,64},{64,128},{128,192},{192,0},{1,65},{65,129},{129,193},{193,1... | collective-permute-start | bytes 884744 | tf_op jit(solution)/shard_map/ppermute | solution.py:32
  105.5 1.9 %collective-permute-start.8 = (bf16[128,1536]{0,1:T(8,128)(2,1)S(1)}, bf16[128,1536]{0,1:T(8,128)(2,1)S(1)}, u32[]{:S(2)}, u32[]{:S(2)}) collective-permute-start(bf16[128,1536]{0,1:T(8,128)(2,1)S(1)} %copy.22), channel_id=1, source_target_pairs={{0,32},{32,0},{1,33},{33,1},{2,34},{34,2},{3,35},{35,3},{4,36},{36... | collective-permute-start | bytes 1179656 | tf_op jit(solution)/shard_map/ppermute | solution.py:159
  107.5 5.1 %collective-permute-done.10 = bf16[96,1536]{1,0:T(8,128)(2,1)} collective-permute-done((bf16[96,1536]{1,0:T(8,128)(2,1)}, bf16[96,1536]{1,0:T(8,128)(2,1)}, u32[]{:S(2)}, u32[]{:S(2)}) %collective-permute-start.10) | collective-permute-done | bytes 294944 | tf_op jit(solution)/shard_map/ppermute | solution.py:32
  114.6 1.2 fusion.2.inputs_ref
  115.9 2.3 %copy-done.1 = bf16[1536,1536]{1,0:T(8,128)(2,1)S(1)} copy-done((bf16[1536,1536]{1,0:T(8,128)(2,1)S(1)}, bf16[1536,1536]{1,0:T(8,128)(2,1)}, u32[]{:S(2)}) %copy-start.1) | copy-done | bytes 4718616
  118.2 3.7 %shard_map.101 = (bf16[128,1536]{1,0:T(8,128)(2,1)S(1)}, bf16[128,1536]{1,0:T(8,128)(2,1)S(1)}) custom-call(s32[4]{0:T(128)S(1)} %and_select_fusion.at_ref, bf16[1536,256]{1,0:T(8,128)(2,1)S(1)} %fusion.2.inputs_ref, f32[256,1]{1,0:T(8,128)S(1)} %copy.24.score_ref, bf16[4,384,1536]{2,1,0:T(8,128)(2,1)S(1)} %bitcast.60, bf16[192,1536]{1,0:T(8,128)(2,1)S(1)} %bitcast.63, ...), custom_call_target="tpu_custom_call" | custom-call | tf_op jit(solution)/shard_map/pallas_call | solution.py:167
  121.9 1.9 %collective-permute-start.13 = (bf16[128,1536]{1,0:T(8,128)(2,1)S(1)}, bf16[128,1536]{1,0:T(8,128)(2,1)S(1)}, u32[]{:S(2)}, u32[]{:S(2)}) collective-permute-start(bf16[128,1536]{1,0:T(8,128)(2,1)S(1)} %get-tuple-element.7), channel_id=1, source_target_pairs={{0,32},{32,0},{1,33},{33,1},{2,34},{34,2},{3,35},{35,3},{4,36},{36... | collective-permute-start | bytes 1179656 | tf_op jit(solution)/shard_map/ppermute | solution.py:188
  123.8 1.7 %collective-permute-done.13 = bf16[128,1536]{1,0:T(8,128)(2,1)S(1)} collective-permute-done((bf16[128,1536]{1,0:T(8,128)(2,1)S(1)}, bf16[128,1536]{1,0:T(8,128)(2,1)S(1)}, u32[]{:S(2)}, u32[]{:S(2)}) %collective-permute-start.13) | collective-permute-done | bytes 393248 | tf_op jit(solution)/shard_map/ppermute | solution.py:188
  125.7 29.4 %all_to_all.10 = bf16[64,2,1536]{2,1,0:T(2,128)(2,1)S(1)} all-to-all(bf16[64,2,1536]{2,1,0:T(2,128)(2,1)S(1)} %reshape.57), channel_id=1, replica_groups=mesh['yh'=2,'x'=4,'c'=2,'yl'=4,'z'=8] {'yh','yl','z'}, dimensions={0} | all-to-all | bytes 786432 | tf_op jit(solution)/shard_map/all_to_all | solution.py:190
  (100 shorter events, 13.4 us)
Async XLA Ops:
  6.5 107.2 %copy-start = (bf16[2,1536,1]{1,0,2:T(2,128)(2,1)S(1)}, bf16[2,1536,1]{1,0,2:T(2,128)(2,1)}, u32[]{:S(2)}) copy-start(bf16[2,1536,1]{1,0,2:T(2,128)(2,1)} %param.15) | copy-start | bytes 18436
  6.5 109.3 %all-gather.3.cloned.1.call-start = ((), (), s32[]{:S(2)}) async-start(), calls=%async_computation.2 | async-start | bytes 5898240 | tf_op jit(solution)/shard_map/all_gather | solution.py:130
  6.5 29.6 %collective-permute-start.2 = (bf16[96,128]{1,0:T(8,128)(2,1)}, bf16[96,128]{1,0:T(8,128)(2,1)S(1)}, u32[]{:S(2)}, u32[]{:S(2)}) collective-permute-start(bf16[96,128]{1,0:T(8,128)(2,1)} %bitcast.80), channel_id=1, source_target_pairs={{0,64},{64,128},{128,192},{192,0},{1,65},{65,129},{129,193},{193,1... | collective-permute-start | bytes 73736 | tf_op jit(solution)/shard_map/ppermute | solution.py:32
  10.1 26.1 %collective-permute-start.1 = (bf16[96,128]{1,0:T(8,128)(2,1)}, bf16[96,128]{1,0:T(8,128)(2,1)S(1)}, u32[]{:S(2)}, u32[]{:S(2)}) collective-permute-start(bf16[96,128]{1,0:T(8,128)(2,1)} %bitcast.81), channel_id=1, source_target_pairs={{0,128},{64,192},{128,0},{192,64},{1,129},{65,193},{129,1},{193,65... | collective-permute-start | bytes 73736 | tf_op jit(solution)/shard_map/ppermute | solution.py:32
  14.7 21.5 %collective-permute-start = (bf16[96,128]{1,0:T(8,128)(2,1)}, bf16[96,128]{1,0:T(8,128)(2,1)S(1)}, u32[]{:S(2)}, u32[]{:S(2)}) collective-permute-start(bf16[96,128]{1,0:T(8,128)(2,1)} %bitcast.82), channel_id=1, source_target_pairs={{0,192},{64,0},{128,64},{192,128},{1,193},{65,1},{129,65},{193,129... | collective-permute-start | bytes 73736 | tf_op jit(solution)/shard_map/ppermute | solution.py:32
  18.9 24.2 %collective-permute-start.5 = (bf16[2,1,64,128]{3,2,1,0:T(8,128)(2,1)S(1)}, bf16[2,1,64,128]{3,2,1,0:T(8,128)(2,1)S(1)}, u32[]{:S(2)}, u32[]{:S(2)}) collective-permute-start(bf16[2,1,64,128]{3,2,1,0:T(8,128)(2,1)S(1)} %get-tuple-element.19), channel_id=1, source_target_pairs={{0,1},{1,2},{2,3},{3,4},{4,5},{5,6},{6,7},{7,8},{8,9},{9,10},{10,1... | collective-permute-start | bytes 98312 | tf_op jit(solution)/shard_map/ppermute | solution.py:28
  23.1 20.0 %collective-permute-start.6 = (bf16[2,1,64,128]{3,2,1,0:T(8,128)(2,1)S(1)}, bf16[2,1,64,128]{3,2,1,0:T(8,128)(2,1)S(1)}, u32[]{:S(2)}, u32[]{:S(2)}) collective-permute-start(bf16[2,1,64,128]{3,2,1,0:T(8,128)(2,1)S(1)} %get-tuple-element.18), channel_id=1, source_target_pairs={{1,0},{2,1},{3,2},{4,3},{5,4},{6,5},{7,6},{8,7},{9,8},{10,9},{11,1... | collective-permute-start | bytes 98312 | tf_op jit(solution)/shard_map/ppermute | solution.py:28
  34.0 1.2 copy-start.6
  34.0 2.2 %copy-start.8 = (bf16[128,96]{0,1:T(8,128)(2,1)S(1)}, bf16[128,96]{0,1:T(8,128)(2,1)}, u32[]{:S(2)}) copy-start(bf16[128,96]{0,1:T(8,128)(2,1)} %param.13) | copy-start | bytes 73732
  35.2 7.9 %copy-start.4 = (bf16[2,4,64,128]{3,2,1,0:T(8,128)(2,1)S(1)}, bf16[2,4,64,128]{3,2,1,0:T(8,128)(2,1)}, u32[]{:S(2)}) copy-start(bf16[2,4,64,128]{3,2,1,0:T(8,128)(2,1)} %param.10) | copy-start | bytes 393220
  36.2 10.4 %collective-permute-start.3 = (bf16[4,96,128]{2,1,0:T(8,128)(2,1)S(1)}, bf16[4,96,128]{2,1,0:T(8,128)(2,1)S(1)}, u32[]{:S(2)}, u32[]{:S(2)}) collective-permute-start(bf16[4,96,128]{2,1,0:T(8,128)(2,1)S(1)} %get-tuple-element.21), channel_id=1, source_target_pairs={{0,256},{256,0},{1,257},{257,1},{2,258},{258,2},{3,259},{259,3},{4... | collective-permute-start | bytes 294920 | tf_op jit(solution)/shard_map/ppermute | solution.py:134
  43.2 6.1 %collective-permute-start.7 = (bf16[2,6,64,128]{3,2,1,0:T(8,128)(2,1)S(1)}, bf16[2,6,64,128]{3,2,1,0:T(8,128)(2,1)S(1)}, u32[]{:S(2)}, u32[]{:S(2)}) collective-permute-start(bf16[2,6,64,128]{3,2,1,0:T(8,128)(2,1)S(1)} %constant_dynamic-update-slice_fusion), channel_id=1, source_target_pairs={{0,32},{32,64},{64,96},{96,128},{128,160},{160,192},{192,224},{224... | collective-permute-start | bytes 589832 | tf_op jit(solution)/shard_map/ppermute | solution.py:28
  46.7 4.9 %collective-permute-start.4 = (bf16[2,4,96,128]{3,2,1,0:T(8,128)(2,1)S(1)}, bf16[2,4,96,128]{3,2,1,0:T(8,128)(2,1)S(1)}, u32[]{:S(2)}, u32[]{:S(2)}) collective-permute-start(bf16[2,4,96,128]{3,2,1,0:T(8,128)(2,1)S(1)} %pad_maximum_fusion.5.own_ref), channel_id=1, source_target_pairs={{0,32},{32,0},{1,33},{33,1},{2,34},{34,2},{3,35},{35,3},{4,36},{36... | collective-permute-start | bytes 589832 | tf_op jit(solution)/shard_map/ppermute | solution.py:135
  50.5 1.1 copy-start.3
  51.5 17.2 %copy-start.2 = (bf16[1,192,1536]{2,1,0:T(8,128)(2,1)S(1)}, bf16[1,192,1536]{2,1,0:T(8,128)(2,1)}, u32[]{:S(2)}) copy-start(bf16[1,192,1536]{2,1,0:T(8,128)(2,1)} %param.18) | copy-start | bytes 1769476
  53.6 51.4 %all-to-all-start = ((bf16[64,2,1536]{2,1,0:T(2,128)(2,1)}), bf16[64,2,1536]{2,1,0:T(2,128)(2,1)S(1)}, u32[]{:S(2)}, u32[]{:S(2)}) async-start(bf16[64,2,1536]{2,1,0:T(2,128)(2,1)} %reshape.54), calls=%async_computation | async-start | bytes 786432 | tf_op jit(solution)/shard_map/all_to_all | solution.py:157
  68.7 29.0 %collective-permute-start.11 = (bf16[192,1536]{1,0:T(8,128)(2,1)S(1)}, bf16[192,1536]{1,0:T(8,128)(2,1)S(1)}, u32[]{:S(2)}, u32[]{:S(2)}) collective-permute-start(bf16[192,1536]{1,0:T(8,128)(2,1)S(1)} %bitcast.61), channel_id=1, source_target_pairs={{0,192},{64,0},{128,64},{192,128},{1,193},{65,1},{129,65},{193,129... | collective-permute-start | bytes 1769480 | tf_op jit(solution)/shard_map/ppermute | solution.py:32
  70.7 31.1 %collective-permute-start.9 = (bf16[192,1536]{1,0:T(8,128)(2,1)S(1)}, bf16[192,1536]{1,0:T(8,128)(2,1)S(1)}, u32[]{:S(2)}, u32[]{:S(2)}) collective-permute-start(bf16[192,1536]{1,0:T(8,128)(2,1)S(1)} %bitcast.62), channel_id=1, source_target_pairs={{0,64},{64,128},{128,192},{192,0},{1,65},{65,129},{129,193},{193,1... | collective-permute-start | bytes 1769480 | tf_op jit(solution)/shard_map/ppermute | solution.py:32
  98.5 9.0 %collective-permute-start.12 = (bf16[96,1536]{1,0:T(8,128)(2,1)}, bf16[96,1536]{1,0:T(8,128)(2,1)}, u32[]{:S(2)}, u32[]{:S(2)}) collective-permute-start(bf16[96,1536]{1,0:T(8,128)(2,1)} %slice.151), channel_id=1, source_target_pairs={{0,192},{64,0},{128,64},{192,128},{1,193},{65,1},{129,65},{193,129... | collective-permute-start | bytes 884744 | tf_op jit(solution)/shard_map/ppermute | solution.py:32
  102.5 10.1 %collective-permute-start.10 = (bf16[96,1536]{1,0:T(8,128)(2,1)}, bf16[96,1536]{1,0:T(8,128)(2,1)}, u32[]{:S(2)}, u32[]{:S(2)}) collective-permute-start(bf16[96,1536]{1,0:T(8,128)(2,1)} %slice.150), channel_id=1, source_target_pairs={{0,64},{64,128},{128,192},{192,0},{1,65},{65,129},{129,193},{193,1... | collective-permute-start | bytes 884744 | tf_op jit(solution)/shard_map/ppermute | solution.py:32
  105.5 8.5 %copy-start.5 = (bf16[128,1536]{0,1:T(8,128)(2,1)}, bf16[128,1536]{0,1:T(8,128)(2,1)S(1)}, u32[]{:S(2)}) copy-start(bf16[128,1536]{0,1:T(8,128)(2,1)S(1)} %copy.22) | copy-start | bytes 1179652
  105.5 8.2 %collective-permute-start.8 = (bf16[128,1536]{0,1:T(8,128)(2,1)S(1)}, bf16[128,1536]{0,1:T(8,128)(2,1)S(1)}, u32[]{:S(2)}, u32[]{:S(2)}) collective-permute-start(bf16[128,1536]{0,1:T(8,128)(2,1)S(1)} %copy.22), channel_id=1, source_target_pairs={{0,32},{32,0},{1,33},{33,1},{2,34},{34,2},{3,35},{35,3},{4,36},{36... | collective-permute-start | bytes 1179656 | tf_op jit(solution)/shard_map/ppermute | solution.py:159
  115.8 2.3 %copy-start.1 = (bf16[1536,1536]{1,0:T(8,128)(2,1)S(1)}, bf16[1536,1536]{1,0:T(8,128)(2,1)}, u32[]{:S(2)}) copy-start(bf16[1536,1536]{1,0:T(8,128)(2,1)} %all-gather.3.cloned.1.call-done) | copy-start | bytes 14155780
  121.9 3.6 %collective-permute-start.13 = (bf16[128,1536]{1,0:T(8,128)(2,1)S(1)}, bf16[128,1536]{1,0:T(8,128)(2,1)S(1)}, u32[]{:S(2)}, u32[]{:S(2)}) collective-permute-start(bf16[128,1536]{1,0:T(8,128)(2,1)S(1)} %get-tuple-element.7), channel_id=1, source_target_pairs={{0,32},{32,0},{1,33},{33,1},{2,34},{34,2},{3,35},{35,3},{4,36},{36... | collective-permute-start | bytes 1179656 | tf_op jit(solution)/shard_map/ppermute | solution.py:188
  (3 other events, 2.2 us)
Sparse Core Ops, SparseCore 0:
  34.1 67.2 all-gather.2

commit v3 on v1

--- a/solution.py
+++ b/solution.py
@@ -1,6 +1,8 @@
 import jax
 import jax.numpy as jnp
 from jax import lax
+from jax.experimental import pallas as pl
+from jax.experimental.pallas import tpu as pltpu
 from jax.sharding import Mesh, PartitionSpec as P
 
 FRAME = ("yh", "x", "c")
@@ -10,6 +12,10 @@
 NAMES = ("yh", "x", "c", "yl", "z")
 BF = jnp.bfloat16
 F32 = jnp.float32
+SWAP = [(0, 1), (1, 0)]
+XOR1 = [(i, i ^ 1) for i in range(4)]
+XOR2 = [(i, i ^ 2) for i in range(4)]
+VMEM_BYTES = 40 * 1024 * 1024
 
 
 def dot(a, b, dims=((1,), (0,))):
@@ -20,6 +26,10 @@
     count = lax.axis_size(axes)
     pairs = [(i, i + step) for i in range(count) if 0 <= i + step < count]
     return lax.ppermute(value, axes, pairs)
+
+
+def ring(value, step):
+    return lax.ppermute(value, "x", [(i, (i - step) % 4) for i in range(4)])
 
 
 def encode(video, conv_weight, latent_weight):
@@ -55,6 +65,56 @@
     slots = jnp.arange(experts * capacity, dtype=jnp.int32)[None, :]
     hit = (place[:, :1] == slots) | (place[:, 1:] == slots)
     return hit.astype(BF)
+
+
+def dispatch_kernel(at_ref, near_ref, far_ref, patches_ref, context_ref, table_ref, out_ref, embed_ref):
+    me = at_ref[0]
+    for shard in range(16):
+        apart = shard ^ me
+        near, far = near_ref[apart // 2], far_ref[apart // 2]
+        embed_ref[shard] = jnp.where(apart % 2 == 0, near, far)
+    width = context_ref.shape[1]
+    embed = embed_ref[...].reshape(width, embed_ref.shape[2])
+    embedded = dot(patches_ref[...], embed, ((1,), (1,))).astype(BF)
+    total = embedded.astype(F32) + context_ref[...].astype(F32)
+    meansq = jnp.mean(total * total, axis=1, keepdims=True)
+    tokens = (total * lax.rsqrt(meansq + 1e-06)).astype(BF)
+    out_ref[...] = dot(table_ref[...], tokens, ((0,), (0,))).astype(BF)
+
+
+def turn_kernel(mine_ref, theirs_ref, router_ref, out_ref, score_ref):
+    rows = mine_ref.shape[0]
+    for half, ref in enumerate((theirs_ref, mine_ref)):
+        block = ref[...]
+        at = slice(half * rows, (half + 1) * rows)
+        out_ref[:, at] = block.T
+        logit = jnp.sum(block.astype(F32) * router_ref[...].astype(F32), axis=1, keepdims=True)
+        score_ref[at] = 1.0 / (1.0 + jnp.exp(-logit))
+
+
+def expert_kernel(inputs_ref, score_ref, gate_ref, up_ref, down_ref, *refs):
+    firsts, seconds = refs[0:3], refs[3:6]
+    other_ref, own_ref, hidden_ref, held_ref = refs[6:]
+    share, width = down_ref.shape
+    inputs = inputs_ref[...]
+    for chunk in range(4):
+        gate = gate_ref[...] if chunk == 0 else firsts[chunk - 1][:share]
+        up = up_ref[...] if chunk == 0 else seconds[chunk - 1][:share]
+        gate, up = dot(gate, inputs), dot(up, inputs)
+        at = chunk * share
+        hidden_ref[:, at : at + share] = (gate / (1.0 + jnp.exp(-gate)) * up).T.astype(BF)
+        if chunk == 0:
+            held_ref[at : at + share] = down_ref[...]
+        else:
+            held_ref[at : at + share // 2] = firsts[chunk - 1][share:]
+            held_ref[at + share // 2 : at + share] = seconds[chunk - 1][share:]
+    rows, tile = other_ref.shape[0], 512
+    for at in range(0, width, tile):
+        part = slice(at, at + tile)
+        total = dot(hidden_ref[...], held_ref[:, part])
+        total = (total * score_ref[...]).astype(BF)
+        other_ref[:, part] = total[:rows]
+        own_ref[:, part] = total[rows:]
 
 
 def local(
@@ -72,45 +132,72 @@
     rows, cols = video.shape[1:3]
     tok, width = context.shape
     experts, capacity = 64, 2
+    slots = experts * capacity
     share = down_weight.shape[1]
 
-    held = jnp.concatenate([gate_weight[0].T, up_weight[0].T, down_weight[0]], axis=0)
-    held = lax.all_gather(held, "x", axis=0, tiled=False)
-
-    part = embed_weight.T
-    spread = lax.all_gather(jnp.concatenate([part] * 3, axis=0), FRAME, axis=0, tiled=False)
-    embed = spread[:, : part.shape[0]].reshape(width, part.shape[1])
+    gate, up, down = gate_weight[0].T, up_weight[0].T, down_weight[0]
+    first = jnp.concatenate([gate, down[: share // 2]], axis=0)
+    second = jnp.concatenate([up, down[share // 2 :]], axis=0)
+    first_behind, second_ahead = ring(first, -1), ring(second, 1)
+
+    near = embed_weight.T[None]
+    for axis, pairs in (("x", XOR1), ("x", XOR2), ("yh", SWAP)):
+        near = jnp.concatenate([near, lax.ppermute(near, axis, pairs)], axis=0)
+    far = lax.ppermute(near, "c", SWAP)
 
     table = place_table(routes, experts, capacity)
     latent = encode(video, conv_weight, latent_weight)
     lat = latent.shape[1]
     blocks = latent.reshape(2, rows // 2, 2, cols // 2, 2, lat)
     patches = blocks.transpose(1, 3, 0, 2, 4, 5).reshape(tok, 8 * lat)
-    embedded = dot(patches, embed, ((1,), (1,))).astype(BF)
-    total = embedded.astype(F32) + context.astype(F32)
-    meansq = jnp.mean(total * total, axis=1, keepdims=True)
-    tokens = (total * lax.rsqrt(meansq + 1e-06)).astype(BF)
-
-    outgoing = dot(table, tokens, ((0,), (0,))).astype(BF).reshape(experts, capacity, width)
-    arrived = lax.all_to_all(outgoing, SOURCES, split_axis=0, concat_axis=0, tiled=True)
-    mine = arrived.reshape(experts * capacity, width)
-    swap = [(0, 1), (1, 0)]
-    theirs = lax.ppermute(mine, "c", swap)
-    inputs = jnp.concatenate([theirs, mine], axis=0)
+
+    patches, first, second, first_behind, second_ahead = lax.optimization_barrier(
+        (patches, first, second, first_behind, second_ahead)
+    )
+    first_ahead, second_behind = ring(first, 1), ring(second, -1)
+    first_opposite, second_opposite = ring(first_behind, -1), ring(second_ahead, 1)
+
+    vmem = pl.BlockSpec(memory_space=pltpu.VMEM)
+    params = pltpu.CompilerParams(vmem_limit_bytes=VMEM_BYTES)
+    outgoing = pl.pallas_call(
+        dispatch_kernel,
+        out_shape=jax.ShapeDtypeStruct((slots, width), BF),
+        in_specs=[pl.BlockSpec(memory_space=pltpu.SMEM)] + [vmem] * 5,
+        out_specs=vmem,
+        scratch_shapes=[pltpu.VMEM((16, *near.shape[1:]), BF)],
+        compiler_params=params,
+    )(lax.axis_index(FRAME).astype(jnp.int32).reshape(1), near, far, patches, context, table)
+
+    arrived = lax.cond(
+        lax.axis_index("yh") < 2,
+        lambda block: lax.all_to_all(block, SOURCES, split_axis=0, concat_axis=0, tiled=True),
+        lambda block: block,
+        outgoing.reshape(experts, capacity, width),
+    )
+    mine = arrived.reshape(slots, width)
+    theirs = lax.ppermute(mine, "c", SWAP)
     router = lax.dynamic_index_in_dim(router_weight, lax.axis_index("yh"), 0, keepdims=False)
-    score = jax.nn.sigmoid(dot(inputs, router))
-    result = jnp.zeros((2 * experts * capacity, width), F32)
-    for chunk in range(held.shape[0]):
-        gate = dot(inputs, held[chunk, :share], ((1,), (1,)))
-        up = dot(inputs, held[chunk, share : 2 * share], ((1,), (1,)))
-        hidden = (jax.nn.silu(gate) * up).astype(BF)
-        result = result + dot(hidden, held[chunk, 2 * share :])
-    result = (score * result).astype(BF)
-    other, own = result[: experts * capacity], result[experts * capacity :]
-    back = lax.ppermute(other, "c", swap)
+    inputs, score = pl.pallas_call(
+        turn_kernel,
+        out_shape=[jax.ShapeDtypeStruct((width, 2 * slots), BF), jax.ShapeDtypeStruct((2 * slots, 1), F32)],
+        in_specs=[vmem] * 3,
+        out_specs=[vmem] * 2,
+        compiler_params=params,
+    )(mine, theirs, router.reshape(1, width))
+
+    other, own = pl.pallas_call(
+        expert_kernel,
+        out_shape=[jax.ShapeDtypeStruct((slots, width), BF)] * 2,
+        in_specs=[vmem] * 11,
+        out_specs=[vmem] * 2,
+        scratch_shapes=[pltpu.VMEM((2 * slots, 4 * share), BF), pltpu.VMEM((4 * share, width), BF)],
+        compiler_params=params,
+    )(inputs, score, gate, up, down, first_behind, first_ahead, first_opposite, second_behind, second_ahead, second_opposite)
+
+    back = lax.ppermute(other, "c", SWAP)
     summed = (back.astype(F32) + own.astype(F32)).astype(BF).reshape(experts, capacity, width)
     homeward = lax.all_to_all(summed, SOURCES, split_axis=0, concat_axis=0, tiled=True)
-    return dot(table, homeward.reshape(experts * capacity, width)).astype(BF)
+    return dot(table, homeward.reshape(slots, width)).astype(BF)
 
 
 def solution(mesh):

time: 215 us -> 168 us (0.78)
  the two profiles are of different devices: /device:TPU:6 before, /device:TPU:16 now
where the time goes in v3:
time: 168 us; the launch traced here: 167 us
  starting transfers between devices  62.3 us (37%)
  blocking collectives  52.2 us (31%)
  waiting for transfers between devices  19.5 us (12%)
  local copies, waits for them, and re-layouts  16.8 us (10%)
  Pallas kernels  7.24 us (4%)
  other arithmetic  5.12 us (3%)
  matrix products  3.07 us (2%)
    all_to_all x1, blocking collectives, local(): lax.all_to_all(block, SOURCES, split_axis=0, concat_axis=0, tiled=True)  30.3 us
    ppermute x3, starting transfers between devices, local(): near = jnp.concatenate([near, lax.ppermute(near, axis, pairs)], axis=0)  22.2 us
    all_to_all x1, blocking collectives, local(): lax.all_to_all(summed, SOURCES, split_axis=0, concat_axis=0, tiled=True)  21.9 us
    ppermute x6, starting transfers between devices, ring(): return lax.ppermute(value, 'x', [(i, (i - step) % 4) for i in range(4)])  20.2 us
    ppermute x3, waiting for transfers between devices, local(): near = jnp.concatenate([near, lax.ppermute(near, axis, pairs)], axis=0)  15.9 us
    ppermute x3, starting transfers between devices, shifted(): return lax.ppermute(value, axes, pairs)  14 us
    pallas_call x1, Pallas kernels, local(): pl.pallas_call(expert_kernel, out_shape=[jax.ShapeDtypeStruct((slots, wid...  4.27 us
    unnamed x45, local copies, waits for them, and re-layouts  4.13 us
  transfers between devices with their start and end apart: 15, of which 4 were waited for; matrix products, arithmetic and copies ran while one was open for 12% of the time, Pallas kernels for 2%

profile of v3, /device:TPU:16, one launch (start us, length us, event | category | flops | bytes accessed | tf_op | source)
XLA Modules:
  0.0 166.7 jit_solution(8291762449397550868)
XLA Ops:
  1.5 4.3 %collective-permute-start.4 = (bf16[2,1,64,128]{3,2,1,0:T(8,128)(2,1)}, bf16[2,1,64,128]{3,2,1,0:T(8,128)(2,1)}, u32[]{:S(2)}, u32[]{:S(2)}) collective-permute-start(bf16[2,1,64,128]{3,2,1,0:T(8,128)(2,1)} %get-tuple-element.44), channel_id=1, source_target_pairs={{0,1},{1,2},{2,3},{3,4},{4,5},{5,6},{6,7},{7,8},{8,9},{9,10},{10,1... | collective-permute-start | bytes 98312 | tf_op jit(solution)/shard_map/ppermute | solution.py:28
  5.7 8.5 %collective-permute-start.5 = (bf16[2,1,64,128]{3,2,1,0:T(8,128)(2,1)}, bf16[2,1,64,128]{3,2,1,0:T(8,128)(2,1)S(1)}, u32[]{:S(2)}, u32[]{:S(2)}) collective-permute-start(bf16[2,1,64,128]{3,2,1,0:T(8,128)(2,1)} %get-tuple-element.43), channel_id=1, source_target_pairs={{1,0},{2,1},{3,2},{4,3},{5,4},{6,5},{7,6},{8,7},{9,8},{10,9},{11,1... | collective-permute-start | bytes 98312 | tf_op jit(solution)/shard_map/ppermute | solution.py:28
  16.3 3.5 %collective-permute-start.7 = (bf16[288,1536]{1,0:T(8,128)(2,1)}, bf16[288,1536]{1,0:T(8,128)(2,1)S(1)}, u32[]{:S(2)}, u32[]{:S(2)}) collective-permute-start(bf16[288,1536]{1,0:T(8,128)(2,1)} %pad_maximum_fusion), channel_id=1, source_target_pairs={{0,64},{64,128},{128,192},{192,0},{1,65},{65,129},{129,193},{193,1... | collective-permute-start | bytes 2654216 | tf_op jit(solution)/shard_map/ppermute | solution.py:32
  20.9 3.8 %collective-permute-start.8 = (bf16[288,1536]{1,0:T(8,128)(2,1)}, bf16[288,1536]{1,0:T(8,128)(2,1)S(1)}, u32[]{:S(2)}, u32[]{:S(2)}) collective-permute-start(bf16[288,1536]{1,0:T(8,128)(2,1)} %pad_maximum_fusion.1), channel_id=1, source_target_pairs={{0,192},{64,0},{128,64},{192,128},{1,193},{65,1},{129,65},{193,129... | collective-permute-start | bytes 2654216 | tf_op jit(solution)/shard_map/ppermute | solution.py:32
  24.7 2.2 %collective-permute-start = (bf16[1,96,128]{2,1,0:T(8,128)(2,1)S(1)}, bf16[1,96,128]{2,1,0:T(8,128)(2,1)S(1)}, u32[]{:S(2)}, u32[]{:S(2)}) collective-permute-start(bf16[1,96,128]{2,1,0:T(8,128)(2,1)S(1)} %bitcast.65), channel_id=1, source_target_pairs={{0,64},{64,0},{128,192},{192,128},{1,65},{65,1},{129,193},{193,129... | collective-permute-start | bytes 73736 | tf_op jit(solution)/shard_map/ppermute | solution.py:145
  27.0 2.0 %fusion.25 = (bf16[1,3,3,128,128]{4,3,2,1,0:T(8,128)(2,1)S(1)}, bf16[1,3,3,128,128]{4,3,2,1,0:T(8,128)(2,1)}, bf16[1,3,3,128,128]{4,3,2,1,0:T(8,128)(2,1)}) fusion(bf16[3,3,3,128,128]{4,3,2,1,0:T(8,128)(2,1)} %param.13), kind=kLoop, calls=%fused_computation.71 | loop fusion | bytes 1769472 | tf_op jit(solution)/shard_map/slice | solution.py:49
  31.0 13.5 %collective-permute-done = bf16[1,96,128]{2,1,0:T(8,128)(2,1)S(1)} collective-permute-done((bf16[1,96,128]{2,1,0:T(8,128)(2,1)S(1)}, bf16[1,96,128]{2,1,0:T(8,128)(2,1)S(1)}, u32[]{:S(2)}, u32[]{:S(2)}) %collective-permute-start) | collective-permute-done | bytes 24608 | tf_op jit(solution)/shard_map/ppermute | solution.py:145
  45.1 4.6 %collective-permute-start.1 = (bf16[2,96,128]{2,1,0:T(8,128)(2,1)}, bf16[2,96,128]{2,1,0:T(8,128)(2,1)S(1)}, u32[]{:S(2)}, u32[]{:S(2)}) collective-permute-start(bf16[2,96,128]{2,1,0:T(8,128)(2,1)} %pad_maximum_fusion.7), channel_id=1, source_target_pairs={{0,128},{64,192},{128,0},{192,64},{1,129},{65,193},{129,1},{193,65... | collective-permute-start | bytes 147464 | tf_op jit(solution)/shard_map/ppermute | solution.py:145
  58.0 3.9 %collective-permute-start.10 = (bf16[288,1536]{1,0:T(8,128)(2,1)}, bf16[288,1536]{1,0:T(8,128)(2,1)}, u32[]{:S(2)}, u32[]{:S(2)}) collective-permute-start(bf16[288,1536]{1,0:T(8,128)(2,1)} %pad_maximum_fusion), channel_id=1, source_target_pairs={{0,192},{64,0},{128,64},{192,128},{1,193},{65,1},{129,65},{193,129... | collective-permute-start | bytes 2654216 | tf_op jit(solution)/shard_map/ppermute | solution.py:32
  61.9 1.9 %collective-permute-start.11 = (bf16[288,1536]{1,0:T(8,128)(2,1)S(1)}, bf16[288,1536]{1,0:T(8,128)(2,1)}, u32[]{:S(2)}, u32[]{:S(2)}) collective-permute-start(bf16[288,1536]{1,0:T(8,128)(2,1)S(1)} %collective-permute-done.7.refs_0_), channel_id=1, source_target_pairs={{0,64},{64,128},{128,192},{192,0},{1,65},{65,129},{129,193},{193,1... | collective-permute-start | bytes 2654216 | tf_op jit(solution)/shard_map/ppermute | solution.py:32
  63.9 3.4 %collective-permute-start.12 = (bf16[288,1536]{1,0:T(8,128)(2,1)}, bf16[288,1536]{1,0:T(8,128)(2,1)}, u32[]{:S(2)}, u32[]{:S(2)}) collective-permute-start(bf16[288,1536]{1,0:T(8,128)(2,1)} %pad_maximum_fusion.1), channel_id=1, source_target_pairs={{0,64},{64,128},{128,192},{192,0},{1,65},{65,129},{129,193},{193,1... | collective-permute-start | bytes 2654216 | tf_op jit(solution)/shard_map/ppermute | solution.py:32
  67.3 3.7 %collective-permute-start.13 = (bf16[288,1536]{1,0:T(8,128)(2,1)S(1)}, bf16[288,1536]{1,0:T(8,128)(2,1)}, u32[]{:S(2)}, u32[]{:S(2)}) collective-permute-start(bf16[288,1536]{1,0:T(8,128)(2,1)S(1)} %collective-permute-done.8.refs_4_), channel_id=1, source_target_pairs={{0,192},{64,0},{128,64},{192,128},{1,193},{65,1},{129,65},{193,129... | collective-permute-start | bytes 2654216 | tf_op jit(solution)/shard_map/ppermute | solution.py:32
  71.0 15.4 %collective-permute-start.2 = (bf16[4,96,128]{2,1,0:T(8,128)(2,1)S(1)}, bf16[4,96,128]{2,1,0:T(8,128)(2,1)S(1)}, u32[]{:S(2)}, u32[]{:S(2)}) collective-permute-start(bf16[4,96,128]{2,1,0:T(8,128)(2,1)S(1)} %pad_maximum_fusion.6), channel_id=1, source_target_pairs={{0,256},{256,0},{1,257},{257,1},{2,258},{258,2},{3,259},{259,3},{4... | collective-permute-start | bytes 294920 | tf_op jit(solution)/shard_map/ppermute | solution.py:145
  86.5 2.4 %collective-permute-done.2 = bf16[4,96,128]{2,1,0:T(8,128)(2,1)S(1)} collective-permute-done((bf16[4,96,128]{2,1,0:T(8,128)(2,1)S(1)}, bf16[4,96,128]{2,1,0:T(8,128)(2,1)S(1)}, u32[]{:S(2)}, u32[]{:S(2)}) %collective-permute-start.2) | collective-permute-done | bytes 98336 | tf_op jit(solution)/shard_map/ppermute | solution.py:145
  89.0 1.9 %collective-permute-start.3 = (bf16[8,96,128]{2,1,0:T(8,128)(2,1)S(1)}, bf16[8,96,128]{2,1,0:T(8,128)(2,1)S(1)}, u32[]{:S(2)}, u32[]{:S(2)}) collective-permute-start(bf16[8,96,128]{2,1,0:T(8,128)(2,1)S(1)} %pad_maximum_fusion.3.near_ref), channel_id=1, source_target_pairs={{0,32},{32,0},{1,33},{33,1},{2,34},{34,2},{3,35},{35,3},{4,36},{36... | collective-permute-start | bytes 589832 | tf_op jit(solution)/shard_map/ppermute | solution.py:146
  95.9 34.1 %conditional.1 = (bf16[128,1536]{1,0:T(8,128)(2,1)}) conditional(s32[]{:T(128)} %convert_element_type.51, bf16[128,1536]{1,0:T(8,128)(2,1)} %shard_map.100, bf16[128,1536]{1,0:T(8,128)(2,1)} %shard_map.100), branch_computations={%region_1.2_spmd, %region_2.3_spmd} | conditional | bytes 2359304 | solution.py:171
  95.9 2.0 %reshape.51 = bf16[64,2,1536]{2,1,0:T(2,128)(2,1)} reshape(bf16[128,1536]{1,0:T(8,128)(2,1)} %param.1) | data formatting | bytes 786432 | tf_op jit(solution)/shard_map/reshape | solution.py:175
  97.9 30.3 %all_to_all.9 = bf16[64,2,1536]{2,1,0:T(2,128)(2,1)} all-to-all(bf16[64,2,1536]{2,1,0:T(2,128)(2,1)} %reshape.51), channel_id=1, replica_groups=mesh['yh'=2,'x'=4,'c'=2,'yl'=4,'z'=8] {'yh','yl','z'}, dimensions={0} | all-to-all | bytes 786432 | tf_op jit(solution)/shard_map/cond/branch_1_fun/all_to_all | solution.py:173
  128.1 1.9 %reshape.52 = bf16[128,1536]{1,0:T(8,128)(2,1)} reshape(bf16[64,2,1536]{2,1,0:T(2,128)(2,1)} %all_to_all.9) | data formatting | bytes 786432 | tf_op jit(solution)/shard_map/reshape | solution.py:177
  130.0 1.9 %collective-permute-start.9 = (bf16[128,1536]{1,0:T(8,128)(2,1)}, bf16[128,1536]{1,0:T(8,128)(2,1)}, u32[]{:S(2)}, u32[]{:S(2)}) collective-permute-start(bf16[128,1536]{1,0:T(8,128)(2,1)} %get-tuple-element.45.mine_ref), channel_id=1, source_target_pairs={{0,32},{32,0},{1,33},{33,1},{2,34},{34,2},{3,35},{35,3},{4,36},{36... | collective-permute-start | bytes 1179656 | tf_op jit(solution)/shard_map/ppermute | solution.py:178
  132.0 2.0 %collective-permute-done.9.theirs_ref = bf16[128,1536]{1,0:T(8,128)(2,1)} collective-permute-done((bf16[128,1536]{1,0:T(8,128)(2,1)}, bf16[128,1536]{1,0:T(8,128)(2,1)}, u32[]{:S(2)}, u32[]{:S(2)}) %collective-permute-start.9) | collective-permute-done | bytes 393248 | tf_op jit(solution)/shard_map/ppermute | solution.py:178
  135.6 4.3 %shard_map.102 = (bf16[128,1536]{1,0:T(8,128)(2,1)S(1)}, bf16[128,1536]{1,0:T(8,128)(2,1)S(1)}) custom-call(bf16[1536,256]{1,0:T(8,128)(2,1)S(1)} %get-tuple-element.24.inputs_ref, f32[256,1]{1,0:T(8,128)S(1)} %get-tuple-element.25.score_ref, bf16[192,1536]{1,0:T(8,128)(2,1)S(1)} %bitcast.48, bf16[192,1536]{1,0:T(8,128)(2,1)S(1)} %bitcast.50, ...), custom_call_target="tpu_custom_call" | custom-call | tf_op jit(solution)/shard_map/pallas_call | solution.py:188
  139.9 2.0 %collective-permute-start.14 = (bf16[128,1536]{1,0:T(8,128)(2,1)S(1)}, bf16[128,1536]{1,0:T(8,128)(2,1)S(1)}, u32[]{:S(2)}, u32[]{:S(2)}) collective-permute-start(bf16[128,1536]{1,0:T(8,128)(2,1)S(1)} %get-tuple-element.30), channel_id=1, source_target_pairs={{0,32},{32,0},{1,33},{33,1},{2,34},{34,2},{3,35},{35,3},{4,36},{36... | collective-permute-start | bytes 1179656 | tf_op jit(solution)/shard_map/ppermute | solution.py:197
  143.7 21.9 %all_to_all.10 = bf16[64,2,1536]{2,1,0:T(2,128)(2,1)S(1)} all-to-all(bf16[64,2,1536]{2,1,0:T(2,128)(2,1)S(1)} %reshape.63), channel_id=1, replica_groups=mesh['yh'=2,'x'=4,'c'=2,'yl'=4,'z'=8] {'yh','yl','z'}, dimensions={0} | all-to-all | bytes 786432 | tf_op jit(solution)/shard_map/all_to_all | solution.py:199
  (100 shorter events, 25.0 us)
Async XLA Ops:
  0.0 132.0 %copy-start = (bf16[2,1536,1]{1,0,2:T(2,128)(2,1)S(1)}, bf16[2,1536,1]{1,0,2:T(2,128)(2,1)}, u32[]{:S(2)}) copy-start(bf16[2,1536,1]{1,0,2:T(2,128)(2,1)} %param.17) | copy-start | bytes 18436
  0.0 15.3 %copy-start.1 = (bf16[1,1536,192]{1,2,0:T(8,128)(2,1)S(1)}, bf16[1,1536,192]{1,2,0:T(8,128)(2,1)}, u32[]{:S(2)}) copy-start(bf16[1,1536,192]{1,2,0:T(8,128)(2,1)} %param.18) | copy-start | bytes 1769476
  1.5 48.3 %collective-permute-start.4 = (bf16[2,1,64,128]{3,2,1,0:T(8,128)(2,1)}, bf16[2,1,64,128]{3,2,1,0:T(8,128)(2,1)}, u32[]{:S(2)}, u32[]{:S(2)}) collective-permute-start(bf16[2,1,64,128]{3,2,1,0:T(8,128)(2,1)} %get-tuple-element.44), channel_id=1, source_target_pairs={{0,1},{1,2},{2,3},{3,4},{4,5},{5,6},{6,7},{7,8},{8,9},{9,10},{10,1... | collective-permute-start | bytes 98312 | tf_op jit(solution)/shard_map/ppermute | solution.py:28
  5.7 44.8 %collective-permute-start.5 = (bf16[2,1,64,128]{3,2,1,0:T(8,128)(2,1)}, bf16[2,1,64,128]{3,2,1,0:T(8,128)(2,1)S(1)}, u32[]{:S(2)}, u32[]{:S(2)}) collective-permute-start(bf16[2,1,64,128]{3,2,1,0:T(8,128)(2,1)} %get-tuple-element.43), channel_id=1, source_target_pairs={{1,0},{2,1},{3,2},{4,3},{5,4},{6,5},{7,6},{8,7},{9,8},{10,9},{11,1... | collective-permute-start | bytes 98312 | tf_op jit(solution)/shard_map/ppermute | solution.py:28
  15.3 4.5 %copy-start.2 = (bf16[1,1536,192]{1,2,0:T(8,128)(2,1)S(1)}, bf16[1,1536,192]{1,2,0:T(8,128)(2,1)}, u32[]{:S(2)}) copy-start(bf16[1,1536,192]{1,2,0:T(8,128)(2,1)} %param.19) | copy-start | bytes 1769476
  16.3 8.3 %copy-start.11 = (bf16[128,96]{0,1:T(8,128)(2,1)S(1)}, bf16[128,96]{0,1:T(8,128)(2,1)}, u32[]{:S(2)}) copy-start(bf16[128,96]{0,1:T(8,128)(2,1)} %param.15) | copy-start | bytes 73732
  16.3 10.5 %copy-start.13 = (s32[64,2]{0,1:T(2,128)S(1)}, s32[64,2]{0,1:T(2,128)}, u32[]{:S(2)}) copy-start(s32[64,2]{0,1:T(2,128)} %param.21) | copy-start | bytes 1540
  16.3 41.7 %collective-permute-start.7 = (bf16[288,1536]{1,0:T(8,128)(2,1)}, bf16[288,1536]{1,0:T(8,128)(2,1)S(1)}, u32[]{:S(2)}, u32[]{:S(2)}) collective-permute-start(bf16[288,1536]{1,0:T(8,128)(2,1)} %pad_maximum_fusion), channel_id=1, source_target_pairs={{0,64},{64,128},{128,192},{192,0},{1,65},{65,129},{129,193},{193,1... | collective-permute-start | bytes 2654216 | tf_op jit(solution)/shard_map/ppermute | solution.py:32
  20.9 29.6 %copy-start.7 = (bf16[2,4,64,128]{3,2,1,0:T(8,128)(2,1)S(1)}, bf16[2,4,64,128]{3,2,1,0:T(8,128)(2,1)}, u32[]{:S(2)}) copy-start(bf16[2,4,64,128]{3,2,1,0:T(8,128)(2,1)} %param.12) | copy-start | bytes 393220
  20.9 37.1 %collective-permute-start.8 = (bf16[288,1536]{1,0:T(8,128)(2,1)}, bf16[288,1536]{1,0:T(8,128)(2,1)S(1)}, u32[]{:S(2)}, u32[]{:S(2)}) collective-permute-start(bf16[288,1536]{1,0:T(8,128)(2,1)} %pad_maximum_fusion.1), channel_id=1, source_target_pairs={{0,192},{64,0},{128,64},{192,128},{1,193},{65,1},{129,65},{193,129... | collective-permute-start | bytes 2654216 | tf_op jit(solution)/shard_map/ppermute | solution.py:32
  24.7 19.8 %collective-permute-start = (bf16[1,96,128]{2,1,0:T(8,128)(2,1)S(1)}, bf16[1,96,128]{2,1,0:T(8,128)(2,1)S(1)}, u32[]{:S(2)}, u32[]{:S(2)}) collective-permute-start(bf16[1,96,128]{2,1,0:T(8,128)(2,1)S(1)} %bitcast.65), channel_id=1, source_target_pairs={{0,64},{64,0},{128,192},{192,128},{1,65},{65,1},{129,193},{193,129... | collective-permute-start | bytes 73736 | tf_op jit(solution)/shard_map/ppermute | solution.py:145
  45.1 25.9 %collective-permute-start.1 = (bf16[2,96,128]{2,1,0:T(8,128)(2,1)}, bf16[2,96,128]{2,1,0:T(8,128)(2,1)S(1)}, u32[]{:S(2)}, u32[]{:S(2)}) collective-permute-start(bf16[2,96,128]{2,1,0:T(8,128)(2,1)} %pad_maximum_fusion.7), channel_id=1, source_target_pairs={{0,128},{64,192},{128,0},{192,64},{1,129},{65,193},{129,1},{193,65... | collective-permute-start | bytes 147464 | tf_op jit(solution)/shard_map/ppermute | solution.py:145
  50.5 4.4 %collective-permute-start.6 = (bf16[2,6,64,128]{3,2,1,0:T(8,128)(2,1)S(1)}, bf16[2,6,64,128]{3,2,1,0:T(8,128)(2,1)S(1)}, u32[]{:S(2)}, u32[]{:S(2)}) collective-permute-start(bf16[2,6,64,128]{3,2,1,0:T(8,128)(2,1)S(1)} %constant_dynamic-update-slice_fusion), channel_id=1, source_target_pairs={{0,32},{32,64},{64,96},{96,128},{128,160},{160,192},{192,224},{224... | collective-permute-start | bytes 589832 | tf_op jit(solution)/shard_map/ppermute | solution.py:28
  53.1 1.3 copy-start.9
  56.8 36.2 %copy-start.4 = (bf16[64,1536]{1,0:T(8,128)(2,1)S(1)}, bf16[64,1536]{1,0:T(8,128)(2,1)}, u32[]{:S(2)}) copy-start(bf16[64,1536]{1,0:T(8,128)(2,1)} %context_ref.1) | copy-start | bytes 589828
  58.0 77.5 %collective-permute-start.10 = (bf16[288,1536]{1,0:T(8,128)(2,1)}, bf16[288,1536]{1,0:T(8,128)(2,1)}, u32[]{:S(2)}, u32[]{:S(2)}) collective-permute-start(bf16[288,1536]{1,0:T(8,128)(2,1)} %pad_maximum_fusion), channel_id=1, source_target_pairs={{0,192},{64,0},{128,64},{192,128},{1,193},{65,1},{129,65},{193,129... | collective-permute-start | bytes 2654216 | tf_op jit(solution)/shard_map/ppermute | solution.py:32
  61.9 73.6 %collective-permute-start.11 = (bf16[288,1536]{1,0:T(8,128)(2,1)S(1)}, bf16[288,1536]{1,0:T(8,128)(2,1)}, u32[]{:S(2)}, u32[]{:S(2)}) collective-permute-start(bf16[288,1536]{1,0:T(8,128)(2,1)S(1)} %collective-permute-done.7.refs_0_), channel_id=1, source_target_pairs={{0,64},{64,128},{128,192},{192,0},{1,65},{65,129},{129,193},{193,1... | collective-permute-start | bytes 2654216 | tf_op jit(solution)/shard_map/ppermute | solution.py:32
  63.9 71.7 %collective-permute-start.12 = (bf16[288,1536]{1,0:T(8,128)(2,1)}, bf16[288,1536]{1,0:T(8,128)(2,1)}, u32[]{:S(2)}, u32[]{:S(2)}) collective-permute-start(bf16[288,1536]{1,0:T(8,128)(2,1)} %pad_maximum_fusion.1), channel_id=1, source_target_pairs={{0,64},{64,128},{128,192},{192,0},{1,65},{65,129},{129,193},{193,1... | collective-permute-start | bytes 2654216 | tf_op jit(solution)/shard_map/ppermute | solution.py:32
  67.3 68.3 %collective-permute-start.13 = (bf16[288,1536]{1,0:T(8,128)(2,1)S(1)}, bf16[288,1536]{1,0:T(8,128)(2,1)}, u32[]{:S(2)}, u32[]{:S(2)}) collective-permute-start(bf16[288,1536]{1,0:T(8,128)(2,1)S(1)} %collective-permute-done.8.refs_4_), channel_id=1, source_target_pairs={{0,192},{64,0},{128,64},{192,128},{1,193},{65,1},{129,65},{193,129... | collective-permute-start | bytes 2654216 | tf_op jit(solution)/shard_map/ppermute | solution.py:32
  71.0 18.0 %collective-permute-start.2 = (bf16[4,96,128]{2,1,0:T(8,128)(2,1)S(1)}, bf16[4,96,128]{2,1,0:T(8,128)(2,1)S(1)}, u32[]{:S(2)}, u32[]{:S(2)}) collective-permute-start(bf16[4,96,128]{2,1,0:T(8,128)(2,1)S(1)} %pad_maximum_fusion.6), channel_id=1, source_target_pairs={{0,256},{256,0},{1,257},{257,1},{2,258},{258,2},{3,259},{259,3},{4... | collective-permute-start | bytes 294920 | tf_op jit(solution)/shard_map/ppermute | solution.py:145
  89.0 4.1 %collective-permute-start.3 = (bf16[8,96,128]{2,1,0:T(8,128)(2,1)S(1)}, bf16[8,96,128]{2,1,0:T(8,128)(2,1)S(1)}, u32[]{:S(2)}, u32[]{:S(2)}) collective-permute-start(bf16[8,96,128]{2,1,0:T(8,128)(2,1)S(1)} %pad_maximum_fusion.3.near_ref), channel_id=1, source_target_pairs={{0,32},{32,0},{1,33},{33,1},{2,34},{34,2},{3,35},{35,3},{4,36},{36... | collective-permute-start | bytes 589832 | tf_op jit(solution)/shard_map/ppermute | solution.py:146
  95.9 39.7 %copy-start.3 = (bf16[1,192,1536]{2,1,0:T(8,128)(2,1)S(1)}, bf16[1,192,1536]{2,1,0:T(8,128)(2,1)}, u32[]{:S(2)}) copy-start(bf16[1,192,1536]{2,1,0:T(8,128)(2,1)} %param.20) | copy-start | bytes 1769476
  130.0 3.9 %collective-permute-start.9 = (bf16[128,1536]{1,0:T(8,128)(2,1)}, bf16[128,1536]{1,0:T(8,128)(2,1)}, u32[]{:S(2)}, u32[]{:S(2)}) collective-permute-start(bf16[128,1536]{1,0:T(8,128)(2,1)} %get-tuple-element.45.mine_ref), channel_id=1, source_target_pairs={{0,32},{32,0},{1,33},{33,1},{2,34},{34,2},{3,35},{35,3},{4,36},{36... | collective-permute-start | bytes 1179656 | tf_op jit(solution)/shard_map/ppermute | solution.py:178
  139.9 3.6 %collective-permute-start.14 = (bf16[128,1536]{1,0:T(8,128)(2,1)S(1)}, bf16[128,1536]{1,0:T(8,128)(2,1)S(1)}, u32[]{:S(2)}, u32[]{:S(2)}) collective-permute-start(bf16[128,1536]{1,0:T(8,128)(2,1)S(1)} %get-tuple-element.30), channel_id=1, source_target_pairs={{0,32},{32,0},{1,33},{33,1},{2,34},{34,2},{3,35},{35,3},{4,36},{36... | collective-permute-start | bytes 1179656 | tf_op jit(solution)/shard_map/ppermute | solution.py:197
  (5 other events, 4.3 us)

commit v4 on v1

v4 whole, which is shorter than its diff:
```python
import jax
import jax.numpy as jnp
from jax import lax
from jax.experimental import pallas as pl
from jax.experimental.pallas import tpu as pltpu
from jax.sharding import Mesh, PartitionSpec as P

FRAME = ("yh", "x", "c")
EXPERT = ("yl", "z")
SOURCES = ("yh", "yl", "z")
SIZES = (2, 4, 2, 4, 8)
NAMES = ("yh", "x", "c", "yl", "z")
BF = jnp.bfloat16
F32 = jnp.float32
SWAP = [(0, 1), (1, 0)]
XOR1 = [(i, i ^ 1) for i in range(4)]
XOR3 = [(i, i ^ 3) for i in range(4)]
VMEM_BYTES = 16 * 1024 * 1024
WIDE_BYTES = 65_600_000


def dot(a, b, dims=((1,), (0,))):
    return lax.dot_general(a, b, (dims, ((), ())), preferred_element_type=F32)


def shifted(value, axes, step):
    count = lax.axis_size(axes)
    pairs = [(i, i + step) for i in range(count) if 0 <= i + step < count]
    return lax.ppermute(value, axes, pairs)


def encode(video, past, conv_weight, latent_weight):
    frames, rows, cols, chans = video.shape
    stacked = jnp.concatenate([past, video], axis=0)
    above = shifted(stacked[:, rows - 1 :], EXPERT, 1)
    below = shifted(stacked[:, :1], EXPERT, -1)
    tall = jnp.concatenate([above, stacked, below], axis=1)

    def windows(block):
        wide = jnp.pad(block, ((0, 0), (0, 0), (1, 1), (0, 0)))
        taps = [wide[:, b : b + rows, q : q + cols] for b in range(3) for q in range(3)]
        return jnp.concatenate(taps, axis=-1).reshape(block.shape[0], rows * cols, 9 * chans)

    kernel = conv_weight.reshape(3, 9 * chans, chans)
    seen = windows(tall)
    mixed = sum(dot(seen[a : a + frames].reshape(-1, 9 * chans), kernel[a]) for a in range(3))
    feature = (video.reshape(-1, chans).astype(F32) + jax.nn.silu(mixed)).astype(BF)
    return dot(feature, latent_weight).astype(BF)


def place_table(routes, experts, capacity):
    tok = routes.shape[0]
    flat = routes.reshape(-1)
    count = flat.shape[0]
    chosen = (flat[:, None] == jnp.arange(experts, dtype=jnp.int32)[None, :]).astype(BF)
    at = jnp.arange(count, dtype=jnp.int32)
    before = (at[:, None] > at[None, :]).astype(BF)
    rank = jnp.sum(dot(before, chosen) * chosen.astype(F32), axis=1).astype(jnp.int32)
    place = jnp.where(rank < capacity, flat * capacity + rank, -1).reshape(tok, 2)
    slots = jnp.arange(experts * capacity, dtype=jnp.int32)[None, :]
    hit = (place[:, :1] == slots) | (place[:, 1:] == slots)
    return hit.astype(BF)


def pack_kernel(gate_ref, up_ref, down_ref, out_ref, sems):
    share = down_ref.shape[0]
    copies = [
        pltpu.make_async_copy(ref, out_ref.at[pl.ds(i * share, share)], sems.at[i])
        for i, ref in enumerate((gate_ref, up_ref, down_ref))
    ]
    for copy in copies:
        copy.start()
    for copy in copies:
        copy.wait()


def dispatch_kernel(patches_ref, context_ref, table_ref, out_ref):
    width = context_ref.shape[1]
    table = table_ref[...]
    out_ref[:, :width] = dot(table, context_ref[...], ((0,), (0,))).astype(BF)
    out_ref[:, width:] = dot(table, patches_ref[...], ((0,), (0,))).astype(BF)


def embed_kernel(at_ref, parts_ref, out_ref):
    yh, x, c = at_ref[0], at_ref[1], at_ref[2]
    size = parts_ref.shape[1]
    for shard in range(16):
        apart = shard // 2 % 4 ^ x
        mirror = apart // 2
        at = (apart % 2 ^ mirror) + mirror * 2 + (shard // 8 ^ yh) * 4 + (shard % 2 ^ c) * 8
        out_ref[shard * size : (shard + 1) * size] = parts_ref[at]


def expert_kernel(rows_ref, embed_ref, router_ref, w0_ref, w1_ref, w2_ref, w3_ref, out_ref, held_ref, sems):
    width = out_ref.shape[1]
    share = w0_ref.shape[0] // 3
    copies = [
        pltpu.make_async_copy(ref, held_ref.at[i], sems.at[i])
        for i, ref in enumerate((w0_ref, w1_ref, w2_ref, w3_ref))
    ]
    for copy in copies:
        copy.start()
    embedded = dot(rows_ref[:, width:], embed_ref[...], ((1,), (1,))).astype(BF)
    total = embedded.astype(F32) + rows_ref[:, :width].astype(F32)
    meansq = jnp.mean(total * total, axis=1, keepdims=True)
    tokens = (total * lax.rsqrt(meansq + 1e-06)).astype(BF)
    logit = jnp.sum(tokens.astype(F32) * router_ref[...].astype(F32), axis=1, keepdims=True)
    score = 1.0 / (1.0 + jnp.exp(-logit))
    hidden = []
    for i, copy in enumerate(copies):
        copy.wait()
        both = dot(tokens, held_ref[i, : 2 * share], ((1,), (1,)))
        gate, up = both[:, :share], both[:, share:]
        hidden.append((gate / (1.0 + jnp.exp(-gate)) * up).astype(BF))
    hidden = jnp.concatenate(hidden, axis=1)
    tile = 512
    for at in range(0, width, tile):
        down = jnp.concatenate([held_ref[i, 2 * share :, at : at + tile] for i in range(4)], axis=0)
        out_ref[:, at : at + tile] = (dot(hidden, down) * score).astype(BF)


def local(
    video,
    conv_weight,
    latent_weight,
    embed_weight,
    context,
    router_weight,
    gate_weight,
    up_weight,
    down_weight,
    routes,
):
    rows, cols = video.shape[1:3]
    tok, width = context.shape
    experts, capacity = 64, 2
    slots = experts * capacity
    share = down_weight.shape[1]
    hbm = pl.BlockSpec(memory_space=pltpu.HBM)
    vmem = pl.BlockSpec(memory_space=pltpu.VMEM)
    smem = pl.BlockSpec(memory_space=pltpu.SMEM)
    params = pltpu.CompilerParams(vmem_limit_bytes=VMEM_BYTES)

    past = shifted(video, FRAME, 1)
    held = pl.pallas_call(
        pack_kernel,
        out_shape=jax.ShapeDtypeStruct((3 * share, width), BF),
        in_specs=[hbm] * 3,
        out_specs=hbm,
        scratch_shapes=[pltpu.SemaphoreType.DMA((3,))],
        compiler_params=params,
    )(gate_weight[0].T, up_weight[0].T, down_weight[0])
    parts = embed_weight.T[None]
    for axis, pairs in (("x", XOR1), ("x", XOR3)):
        parts = jnp.concatenate([parts, lax.ppermute(parts, axis, pairs)], axis=0)
    held, past, parts = lax.optimization_barrier((held, past, parts))
    across = lax.ppermute(held, "x", XOR1)
    beside = lax.ppermute(held, "c", SWAP)

    table = place_table(routes, experts, capacity)
    latent = encode(video, past, conv_weight, latent_weight)
    lat = latent.shape[1]
    blocks = latent.reshape(2, rows // 2, 2, cols // 2, 2, lat)
    patches = blocks.transpose(1, 3, 0, 2, 4, 5).reshape(tok, 8 * lat)
    for axis in ("yh", "c"):
        parts = jnp.concatenate([parts, lax.ppermute(parts, axis, SWAP)], axis=0)
    patches, parts = lax.optimization_barrier((patches, parts))
    raw = width + patches.shape[1]
    outgoing = pl.pallas_call(
        dispatch_kernel,
        out_shape=jax.ShapeDtypeStruct((slots, raw), BF),
        in_specs=[vmem] * 3,
        out_specs=vmem,
        compiler_params=pltpu.CompilerParams(vmem_limit_bytes=WIDE_BYTES),
    )(patches, context, table)

    arrived = lax.all_to_all(outgoing.reshape(experts, capacity, raw), SOURCES, split_axis=0, concat_axis=0, tiled=True)
    mine = arrived.reshape(slots, raw)
    theirs = lax.ppermute(mine, "x", XOR3)
    across, mine = lax.optimization_barrier((across, mine))
    corner = lax.ppermute(across, "c", SWAP)
    weights = (held, beside, across, corner)

    embed = pl.pallas_call(
        embed_kernel,
        out_shape=jax.ShapeDtypeStruct((width, parts.shape[2]), BF),
        in_specs=[smem, vmem],
        out_specs=vmem,
        compiler_params=params,
    )(jnp.stack([lax.axis_index(axis) for axis in FRAME]).astype(jnp.int32), parts)

    router = lax.dynamic_index_in_dim(router_weight, lax.axis_index("yh"), 0, keepdims=False).reshape(1, width)

    def expert(block):
        return pl.pallas_call(
            expert_kernel,
            out_shape=jax.ShapeDtypeStruct((slots, width), BF),
            in_specs=[vmem] * 3 + [hbm] * 4,
            out_specs=vmem,
            scratch_shapes=[pltpu.VMEM((4, 3 * share, width), BF), pltpu.SemaphoreType.DMA((4,))],
            compiler_params=params,
        )(block, embed, router, *weights)

    back = lax.ppermute(expert(theirs), "x", XOR3)
    own = expert(mine)
    summed = (back.astype(F32) + own.astype(F32)).astype(BF).reshape(experts, capacity, width)
    homeward = lax.all_to_all(summed, SOURCES, split_axis=0, concat_axis=0, tiled=True)
    return dot(table, homeward.reshape(slots, width)).astype(BF)


def solution(mesh):
    fine = Mesh(mesh.devices.reshape(SIZES), NAMES)
    return jax.shard_map(
        local,
        mesh=fine,
        in_specs=(
            P(FRAME, EXPERT, None, None),
            P(),
            P(),
            P(None, FRAME),
            P((*FRAME, *EXPERT), None),
            P(None, None, EXPERT),
            P(EXPERT, None, FRAME),
            P(EXPERT, None, FRAME),
            P(EXPERT, FRAME, None),
            P((*FRAME, *EXPERT), None),
        ),
        out_specs=P((*FRAME, *EXPERT), None),
        check_vma=False,
    )
```

time: 215 us -> 140 us (0.65)
  waiting for transfers between devices: 97.1 us -> 34.1 us
  starting transfers between devices: 12 us -> 55.9 us
  blocking collectives: 58.9 us -> 22.4 us
  matrix products: 21.4 us -> 2.69 us
  between operations: 13.8 us -> 0.49 us
  Pallas kernels: 0 us -> 12.9 us
  other arithmetic: 5.22 us -> 2.64 us
  local copies, waits for them, and re-layouts: 4.68 us -> 7.1 us
    all_gather x2 -> x0, waiting for transfers between devices: 89.5 us -> none  [the longest x1 47.1 us: local(): lax.all_gather(jnp.concatenate([part] * 3, axis=0), FRAME, axis=0, tiled=...]
    ppermute x2 -> x9, starting transfers between devices: 3.84 us -> 33 us  [the longest x2 11.4 us: local(): parts = jnp.concatenate([parts, lax.ppermute(parts, axis, SWAP)], axis=0)]
    all_to_all x1 -> x0, blocking collectives: 28.4 us -> none  [local(): lax.all_to_all(outgoing, SOURCES, split_axis=0, concat_axis=0, tiled=True)]
    dot_general x20 -> x5, matrix products: 21.4 us -> 2.69 us  [dot(): return lax.dot_general(a, b, (dims, ((), ())), preferred_element_type=F32)]
    all_to_all x0 -> x1, starting transfers between devices: none -> 16.6 us  [local(): lax.all_to_all(outgoing.reshape(experts, capacity, raw), SOURCES, split_a...]
    all_to_all x0 -> x1, waiting for transfers between devices: none -> 15.7 us  [local(): lax.all_to_all(outgoing.reshape(experts, capacity, raw), SOURCES, split_a...]
    ppermute x2 -> x9, waiting for transfers between devices: 3.37 us -> 18.3 us  [the longest x1 11.5 us: local(): theirs = lax.ppermute(mine, 'x', XOR3)]
    pallas_call x0 -> x5, Pallas kernels: none -> 12.9 us  [the longest x2 9.03 us: expert(): pl.pallas_call(expert_kernel, out_shape=jax.ShapeDtypeStruct((slots, widt...]
  transfers between devices with their start and end apart: 7 -> 13, of which waited for: 6 -> 4; matrix products, arithmetic and copies ran while one was open for 5% -> 8% of each run, Pallas kernels for 0% -> 6%
where the time goes in v4:
time: 140 us; the launch traced here: 138 us
  starting transfers between devices  55.9 us (40%)
  waiting for transfers between devices  34.1 us (24%)
  blocking collectives  22.4 us (16%)
  Pallas kernels  12.9 us (9%)
  local copies, waits for them, and re-layouts  7.1 us (5%)
  matrix products  2.69 us (2%)
  other arithmetic  2.64 us (2%)
    all_to_all x1, blocking collectives, local(): lax.all_to_all(summed, SOURCES, split_axis=0, concat_axis=0, tiled=True)  22.4 us
    all_to_all x1, starting transfers between devices, local(): lax.all_to_all(outgoing.reshape(experts, capacity, raw), SOURCES, split_a...  16.6 us
    all_to_all x1, waiting for transfers between devices, local(): lax.all_to_all(outgoing.reshape(experts, capacity, raw), SOURCES, split_a...  15.7 us
    ppermute x1, waiting for transfers between devices, local(): theirs = lax.ppermute(mine, 'x', XOR3)  11.5 us
    ppermute x2, starting transfers between devices, local(): parts = jnp.concatenate([parts, lax.ppermute(parts, axis, SWAP)], axis=0)  11.4 us
    ppermute x2, starting transfers between devices, local(): parts = jnp.concatenate([parts, lax.ppermute(parts, axis, pairs)], axis=0)  9.17 us
    pallas_call x2, Pallas kernels, expert(): pl.pallas_call(expert_kernel, out_shape=jax.ShapeDtypeStruct((slots, widt...  9.03 us
    ppermute x3, starting transfers between devices, shifted(): return lax.ppermute(value, axes, pairs)  6.31 us
  transfers between devices with their start and end apart: 13, of which 4 were waited for; matrix products, arithmetic and copies ran while one was open for 8% of the time, Pallas kernels for 6%

profile of v4, /device:TPU:6, one launch (start us, length us, event | category | flops | bytes accessed | tf_op | source)
XLA Modules:
  0.0 138.1 jit_solution(10828332696263814434)
XLA Ops:
  0.0 2.9 %collective-permute-start.1 = (bf16[1,96,128]{2,1,0:T(8,128)(2,1)}, bf16[1,96,128]{2,1,0:T(8,128)(2,1)S(1)}, u32[]{:S(2)}, u32[]{:S(2)}) collective-permute-start(bf16[1,96,128]{2,1,0:T(8,128)(2,1)} %bitcast.47), channel_id=1, source_target_pairs={{0,64},{64,0},{128,192},{192,128},{1,65},{65,1},{129,193},{193,129... | collective-permute-start | bytes 73736 | tf_op jit(solution)/shard_map/ppermute | solution.py:155
  2.9 1.9 %collective-permute-start = (bf16[2,4,64,128]{3,2,1,0:T(8,128)(2,1)}, bf16[2,4,64,128]{3,2,1,0:T(8,128)(2,1)S(1)}, u32[]{:S(2)}, u32[]{:S(2)}) collective-permute-start(bf16[2,4,64,128]{3,2,1,0:T(8,128)(2,1)} %param.10), channel_id=1, source_target_pairs={{0,32},{32,64},{64,96},{96,128},{128,160},{160,192},{192,224},{224... | collective-permute-start | bytes 393224 | tf_op jit(solution)/shard_map/ppermute | solution.py:29
  6.3 1.2 fusion.20
  8.8 6.3 %collective-permute-start.2 = (bf16[2,96,128]{2,1,0:T(8,128)(2,1)S(1)}, bf16[2,96,128]{2,1,0:T(8,128)(2,1)S(1)}, u32[]{:S(2)}, u32[]{:S(2)}) collective-permute-start(bf16[2,96,128]{2,1,0:T(8,128)(2,1)S(1)} %pad_maximum_fusion.5), channel_id=1, source_target_pairs={{0,192},{64,128},{128,64},{192,0},{1,193},{65,129},{129,65},{193,1... | collective-permute-start | bytes 147464 | tf_op jit(solution)/shard_map/ppermute | solution.py:155
  15.4 1.3 shard_map.100.w0_ref
  17.3 3.1 %collective-permute-start.3 = (bf16[4,1,64,128]{3,2,1,0:T(8,128)(2,1)S(1)}, bf16[4,1,64,128]{3,2,1,0:T(8,128)(2,1)S(1)}, u32[]{:S(2)}, u32[]{:S(2)}) collective-permute-start(bf16[4,1,64,128]{3,2,1,0:T(8,128)(2,1)S(1)} %get-tuple-element.27), channel_id=1, source_target_pairs={{0,1},{1,2},{2,3},{3,4},{4,5},{5,6},{6,7},{7,8},{8,9},{9,10},{10,1... | collective-permute-start | bytes 196616 | tf_op jit(solution)/shard_map/ppermute | solution.py:29
  20.4 1.3 collective-permute-start.4
  22.4 7.7 %collective-permute-start.5 = (bf16[4,96,128]{2,1,0:T(8,128)(2,1)S(1)}, bf16[4,96,128]{2,1,0:T(8,128)(2,1)S(1)}, u32[]{:S(2)}, u32[]{:S(2)}) collective-permute-start(bf16[4,96,128]{2,1,0:T(8,128)(2,1)S(1)} %pad_maximum_fusion.4), channel_id=1, source_target_pairs={{0,256},{256,0},{1,257},{257,1},{2,258},{258,2},{3,259},{259,3},{4... | collective-permute-start | bytes 294920 | tf_op jit(solution)/shard_map/ppermute | solution.py:166
  30.1 2.4 %collective-permute-start.9 = (bf16[576,1536]{1,0:T(8,128)(2,1)}, bf16[576,1536]{1,0:T(8,128)(2,1)}, u32[]{:S(2)}, u32[]{:S(2)}) collective-permute-start(bf16[576,1536]{1,0:T(8,128)(2,1)} %shard_map.100.w0_ref), channel_id=1, source_target_pairs={{0,64},{64,0},{128,192},{192,128},{1,65},{65,1},{129,193},{193,129... | collective-permute-start | bytes 5308424 | tf_op jit(solution)/shard_map/ppermute | solution.py:157
  35.0 3.7 %collective-permute-start.6 = (bf16[8,96,128]{2,1,0:T(8,128)(2,1)S(1)}, bf16[8,96,128]{2,1,0:T(8,128)(2,1)S(1)}, u32[]{:S(2)}, u32[]{:S(2)}) collective-permute-start(bf16[8,96,128]{2,1,0:T(8,128)(2,1)S(1)} %pad_maximum_fusion.3), channel_id=1, source_target_pairs={{0,32},{32,0},{1,33},{33,1},{2,34},{34,2},{3,35},{35,3},{4,36},{36... | collective-permute-start | bytes 589832 | tf_op jit(solution)/shard_map/ppermute | solution.py:166
  40.5 2.0 %shard_map.101 = bf16[128,1664]{1,0:T(8,128)(2,1)} custom-call(bf16[64,128]{1,0:T(8,128)(2,1)} %copy.20.patches_ref, bf16[64,1536]{1,0:T(8,128)(2,1)} %context_ref.1, bf16[64,128]{1,0:T(8,128)(2,1)} %fusion.14.table_ref), custom_call_target="tpu_custom_call" | custom-call | tf_op jit(solution)/shard_map/pallas_call | solution.py:169
  42.5 1.9 %reshape.58 = bf16[64,2,1664]{2,1,0:T(2,128)(2,1)} reshape(bf16[128,1664]{1,0:T(8,128)(2,1)} %shard_map.101) | data formatting | bytes 851968 | tf_op jit(solution)/shard_map/reshape | solution.py:177
  44.4 16.6 %all-to-all-start = ((bf16[64,2,1664]{2,1,0:T(2,128)(2,1)}), bf16[64,2,1664]{2,1,0:T(2,128)(2,1)S(1)}, u32[]{:S(2)}, u32[]{:S(2)}) async-start(bf16[64,2,1664]{2,1,0:T(2,128)(2,1)} %reshape.58), calls=%async_computation | async-start | bytes 851968 | tf_op jit(solution)/shard_map/all_to_all | solution.py:177
  60.9 1.9 %collective-permute-start.8 = (bf16[576,1536]{1,0:T(8,128)(2,1)}, bf16[576,1536]{1,0:T(8,128)(2,1)S(1)}, u32[]{:S(2)}, u32[]{:S(2)}) collective-permute-start(bf16[576,1536]{1,0:T(8,128)(2,1)} %shard_map.100.w0_ref), channel_id=1, source_target_pairs={{0,32},{32,0},{1,33},{33,1},{2,34},{34,2},{3,35},{35,3},{4,36},{36... | collective-permute-start | bytes 5308424 | tf_op jit(solution)/shard_map/ppermute | solution.py:158
  62.9 15.7 %all-to-all-done = bf16[64,2,1664]{2,1,0:T(2,128)(2,1)S(1)} async-done(((bf16[64,2,1664]{2,1,0:T(2,128)(2,1)}), bf16[64,2,1664]{2,1,0:T(2,128)(2,1)S(1)}, u32[]{:S(2)}, u32[]{:S(2)}) %all-to-all-start) | async-done | bytes 426016 | tf_op jit(solution)/shard_map/all_to_all | solution.py:177
  78.8 1.9 %collective-permute-start.10 = (bf16[576,1536]{1,0:T(8,128)(2,1)}, bf16[576,1536]{1,0:T(8,128)(2,1)}, u32[]{:S(2)}, u32[]{:S(2)}) collective-permute-start(bf16[576,1536]{1,0:T(8,128)(2,1)} %collective-permute-done.9.w2_ref), channel_id=1, source_target_pairs={{0,32},{32,0},{1,33},{33,1},{2,34},{34,2},{3,35},{35,3},{4,36},{36... | collective-permute-start | bytes 5308424 | tf_op jit(solution)/shard_map/ppermute | solution.py:181
  80.7 3.1 %collective-permute-start.7 = (bf16[128,1664]{1,0:T(8,128)(2,1)S(1)}, bf16[128,1664]{1,0:T(8,128)(2,1)S(1)}, u32[]{:S(2)}, u32[]{:S(2)}) collective-permute-start(bf16[128,1664]{1,0:T(8,128)(2,1)S(1)} %reshape.59.rows_ref), channel_id=1, source_target_pairs={{0,192},{64,128},{128,64},{192,0},{1,193},{65,129},{129,65},{193,1... | collective-permute-start | bytes 1277960 | tf_op jit(solution)/shard_map/ppermute | solution.py:179
  84.5 11.5 %collective-permute-done.7.rows_ref = bf16[128,1664]{1,0:T(8,128)(2,1)S(1)} collective-permute-done((bf16[128,1664]{1,0:T(8,128)(2,1)S(1)}, bf16[128,1664]{1,0:T(8,128)(2,1)S(1)}, u32[]{:S(2)}, u32[]{:S(2)}) %collective-permute-start.7) | collective-permute-done | bytes 426016 | tf_op jit(solution)/shard_map/ppermute | solution.py:179
  96.0 4.5 %shard_map.103 = bf16[128,1536]{1,0:T(8,128)(2,1)S(1)} custom-call(bf16[128,1664]{1,0:T(8,128)(2,1)S(1)} %collective-permute-done.7.rows_ref, bf16[1536,128]{1,0:T(8,128)(2,1)S(1)} %shard_map.102.embed_ref, bf16[1,1536]{1,0:T(2,128)(2,1)S(1)} %dynamic-slice_bitcast_fusion.router_ref, bf16[576,1536]{1,0:T(8,128)(2,1)} %shard_map.100.w0_ref, ...), custom_call_target="tpu_custom_call" | custom-call | tf_op jit(solution)/shard_map/pallas_call | solution.py:195
  100.5 3.1 %collective-permute-start.11 = (bf16[128,1536]{1,0:T(8,128)(2,1)S(1)}, bf16[128,1536]{1,0:T(8,128)(2,1)S(1)}, u32[]{:S(2)}, u32[]{:S(2)}) collective-permute-start(bf16[128,1536]{1,0:T(8,128)(2,1)S(1)} %shard_map.103), channel_id=1, source_target_pairs={{0,192},{64,128},{128,64},{192,0},{1,193},{65,129},{129,65},{193,1... | collective-permute-start | bytes 1179656 | tf_op jit(solution)/shard_map/ppermute | solution.py:204
  103.7 4.5 %shard_map.104 = bf16[128,1536]{1,0:T(8,128)(2,1)S(1)} custom-call(bf16[128,1664]{1,0:T(8,128)(2,1)S(1)} %reshape.59.rows_ref, bf16[1536,128]{1,0:T(8,128)(2,1)S(1)} %shard_map.102.embed_ref, bf16[1,1536]{1,0:T(2,128)(2,1)S(1)} %dynamic-slice_bitcast_fusion.router_ref, bf16[576,1536]{1,0:T(8,128)(2,1)} %shard_map.100.w0_ref, ...), custom_call_target="tpu_custom_call" | custom-call | tf_op jit(solution)/shard_map/pallas_call | solution.py:195
  108.2 6.2 %collective-permute-done.11 = bf16[128,1536]{1,0:T(8,128)(2,1)S(1)} collective-permute-done((bf16[128,1536]{1,0:T(8,128)(2,1)S(1)}, bf16[128,1536]{1,0:T(8,128)(2,1)S(1)}, u32[]{:S(2)}, u32[]{:S(2)}) %collective-permute-start.11) | collective-permute-done | bytes 393248 | tf_op jit(solution)/shard_map/ppermute | solution.py:204
  114.6 22.4 %all_to_all.10 = bf16[64,2,1536]{2,1,0:T(2,128)(2,1)S(1)} all-to-all(bf16[64,2,1536]{2,1,0:T(2,128)(2,1)S(1)} %reshape.61), channel_id=1, replica_groups=mesh['yh'=2,'x'=4,'c'=2,'yl'=4,'z'=8] {'yh','yl','z'}, dimensions={0} | all-to-all | bytes 786432 | tf_op jit(solution)/shard_map/all_to_all | solution.py:207
  137.2 0.9 convolution_convert_fusion
  (67 shorter events, 9.6 us)
Async XLA Ops:
  0.0 83.9 %copy-start = (bf16[2,1536,1]{1,0,2:T(2,128)(2,1)S(1)}, bf16[2,1536,1]{1,0,2:T(2,128)(2,1)}, u32[]{:S(2)}) copy-start(bf16[2,1536,1]{1,0,2:T(2,128)(2,1)} %param.15) | copy-start | bytes 18436
  0.0 15.3 %copy-start.1 = (bf16[1,1536,192]{1,2,0:T(8,128)(2,1)S(1)}, bf16[1,1536,192]{1,2,0:T(8,128)(2,1)}, u32[]{:S(2)}) copy-start(bf16[1,1536,192]{1,2,0:T(8,128)(2,1)} %param.16) | copy-start | bytes 1769476
  0.0 15.3 %copy-start.2 = (bf16[1,1536,192]{1,2,0:T(8,128)(2,1)S(1)}, bf16[1,1536,192]{1,2,0:T(8,128)(2,1)}, u32[]{:S(2)}) copy-start(bf16[1,1536,192]{1,2,0:T(8,128)(2,1)} %param.17) | copy-start | bytes 1769476
  0.0 15.3 %copy-start.3 = (bf16[1,192,1536]{2,1,0:T(8,128)(2,1)S(1)}, bf16[1,192,1536]{2,1,0:T(8,128)(2,1)}, u32[]{:S(2)}) copy-start(bf16[1,192,1536]{2,1,0:T(8,128)(2,1)} %param.18) | copy-start | bytes 1769476
  0.0 8.1 %collective-permute-start.1 = (bf16[1,96,128]{2,1,0:T(8,128)(2,1)}, bf16[1,96,128]{2,1,0:T(8,128)(2,1)S(1)}, u32[]{:S(2)}, u32[]{:S(2)}) collective-permute-start(bf16[1,96,128]{2,1,0:T(8,128)(2,1)} %bitcast.47), channel_id=1, source_target_pairs={{0,64},{64,0},{128,192},{192,128},{1,65},{65,1},{129,193},{193,129... | collective-permute-start | bytes 73736 | tf_op jit(solution)/shard_map/ppermute | solution.py:155
  2.9 14.3 %collective-permute-start = (bf16[2,4,64,128]{3,2,1,0:T(8,128)(2,1)}, bf16[2,4,64,128]{3,2,1,0:T(8,128)(2,1)S(1)}, u32[]{:S(2)}, u32[]{:S(2)}) collective-permute-start(bf16[2,4,64,128]{3,2,1,0:T(8,128)(2,1)} %param.10), channel_id=1, source_target_pairs={{0,32},{32,64},{64,96},{96,128},{128,160},{160,192},{192,224},{224... | collective-permute-start | bytes 393224 | tf_op jit(solution)/shard_map/ppermute | solution.py:29
  7.5 9.7 %copy-start.5 = (bf16[128,96]{0,1:T(8,128)(2,1)S(1)}, bf16[128,96]{0,1:T(8,128)(2,1)}, u32[]{:S(2)}) copy-start(bf16[128,96]{0,1:T(8,128)(2,1)} %param.13) | copy-start | bytes 73732
  7.5 9.8 %copy-start.4 = (bf16[2,4,64,128]{3,2,1,0:T(8,128)(2,1)S(1)}, bf16[2,4,64,128]{3,2,1,0:T(8,128)(2,1)}, u32[]{:S(2)}) copy-start(bf16[2,4,64,128]{3,2,1,0:T(8,128)(2,1)} %param.10) | copy-start | bytes 393220
  8.8 8.4 %collective-permute-start.2 = (bf16[2,96,128]{2,1,0:T(8,128)(2,1)S(1)}, bf16[2,96,128]{2,1,0:T(8,128)(2,1)S(1)}, u32[]{:S(2)}, u32[]{:S(2)}) collective-permute-start(bf16[2,96,128]{2,1,0:T(8,128)(2,1)S(1)} %pad_maximum_fusion.5), channel_id=1, source_target_pairs={{0,192},{64,128},{128,64},{192,0},{1,193},{65,129},{129,65},{193,1... | collective-permute-start | bytes 147464 | tf_op jit(solution)/shard_map/ppermute | solution.py:155
  17.3 15.2 %collective-permute-start.3 = (bf16[4,1,64,128]{3,2,1,0:T(8,128)(2,1)S(1)}, bf16[4,1,64,128]{3,2,1,0:T(8,128)(2,1)S(1)}, u32[]{:S(2)}, u32[]{:S(2)}) collective-permute-start(bf16[4,1,64,128]{3,2,1,0:T(8,128)(2,1)S(1)} %get-tuple-element.27), channel_id=1, source_target_pairs={{0,1},{1,2},{2,3},{3,4},{4,5},{5,6},{6,7},{7,8},{8,9},{9,10},{10,1... | collective-permute-start | bytes 196616 | tf_op jit(solution)/shard_map/ppermute | solution.py:29
  20.4 12.1 %collective-permute-start.4 = (bf16[4,1,64,128]{3,2,1,0:T(8,128)(2,1)S(1)}, bf16[4,1,64,128]{3,2,1,0:T(8,128)(2,1)S(1)}, u32[]{:S(2)}, u32[]{:S(2)}) collective-permute-start(bf16[4,1,64,128]{3,2,1,0:T(8,128)(2,1)S(1)} %get-tuple-element.28), channel_id=1, source_target_pairs={{1,0},{2,1},{3,2},{4,3},{5,4},{6,5},{7,6},{8,7},{9,8},{10,9},{11,1... | collective-permute-start | bytes 196616 | tf_op jit(solution)/shard_map/ppermute | solution.py:29
  22.4 12.6 %collective-permute-start.5 = (bf16[4,96,128]{2,1,0:T(8,128)(2,1)S(1)}, bf16[4,96,128]{2,1,0:T(8,128)(2,1)S(1)}, u32[]{:S(2)}, u32[]{:S(2)}) collective-permute-start(bf16[4,96,128]{2,1,0:T(8,128)(2,1)S(1)} %pad_maximum_fusion.4), channel_id=1, source_target_pairs={{0,256},{256,0},{1,257},{257,1},{2,258},{258,2},{3,259},{259,3},{4... | collective-permute-start | bytes 294920 | tf_op jit(solution)/shard_map/ppermute | solution.py:166
  30.1 48.6 %collective-permute-start.9 = (bf16[576,1536]{1,0:T(8,128)(2,1)}, bf16[576,1536]{1,0:T(8,128)(2,1)}, u32[]{:S(2)}, u32[]{:S(2)}) collective-permute-start(bf16[576,1536]{1,0:T(8,128)(2,1)} %shard_map.100.w0_ref), channel_id=1, source_target_pairs={{0,64},{64,0},{128,192},{192,128},{1,65},{65,1},{129,193},{193,129... | collective-permute-start | bytes 5308424 | tf_op jit(solution)/shard_map/ppermute | solution.py:157
  34.0 4.7 %copy-start.6 = (bf16[128,16]{0,1:T(8,128)(2,1)S(1)}, bf16[128,16]{0,1:T(8,128)(2,1)}, u32[]{:S(2)}) copy-start(bf16[128,16]{0,1:T(8,128)(2,1)} %param.12) | copy-start | bytes 12292
  35.0 4.7 %collective-permute-start.6 = (bf16[8,96,128]{2,1,0:T(8,128)(2,1)S(1)}, bf16[8,96,128]{2,1,0:T(8,128)(2,1)S(1)}, u32[]{:S(2)}, u32[]{:S(2)}) collective-permute-start(bf16[8,96,128]{2,1,0:T(8,128)(2,1)S(1)} %pad_maximum_fusion.3), channel_id=1, source_target_pairs={{0,32},{32,0},{1,33},{33,1},{2,34},{34,2},{3,35},{35,3},{4,36},{36... | collective-permute-start | bytes 589832 | tf_op jit(solution)/shard_map/ppermute | solution.py:166
  44.4 34.2 %all-to-all-start = ((bf16[64,2,1664]{2,1,0:T(2,128)(2,1)}), bf16[64,2,1664]{2,1,0:T(2,128)(2,1)S(1)}, u32[]{:S(2)}, u32[]{:S(2)}) async-start(bf16[64,2,1664]{2,1,0:T(2,128)(2,1)} %reshape.58), calls=%async_computation | async-start | bytes 851968 | tf_op jit(solution)/shard_map/all_to_all | solution.py:177
  60.9 35.1 %collective-permute-start.8 = (bf16[576,1536]{1,0:T(8,128)(2,1)}, bf16[576,1536]{1,0:T(8,128)(2,1)S(1)}, u32[]{:S(2)}, u32[]{:S(2)}) collective-permute-start(bf16[576,1536]{1,0:T(8,128)(2,1)} %shard_map.100.w0_ref), channel_id=1, source_target_pairs={{0,32},{32,0},{1,33},{33,1},{2,34},{34,2},{3,35},{35,3},{4,36},{36... | collective-permute-start | bytes 5308424 | tf_op jit(solution)/shard_map/ppermute | solution.py:158
  78.8 17.3 %collective-permute-start.10 = (bf16[576,1536]{1,0:T(8,128)(2,1)}, bf16[576,1536]{1,0:T(8,128)(2,1)}, u32[]{:S(2)}, u32[]{:S(2)}) collective-permute-start(bf16[576,1536]{1,0:T(8,128)(2,1)} %collective-permute-done.9.w2_ref), channel_id=1, source_target_pairs={{0,32},{32,0},{1,33},{33,1},{2,34},{34,2},{3,35},{35,3},{4,36},{36... | collective-permute-start | bytes 5308424 | tf_op jit(solution)/shard_map/ppermute | solution.py:181
  80.7 15.3 %collective-permute-start.7 = (bf16[128,1664]{1,0:T(8,128)(2,1)S(1)}, bf16[128,1664]{1,0:T(8,128)(2,1)S(1)}, u32[]{:S(2)}, u32[]{:S(2)}) collective-permute-start(bf16[128,1664]{1,0:T(8,128)(2,1)S(1)} %reshape.59.rows_ref), channel_id=1, source_target_pairs={{0,192},{64,128},{128,64},{192,0},{1,193},{65,129},{129,65},{193,1... | collective-permute-start | bytes 1277960 | tf_op jit(solution)/shard_map/ppermute | solution.py:179
  100.5 13.8 %collective-permute-start.11 = (bf16[128,1536]{1,0:T(8,128)(2,1)S(1)}, bf16[128,1536]{1,0:T(8,128)(2,1)S(1)}, u32[]{:S(2)}, u32[]{:S(2)}) collective-permute-start(bf16[128,1536]{1,0:T(8,128)(2,1)S(1)} %shard_map.103), channel_id=1, source_target_pairs={{0,192},{64,128},{128,64},{192,0},{1,193},{65,129},{129,65},{193,1... | collective-permute-start | bytes 1179656 | tf_op jit(solution)/shard_map/ppermute | solution.py:204

commit v5 on v4

--- a/solution.py
+++ b/solution.py
@@ -29,6 +29,10 @@
     return lax.ppermute(value, axes, pairs)
 
 
+def ring(value, step):
+    return lax.ppermute(value, "x", [(i, (i - step) % 4) for i in range(4)])
+
+
 def encode(video, past, conv_weight, latent_weight):
     frames, rows, cols, chans = video.shape
     stacked = jnp.concatenate([past, video], axis=0)
@@ -87,36 +91,62 @@
     for shard in range(16):
         apart = shard // 2 % 4 ^ x
         mirror = apart // 2
-        at = (apart % 2 ^ mirror) + mirror * 2 + (shard // 8 ^ yh) * 4 + (shard % 2 ^ c) * 8
+        at = mirror * 8 + (apart % 2 ^ mirror) * 4 + (shard % 2 ^ c) * 2 + (shard // 8 ^ yh)
         out_ref[shard * size : (shard + 1) * size] = parts_ref[at]
 
 
-def expert_kernel(rows_ref, embed_ref, router_ref, w0_ref, w1_ref, w2_ref, w3_ref, out_ref, held_ref, sems):
-    width = out_ref.shape[1]
+def silu(value):
+    return value / (1.0 + jnp.exp(-value))
+
+
+def near_kernel(
+    mine_ref, theirs_ref, embed_ref, router_ref, w0_ref, w1_ref, w2_ref, tokens_ref, score_ref, total_ref, held_ref, sems
+):
+    rows, width = mine_ref.shape[0], total_ref.shape[1]
     share = w0_ref.shape[0] // 3
-    copies = [
-        pltpu.make_async_copy(ref, held_ref.at[i], sems.at[i])
-        for i, ref in enumerate((w0_ref, w1_ref, w2_ref, w3_ref))
-    ]
+    copies = [pltpu.make_async_copy(ref, held_ref.at[i], sems.at[i]) for i, ref in enumerate((w0_ref, w1_ref, w2_ref))]
     for copy in copies:
         copy.start()
-    embedded = dot(rows_ref[:, width:], embed_ref[...], ((1,), (1,))).astype(BF)
-    total = embedded.astype(F32) + rows_ref[:, :width].astype(F32)
-    meansq = jnp.mean(total * total, axis=1, keepdims=True)
-    tokens = (total * lax.rsqrt(meansq + 1e-06)).astype(BF)
-    logit = jnp.sum(tokens.astype(F32) * router_ref[...].astype(F32), axis=1, keepdims=True)
-    score = 1.0 / (1.0 + jnp.exp(-logit))
+    for half, ref in enumerate((theirs_ref, mine_ref)):
+        embedded = dot(ref[:, width:], embed_ref[...], ((1,), (1,))).astype(BF)
+        total = embedded.astype(F32) + ref[:, :width].astype(F32)
+        meansq = jnp.mean(total * total, axis=1, keepdims=True)
+        tokens = (total * lax.rsqrt(meansq + 1e-06)).astype(BF)
+        logit = jnp.sum(tokens.astype(F32) * router_ref[...].astype(F32), axis=1, keepdims=True)
+        at = slice(half * rows, (half + 1) * rows)
+        tokens_ref[at] = tokens
+        score_ref[at] = 1.0 / (1.0 + jnp.exp(-logit))
     hidden = []
     for i, copy in enumerate(copies):
         copy.wait()
-        both = dot(tokens, held_ref[i, : 2 * share], ((1,), (1,)))
-        gate, up = both[:, :share], both[:, share:]
-        hidden.append((gate / (1.0 + jnp.exp(-gate)) * up).astype(BF))
+        both = dot(tokens_ref[...], held_ref[i, : 2 * share], ((1,), (1,)))
+        hidden.append((silu(both[:, :share]) * both[:, share:]).astype(BF))
     hidden = jnp.concatenate(hidden, axis=1)
     tile = 512
     for at in range(0, width, tile):
-        down = jnp.concatenate([held_ref[i, 2 * share :, at : at + tile] for i in range(4)], axis=0)
-        out_ref[:, at : at + tile] = (dot(hidden, down) * score).astype(BF)
+        down = jnp.concatenate([held_ref[i, 2 * share :, at : at + tile] for i in range(3)], axis=0)
+        total_ref[:, at : at + tile] = dot(hidden, down)
+
+
+def last_kernel(tokens_ref, score_ref, total_ref, w0_ref, w1_ref, other_ref, own_ref, held_ref, sems):
+    rows, width = other_ref.shape
+    part, share = w0_ref.shape[0], held_ref.shape[0] // 3
+    copies = [
+        pltpu.make_async_copy(ref, held_ref.at[pl.ds(i * part, part)], sems.at[i]) for i, ref in enumerate((w0_ref, w1_ref))
+    ]
+    for copy in copies:
+        copy.start()
+    for copy in copies:
+        copy.wait()
+    both = dot(tokens_ref[...], held_ref[: 2 * share], ((1,), (1,)))
+    hidden = (silu(both[:, :share]) * both[:, share:]).astype(BF)
+    tile = 512
+    for at in range(0, width, tile):
+        cut = slice(at, at + tile)
+        total = total_ref[:, cut] + dot(hidden, held_ref[2 * share :, cut])
+        total = (total * score_ref[...]).astype(BF)
+        other_ref[:, cut] = total[:rows]
+        own_ref[:, cut] = total[rows:]
 
 
 def local(
@@ -150,59 +180,64 @@
         scratch_shapes=[pltpu.SemaphoreType.DMA((3,))],
         compiler_params=params,
     )(gate_weight[0].T, up_weight[0].T, down_weight[0])
-    parts = embed_weight.T[None]
-    for axis, pairs in (("x", XOR1), ("x", XOR3)):
-        parts = jnp.concatenate([parts, lax.ppermute(parts, axis, pairs)], axis=0)
-    held, past, parts = lax.optimization_barrier((held, past, parts))
-    across = lax.ppermute(held, "x", XOR1)
-    beside = lax.ppermute(held, "c", SWAP)
+    held, past = lax.optimization_barrier((held, past))
+    behind, ahead = ring(held, -1), ring(held, 1)
 
     table = place_table(routes, experts, capacity)
     latent = encode(video, past, conv_weight, latent_weight)
     lat = latent.shape[1]
     blocks = latent.reshape(2, rows // 2, 2, cols // 2, 2, lat)
     patches = blocks.transpose(1, 3, 0, 2, 4, 5).reshape(tok, 8 * lat)
-    for axis in ("yh", "c"):
-        parts = jnp.concatenate([parts, lax.ppermute(parts, axis, SWAP)], axis=0)
-    patches, parts = lax.optimization_barrier((patches, parts))
     raw = width + patches.shape[1]
     outgoing = pl.pallas_call(
         dispatch_kernel,
         out_shape=jax.ShapeDtypeStruct((slots, raw), BF),
         in_specs=[vmem] * 3,
         out_specs=vmem,
-        compiler_params=pltpu.CompilerParams(vmem_limit_bytes=WIDE_BYTES),
+        compiler_params=params,
     )(patches, context, table)
 
     arrived = lax.all_to_all(outgoing.reshape(experts, capacity, raw), SOURCES, split_axis=0, concat_axis=0, tiled=True)
+    parts = embed_weight.T[None]
+    for axis, pairs in (("yh", SWAP), ("c", SWAP), ("x", XOR1), ("x", XOR3)):
+        parts = jnp.concatenate([parts, lax.ppermute(parts, axis, pairs)], axis=0)
+    part = 3 * share // 2
+    arrived, parts, first, second = lax.optimization_barrier((arrived, parts, behind[:part], ahead[part:]))
+    first, second = ring(first, -1), ring(second, 1)
+
     mine = arrived.reshape(slots, raw)
-    theirs = lax.ppermute(mine, "x", XOR3)
-    across, mine = lax.optimization_barrier((across, mine))
-    corner = lax.ppermute(across, "c", SWAP)
-    weights = (held, beside, across, corner)
-
+    theirs = lax.ppermute(mine, "c", SWAP)
     embed = pl.pallas_call(
         embed_kernel,
         out_shape=jax.ShapeDtypeStruct((width, parts.shape[2]), BF),
         in_specs=[smem, vmem],
         out_specs=vmem,
-        compiler_params=params,
+        compiler_params=pltpu.CompilerParams(vmem_limit_bytes=WIDE_BYTES),
     )(jnp.stack([lax.axis_index(axis) for axis in FRAME]).astype(jnp.int32), parts)
 
     router = lax.dynamic_index_in_dim(router_weight, lax.axis_index("yh"), 0, keepdims=False).reshape(1, width)
 
-    def expert(block):
-        return pl.pallas_call(
-            expert_kernel,
-            out_shape=jax.ShapeDtypeStruct((slots, width), BF),
-            in_specs=[vmem] * 3 + [hbm] * 4,
-            out_specs=vmem,
-            scratch_shapes=[pltpu.VMEM((4, 3 * share, width), BF), pltpu.SemaphoreType.DMA((4,))],
-            compiler_params=params,
-        )(block, embed, router, *weights)
-
-    back = lax.ppermute(expert(theirs), "x", XOR3)
-    own = expert(mine)
+    tokens, score, total = pl.pallas_call(
+        near_kernel,
+        out_shape=[
+            jax.ShapeDtypeStruct((2 * slots, width), BF),
+            jax.ShapeDtypeStruct((2 * slots, 1), F32),
+            jax.ShapeDtypeStruct((2 * slots, width), F32),
+        ],
+        in_specs=[vmem] * 4 + [hbm] * 3,
+        out_specs=[vmem] * 3,
+        scratch_shapes=[pltpu.VMEM((3, 3 * share, width), BF), pltpu.SemaphoreType.DMA((3,))],
+        compiler_params=params,
+    )(mine, theirs, embed, router, held, behind, ahead)
+    other, own = pl.pallas_call(
+        last_kernel,
+        out_shape=[jax.ShapeDtypeStruct((slots, width), BF)] * 2,
+        in_specs=[vmem] * 3 + [hbm] * 2,
+        out_specs=[vmem] * 2,
+        scratch_shapes=[pltpu.VMEM((3 * share, width), BF), pltpu.SemaphoreType.DMA((2,))],
+        compiler_params=params,
+    )(tokens, score, total, first, second)
+    back = lax.ppermute(other, "c", SWAP)
     summed = (back.astype(F32) + own.astype(F32)).astype(BF).reshape(experts, capacity, width)
     homeward = lax.all_to_all(summed, SOURCES, split_axis=0, concat_axis=0, tiled=True)
     return dot(table, homeward.reshape(slots, width)).astype(BF)

time: 140 us -> 154 us (1.10)
  local copies, waits for them, and re-layouts: 7.1 us -> 20.4 us
  waiting for transfers between devices: 34.1 us -> 22.8 us
  blocking collectives: 22.4 us -> 33.2 us
  Pallas kernels: 12.9 us -> 9.8 us
  matrix products: 2.69 us -> 4.52 us
  starting transfers between devices: 55.9 us -> 57.6 us
    all_to_all x1, waiting for transfers between devices: 15.7 us -> 0.01 us  [local(): lax.all_to_all(outgoing.reshape(experts, capacity, raw), SOURCES, split_a...]
    ppermute x2 -> x4, waiting for transfers between devices: 0.58 us -> 13.4 us  [local(): parts = jnp.concatenate([parts, lax.ppermute(parts, axis, pairs)], axis=0)]
    all_to_all x1, blocking collectives: 22.4 us -> 33.2 us  [local(): lax.all_to_all(summed, SOURCES, split_axis=0, concat_axis=0, tiled=True)]
    ppermute x7 -> x6, waiting for transfers between devices: 17.8 us -> 9.46 us  [the longest x4 7.77 us: ring(): return lax.ppermute(value, 'x', [(i, (i - step) % 4) for i in range(4)])]
    unnamed x23 -> x45, local copies, waits for them, and re-layouts: 1.3 us -> 9.43 us
    ppermute x7 -> x6, starting transfers between devices: 23.8 us -> 16 us  [the longest x4 12.2 us: ring(): return lax.ppermute(value, 'x', [(i, (i - step) % 4) for i in range(4)])]
    ppermute x2 -> x4, starting transfers between devices: 9.17 us -> 16.4 us  [local(): parts = jnp.concatenate([parts, lax.ppermute(parts, axis, pairs)], axis=0)]
    slice x0 -> x2, local copies, waits for them, and re-layouts: none -> 4.3 us  [the longest x1 2.15 us: local(): behind[:part]]
  transfers between devices with their start and end apart: 13 -> 14, of which waited for: 4 -> 5; matrix products, arithmetic and copies ran while one was open for 8% -> 15% of each run, Pallas kernels for 6% -> 5%
where the time goes in v5:
time: 154 us; the launch traced here: 153 us
  starting transfers between devices  57.6 us (37%)
  blocking collectives  33.2 us (22%)
  waiting for transfers between devices  22.8 us (15%)
  local copies, waits for them, and re-layouts  20.4 us (13%)
  Pallas kernels  9.8 us (6%)
  matrix products  4.52 us (3%)
  other arithmetic  4.14 us (3%)
    all_to_all x1, blocking collectives, local(): lax.all_to_all(summed, SOURCES, split_axis=0, concat_axis=0, tiled=True)  33.2 us
    all_to_all x1, starting transfers between devices, local(): lax.all_to_all(outgoing.reshape(experts, capacity, raw), SOURCES, split_a...  17.5 us
    ppermute x4, starting transfers between devices, local(): parts = jnp.concatenate([parts, lax.ppermute(parts, axis, pairs)], axis=0)  16.4 us
    ppermute x4, waiting for transfers between devices, local(): parts = jnp.concatenate([parts, lax.ppermute(parts, axis, pairs)], axis=0)  13.4 us
    ppermute x4, starting transfers between devices, ring(): return lax.ppermute(value, 'x', [(i, (i - step) % 4) for i in range(4)])  12.2 us
    unnamed x45, local copies, waits for them, and re-layouts  9.43 us
    ppermute x4, waiting for transfers between devices, ring(): return lax.ppermute(value, 'x', [(i, (i - step) % 4) for i in range(4)])  7.77 us
    ppermute x3, starting transfers between devices, shifted(): return lax.ppermute(value, axes, pairs)  7.63 us
  transfers between devices with their start and end apart: 14, of which 5 were waited for; matrix products, arithmetic and copies ran while one was open for 15% of the time, Pallas kernels for 5%

profile of v5, /device:TPU:6, one launch (start us, length us, event | category | flops | bytes accessed | tf_op | source)
XLA Modules:
  0.0 153.1 jit_solution(16879168698664855622)
XLA Ops:
  0.0 2.1 %collective-permute-start = (bf16[2,4,64,128]{3,2,1,0:T(8,128)(2,1)}, bf16[2,4,64,128]{3,2,1,0:T(8,128)(2,1)S(1)}, u32[]{:S(2)}, u32[]{:S(2)}) collective-permute-start(bf16[2,4,64,128]{3,2,1,0:T(8,128)(2,1)} %param.10), channel_id=1, source_target_pairs={{0,32},{32,64},{64,96},{96,128},{128,160},{160,192},{192,224},{224... | collective-permute-start | bytes 393224 | tf_op jit(solution)/shard_map/ppermute | solution.py:29
  2.1 7.7 %collective-permute-start.3 = (bf16[1,96,128]{2,1,0:T(8,128)(2,1)}, bf16[1,96,128]{2,1,0:T(8,128)(2,1)}, u32[]{:S(2)}, u32[]{:S(2)}) collective-permute-start(bf16[1,96,128]{2,1,0:T(8,128)(2,1)} %bitcast.47), channel_id=1, source_target_pairs={{0,256},{256,0},{1,257},{257,1},{2,258},{258,2},{3,259},{259,3},{4... | collective-permute-start | bytes 73736 | tf_op jit(solution)/shard_map/ppermute | solution.py:203
  11.3 2.0 %fusion.20 = (bf16[1,3,3,128,128]{4,3,2,1,0:T(8,128)(2,1)}, bf16[1,3,3,128,128]{4,3,2,1,0:T(8,128)(2,1)}, bf16[1,3,3,128,128]{4,3,2,1,0:T(8,128)(2,1)S(1)}) fusion(bf16[3,3,3,128,128]{4,3,2,1,0:T(8,128)(2,1)} %param.11), kind=kLoop, calls=%fused_computation.58 | loop fusion | bytes 1769472 | tf_op jit(solution)/shard_map/slice | solution.py:50
  15.8 4.3 %collective-permute-start.1 = (bf16[4,1,64,128]{3,2,1,0:T(8,128)(2,1)S(1)}, bf16[4,1,64,128]{3,2,1,0:T(8,128)(2,1)S(1)}, u32[]{:S(2)}, u32[]{:S(2)}) collective-permute-start(bf16[4,1,64,128]{3,2,1,0:T(8,128)(2,1)S(1)} %get-tuple-element.35), channel_id=1, source_target_pairs={{0,1},{1,2},{2,3},{3,4},{4,5},{5,6},{6,7},{7,8},{8,9},{9,10},{10,1... | collective-permute-start | bytes 196616 | tf_op jit(solution)/shard_map/ppermute | solution.py:29
  22.1 1.9 %collective-permute-start.4 = (bf16[2,96,128]{2,1,0:T(8,128)(2,1)S(1)}, bf16[2,96,128]{2,1,0:T(8,128)(2,1)}, u32[]{:S(2)}, u32[]{:S(2)}) collective-permute-start(bf16[2,96,128]{2,1,0:T(8,128)(2,1)S(1)} %pad_maximum_fusion.4), channel_id=1, source_target_pairs={{0,32},{32,0},{1,33},{33,1},{2,34},{34,2},{3,35},{35,3},{4,36},{36... | collective-permute-start | bytes 147464 | tf_op jit(solution)/shard_map/ppermute | solution.py:203
  24.0 3.4 %collective-permute-start.7 = (bf16[576,1536]{1,0:T(8,128)(2,1)S(1)}, bf16[576,1536]{1,0:T(8,128)(2,1)}, u32[]{:S(2)}, u32[]{:S(2)}) collective-permute-start(bf16[576,1536]{1,0:T(8,128)(2,1)S(1)} %shard_map.100.w0_ref), channel_id=1, source_target_pairs={{0,64},{64,128},{128,192},{192,0},{1,65},{65,129},{129,193},{193,1... | collective-permute-start | bytes 5308424 | tf_op jit(solution)/shard_map/ppermute | solution.py:33
  27.4 2.4 %collective-permute-start.8 = (bf16[576,1536]{1,0:T(8,128)(2,1)S(1)}, bf16[576,1536]{1,0:T(8,128)(2,1)}, u32[]{:S(2)}, u32[]{:S(2)}) collective-permute-start(bf16[576,1536]{1,0:T(8,128)(2,1)S(1)} %shard_map.100.w0_ref), channel_id=1, source_target_pairs={{0,192},{64,0},{128,64},{192,128},{1,193},{65,1},{129,65},{193,129... | collective-permute-start | bytes 5308424 | tf_op jit(solution)/shard_map/ppermute | solution.py:33
  37.0 17.5 %all-to-all-start = ((bf16[64,2,1664]{2,1,0:T(2,128)(2,1)}), bf16[64,2,1664]{2,1,0:T(2,128)(2,1)}, u32[]{:S(2)}, u32[]{:S(2)}) async-start(bf16[64,2,1664]{2,1,0:T(2,128)(2,1)} %reshape.58), calls=%async_computation | async-start | bytes 851968 | tf_op jit(solution)/shard_map/all_to_all | solution.py:200
  56.0 1.9 %collective-permute-start.5 = (bf16[4,96,128]{2,1,0:T(8,128)(2,1)S(1)}, bf16[4,96,128]{2,1,0:T(8,128)(2,1)S(1)}, u32[]{:S(2)}, u32[]{:S(2)}) collective-permute-start(bf16[4,96,128]{2,1,0:T(8,128)(2,1)S(1)} %pad_maximum_fusion.3), channel_id=1, source_target_pairs={{0,64},{64,0},{128,192},{192,128},{1,65},{65,1},{129,193},{193,129... | collective-permute-start | bytes 294920 | tf_op jit(solution)/shard_map/ppermute | solution.py:203
  59.2 11.0 %collective-permute-done.5 = bf16[4,96,128]{2,1,0:T(8,128)(2,1)S(1)} collective-permute-done((bf16[4,96,128]{2,1,0:T(8,128)(2,1)S(1)}, bf16[4,96,128]{2,1,0:T(8,128)(2,1)S(1)}, u32[]{:S(2)}, u32[]{:S(2)}) %collective-permute-start.5) | collective-permute-done | bytes 98336 | tf_op jit(solution)/shard_map/ppermute | solution.py:203
  71.0 4.9 %collective-permute-start.6 = (bf16[8,96,128]{2,1,0:T(8,128)(2,1)S(1)}, bf16[8,96,128]{2,1,0:T(8,128)(2,1)S(1)}, u32[]{:S(2)}, u32[]{:S(2)}) collective-permute-start(bf16[8,96,128]{2,1,0:T(8,128)(2,1)S(1)} %pad_maximum_fusion.2), channel_id=1, source_target_pairs={{0,192},{64,128},{128,64},{192,0},{1,193},{65,129},{129,65},{193,1... | collective-permute-start | bytes 589832 | tf_op jit(solution)/shard_map/ppermute | solution.py:203
  78.0 2.4 %collective-permute-done.6 = bf16[8,96,128]{2,1,0:T(8,128)(2,1)S(1)} collective-permute-done((bf16[8,96,128]{2,1,0:T(8,128)(2,1)S(1)}, bf16[8,96,128]{2,1,0:T(8,128)(2,1)S(1)}, u32[]{:S(2)}, u32[]{:S(2)}) %collective-permute-start.6) | collective-permute-done | bytes 196640 | tf_op jit(solution)/shard_map/ppermute | solution.py:203
  81.1 2.1 %slice.105 = bf16[288,1536]{1,0:T(8,128)(2,1)} slice(bf16[576,1536]{1,0:T(8,128)(2,1)} %collective-permute-done.7.w1_ref), slice={[0:288], [0:1536]} | slice | bytes 1769472 | tf_op jit(solution)/shard_map/slice | solution.py:205
  83.2 2.1 %slice.106 = bf16[288,1536]{1,0:T(8,128)(2,1)} slice(bf16[576,1536]{1,0:T(8,128)(2,1)} %collective-permute-done.8.w2_ref), slice={[288:576], [0:1536]} | slice | bytes 1769472 | tf_op jit(solution)/shard_map/slice | solution.py:205
  85.4 4.4 %collective-permute-start.10 = (bf16[288,1536]{1,0:T(8,128)(2,1)}, bf16[288,1536]{1,0:T(8,128)(2,1)S(1)}, u32[]{:S(2)}, u32[]{:S(2)}) collective-permute-start(bf16[288,1536]{1,0:T(8,128)(2,1)} %slice.105), channel_id=1, source_target_pairs={{0,64},{64,128},{128,192},{192,0},{1,65},{65,129},{129,193},{193,1... | collective-permute-start | bytes 2654216 | tf_op jit(solution)/shard_map/ppermute | solution.py:33
  89.8 1.9 %collective-permute-start.11 = (bf16[288,1536]{1,0:T(8,128)(2,1)}, bf16[288,1536]{1,0:T(8,128)(2,1)}, u32[]{:S(2)}, u32[]{:S(2)}) collective-permute-start(bf16[288,1536]{1,0:T(8,128)(2,1)} %slice.106), channel_id=1, source_target_pairs={{0,192},{64,0},{128,64},{192,128},{1,193},{65,1},{129,65},{193,129... | collective-permute-start | bytes 2654216 | tf_op jit(solution)/shard_map/ppermute | solution.py:33
  92.9 1.9 %collective-permute-start.9 = (bf16[128,1664]{1,0:T(8,128)(2,1)S(1)}, bf16[128,1664]{1,0:T(8,128)(2,1)}, u32[]{:S(2)}, u32[]{:S(2)}) collective-permute-start(bf16[128,1664]{1,0:T(8,128)(2,1)S(1)} %reshape.59.mine_ref), channel_id=1, source_target_pairs={{0,32},{32,0},{1,33},{33,1},{2,34},{34,2},{3,35},{35,3},{4,36},{36... | collective-permute-start | bytes 1277960 | tf_op jit(solution)/shard_map/ppermute | solution.py:209
  95.5 1.9 %shard_map.102.embed_ref = bf16[1536,128]{1,0:T(8,128)(2,1)} custom-call(s32[3]{0:T(128)} %pad_add_fusion.at_ref, bf16[16,96,128]{2,1,0:T(8,128)(2,1)} %constant_dynamic-update-slice_fusion.4.parts_ref), custom_call_target="tpu_custom_call" | custom-call | tf_op jit(solution)/shard_map/pallas_call | solution.py:210
  99.8 4.9 %shard_map.103 = (bf16[256,1536]{1,0:T(8,128)(2,1)S(1)}, f32[256,1]{1,0:T(8,128)S(1)}, f32[256,1536]{1,0:T(8,128)S(1)}) custom-call(bf16[128,1664]{1,0:T(8,128)(2,1)S(1)} %reshape.59.mine_ref, bf16[128,1664]{1,0:T(8,128)(2,1)} %collective-permute-done.9.theirs_ref, bf16[1536,128]{1,0:T(8,128)(2,1)S(1)} %copy-done.3, ...), custom_call_target="tpu_custom_call" | custom-call | tf_op jit(solution)/shard_map/pallas_call | solution.py:220
  104.7 2.7 %collective-permute-done.10.w0_ref = bf16[288,1536]{1,0:T(8,128)(2,1)S(1)} collective-permute-done((bf16[288,1536]{1,0:T(8,128)(2,1)}, bf16[288,1536]{1,0:T(8,128)(2,1)S(1)}, u32[]{:S(2)}, u32[]{:S(2)}) %collective-permute-start.10) | collective-permute-done | bytes 884768 | tf_op jit(solution)/shard_map/ppermute | solution.py:33
  107.5 5.0 %collective-permute-done.11.w1_ref = bf16[288,1536]{1,0:T(8,128)(2,1)} collective-permute-done((bf16[288,1536]{1,0:T(8,128)(2,1)}, bf16[288,1536]{1,0:T(8,128)(2,1)}, u32[]{:S(2)}, u32[]{:S(2)}) %collective-permute-start.11) | collective-permute-done | bytes 884768 | tf_op jit(solution)/shard_map/ppermute | solution.py:33
  112.5 2.3 %shard_map.104 = (bf16[128,1536]{1,0:T(8,128)(2,1)S(1)}, bf16[128,1536]{1,0:T(8,128)(2,1)S(1)}) custom-call(bf16[256,1536]{1,0:T(8,128)(2,1)S(1)} %get-tuple-element.20.tokens_ref, f32[256,1]{1,0:T(8,128)S(1)} %get-tuple-element.21.score_ref, f32[256,1536]{1,0:T(8,128)S(1)} %get-tuple-element.22.total_ref, ...), custom_call_target="tpu_custom_call" | custom-call | tf_op jit(solution)/shard_map/pallas_call | solution.py:232
  114.9 1.9 %collective-permute-start.12 = (bf16[128,1536]{1,0:T(8,128)(2,1)S(1)}, bf16[128,1536]{1,0:T(8,128)(2,1)S(1)}, u32[]{:S(2)}, u32[]{:S(2)}) collective-permute-start(bf16[128,1536]{1,0:T(8,128)(2,1)S(1)} %get-tuple-element.25), channel_id=1, source_target_pairs={{0,32},{32,0},{1,33},{33,1},{2,34},{34,2},{3,35},{35,3},{4,36},{36... | collective-permute-start | bytes 1179656 | tf_op jit(solution)/shard_map/ppermute | solution.py:240
  118.7 33.2 %all_to_all.10 = bf16[64,2,1536]{2,1,0:T(2,128)(2,1)S(1)} all-to-all(bf16[64,2,1536]{2,1,0:T(2,128)(2,1)S(1)} %reshape.61), channel_id=1, replica_groups=mesh['yh'=2,'x'=4,'c'=2,'yl'=4,'z'=8] {'yh','yl','z'}, dimensions={0} | all-to-all | bytes 786432 | tf_op jit(solution)/shard_map/all_to_all | solution.py:242
  (93 shorter events, 26.4 us)
Async XLA Ops:
  0.0 95.4 %copy-start = (bf16[2,1536,1]{1,0,2:T(2,128)(2,1)S(1)}, bf16[2,1536,1]{1,0,2:T(2,128)(2,1)}, u32[]{:S(2)}) copy-start(bf16[2,1536,1]{1,0,2:T(2,128)(2,1)} %param.15) | copy-start | bytes 18436
  0.0 14.1 %copy-start.4 = (bf16[1,1536,192]{1,2,0:T(8,128)(2,1)S(1)}, bf16[1,1536,192]{1,2,0:T(8,128)(2,1)}, u32[]{:S(2)}) copy-start(bf16[1,1536,192]{1,2,0:T(8,128)(2,1)} %param.16) | copy-start | bytes 1769476
  0.0 14.1 %copy-start.5 = (bf16[1,1536,192]{1,2,0:T(8,128)(2,1)S(1)}, bf16[1,1536,192]{1,2,0:T(8,128)(2,1)}, u32[]{:S(2)}) copy-start(bf16[1,1536,192]{1,2,0:T(8,128)(2,1)} %param.17) | copy-start | bytes 1769476
  0.0 15.7 %collective-permute-start = (bf16[2,4,64,128]{3,2,1,0:T(8,128)(2,1)}, bf16[2,4,64,128]{3,2,1,0:T(8,128)(2,1)S(1)}, u32[]{:S(2)}, u32[]{:S(2)}) collective-permute-start(bf16[2,4,64,128]{3,2,1,0:T(8,128)(2,1)} %param.10), channel_id=1, source_target_pairs={{0,32},{32,64},{64,96},{96,128},{128,160},{160,192},{192,224},{224... | collective-permute-start | bytes 393224 | tf_op jit(solution)/shard_map/ppermute | solution.py:29
  2.1 19.3 %collective-permute-start.3 = (bf16[1,96,128]{2,1,0:T(8,128)(2,1)}, bf16[1,96,128]{2,1,0:T(8,128)(2,1)}, u32[]{:S(2)}, u32[]{:S(2)}) collective-permute-start(bf16[1,96,128]{2,1,0:T(8,128)(2,1)} %bitcast.47), channel_id=1, source_target_pairs={{0,256},{256,0},{1,257},{257,1},{2,258},{258,2},{3,259},{259,3},{4... | collective-permute-start | bytes 73736 | tf_op jit(solution)/shard_map/ppermute | solution.py:203
  13.3 8.0 %copy-start.10 = (bf16[128,96]{0,1:T(8,128)(2,1)S(1)}, bf16[128,96]{0,1:T(8,128)(2,1)}, u32[]{:S(2)}) copy-start(bf16[128,96]{0,1:T(8,128)(2,1)} %param.13) | copy-start | bytes 73732
  14.1 16.0 %copy-start.11 = (s32[64]{0:T(128)}, s32[64]{0:T(128)S(1)}, u32[]{:S(2)}) copy-start(s32[64]{0:T(128)S(1)} %get-tuple-element.27) | copy-start | bytes 772
  14.1 16.0 %copy-start.13 = (s32[64]{0:T(128)}, s32[64]{0:T(128)S(1)}, u32[]{:S(2)}) copy-start(s32[64]{0:T(128)S(1)} %get-tuple-element.28) | copy-start | bytes 772
  15.6 15.0 %copy-start.1 = (bf16[576,1536]{1,0:T(8,128)(2,1)}, bf16[576,1536]{1,0:T(8,128)(2,1)S(1)}, u32[]{:S(2)}) copy-start(bf16[576,1536]{1,0:T(8,128)(2,1)S(1)} %shard_map.100.w0_ref) | copy-start | bytes 5308420
  15.8 14.1 %collective-permute-start.1 = (bf16[4,1,64,128]{3,2,1,0:T(8,128)(2,1)S(1)}, bf16[4,1,64,128]{3,2,1,0:T(8,128)(2,1)S(1)}, u32[]{:S(2)}, u32[]{:S(2)}) collective-permute-start(bf16[4,1,64,128]{3,2,1,0:T(8,128)(2,1)S(1)} %get-tuple-element.35), channel_id=1, source_target_pairs={{0,1},{1,2},{2,3},{3,4},{4,5},{5,6},{6,7},{7,8},{8,9},{9,10},{10,1... | collective-permute-start | bytes 196616 | tf_op jit(solution)/shard_map/ppermute | solution.py:29
  20.0 9.9 %collective-permute-start.2 = (bf16[4,1,64,128]{3,2,1,0:T(8,128)(2,1)S(1)}, bf16[4,1,64,128]{3,2,1,0:T(8,128)(2,1)S(1)}, u32[]{:S(2)}, u32[]{:S(2)}) collective-permute-start(bf16[4,1,64,128]{3,2,1,0:T(8,128)(2,1)S(1)} %get-tuple-element.36), channel_id=1, source_target_pairs={{1,0},{2,1},{3,2},{4,3},{5,4},{6,5},{7,6},{8,7},{9,8},{10,9},{11,1... | collective-permute-start | bytes 196616 | tf_op jit(solution)/shard_map/ppermute | solution.py:29
  22.1 33.0 %collective-permute-start.4 = (bf16[2,96,128]{2,1,0:T(8,128)(2,1)S(1)}, bf16[2,96,128]{2,1,0:T(8,128)(2,1)}, u32[]{:S(2)}, u32[]{:S(2)}) collective-permute-start(bf16[2,96,128]{2,1,0:T(8,128)(2,1)S(1)} %pad_maximum_fusion.4), channel_id=1, source_target_pairs={{0,32},{32,0},{1,33},{33,1},{2,34},{34,2},{3,35},{35,3},{4,36},{36... | collective-permute-start | bytes 147464 | tf_op jit(solution)/shard_map/ppermute | solution.py:203
  24.0 57.0 %collective-permute-start.7 = (bf16[576,1536]{1,0:T(8,128)(2,1)S(1)}, bf16[576,1536]{1,0:T(8,128)(2,1)}, u32[]{:S(2)}, u32[]{:S(2)}) collective-permute-start(bf16[576,1536]{1,0:T(8,128)(2,1)S(1)} %shard_map.100.w0_ref), channel_id=1, source_target_pairs={{0,64},{64,128},{128,192},{192,0},{1,65},{65,129},{129,193},{193,1... | collective-permute-start | bytes 5308424 | tf_op jit(solution)/shard_map/ppermute | solution.py:33
  27.4 55.8 %collective-permute-start.8 = (bf16[576,1536]{1,0:T(8,128)(2,1)S(1)}, bf16[576,1536]{1,0:T(8,128)(2,1)}, u32[]{:S(2)}, u32[]{:S(2)}) collective-permute-start(bf16[576,1536]{1,0:T(8,128)(2,1)S(1)} %shard_map.100.w0_ref), channel_id=1, source_target_pairs={{0,192},{64,0},{128,64},{192,128},{1,193},{65,1},{129,65},{193,129... | collective-permute-start | bytes 5308424 | tf_op jit(solution)/shard_map/ppermute | solution.py:33
  32.3 3.4 %copy-start.7 = (bf16[64,1536]{1,0:T(8,128)(2,1)S(1)}, bf16[64,1536]{1,0:T(8,128)(2,1)}, u32[]{:S(2)}) copy-start(bf16[64,1536]{1,0:T(8,128)(2,1)} %context_ref.1) | copy-start | bytes 589828
  37.0 48.4 %all-to-all-start = ((bf16[64,2,1664]{2,1,0:T(2,128)(2,1)}), bf16[64,2,1664]{2,1,0:T(2,128)(2,1)}, u32[]{:S(2)}, u32[]{:S(2)}) async-start(bf16[64,2,1664]{2,1,0:T(2,128)(2,1)} %reshape.58), calls=%async_computation | async-start | bytes 851968 | tf_op jit(solution)/shard_map/all_to_all | solution.py:200
  56.0 14.3 %collective-permute-start.5 = (bf16[4,96,128]{2,1,0:T(8,128)(2,1)S(1)}, bf16[4,96,128]{2,1,0:T(8,128)(2,1)S(1)}, u32[]{:S(2)}, u32[]{:S(2)}) collective-permute-start(bf16[4,96,128]{2,1,0:T(8,128)(2,1)S(1)} %pad_maximum_fusion.3), channel_id=1, source_target_pairs={{0,64},{64,0},{128,192},{192,128},{1,65},{65,1},{129,193},{193,129... | collective-permute-start | bytes 294920 | tf_op jit(solution)/shard_map/ppermute | solution.py:203
  71.0 9.3 %collective-permute-start.6 = (bf16[8,96,128]{2,1,0:T(8,128)(2,1)S(1)}, bf16[8,96,128]{2,1,0:T(8,128)(2,1)S(1)}, u32[]{:S(2)}, u32[]{:S(2)}) collective-permute-start(bf16[8,96,128]{2,1,0:T(8,128)(2,1)S(1)} %pad_maximum_fusion.2), channel_id=1, source_target_pairs={{0,192},{64,128},{128,64},{192,0},{1,193},{65,129},{129,65},{193,1... | collective-permute-start | bytes 589832 | tf_op jit(solution)/shard_map/ppermute | solution.py:203
  85.4 22.1 %collective-permute-start.10 = (bf16[288,1536]{1,0:T(8,128)(2,1)}, bf16[288,1536]{1,0:T(8,128)(2,1)S(1)}, u32[]{:S(2)}, u32[]{:S(2)}) collective-permute-start(bf16[288,1536]{1,0:T(8,128)(2,1)} %slice.105), channel_id=1, source_target_pairs={{0,64},{64,128},{128,192},{192,0},{1,65},{65,129},{129,193},{193,1... | collective-permute-start | bytes 2654216 | tf_op jit(solution)/shard_map/ppermute | solution.py:33
  89.8 22.7 %collective-permute-start.11 = (bf16[288,1536]{1,0:T(8,128)(2,1)}, bf16[288,1536]{1,0:T(8,128)(2,1)}, u32[]{:S(2)}, u32[]{:S(2)}) collective-permute-start(bf16[288,1536]{1,0:T(8,128)(2,1)} %slice.106), channel_id=1, source_target_pairs={{0,192},{64,0},{128,64},{192,128},{1,193},{65,1},{129,65},{193,129... | collective-permute-start | bytes 2654216 | tf_op jit(solution)/shard_map/ppermute | solution.py:33
  92.9 4.4 %collective-permute-start.9 = (bf16[128,1664]{1,0:T(8,128)(2,1)S(1)}, bf16[128,1664]{1,0:T(8,128)(2,1)}, u32[]{:S(2)}, u32[]{:S(2)}) collective-permute-start(bf16[128,1664]{1,0:T(8,128)(2,1)S(1)} %reshape.59.mine_ref), channel_id=1, source_target_pairs={{0,32},{32,0},{1,33},{33,1},{2,34},{34,2},{3,35},{35,3},{4,36},{36... | collective-permute-start | bytes 1277960 | tf_op jit(solution)/shard_map/ppermute | solution.py:209
  114.8 37.3 %copy-start.12 = (s32[64]{0:T(128)S(1)}, s32[64]{0:T(128)}, u32[]{:S(2)}) copy-start(s32[64]{0:T(128)} %copy-done.11) | copy-start | bytes 772
  114.8 37.3 %copy-start.14 = (s32[64]{0:T(128)S(1)}, s32[64]{0:T(128)}, u32[]{:S(2)}) copy-start(s32[64]{0:T(128)} %copy-done.13) | copy-start | bytes 772
  114.9 3.6 %collective-permute-start.12 = (bf16[128,1536]{1,0:T(8,128)(2,1)S(1)}, bf16[128,1536]{1,0:T(8,128)(2,1)S(1)}, u32[]{:S(2)}, u32[]{:S(2)}) collective-permute-start(bf16[128,1536]{1,0:T(8,128)(2,1)S(1)} %get-tuple-element.25), channel_id=1, source_target_pairs={{0,32},{32,0},{1,33},{33,1},{2,34},{34,2},{3,35},{35,3},{4,36},{36... | collective-permute-start | bytes 1179656 | tf_op jit(solution)/shard_map/ppermute | solution.py:240
  (6 other events, 9.2 us)

commit v6 on v5

--- a/solution.py
+++ b/solution.py
@@ -13,8 +13,6 @@
 BF = jnp.bfloat16
 F32 = jnp.float32
 SWAP = [(0, 1), (1, 0)]
-XOR1 = [(i, i ^ 1) for i in range(4)]
-XOR3 = [(i, i ^ 3) for i in range(4)]
 VMEM_BYTES = 16 * 1024 * 1024
 WIDE_BYTES = 65_600_000
 
@@ -66,11 +64,14 @@
     return hit.astype(BF)
 
 
-def pack_kernel(gate_ref, up_ref, down_ref, out_ref, sems):
+def pack_kernel(gate_ref, up_ref, down_ref, first_ref, second_ref, sems):
     share = down_ref.shape[0]
+    half = share // 2
     copies = [
-        pltpu.make_async_copy(ref, out_ref.at[pl.ds(i * share, share)], sems.at[i])
-        for i, ref in enumerate((gate_ref, up_ref, down_ref))
+        pltpu.make_async_copy(gate_ref, first_ref.at[pl.ds(0, share)], sems.at[0]),
+        pltpu.make_async_copy(up_ref.at[pl.ds(0, half)], first_ref.at[pl.ds(share, half)], sems.at[1]),
+        pltpu.make_async_copy(up_ref.at[pl.ds(half, half)], second_ref.at[pl.ds(0, half)], sems.at[2]),
+        pltpu.make_async_copy(down_ref, second_ref.at[pl.ds(half, share)], sems.at[3]),
     ]
     for copy in copies:
         copy.start()
@@ -89,9 +90,7 @@
     yh, x, c = at_ref[0], at_ref[1], at_ref[2]
     size = parts_ref.shape[1]
     for shard in range(16):
-        apart = shard // 2 % 4 ^ x
-        mirror = apart // 2
-        at = mirror * 8 + (apart % 2 ^ mirror) * 4 + (shard % 2 ^ c) * 2 + (shard // 8 ^ yh)
+        at = lax.rem(shard // 2 % 4 - x + 4, 4) + (shard // 8 ^ yh) * 4 + (shard % 2 ^ c) * 8
         out_ref[shard * size : (shard + 1) * size] = parts_ref[at]
 
 
@@ -100,11 +99,14 @@
 
 
 def near_kernel(
-    mine_ref, theirs_ref, embed_ref, router_ref, w0_ref, w1_ref, w2_ref, tokens_ref, score_ref, total_ref, held_ref, sems
+    mine_ref, theirs_ref, embed_ref, router_ref, a0_ref, b0_ref, a1_ref, b1_ref, a2_ref, b2_ref, tokens_ref, score_ref, total_ref, held_ref, sems
 ):
     rows, width = mine_ref.shape[0], total_ref.shape[1]
-    share = w0_ref.shape[0] // 3
-    copies = [pltpu.make_async_copy(ref, held_ref.at[i], sems.at[i]) for i, ref in enumerate((w0_ref, w1_ref, w2_ref))]
+    part, share = a0_ref.shape[0], held_ref.shape[1] // 3
+    copies = [
+        pltpu.make_async_copy(ref, held_ref.at[i // 2, pl.ds(i % 2 * part, part)], sems.at[i])
+        for i, ref in enumerate((a0_ref, b0_ref, a1_ref, b1_ref, a2_ref, b2_ref))
+    ]
     for copy in copies:
         copy.start()
     for half, ref in enumerate((theirs_ref, mine_ref)):
@@ -117,8 +119,9 @@
         tokens_ref[at] = tokens
         score_ref[at] = 1.0 / (1.0 + jnp.exp(-logit))
     hidden = []
-    for i, copy in enumerate(copies):
-        copy.wait()
+    for i in range(3):
+        copies[2 * i].wait()
+        copies[2 * i + 1].wait()
         both = dot(tokens_ref[...], held_ref[i, : 2 * share], ((1,), (1,)))
         hidden.append((silu(both[:, :share]) * both[:, share:]).astype(BF))
     hidden = jnp.concatenate(hidden, axis=1)
@@ -172,38 +175,53 @@
     params = pltpu.CompilerParams(vmem_limit_bytes=VMEM_BYTES)
 
     past = shifted(video, FRAME, 1)
-    held = pl.pallas_call(
+    part = embed_weight.T
+    parts = jnp.stack([part, ring(part, 1), ring(part, 2), ring(part, 3)])
+    first, second = pl.pallas_call(
         pack_kernel,
-        out_shape=jax.ShapeDtypeStruct((3 * share, width), BF),
+        out_shape=[jax.ShapeDtypeStruct((3 * share // 2, width), BF)] * 2,
         in_specs=[hbm] * 3,
-        out_specs=hbm,
-        scratch_shapes=[pltpu.SemaphoreType.DMA((3,))],
+        out_specs=[hbm] * 2,
+        scratch_shapes=[pltpu.SemaphoreType.DMA((4,))],
         compiler_params=params,
     )(gate_weight[0].T, up_weight[0].T, down_weight[0])
-    held, past = lax.optimization_barrier((held, past))
-    behind, ahead = ring(held, -1), ring(held, 1)
+    first, second, past, parts = lax.optimization_barrier((first, second, past, parts))
+    first_behind, second_ahead = ring(first, -1), ring(second, 1)
+    first_ahead, second_behind = ring(first, 1), ring(second, -1)
 
     table = place_table(routes, experts, capacity)
-    latent = encode(video, past, conv_weight, latent_weight)
-    lat = latent.shape[1]
-    blocks = latent.reshape(2, rows // 2, 2, cols // 2, 2, lat)
-    patches = blocks.transpose(1, 3, 0, 2, 4, 5).reshape(tok, 8 * lat)
-    raw = width + patches.shape[1]
-    outgoing = pl.pallas_call(
-        dispatch_kernel,
-        out_shape=jax.ShapeDtypeStruct((slots, raw), BF),
-        in_specs=[vmem] * 3,
-        out_specs=vmem,
-        compiler_params=params,
-    )(patches, context, table)
-
-    arrived = lax.all_to_all(outgoing.reshape(experts, capacity, raw), SOURCES, split_axis=0, concat_axis=0, tiled=True)
-    parts = embed_weight.T[None]
-    for axis, pairs in (("yh", SWAP), ("c", SWAP), ("x", XOR1), ("x", XOR3)):
-        parts = jnp.concatenate([parts, lax.ppermute(parts, axis, pairs)], axis=0)
-    part = 3 * share // 2
-    arrived, parts, first, second = lax.optimization_barrier((arrived, parts, behind[:part], ahead[part:]))
-    first, second = ring(first, -1), ring(second, 1)
+    raw = width + embed_weight.shape[0]
+
+    def front(video, past, conv_weight, latent_weight, context, table):
+        latent = encode(video, past, conv_weight, latent_weight)
+        lat = latent.shape[1]
+        blocks = latent.reshape(2, rows // 2, 2, cols // 2, 2, lat)
+        patches = blocks.transpose(1, 3, 0, 2, 4, 5).reshape(tok, 8 * lat)
+        return pl.pallas_call(
+            dispatch_kernel,
+            out_shape=jax.ShapeDtypeStruct((slots, raw), BF),
+            in_specs=[vmem] * 3,
+            out_specs=vmem,
+            compiler_params=params,
+        )(patches, context, table).reshape(experts, capacity, raw)
+
+    outgoing = lax.cond(
+        lax.axis_index("yh") < 2,
+        front,
+        lambda *unused: jnp.zeros((experts, capacity, raw), BF),
+        video,
+        past,
+        conv_weight,
+        latent_weight,
+        context,
+        table,
+    )
+    arrived = lax.all_to_all(outgoing, SOURCES, split_axis=0, concat_axis=0, tiled=True)
+    parts = jnp.concatenate([parts, lax.ppermute(parts, "yh", SWAP)], axis=0)
+    parts, first_behind, second_ahead = lax.optimization_barrier((parts, first_behind, second_ahead))
+    first_opposite, second_opposite = ring(first_behind, -1), ring(second_ahead, 1)
+    parts = jnp.concatenate([parts, lax.ppermute(parts, "c", SWAP)], axis=0)
+    arrived, parts, first_ahead, second_behind = lax.optimization_barrier((arrived, parts, first_ahead, second_behind))
 
     mine = arrived.reshape(slots, raw)
     theirs = lax.ppermute(mine, "c", SWAP)
@@ -224,11 +242,11 @@
             jax.ShapeDtypeStruct((2 * slots, 1), F32),
             jax.ShapeDtypeStruct((2 * slots, width), F32),
         ],
-        in_specs=[vmem] * 4 + [hbm] * 3,
+        in_specs=[vmem] * 4 + [hbm] * 6,
         out_specs=[vmem] * 3,
-        scratch_shapes=[pltpu.VMEM((3, 3 * share, width), BF), pltpu.SemaphoreType.DMA((3,))],
+        scratch_shapes=[pltpu.VMEM((3, 3 * share, width), BF), pltpu.SemaphoreType.DMA((6,))],
         compiler_params=params,
-    )(mine, theirs, embed, router, held, behind, ahead)
+    )(mine, theirs, embed, router, first, second, first_behind, second_behind, first_ahead, second_ahead)
     other, own = pl.pallas_call(
         last_kernel,
         out_shape=[jax.ShapeDtypeStruct((slots, width), BF)] * 2,
@@ -236,7 +254,7 @@
         out_specs=[vmem] * 2,
         scratch_shapes=[pltpu.VMEM((3 * share, width), BF), pltpu.SemaphoreType.DMA((2,))],
         compiler_params=params,
-    )(tokens, score, total, first, second)
+    )(tokens, score, total, first_opposite, second_opposite)
     back = lax.ppermute(other, "c", SWAP)
     summed = (back.astype(F32) + own.astype(F32)).astype(BF).reshape(experts, capacity, width)
     homeward = lax.all_to_all(summed, SOURCES, split_axis=0, concat_axis=0, tiled=True)

time: 154 us -> 144 us (0.935); the launches traced: 153 us -> 141 us
  starting transfers between devices: 57.6 us -> 70.4 us
  waiting for transfers between devices: 22.8 us -> 13.3 us
  local copies, waits for them, and re-layouts: 20.4 us -> 11.9 us
  blocking collectives: 33.2 us -> 28.2 us
    ppermute x4 -> x9, starting transfers between devices: 12.2 us -> 32.6 us  [ring(): return lax.ppermute(value, 'x', [(i, (i - step) % 4) for i in range(4)])]
    ppermute x4 -> x9, waiting for transfers between devices: 7.77 us -> 0.02 us  [ring(): return lax.ppermute(value, 'x', [(i, (i - step) % 4) for i in range(4)])]
    ppermute x4 -> x2, starting transfers between devices: 16.4 us -> 9.41 us  [the longest x1 7.49 us: local(): parts = jnp.concatenate([parts, lax.ppermute(parts, 'yh', SWAP)], axis=0)]
    ppermute x4 -> x2, waiting for transfers between devices: 13.4 us -> 8.28 us  [the longest x1 6.87 us: local(): parts = jnp.concatenate([parts, lax.ppermute(parts, 'yh', SWAP)], axis=0)]
    all_to_all x1, blocking collectives: 33.2 us -> 28.2 us  [local(): lax.all_to_all(summed, SOURCES, split_axis=0, concat_axis=0, tiled=True)]
    slice x2 -> x0, local copies, waits for them, and re-layouts: 4.3 us -> none  [the longest x1 2.15 us: local(): behind[:part]]
    ppermute x3, waiting for transfers between devices: 0.01 us -> 3.65 us  [shifted(): return lax.ppermute(value, axes, pairs)]
    unnamed x45 -> x19, local copies, waits for them, and re-layouts: 9.43 us -> 6.14 us
  transfers between devices with their start and end apart: 14 -> 17, of which waited for: 5 -> 4; matrix products, arithmetic and copies ran while one was open for 15% -> 9% of each run, Pallas kernels for 5% -> 5%
where the time goes in v6:
time: 144 us; the launch traced here: 141 us
  starting transfers between devices  70.4 us (49%)
  blocking collectives  28.2 us (20%)
  waiting for transfers between devices  13.3 us (9%)
  local copies, waits for them, and re-layouts  11.9 us (8%)
  Pallas kernels  9.8 us (7%)
  matrix products  4 us (3%)
  other arithmetic  3.36 us (2%)
    ppermute x9, starting transfers between devices, ring(): return lax.ppermute(value, 'x', [(i, (i - step) % 4) for i in range(4)])  32.6 us
    all_to_all x1, blocking collectives, local(): lax.all_to_all(summed, SOURCES, split_axis=0, concat_axis=0, tiled=True)  28.2 us
    all_to_all x1, starting transfers between devices, local(): lax.all_to_all(outgoing, SOURCES, split_axis=0, concat_axis=0, tiled=True)  19.6 us
    ppermute x1, starting transfers between devices, local(): parts = jnp.concatenate([parts, lax.ppermute(parts, 'yh', SWAP)], axis=0)  7.49 us
    ppermute x1, waiting for transfers between devices, local(): parts = jnp.concatenate([parts, lax.ppermute(parts, 'yh', SWAP)], axis=0)  6.87 us
    unnamed x19, local copies, waits for them, and re-layouts  6.14 us
    pallas_call x1, Pallas kernels, local(): pl.pallas_call(near_kernel, out_shape=[jax.ShapeDtypeStruct((2 * slots, w...  4.91 us
    ppermute x3, starting transfers between devices, shifted(): return lax.ppermute(value, axes, pairs)  4.51 us
  transfers between devices with their start and end apart: 17, of which 4 were waited for; matrix products, arithmetic and copies ran while one was open for 9% of the time, Pallas kernels for 5%

profile of v6, /device:TPU:6, one launch (start us, length us, event | category | flops | bytes accessed | tf_op | source)
XLA Modules:
  0.0 141.4 jit_solution(9731286975295307787)
XLA Ops:
  0.0 3.4 %collective-permute-start.4 = (bf16[96,128]{1,0:T(8,128)(2,1)}, bf16[96,128]{1,0:T(8,128)(2,1)S(1)}, u32[]{:S(2)}, u32[]{:S(2)}) collective-permute-start(bf16[96,128]{1,0:T(8,128)(2,1)} %bitcast.50), channel_id=1, source_target_pairs={{0,128},{64,192},{128,0},{192,64},{1,129},{65,193},{129,1},{193,65... | collective-permute-start | bytes 73736 | tf_op jit(solution)/shard_map/ppermute | solution.py:31
  3.5 7.2 %collective-permute-start.3 = (bf16[96,128]{1,0:T(8,128)(2,1)}, bf16[96,128]{1,0:T(8,128)(2,1)S(1)}, u32[]{:S(2)}, u32[]{:S(2)}) collective-permute-start(bf16[96,128]{1,0:T(8,128)(2,1)} %bitcast.51), channel_id=1, source_target_pairs={{0,192},{64,0},{128,64},{192,128},{1,193},{65,1},{129,65},{193,129... | collective-permute-start | bytes 73736 | tf_op jit(solution)/shard_map/ppermute | solution.py:31
  10.7 1.9 %collective-permute-start.5 = (bf16[96,128]{1,0:T(8,128)(2,1)}, bf16[96,128]{1,0:T(8,128)(2,1)S(1)}, u32[]{:S(2)}, u32[]{:S(2)}) collective-permute-start(bf16[96,128]{1,0:T(8,128)(2,1)} %bitcast.52), channel_id=1, source_target_pairs={{0,64},{64,128},{128,192},{192,0},{1,65},{65,129},{129,193},{193,1... | collective-permute-start | bytes 73736 | tf_op jit(solution)/shard_map/ppermute | solution.py:31
  12.6 1.9 %collective-permute-start.2 = (bf16[2,4,64,128]{3,2,1,0:T(8,128)(2,1)}, bf16[2,4,64,128]{3,2,1,0:T(8,128)(2,1)S(1)}, u32[]{:S(2)}, u32[]{:S(2)}) collective-permute-start(bf16[2,4,64,128]{3,2,1,0:T(8,128)(2,1)} %param.12), channel_id=1, source_target_pairs={{0,32},{32,64},{64,96},{96,128},{128,160},{160,192},{192,224},{224... | collective-permute-start | bytes 393224 | tf_op jit(solution)/shard_map/ppermute | solution.py:27
  21.0 2.5 %collective-permute-start.7 = (bf16[288,1536]{1,0:T(8,128)(2,1)S(1)}, bf16[288,1536]{1,0:T(8,128)(2,1)}, u32[]{:S(2)}, u32[]{:S(2)}) collective-permute-start(bf16[288,1536]{1,0:T(8,128)(2,1)S(1)} %get-tuple-element.48.a0_ref), channel_id=1, source_target_pairs={{0,64},{64,128},{128,192},{192,0},{1,65},{65,129},{129,193},{193,1... | collective-permute-start | bytes 2654216 | tf_op jit(solution)/shard_map/ppermute | solution.py:31
  23.5 3.4 %collective-permute-start.8 = (bf16[288,1536]{1,0:T(8,128)(2,1)S(1)}, bf16[288,1536]{1,0:T(8,128)(2,1)}, u32[]{:S(2)}, u32[]{:S(2)}) collective-permute-start(bf16[288,1536]{1,0:T(8,128)(2,1)S(1)} %get-tuple-element.49.b0_ref), channel_id=1, source_target_pairs={{0,192},{64,0},{128,64},{192,128},{1,193},{65,1},{129,65},{193,129... | collective-permute-start | bytes 2654216 | tf_op jit(solution)/shard_map/ppermute | solution.py:31
  27.2 3.9 %collective-permute-start.10 = (bf16[288,1536]{1,0:T(8,128)(2,1)S(1)}, bf16[288,1536]{1,0:T(8,128)(2,1)}, u32[]{:S(2)}, u32[]{:S(2)}) collective-permute-start(bf16[288,1536]{1,0:T(8,128)(2,1)S(1)} %get-tuple-element.48.a0_ref), channel_id=1, source_target_pairs={{0,192},{64,0},{128,64},{192,128},{1,193},{65,1},{129,65},{193,129... | collective-permute-start | bytes 2654216 | tf_op jit(solution)/shard_map/ppermute | solution.py:31
  31.1 14.6 %conditional.1 = (bf16[64,2,1664]{2,1,0:T(2,128)(2,1)}) conditional(s32[]{:T(128)} %convert_element_type.50, () %tuple.14, (bf16[2,4,64,128]{3,2,1,0:T(8,128)(2,1)S(1)}, bf16[2,4,64,128]{3,2,1,0:T(8,128)(2,1)S(1)}, bf16[3,3,3,128,128]{4,3,2,1,0:T(8,128)(2,1)}, bf16[128,16]{0,1:T(8,128)(2,1)S(1)}, bf16[64,1536]{1,0:T(8,128)(2,1)}, ...), branch_computations={%region_1.2_spmd, %region_2.3_spmd} | conditional | flops 459161600 | bytes 23199860 | solution.py:208
  35.0 3.6 %collective-permute-done.1 = bf16[4,1,64,128]{3,2,1,0:T(8,128)(2,1)S(1)} collective-permute-done((bf16[4,1,64,128]{3,2,1,0:T(8,128)(2,1)S(1)}, bf16[4,1,64,128]{3,2,1,0:T(8,128)(2,1)S(1)}, u32[]{:S(2)}, u32[]{:S(2)}) %collective-permute-start.1) | collective-permute-done | bytes 65568 | tf_op jit(solution)/shard_map/cond/branch_1_fun/ppermute | solution.py:27
  39.6 1.5 %fusion.19 = (bf16[2,4,64,1152]{3,2,1,0:T(8,128)(2,1)}, bf16[2,4,64,1152]{3,2,1,0:T(8,128)(2,1)S(1)}, bf16[2,4,64,1152]{3,2,1,0:T(8,128)(2,1)S(1)}) fusion(bf16[4,4,64,1152]{3,2,1,0:T(8,128)(2,1)S(1)} %slice_dynamic-update-slice_fusion), kind=kLoop, calls=%fused_computation.52 | loop fusion | bytes 7077888 | tf_op jit(solution)/shard_map/cond/branch_1_fun/slice | solution.py:48
  42.1 1.9 %convolution_convert_fusion = bf16[512,16]{0,1:T(8,128)(2,1)S(1)} fusion(bf16[128,16]{0,1:T(8,128)(2,1)S(1)} %get-tuple-element.66, bf16[512,128]{1,0:T(8,128)(2,1)S(1)} %bitcast.48, f32[512,128]{1,0:T(8,128)S(1)} %convolution_add_fusion.1, bf16[512,1152]{1,0:T(8,128)(2,1)} %bitcast.44, bf16[1152,128]{1,0:T(8,128)(2,1)S(1)} %bitcast.49), kind=kOutput, calls=%fused_computation.4 | convolution fusion | flops 153624576 | bytes 1888256 | tf_op jit(solution)/shard_map/cond/branch_1_fun/dot_general | solution.py:21
  45.8 4.4 %collective-permute-start.11 = (bf16[288,1536]{1,0:T(8,128)(2,1)S(1)}, bf16[288,1536]{1,0:T(8,128)(2,1)}, u32[]{:S(2)}, u32[]{:S(2)}) collective-permute-start(bf16[288,1536]{1,0:T(8,128)(2,1)S(1)} %get-tuple-element.49.b0_ref), channel_id=1, source_target_pairs={{0,64},{64,128},{128,192},{192,0},{1,65},{65,129},{129,193},{193,1... | collective-permute-start | bytes 2654216 | tf_op jit(solution)/shard_map/ppermute | solution.py:31
  50.2 19.6 %all-to-all-start = ((bf16[64,2,1664]{2,1,0:T(2,128)(2,1)}), bf16[64,2,1664]{2,1,0:T(2,128)(2,1)S(1)}, u32[]{:S(2)}, u32[]{:S(2)}) async-start(bf16[64,2,1664]{2,1,0:T(2,128)(2,1)} %get-tuple-element.78), calls=%async_computation | async-start | bytes 851968 | tf_op jit(solution)/shard_map/all_to_all | solution.py:219
  69.8 7.5 %collective-permute-start.6 = (bf16[4,96,128]{2,1,0:T(8,128)(2,1)S(1)}, bf16[4,96,128]{2,1,0:T(8,128)(2,1)S(1)}, u32[]{:S(2)}, u32[]{:S(2)}) collective-permute-start(bf16[4,96,128]{2,1,0:T(8,128)(2,1)S(1)} %pad_maximum_fusion.4), channel_id=1, source_target_pairs={{0,256},{256,0},{1,257},{257,1},{2,258},{258,2},{3,259},{259,3},{4... | collective-permute-start | bytes 294920 | tf_op jit(solution)/shard_map/ppermute | solution.py:220
  77.3 6.9 %collective-permute-done.6 = bf16[4,96,128]{2,1,0:T(8,128)(2,1)S(1)} collective-permute-done((bf16[4,96,128]{2,1,0:T(8,128)(2,1)S(1)}, bf16[4,96,128]{2,1,0:T(8,128)(2,1)S(1)}, u32[]{:S(2)}, u32[]{:S(2)}) %collective-permute-start.6) | collective-permute-done | bytes 98336 | tf_op jit(solution)/shard_map/ppermute | solution.py:220
  84.2 2.1 %collective-permute-start.13 = (bf16[288,1536]{1,0:T(8,128)(2,1)}, bf16[288,1536]{1,0:T(8,128)(2,1)}, u32[]{:S(2)}, u32[]{:S(2)}) collective-permute-start(bf16[288,1536]{1,0:T(8,128)(2,1)} %collective-permute-done.7.a1_ref), channel_id=1, source_target_pairs={{0,64},{64,128},{128,192},{192,0},{1,65},{65,129},{129,193},{193,1... | collective-permute-start | bytes 2654216 | tf_op jit(solution)/shard_map/ppermute | solution.py:31
  86.3 3.7 %collective-permute-start.14 = (bf16[288,1536]{1,0:T(8,128)(2,1)}, bf16[288,1536]{1,0:T(8,128)(2,1)}, u32[]{:S(2)}, u32[]{:S(2)}) collective-permute-start(bf16[288,1536]{1,0:T(8,128)(2,1)} %collective-permute-done.8.b2_ref), channel_id=1, source_target_pairs={{0,192},{64,0},{128,64},{192,128},{1,193},{65,1},{129,65},{193,129... | collective-permute-start | bytes 2654216 | tf_op jit(solution)/shard_map/ppermute | solution.py:31
  90.0 1.9 %collective-permute-start.9 = (bf16[8,96,128]{2,1,0:T(8,128)(2,1)S(1)}, bf16[8,96,128]{2,1,0:T(8,128)(2,1)S(1)}, u32[]{:S(2)}, u32[]{:S(2)}) collective-permute-start(bf16[8,96,128]{2,1,0:T(8,128)(2,1)S(1)} %pad_maximum_fusion.3), channel_id=1, source_target_pairs={{0,32},{32,0},{1,33},{33,1},{2,34},{34,2},{3,35},{35,3},{4,36},{36... | collective-permute-start | bytes 589832 | tf_op jit(solution)/shard_map/ppermute | solution.py:223
  94.4 2.0 %collective-permute-start.12 = (bf16[128,1664]{1,0:T(8,128)(2,1)S(1)}, bf16[128,1664]{1,0:T(8,128)(2,1)}, u32[]{:S(2)}, u32[]{:S(2)}) collective-permute-start(bf16[128,1664]{1,0:T(8,128)(2,1)S(1)} %reshape.53.mine_ref), channel_id=1, source_target_pairs={{0,32},{32,0},{1,33},{33,1},{2,34},{34,2},{3,35},{35,3},{4,36},{36... | collective-permute-start | bytes 1277960 | tf_op jit(solution)/shard_map/ppermute | solution.py:227
  97.0 1.8 %shard_map.104.embed_ref = bf16[1536,128]{1,0:T(8,128)(2,1)} custom-call(s32[3]{0:T(128)} %pad_add_fusion.at_ref, bf16[16,96,128]{2,1,0:T(8,128)(2,1)} %pad_maximum_fusion.2.parts_ref), custom_call_target="tpu_custom_call" | custom-call | tf_op jit(solution)/shard_map/pallas_call | solution.py:228
  101.0 4.9 %shard_map.105 = (bf16[256,1536]{1,0:T(8,128)(2,1)S(1)}, f32[256,1]{1,0:T(8,128)S(1)}, f32[256,1536]{1,0:T(8,128)S(1)}) custom-call(bf16[128,1664]{1,0:T(8,128)(2,1)S(1)} %reshape.53.mine_ref, bf16[128,1664]{1,0:T(8,128)(2,1)} %collective-permute-done.12.theirs_ref, bf16[1536,128]{1,0:T(8,128)(2,1)S(1)} %copy-done.1, ...), custom_call_target="tpu_custom_call" | custom-call | tf_op jit(solution)/shard_map/pallas_call | solution.py:238
  105.9 2.4 %shard_map.106 = (bf16[128,1536]{1,0:T(8,128)(2,1)S(1)}, bf16[128,1536]{1,0:T(8,128)(2,1)S(1)}) custom-call(bf16[256,1536]{1,0:T(8,128)(2,1)S(1)} %get-tuple-element.57.tokens_ref, f32[256,1]{1,0:T(8,128)S(1)} %get-tuple-element.58.score_ref, f32[256,1536]{1,0:T(8,128)S(1)} %get-tuple-element.59.total_ref, bf16[288,1536]{1,0:T(8,128)(2,1)} %collective-permute-done.13.w0_ref, ...), custom_call_target="tpu_custom_call" | custom-call | tf_op jit(solution)/shard_map/pallas_call | solution.py:250
  108.3 2.3 %collective-permute-start.15 = (bf16[128,1536]{1,0:T(8,128)(2,1)S(1)}, bf16[128,1536]{1,0:T(8,128)(2,1)S(1)}, u32[]{:S(2)}, u32[]{:S(2)}) collective-permute-start(bf16[128,1536]{1,0:T(8,128)(2,1)S(1)} %get-tuple-element.60), channel_id=1, source_target_pairs={{0,32},{32,0},{1,33},{33,1},{2,34},{34,2},{3,35},{35,3},{4,36},{36... | collective-permute-start | bytes 1179656 | tf_op jit(solution)/shard_map/ppermute | solution.py:258
  112.2 28.2 %all_to_all.10 = bf16[64,2,1536]{2,1,0:T(2,128)(2,1)S(1)} all-to-all(bf16[64,2,1536]{2,1,0:T(2,128)(2,1)S(1)} %reshape.55), channel_id=1, replica_groups=mesh['yh'=2,'x'=4,'c'=2,'yl'=4,'z'=8] {'yh','yl','z'}, dimensions={0} | all-to-all | bytes 786432 | tf_op jit(solution)/shard_map/all_to_all | solution.py:260
  (81 shorter events, 21.9 us)
Async XLA Ops:
  0.0 97.0 %copy-start = (bf16[2,1536,1]{1,0,2:T(2,128)(2,1)S(1)}, bf16[2,1536,1]{1,0,2:T(2,128)(2,1)}, u32[]{:S(2)}) copy-start(bf16[2,1536,1]{1,0,2:T(2,128)(2,1)} %param.17) | copy-start | bytes 18436
  0.0 31.1 %copy-start.7 = (bf16[2,4,64,128]{3,2,1,0:T(8,128)(2,1)S(1)}, bf16[2,4,64,128]{3,2,1,0:T(8,128)(2,1)}, u32[]{:S(2)}) copy-start(bf16[2,4,64,128]{3,2,1,0:T(8,128)(2,1)} %param.12) | copy-start | bytes 393220
  0.0 31.1 %copy-start.9 = (bf16[128,16]{0,1:T(8,128)(2,1)S(1)}, bf16[128,16]{0,1:T(8,128)(2,1)}, u32[]{:S(2)}) copy-start(bf16[128,16]{0,1:T(8,128)(2,1)} %param.14) | copy-start | bytes 12292
  0.0 20.2 %collective-permute-start.4 = (bf16[96,128]{1,0:T(8,128)(2,1)}, bf16[96,128]{1,0:T(8,128)(2,1)S(1)}, u32[]{:S(2)}, u32[]{:S(2)}) collective-permute-start(bf16[96,128]{1,0:T(8,128)(2,1)} %bitcast.50), channel_id=1, source_target_pairs={{0,128},{64,192},{128,0},{192,64},{1,129},{65,193},{129,1},{193,65... | collective-permute-start | bytes 73736 | tf_op jit(solution)/shard_map/ppermute | solution.py:31
  3.5 16.7 %collective-permute-start.3 = (bf16[96,128]{1,0:T(8,128)(2,1)}, bf16[96,128]{1,0:T(8,128)(2,1)S(1)}, u32[]{:S(2)}, u32[]{:S(2)}) collective-permute-start(bf16[96,128]{1,0:T(8,128)(2,1)} %bitcast.51), channel_id=1, source_target_pairs={{0,192},{64,0},{128,64},{192,128},{1,193},{65,1},{129,65},{193,129... | collective-permute-start | bytes 73736 | tf_op jit(solution)/shard_map/ppermute | solution.py:31
  10.7 9.5 %collective-permute-start.5 = (bf16[96,128]{1,0:T(8,128)(2,1)}, bf16[96,128]{1,0:T(8,128)(2,1)S(1)}, u32[]{:S(2)}, u32[]{:S(2)}) collective-permute-start(bf16[96,128]{1,0:T(8,128)(2,1)} %bitcast.52), channel_id=1, source_target_pairs={{0,64},{64,128},{128,192},{192,0},{1,65},{65,129},{129,193},{193,1... | collective-permute-start | bytes 73736 | tf_op jit(solution)/shard_map/ppermute | solution.py:31
  12.6 8.4 %collective-permute-start.2 = (bf16[2,4,64,128]{3,2,1,0:T(8,128)(2,1)}, bf16[2,4,64,128]{3,2,1,0:T(8,128)(2,1)S(1)}, u32[]{:S(2)}, u32[]{:S(2)}) collective-permute-start(bf16[2,4,64,128]{3,2,1,0:T(8,128)(2,1)} %param.12), channel_id=1, source_target_pairs={{0,32},{32,64},{64,96},{96,128},{128,160},{160,192},{192,224},{224... | collective-permute-start | bytes 393224 | tf_op jit(solution)/shard_map/ppermute | solution.py:27
  16.5 1.1 copy-start.4
  20.2 25.6 %copy-start.2 = (bf16[288,1536]{1,0:T(8,128)(2,1)}, bf16[288,1536]{1,0:T(8,128)(2,1)S(1)}, u32[]{:S(2)}) copy-start(bf16[288,1536]{1,0:T(8,128)(2,1)S(1)} %get-tuple-element.49.b0_ref) | copy-start | bytes 2654212
  21.0 63.1 %collective-permute-start.7 = (bf16[288,1536]{1,0:T(8,128)(2,1)S(1)}, bf16[288,1536]{1,0:T(8,128)(2,1)}, u32[]{:S(2)}, u32[]{:S(2)}) collective-permute-start(bf16[288,1536]{1,0:T(8,128)(2,1)S(1)} %get-tuple-element.48.a0_ref), channel_id=1, source_target_pairs={{0,64},{64,128},{128,192},{192,0},{1,65},{65,129},{129,193},{193,1... | collective-permute-start | bytes 2654216 | tf_op jit(solution)/shard_map/ppermute | solution.py:31
  23.5 60.7 %collective-permute-start.8 = (bf16[288,1536]{1,0:T(8,128)(2,1)S(1)}, bf16[288,1536]{1,0:T(8,128)(2,1)}, u32[]{:S(2)}, u32[]{:S(2)}) collective-permute-start(bf16[288,1536]{1,0:T(8,128)(2,1)S(1)} %get-tuple-element.49.b0_ref), channel_id=1, source_target_pairs={{0,192},{64,0},{128,64},{192,128},{1,193},{65,1},{129,65},{193,129... | collective-permute-start | bytes 2654216 | tf_op jit(solution)/shard_map/ppermute | solution.py:31
  27.2 67.0 %collective-permute-start.10 = (bf16[288,1536]{1,0:T(8,128)(2,1)S(1)}, bf16[288,1536]{1,0:T(8,128)(2,1)}, u32[]{:S(2)}, u32[]{:S(2)}) collective-permute-start(bf16[288,1536]{1,0:T(8,128)(2,1)S(1)} %get-tuple-element.48.a0_ref), channel_id=1, source_target_pairs={{0,192},{64,0},{128,64},{192,128},{1,193},{65,1},{129,65},{193,129... | collective-permute-start | bytes 2654216 | tf_op jit(solution)/shard_map/ppermute | solution.py:31
  31.2 3.8 %collective-permute-start = (bf16[4,1,64,128]{3,2,1,0:T(8,128)(2,1)S(1)}, bf16[4,1,64,128]{3,2,1,0:T(8,128)(2,1)S(1)}, u32[]{:S(2)}, u32[]{:S(2)}) collective-permute-start(bf16[4,1,64,128]{3,2,1,0:T(8,128)(2,1)S(1)} %get-tuple-element.76), channel_id=1, source_target_pairs={{0,1},{1,2},{2,3},{3,4},{4,5},{5,6},{6,7},{7,8},{8,9},{9,10},{10,1... | collective-permute-start | bytes 196616 | tf_op jit(solution)/shard_map/cond/branch_1_fun/ppermute | solution.py:27
  32.5 6.2 %collective-permute-start.1 = (bf16[4,1,64,128]{3,2,1,0:T(8,128)(2,1)S(1)}, bf16[4,1,64,128]{3,2,1,0:T(8,128)(2,1)S(1)}, u32[]{:S(2)}, u32[]{:S(2)}) collective-permute-start(bf16[4,1,64,128]{3,2,1,0:T(8,128)(2,1)S(1)} %get-tuple-element.77), channel_id=1, source_target_pairs={{1,0},{2,1},{3,2},{4,3},{5,4},{6,5},{7,6},{8,7},{9,8},{10,9},{11,1... | collective-permute-start | bytes 196616 | tf_op jit(solution)/shard_map/cond/branch_1_fun/ppermute | solution.py:27
  42.1 2.4 %copy-start.8 = (bf16[64,1536]{1,0:T(8,128)(2,1)S(1)}, bf16[64,1536]{1,0:T(8,128)(2,1)}, u32[]{:S(2)}) copy-start(bf16[64,1536]{1,0:T(8,128)(2,1)} %get-tuple-element.67.context_ref) | copy-start | bytes 589828 | tf_op jit(solution)/shard_map/cond
  45.8 48.4 %collective-permute-start.11 = (bf16[288,1536]{1,0:T(8,128)(2,1)S(1)}, bf16[288,1536]{1,0:T(8,128)(2,1)}, u32[]{:S(2)}, u32[]{:S(2)}) collective-permute-start(bf16[288,1536]{1,0:T(8,128)(2,1)S(1)} %get-tuple-element.49.b0_ref), channel_id=1, source_target_pairs={{0,64},{64,128},{128,192},{192,0},{1,65},{65,129},{129,193},{193,1... | collective-permute-start | bytes 2654216 | tf_op jit(solution)/shard_map/ppermute | solution.py:31
  50.2 44.0 %all-to-all-start = ((bf16[64,2,1664]{2,1,0:T(2,128)(2,1)}), bf16[64,2,1664]{2,1,0:T(2,128)(2,1)S(1)}, u32[]{:S(2)}, u32[]{:S(2)}) async-start(bf16[64,2,1664]{2,1,0:T(2,128)(2,1)} %get-tuple-element.78), calls=%async_computation | async-start | bytes 851968 | tf_op jit(solution)/shard_map/all_to_all | solution.py:219
  69.8 14.4 %collective-permute-start.6 = (bf16[4,96,128]{2,1,0:T(8,128)(2,1)S(1)}, bf16[4,96,128]{2,1,0:T(8,128)(2,1)S(1)}, u32[]{:S(2)}, u32[]{:S(2)}) collective-permute-start(bf16[4,96,128]{2,1,0:T(8,128)(2,1)S(1)} %pad_maximum_fusion.4), channel_id=1, source_target_pairs={{0,256},{256,0},{1,257},{257,1},{2,258},{258,2},{3,259},{259,3},{4... | collective-permute-start | bytes 294920 | tf_op jit(solution)/shard_map/ppermute | solution.py:220
  84.2 21.7 %collective-permute-start.13 = (bf16[288,1536]{1,0:T(8,128)(2,1)}, bf16[288,1536]{1,0:T(8,128)(2,1)}, u32[]{:S(2)}, u32[]{:S(2)}) collective-permute-start(bf16[288,1536]{1,0:T(8,128)(2,1)} %collective-permute-done.7.a1_ref), channel_id=1, source_target_pairs={{0,64},{64,128},{128,192},{192,0},{1,65},{65,129},{129,193},{193,1... | collective-permute-start | bytes 2654216 | tf_op jit(solution)/shard_map/ppermute | solution.py:31
  86.3 19.6 %collective-permute-start.14 = (bf16[288,1536]{1,0:T(8,128)(2,1)}, bf16[288,1536]{1,0:T(8,128)(2,1)}, u32[]{:S(2)}, u32[]{:S(2)}) collective-permute-start(bf16[288,1536]{1,0:T(8,128)(2,1)} %collective-permute-done.8.b2_ref), channel_id=1, source_target_pairs={{0,192},{64,0},{128,64},{192,128},{1,193},{65,1},{129,65},{193,129... | collective-permute-start | bytes 2654216 | tf_op jit(solution)/shard_map/ppermute | solution.py:31
  90.0 3.3 %collective-permute-start.9 = (bf16[8,96,128]{2,1,0:T(8,128)(2,1)S(1)}, bf16[8,96,128]{2,1,0:T(8,128)(2,1)S(1)}, u32[]{:S(2)}, u32[]{:S(2)}) collective-permute-start(bf16[8,96,128]{2,1,0:T(8,128)(2,1)S(1)} %pad_maximum_fusion.3), channel_id=1, source_target_pairs={{0,32},{32,0},{1,33},{33,1},{2,34},{34,2},{3,35},{35,3},{4,36},{36... | collective-permute-start | bytes 589832 | tf_op jit(solution)/shard_map/ppermute | solution.py:223
  94.4 4.4 %collective-permute-start.12 = (bf16[128,1664]{1,0:T(8,128)(2,1)S(1)}, bf16[128,1664]{1,0:T(8,128)(2,1)}, u32[]{:S(2)}, u32[]{:S(2)}) collective-permute-start(bf16[128,1664]{1,0:T(8,128)(2,1)S(1)} %reshape.53.mine_ref), channel_id=1, source_target_pairs={{0,32},{32,0},{1,33},{33,1},{2,34},{34,2},{3,35},{35,3},{4,36},{36... | collective-permute-start | bytes 1277960 | tf_op jit(solution)/shard_map/ppermute | solution.py:227
  99.8 1.2 copy-start.3
  108.3 3.6 %collective-permute-start.15 = (bf16[128,1536]{1,0:T(8,128)(2,1)S(1)}, bf16[128,1536]{1,0:T(8,128)(2,1)S(1)}, u32[]{:S(2)}, u32[]{:S(2)}) collective-permute-start(bf16[128,1536]{1,0:T(8,128)(2,1)S(1)} %get-tuple-element.60), channel_id=1, source_target_pairs={{0,32},{32,0},{1,33},{33,1},{2,34},{34,2},{3,35},{35,3},{4,36},{36... | collective-permute-start | bytes 1179656 | tf_op jit(solution)/shard_map/ppermute | solution.py:258
  (3 other events, 3.1 us)

commit v7 on v4

v7 whole, which is shorter than its diff:
```python
import jax
import jax.numpy as jnp
from jax import lax
from jax.experimental import pallas as pl
from jax.experimental.pallas import tpu as pltpu
from jax.sharding import Mesh, PartitionSpec as P

FRAME = ("yh", "x", "c")
EXPERT = ("yl", "z")
SOURCES = ("yh", "yl", "z")
SIZES = (2, 4, 2, 4, 8)
NAMES = ("yh", "x", "c", "yl", "z")
BF = jnp.bfloat16
F32 = jnp.float32
SWAP = [(0, 1), (1, 0)]
XOR1 = [(i, i ^ 1) for i in range(4)]
XOR3 = [(i, i ^ 3) for i in range(4)]
VMEM_BYTES = 16 * 1024 * 1024
PACK_BYTES = 66_400_000


def dot(a, b, dims=((1,), (0,))):
    return lax.dot_general(a, b, (dims, ((), ())), preferred_element_type=F32)


def shifted(value, axes, step):
    count = lax.axis_size(axes)
    pairs = [(i, i + step) for i in range(count) if 0 <= i + step < count]
    return lax.ppermute(value, axes, pairs)


def silu(value):
    return value / (1.0 + jnp.exp(-value))


def pack_kernel(gate_ref, up_ref, down_ref, parts_ref, out_ref, sems):
    share, tall = down_ref.shape[0], parts_ref.shape[0] * 128 // down_ref.shape[1]
    copies = [(ref, out_ref.at[pl.ds(i * share, share)]) for i, ref in enumerate((gate_ref, up_ref, down_ref))]
    for j in range(parts_ref.shape[0] // tall):
        target = out_ref.at[pl.ds(3 * share, tall), pl.ds(j * 128, 128)]
        copies.append((parts_ref.at[pl.ds(j * tall, tall)], target))
    copies = [pltpu.make_async_copy(*pair, sems.at[i]) for i, pair in enumerate(copies)]
    for copy in copies:
        copy.start()
    for copy in copies:
        copy.wait()


def front_kernel(tall_ref, conv_ref, latent_ref, context_ref, routes_ref, out_ref, table_ref, wide_ref):
    frames, rows, cols, chans = tall_ref.shape
    tok, width = context_ref.shape
    slots = table_ref.shape[1]

    flat = tall_ref[...].reshape(frames * rows * cols, chans).astype(F32)
    column = lax.broadcasted_iota(jnp.int32, flat.shape, 0) % cols
    wide_ref[:, :chans] = jnp.where(column == 0, 0.0, pltpu.roll(flat, 1, 0)).astype(BF)
    wide_ref[:, chans : 2 * chans] = flat.astype(BF)
    wide_ref[:, 2 * chans :] = jnp.where(column == cols - 1, 0.0, pltpu.roll(flat, flat.shape[0] - 1, 0)).astype(BF)

    size = (rows - 2) * cols
    out_row = lax.broadcasted_iota(jnp.int32, (size, size), 0)
    kind, token = out_row // (size // 4), out_row % (size // 4)
    source = (token // (cols // 2) * 2 + kind // 2) * cols + token % (cols // 2) * 2 + kind % 2
    sort = (source == lax.broadcasted_iota(jnp.int32, (size, size), 1)).astype(BF)
    lat = latent_ref.shape[1] // 8
    lane = lax.broadcasted_iota(jnp.int32, latent_ref.shape, 1) // lat
    patches = jnp.zeros((tok, 8 * lat), F32)
    for frame in range(frames - 2):
        mixed = jnp.zeros((size, chans), F32)
        for a in range(3):
            for b in range(3):
                at = ((frame + a) * rows + b) * cols
                mixed += dot(wide_ref[at : at + size], conv_ref[a, b])
        video = tall_ref[frame + 2, 1 : rows - 1].reshape(size, chans).astype(F32)
        feature = (video + silu(mixed)).astype(BF)
        feature = dot(sort, feature).astype(BF)
        for part in range(4):
            weight = jnp.where(lane == frame * 4 + part, latent_ref[...], jnp.zeros((), BF))
            patches += dot(feature[part * tok : (part + 1) * tok], weight)
    patches = patches.astype(BF)

    slot = lax.broadcasted_iota(jnp.int32, (tok, slots), 1)
    chosen = (routes_ref[:, :1] == slot // 2) | (routes_ref[:, 1:] == slot // 2)
    order = [lax.broadcasted_iota(jnp.int32, (tok, tok), axis) for axis in (0, 1)]
    before = dot((order[0] > order[1]).astype(BF), chosen.astype(BF))
    table = (chosen & (before == (slot % 2).astype(F32))).astype(BF)
    table_ref[...] = table
    out_ref[:, :width] = dot(table, context_ref[...], ((0,), (0,))).astype(BF)
    out_ref[:, width:] = dot(table, patches, ((0,), (0,))).astype(BF)


def expert_kernel(at_ref, rows_ref, router_ref, w0_ref, w1_ref, w2_ref, w3_ref, out_ref, embed_ref):
    held = (w0_ref, w1_ref, w2_ref, w3_ref)
    yh, x, c = at_ref[0], at_ref[1], at_ref[2]
    width = out_ref.shape[1]
    size = embed_ref.shape[1]
    share = (w0_ref.shape[0] - 4 * size * 128 // width) // 3
    tall = 4 * size * 128 // width
    for i, ref in enumerate(held):
        for m in range(4):
            shard = (yh ^ m % 2) * 8 + (x ^ i // 2 ^ m // 2 * 3) * 2 + (c ^ i % 2)
            for j in range(size // tall):
                lane = (m * (size // tall) + j) * 128
                embed_ref[shard, j * tall : (j + 1) * tall] = ref[3 * share :, lane : lane + 128]
    embed = embed_ref[...].reshape(width, 128)
    embedded = dot(rows_ref[:, width:], embed, ((1,), (1,))).astype(BF)
    total = embedded.astype(F32) + rows_ref[:, :width].astype(F32)
    meansq = jnp.mean(total * total, axis=1, keepdims=True)
    tokens = (total * lax.rsqrt(meansq + 1e-06)).astype(BF)
    router = jnp.where(yh == 0, router_ref[:1], router_ref[1:]).astype(F32)
    score = 1.0 / (1.0 + jnp.exp(-jnp.sum(tokens.astype(F32) * router, axis=1, keepdims=True)))
    hidden = []
    for ref in held:
        both = dot(tokens, ref[: 2 * share], ((1,), (1,)))
        hidden.append((silu(both[:, :share]) * both[:, share:]).astype(BF))
    hidden = jnp.concatenate(hidden, axis=1)
    tile = 512
    for at in range(0, width, tile):
        down = jnp.concatenate([ref[2 * share : 3 * share, at : at + tile] for ref in held], axis=0)
        out_ref[:, at : at + tile] = (dot(hidden, down) * score).astype(BF)


def local(
    video,
    conv_weight,
    latent_weight,
    embed_weight,
    context,
    router_weight,
    gate_weight,
    up_weight,
    down_weight,
    routes,
):
    rows, cols = video.shape[1:3]
    tok, width = context.shape
    experts, capacity = 64, 2
    slots = experts * capacity
    share = down_weight.shape[1]
    hbm = pl.BlockSpec(memory_space=pltpu.HBM)
    vmem = pl.BlockSpec(memory_space=pltpu.VMEM)
    smem = pl.BlockSpec(memory_space=pltpu.SMEM)
    params = pltpu.CompilerParams(vmem_limit_bytes=VMEM_BYTES)

    past = shifted(video, FRAME, 1)
    parts = embed_weight.T
    for axis, pairs in (("yh", SWAP), ("x", XOR3)):
        parts = jnp.concatenate([parts, lax.ppermute(parts, axis, pairs)], axis=0)
    tall = parts.shape[0] * parts.shape[1] // width
    held = pl.pallas_call(
        pack_kernel,
        out_shape=jax.ShapeDtypeStruct((3 * share + tall, width), BF),
        in_specs=[hbm] * 4,
        out_specs=hbm,
        scratch_shapes=[pltpu.SemaphoreType.DMA((3 + width // 128,))],
        compiler_params=pltpu.CompilerParams(vmem_limit_bytes=PACK_BYTES),
    )(gate_weight[0].T, up_weight[0].T, down_weight[0], parts)
    held, past = lax.optimization_barrier((held, past))
    across = lax.ppermute(held, "x", XOR1)
    beside = lax.ppermute(held, "c", SWAP)

    stacked = jnp.concatenate([past, video], axis=0)
    above = shifted(stacked[:, rows - 1 :], EXPERT, 1)
    below = shifted(stacked[:, :1], EXPERT, -1)
    padded = jnp.concatenate([above, stacked, below], axis=1)
    chans = video.shape[3]
    raw = width + embed_weight.shape[0]
    outgoing, table = pl.pallas_call(
        front_kernel,
        out_shape=[jax.ShapeDtypeStruct((slots, raw), BF), jax.ShapeDtypeStruct((tok, slots), BF)],
        in_specs=[vmem] * 5,
        out_specs=[vmem] * 2,
        scratch_shapes=[pltpu.VMEM((padded.size // chans, 3 * chans), BF)],
        compiler_params=params,
    )(padded, conv_weight.reshape(3, 3, 3 * chans, chans), jnp.tile(latent_weight, (1, 8)), context, routes)

    arrived = lax.all_to_all(outgoing.reshape(experts, capacity, raw), SOURCES, split_axis=0, concat_axis=0, tiled=True)
    mine = arrived.reshape(slots, raw)
    theirs = lax.ppermute(mine, "x", XOR3)
    across, mine = lax.optimization_barrier((across, mine))
    corner = lax.ppermute(across, "c", SWAP)
    weights = (held, beside, across, corner)
    place = jnp.stack([lax.axis_index(axis) for axis in FRAME]).astype(jnp.int32)

    def expert(block):
        return pl.pallas_call(
            expert_kernel,
            out_shape=jax.ShapeDtypeStruct((slots, width), BF),
            in_specs=[smem] + [vmem] * 6,
            out_specs=vmem,
            scratch_shapes=[pltpu.VMEM((16, embed_weight.shape[1], 128), BF)],
            compiler_params=params,
        )(place, block, router_weight[:, :, 0], *weights)

    back = lax.ppermute(expert(theirs), "x", XOR3)
    own = expert(mine)
    summed = (back.astype(F32) + own.astype(F32)).astype(BF).reshape(experts, capacity, width)
    homeward = lax.all_to_all(summed, SOURCES, split_axis=0, concat_axis=0, tiled=True)
    return dot(table, homeward.reshape(slots, width)).astype(BF)


def solution(mesh):
    fine = Mesh(mesh.devices.reshape(SIZES), NAMES)
    return jax.shard_map(
        local,
        mesh=fine,
        in_specs=(
            P(FRAME, EXPERT, None, None),
            P(),
            P(),
            P(None, FRAME),
            P((*FRAME, *EXPERT), None),
            P(None, None, EXPERT),
            P(EXPERT, None, FRAME),
            P(EXPERT, None, FRAME),
            P(EXPERT, FRAME, None),
            P((*FRAME, *EXPERT), None),
        ),
        out_specs=P((*FRAME, *EXPERT), None),
        check_vma=False,
    )
```

time: 140 us -> 192 us (1.37)
  Pallas kernels: 12.9 us -> 69.7 us
  starting transfers between devices: 55.9 us -> 47 us
  waiting for transfers between devices: 34.1 us -> 41.4 us
  local copies, waits for them, and re-layouts: 7.1 us -> 2.29 us
  blocking collectives: 22.4 us -> 25.8 us
    pallas_call x3 -> x2, Pallas kernels: 3.84 us -> 59.7 us  [the longest x1 57.8 us: local(): pl.pallas_call(pack_kernel, out_shape=jax.ShapeDtypeStruct((3 * share + t...]
    ppermute x2 -> x0, starting transfers between devices: 11.4 us -> none  [local(): parts = jnp.concatenate([parts, lax.ppermute(parts, axis, SWAP)], axis=0)]
    ppermute x2, starting transfers between devices: 9.17 us -> 15.5 us  [local(): parts = jnp.concatenate([parts, lax.ppermute(parts, axis, pairs)], axis=0)]
    ppermute x3, waiting for transfers between devices: 0.01 us -> 4.97 us  [shifted(): return lax.ppermute(value, axes, pairs)]
    all_to_all x1, blocking collectives: 22.4 us -> 25.8 us  [local(): lax.all_to_all(summed, SOURCES, split_axis=0, concat_axis=0, tiled=True)]
  transfers between devices with their start and end apart: 13 -> 11, of which waited for: 4 -> 7; matrix products, arithmetic and copies ran while one was open for 8% -> 2% of each run, Pallas kernels for 6% -> 34%
where the time goes in v7:
time: 192 us; the launch traced here: 190 us
  Pallas kernels  69.7 us (36%)
  starting transfers between devices  47 us (24%)
  waiting for transfers between devices  41.4 us (22%)
  blocking collectives  25.8 us (13%)
  other arithmetic  2.34 us (1%)
  local copies, waits for them, and re-layouts  2.29 us (1%)
    pallas_call x1, Pallas kernels, local(): pl.pallas_call(pack_kernel, out_shape=jax.ShapeDtypeStruct((3 * share + t...  57.8 us
    all_to_all x1, blocking collectives, local(): lax.all_to_all(summed, SOURCES, split_axis=0, concat_axis=0, tiled=True)  25.8 us
    all_to_all x1, starting transfers between devices, local(): lax.all_to_all(outgoing.reshape(experts, capacity, raw), SOURCES, split_a...  16 us
    ppermute x2, starting transfers between devices, local(): parts = jnp.concatenate([parts, lax.ppermute(parts, axis, pairs)], axis=0)  15.5 us
    all_to_all x1, waiting for transfers between devices, local(): lax.all_to_all(outgoing.reshape(experts, capacity, raw), SOURCES, split_a...  14.9 us
    ppermute x1, waiting for transfers between devices, local(): theirs = lax.ppermute(mine, 'x', XOR3)  12.8 us
    pallas_call x2, Pallas kernels, expert(): pl.pallas_call(expert_kernel, out_shape=jax.ShapeDtypeStruct((slots, widt...  9.97 us
    ppermute x1, waiting for transfers between devices, local(): back = lax.ppermute(expert(theirs), 'x', XOR3)  6.44 us
  transfers between devices with their start and end apart: 11, of which 7 were waited for; matrix products, arithmetic and copies ran while one was open for 2% of the time, Pallas kernels for 34%

profile of v7, /device:TPU:6, one launch (start us, length us, event | category | flops | bytes accessed | tf_op | source)
XLA Modules:
  0.0 189.7 jit_solution(7532676296494257458)
XLA Ops:
  0.0 7.7 %collective-permute-start = (bf16[96,128]{1,0:T(8,128)(2,1)}, bf16[96,128]{1,0:T(8,128)(2,1)S(1)}, u32[]{:S(2)}, u32[]{:S(2)}) collective-permute-start(bf16[96,128]{1,0:T(8,128)(2,1)} %bitcast.23), channel_id=1, source_target_pairs={{0,256},{256,0},{1,257},{257,1},{2,258},{258,2},{3,259},{259,3},{4... | collective-permute-start | bytes 73736 | tf_op jit(solution)/shard_map/ppermute | solution.py:148
  7.7 2.1 %collective-permute-done = bf16[96,128]{1,0:T(8,128)(2,1)S(1)} collective-permute-done((bf16[96,128]{1,0:T(8,128)(2,1)}, bf16[96,128]{1,0:T(8,128)(2,1)S(1)}, u32[]{:S(2)}, u32[]{:S(2)}) %collective-permute-start) | collective-permute-done | bytes 24608 | tf_op jit(solution)/shard_map/ppermute | solution.py:148
  10.6 7.7 %collective-permute-start.1 = (bf16[192,128]{1,0:T(8,128)(2,1)S(1)}, bf16[192,128]{1,0:T(8,128)(2,1)S(1)}, u32[]{:S(2)}, u32[]{:S(2)}) collective-permute-start(bf16[192,128]{1,0:T(8,128)(2,1)S(1)} %pad_maximum_fusion.2), channel_id=1, source_target_pairs={{0,192},{64,128},{128,64},{192,0},{1,193},{65,129},{129,65},{193,1... | collective-permute-start | bytes 147464 | tf_op jit(solution)/shard_map/ppermute | solution.py:148
  18.3 1.9 %collective-permute-start.2 = (bf16[2,4,64,128]{3,2,1,0:T(8,128)(2,1)}, bf16[2,4,64,128]{3,2,1,0:T(8,128)(2,1)S(1)}, u32[]{:S(2)}, u32[]{:S(2)}) collective-permute-start(bf16[2,4,64,128]{3,2,1,0:T(8,128)(2,1)} %param.10), channel_id=1, source_target_pairs={{0,32},{32,64},{64,96},{96,128},{128,160},{160,192},{192,224},{224... | collective-permute-start | bytes 393224 | tf_op jit(solution)/shard_map/ppermute | solution.py:29
  20.4 1.4 pad_maximum_fusion.1.parts_ref
  21.8 57.8 %shard_map.100.w0_ref = bf16[608,1536]{1,0:T(8,128)(2,1)} custom-call(bf16[192,1536]{1,0:T(8,128)(2,1)} %bitcast.19, bf16[192,1536]{1,0:T(8,128)(2,1)} %bitcast.20, bf16[192,1536]{1,0:T(8,128)(2,1)} %bitcast.21, bf16[384,128]{1,0:T(8,128)(2,1)} %pad_maximum_fusion.1.parts_ref), custom_call_target="tpu_custom_call" | custom-call | tf_op jit(solution)/shard_map/pallas_call | solution.py:150
  79.6 2.1 %collective-permute-start.7 = (bf16[608,1536]{1,0:T(8,128)(2,1)}, bf16[608,1536]{1,0:T(8,128)(2,1)}, u32[]{:S(2)}, u32[]{:S(2)}) collective-permute-start(bf16[608,1536]{1,0:T(8,128)(2,1)} %shard_map.100.w0_ref), channel_id=1, source_target_pairs={{0,64},{64,0},{128,192},{192,128},{1,65},{65,1},{129,193},{193,129... | collective-permute-start | bytes 5603336 | tf_op jit(solution)/shard_map/ppermute | solution.py:159
  82.4 1.6 collective-permute-start.3
  84.0 1.3 collective-permute-start.4
  86.2 4.3 %collective-permute-done.4 = bf16[4,1,64,128]{3,2,1,0:T(8,128)(2,1)S(1)} collective-permute-done((bf16[4,1,64,128]{3,2,1,0:T(8,128)(2,1)S(1)}, bf16[4,1,64,128]{3,2,1,0:T(8,128)(2,1)S(1)}, u32[]{:S(2)}, u32[]{:S(2)}) %collective-permute-start.4) | collective-permute-done | bytes 65568 | tf_op jit(solution)/shard_map/ppermute | solution.py:29
  90.6 1.9 shard_map.101
  92.5 0.9 reshape.20
  93.5 16.0 %all-to-all-start = ((bf16[64,2,1664]{2,1,0:T(2,128)(2,1)}), bf16[64,2,1664]{2,1,0:T(2,128)(2,1)S(1)}, u32[]{:S(2)}, u32[]{:S(2)}) async-start(bf16[64,2,1664]{2,1,0:T(2,128)(2,1)} %reshape.20), calls=%async_computation | async-start | bytes 851968 | tf_op jit(solution)/shard_map/all_to_all | solution.py:177
  109.5 1.9 %collective-permute-start.6 = (bf16[608,1536]{1,0:T(8,128)(2,1)S(1)}, bf16[608,1536]{1,0:T(8,128)(2,1)}, u32[]{:S(2)}, u32[]{:S(2)}) collective-permute-start(bf16[608,1536]{1,0:T(8,128)(2,1)S(1)} %copy-done), channel_id=1, source_target_pairs={{0,32},{32,0},{1,33},{33,1},{2,34},{34,2},{3,35},{35,3},{4,36},{36... | collective-permute-start | bytes 5603336 | tf_op jit(solution)/shard_map/ppermute | solution.py:160
  111.5 14.9 %all-to-all-done = bf16[64,2,1664]{2,1,0:T(2,128)(2,1)S(1)} async-done(((bf16[64,2,1664]{2,1,0:T(2,128)(2,1)}), bf16[64,2,1664]{2,1,0:T(2,128)(2,1)S(1)}, u32[]{:S(2)}, u32[]{:S(2)}) %all-to-all-start) | async-done | bytes 426016 | tf_op jit(solution)/shard_map/all_to_all | solution.py:177
  126.5 1.9 %collective-permute-start.8 = (bf16[608,1536]{1,0:T(8,128)(2,1)}, bf16[608,1536]{1,0:T(8,128)(2,1)}, u32[]{:S(2)}, u32[]{:S(2)}) collective-permute-start(bf16[608,1536]{1,0:T(8,128)(2,1)} %collective-permute-done.7.w2_ref), channel_id=1, source_target_pairs={{0,32},{32,0},{1,33},{33,1},{2,34},{34,2},{3,35},{35,3},{4,36},{36... | collective-permute-start | bytes 5603336 | tf_op jit(solution)/shard_map/ppermute | solution.py:181
  128.4 2.4 %collective-permute-start.5 = (bf16[128,1664]{1,0:T(8,128)(2,1)S(1)}, bf16[128,1664]{1,0:T(8,128)(2,1)S(1)}, u32[]{:S(2)}, u32[]{:S(2)}) collective-permute-start(bf16[128,1664]{1,0:T(8,128)(2,1)S(1)} %reshape.21.rows_ref), channel_id=1, source_target_pairs={{0,192},{64,128},{128,64},{192,0},{1,193},{65,129},{129,65},{193,1... | collective-permute-start | bytes 1277960 | tf_op jit(solution)/shard_map/ppermute | solution.py:179
  130.9 12.8 %collective-permute-done.5.rows_ref = bf16[128,1664]{1,0:T(8,128)(2,1)S(1)} collective-permute-done((bf16[128,1664]{1,0:T(8,128)(2,1)S(1)}, bf16[128,1664]{1,0:T(8,128)(2,1)S(1)}, u32[]{:S(2)}, u32[]{:S(2)}) %collective-permute-start.5) | collective-permute-done | bytes 426016 | tf_op jit(solution)/shard_map/ppermute | solution.py:179
  143.8 5.0 %shard_map.102 = bf16[128,1536]{1,0:T(8,128)(2,1)S(1)} custom-call(s32[3]{0:T(128)S(1)} %pad_add_fusion.at_ref, bf16[128,1664]{1,0:T(8,128)(2,1)S(1)} %collective-permute-done.5.rows_ref, bf16[2,1536]{1,0:T(2,128)(2,1)S(1)} %bitcast.17, bf16[608,1536]{1,0:T(8,128)(2,1)S(1)} %copy-done, bf16[608,1536]{1,0:T(8,128)(2,1)} %collective-permute-done.6.w1_ref, ...), custom_call_target="tpu_custom_call" | custom-call | tf_op jit(solution)/shard_map/pallas_call | solution.py:186
  148.8 2.4 %collective-permute-start.9 = (bf16[128,1536]{1,0:T(8,128)(2,1)S(1)}, bf16[128,1536]{1,0:T(8,128)(2,1)S(1)}, u32[]{:S(2)}, u32[]{:S(2)}) collective-permute-start(bf16[128,1536]{1,0:T(8,128)(2,1)S(1)} %shard_map.102), channel_id=1, source_target_pairs={{0,192},{64,128},{128,64},{192,0},{1,193},{65,129},{129,65},{193,1... | collective-permute-start | bytes 1179656 | tf_op jit(solution)/shard_map/ppermute | solution.py:195
  151.2 5.0 %shard_map.103 = bf16[128,1536]{1,0:T(8,128)(2,1)S(1)} custom-call(s32[3]{0:T(128)S(1)} %pad_add_fusion.at_ref, bf16[128,1664]{1,0:T(8,128)(2,1)S(1)} %reshape.21.rows_ref, bf16[2,1536]{1,0:T(2,128)(2,1)S(1)} %bitcast.18, bf16[608,1536]{1,0:T(8,128)(2,1)S(1)} %copy-done, bf16[608,1536]{1,0:T(8,128)(2,1)} %collective-permute-done.6.w1_ref, ...), custom_call_target="tpu_custom_call" | custom-call | tf_op jit(solution)/shard_map/pallas_call | solution.py:186
  156.1 6.4 %collective-permute-done.9 = bf16[128,1536]{1,0:T(8,128)(2,1)S(1)} collective-permute-done((bf16[128,1536]{1,0:T(8,128)(2,1)S(1)}, bf16[128,1536]{1,0:T(8,128)(2,1)S(1)}, u32[]{:S(2)}, u32[]{:S(2)}) %collective-permute-start.9) | collective-permute-done | bytes 393248 | tf_op jit(solution)/shard_map/ppermute | solution.py:195
  162.8 25.8 %all_to_all.10 = bf16[64,2,1536]{2,1,0:T(2,128)(2,1)S(1)} all-to-all(bf16[64,2,1536]{2,1,0:T(2,128)(2,1)S(1)} %reshape.22), channel_id=1, replica_groups=mesh['yh'=2,'x'=4,'c'=2,'yl'=4,'z'=8] {'yh','yl','z'}, dimensions={0} | all-to-all | bytes 786432 | tf_op jit(solution)/shard_map/all_to_all | solution.py:198
  188.8 0.9 convolution_convert_fusion
  (33 shorter events, 3.1 us)
Async XLA Ops:
  0.0 9.8 %collective-permute-start = (bf16[96,128]{1,0:T(8,128)(2,1)}, bf16[96,128]{1,0:T(8,128)(2,1)S(1)}, u32[]{:S(2)}, u32[]{:S(2)}) collective-permute-start(bf16[96,128]{1,0:T(8,128)(2,1)} %bitcast.23), channel_id=1, source_target_pairs={{0,256},{256,0},{1,257},{257,1},{2,258},{258,2},{3,259},{259,3},{4... | collective-permute-start | bytes 73736 | tf_op jit(solution)/shard_map/ppermute | solution.py:148
  10.6 9.8 %collective-permute-start.1 = (bf16[192,128]{1,0:T(8,128)(2,1)S(1)}, bf16[192,128]{1,0:T(8,128)(2,1)S(1)}, u32[]{:S(2)}, u32[]{:S(2)}) collective-permute-start(bf16[192,128]{1,0:T(8,128)(2,1)S(1)} %pad_maximum_fusion.2), channel_id=1, source_target_pairs={{0,192},{64,128},{128,64},{192,0},{1,193},{65,129},{129,65},{193,1... | collective-permute-start | bytes 147464 | tf_op jit(solution)/shard_map/ppermute | solution.py:148
  18.3 61.3 %collective-permute-start.2 = (bf16[2,4,64,128]{3,2,1,0:T(8,128)(2,1)}, bf16[2,4,64,128]{3,2,1,0:T(8,128)(2,1)S(1)}, u32[]{:S(2)}, u32[]{:S(2)}) collective-permute-start(bf16[2,4,64,128]{3,2,1,0:T(8,128)(2,1)} %param.10), channel_id=1, source_target_pairs={{0,32},{32,64},{64,96},{96,128},{128,160},{160,192},{192,224},{224... | collective-permute-start | bytes 393224 | tf_op jit(solution)/shard_map/ppermute | solution.py:29
  21.8 59.9 %copy-start.4 = (bf16[2,4,64,128]{3,2,1,0:T(8,128)(2,1)S(1)}, bf16[2,4,64,128]{3,2,1,0:T(8,128)(2,1)}, u32[]{:S(2)}) copy-start(bf16[2,4,64,128]{3,2,1,0:T(8,128)(2,1)} %param.10) | copy-start | bytes 393220
  21.8 63.6 %copy-start.5 = (bf16[128,16]{0,1:T(8,128)(2,1)S(1)}, bf16[128,16]{0,1:T(8,128)(2,1)}, u32[]{:S(2)}) copy-start(bf16[128,16]{0,1:T(8,128)(2,1)} %param.12) | copy-start | bytes 12292
  21.8 63.7 %copy-start.6 = (s32[64,2]{0,1:T(2,128)S(1)}, s32[64,2]{0,1:T(2,128)}, u32[]{:S(2)}) copy-start(s32[64,2]{0,1:T(2,128)} %param.19) | copy-start | bytes 1540
  21.8 68.8 %copy-start.2 = (bf16[64,1536]{1,0:T(8,128)(2,1)S(1)}, bf16[64,1536]{1,0:T(8,128)(2,1)}, u32[]{:S(2)}) copy-start(bf16[64,1536]{1,0:T(8,128)(2,1)} %context_ref.1) | copy-start | bytes 589828
  79.6 11.0 %copy-start.1 = (bf16[3,3,3,128,128]{4,3,2,1,0:T(8,128)(2,1)S(1)}, bf16[3,3,3,128,128]{4,3,2,1,0:T(8,128)(2,1)}, u32[]{:S(2)}) copy-start(bf16[3,3,3,128,128]{4,3,2,1,0:T(8,128)(2,1)} %param.11) | copy-start | bytes 2654212
  79.6 46.9 %collective-permute-start.7 = (bf16[608,1536]{1,0:T(8,128)(2,1)}, bf16[608,1536]{1,0:T(8,128)(2,1)}, u32[]{:S(2)}, u32[]{:S(2)}) collective-permute-start(bf16[608,1536]{1,0:T(8,128)(2,1)} %shard_map.100.w0_ref), channel_id=1, source_target_pairs={{0,64},{64,0},{128,192},{192,128},{1,65},{65,1},{129,193},{193,129... | collective-permute-start | bytes 5603336 | tf_op jit(solution)/shard_map/ppermute | solution.py:159
  82.4 3.8 %collective-permute-start.3 = (bf16[4,1,64,128]{3,2,1,0:T(8,128)(2,1)}, bf16[4,1,64,128]{3,2,1,0:T(8,128)(2,1)S(1)}, u32[]{:S(2)}, u32[]{:S(2)}) collective-permute-start(bf16[4,1,64,128]{3,2,1,0:T(8,128)(2,1)} %get-tuple-element.17), channel_id=1, source_target_pairs={{0,1},{1,2},{2,3},{3,4},{4,5},{5,6},{6,7},{7,8},{8,9},{9,10},{10,1... | collective-permute-start | bytes 196616 | tf_op jit(solution)/shard_map/ppermute | solution.py:29
  84.0 6.5 %collective-permute-start.4 = (bf16[4,1,64,128]{3,2,1,0:T(8,128)(2,1)S(1)}, bf16[4,1,64,128]{3,2,1,0:T(8,128)(2,1)S(1)}, u32[]{:S(2)}, u32[]{:S(2)}) collective-permute-start(bf16[4,1,64,128]{3,2,1,0:T(8,128)(2,1)S(1)} %get-tuple-element.18), channel_id=1, source_target_pairs={{1,0},{2,1},{3,2},{4,3},{5,4},{6,5},{7,6},{8,7},{9,8},{10,9},{11,1... | collective-permute-start | bytes 196616 | tf_op jit(solution)/shard_map/ppermute | solution.py:29
  85.6 23.9 %copy-start = (bf16[608,1536]{1,0:T(8,128)(2,1)S(1)}, bf16[608,1536]{1,0:T(8,128)(2,1)}, u32[]{:S(2)}) copy-start(bf16[608,1536]{1,0:T(8,128)(2,1)} %shard_map.100.w0_ref) | copy-start | bytes 5603332
  90.6 53.1 %copy-start.3 = (bf16[2,1536,1]{1,0,2:T(2,128)(2,1)S(1)}, bf16[2,1536,1]{1,0,2:T(2,128)(2,1)}, u32[]{:S(2)}) copy-start(bf16[2,1536,1]{1,0,2:T(2,128)(2,1)} %param.15) | copy-start | bytes 18436
  93.5 32.9 %all-to-all-start = ((bf16[64,2,1664]{2,1,0:T(2,128)(2,1)}), bf16[64,2,1664]{2,1,0:T(2,128)(2,1)S(1)}, u32[]{:S(2)}, u32[]{:S(2)}) async-start(bf16[64,2,1664]{2,1,0:T(2,128)(2,1)} %reshape.20), calls=%async_computation | async-start | bytes 851968 | tf_op jit(solution)/shard_map/all_to_all | solution.py:177
  109.5 34.2 %collective-permute-start.6 = (bf16[608,1536]{1,0:T(8,128)(2,1)S(1)}, bf16[608,1536]{1,0:T(8,128)(2,1)}, u32[]{:S(2)}, u32[]{:S(2)}) collective-permute-start(bf16[608,1536]{1,0:T(8,128)(2,1)S(1)} %copy-done), channel_id=1, source_target_pairs={{0,32},{32,0},{1,33},{33,1},{2,34},{34,2},{3,35},{35,3},{4,36},{36... | collective-permute-start | bytes 5603336 | tf_op jit(solution)/shard_map/ppermute | solution.py:160
  126.5 17.3 %collective-permute-start.8 = (bf16[608,1536]{1,0:T(8,128)(2,1)}, bf16[608,1536]{1,0:T(8,128)(2,1)}, u32[]{:S(2)}, u32[]{:S(2)}) collective-permute-start(bf16[608,1536]{1,0:T(8,128)(2,1)} %collective-permute-done.7.w2_ref), channel_id=1, source_target_pairs={{0,32},{32,0},{1,33},{33,1},{2,34},{34,2},{3,35},{35,3},{4,36},{36... | collective-permute-start | bytes 5603336 | tf_op jit(solution)/shard_map/ppermute | solution.py:181
  128.4 15.3 %collective-permute-start.5 = (bf16[128,1664]{1,0:T(8,128)(2,1)S(1)}, bf16[128,1664]{1,0:T(8,128)(2,1)S(1)}, u32[]{:S(2)}, u32[]{:S(2)}) collective-permute-start(bf16[128,1664]{1,0:T(8,128)(2,1)S(1)} %reshape.21.rows_ref), channel_id=1, source_target_pairs={{0,192},{64,128},{128,64},{192,0},{1,193},{65,129},{129,65},{193,1... | collective-permute-start | bytes 1277960 | tf_op jit(solution)/shard_map/ppermute | solution.py:179
  148.8 13.8 %collective-permute-start.9 = (bf16[128,1536]{1,0:T(8,128)(2,1)S(1)}, bf16[128,1536]{1,0:T(8,128)(2,1)S(1)}, u32[]{:S(2)}, u32[]{:S(2)}) collective-permute-start(bf16[128,1536]{1,0:T(8,128)(2,1)S(1)} %shard_map.102), channel_id=1, source_target_pairs={{0,192},{64,128},{128,64},{192,0},{1,193},{65,129},{129,65},{193,1... | collective-permute-start | bytes 1179656 | tf_op jit(solution)/shard_map/ppermute | solution.py:195

commit v8 on v7

--- a/solution.py
+++ b/solution.py
@@ -13,8 +13,6 @@
 BF = jnp.bfloat16
 F32 = jnp.float32
 SWAP = [(0, 1), (1, 0)]
-XOR1 = [(i, i ^ 1) for i in range(4)]
-XOR3 = [(i, i ^ 3) for i in range(4)]
 VMEM_BYTES = 16 * 1024 * 1024
 PACK_BYTES = 66_400_000
 
@@ -29,17 +27,43 @@
     return lax.ppermute(value, axes, pairs)
 
 
+def ring(value, step):
+    return lax.ppermute(value, "x", [(i, (i - step) % 4) for i in range(4)])
+
+
 def silu(value):
     return value / (1.0 + jnp.exp(-value))
 
 
-def pack_kernel(gate_ref, up_ref, down_ref, parts_ref, out_ref, sems):
-    share, tall = down_ref.shape[0], parts_ref.shape[0] * 128 // down_ref.shape[1]
-    copies = [(ref, out_ref.at[pl.ds(i * share, share)]) for i, ref in enumerate((gate_ref, up_ref, down_ref))]
-    for j in range(parts_ref.shape[0] // tall):
-        target = out_ref.at[pl.ds(3 * share, tall), pl.ds(j * 128, 128)]
-        copies.append((parts_ref.at[pl.ds(j * tall, tall)], target))
-    copies = [pltpu.make_async_copy(*pair, sems.at[i]) for i, pair in enumerate(copies)]
+def lay_beside(out_ref, at, *refs):
+    tall = len(refs) * refs[0].shape[0] * 128 // 1536
+    lane = 0
+    for ref in refs:
+        for row in range(0, ref.shape[0], tall):
+            out_ref[at : at + tall, lane : lane + 128] = ref[row : row + tall]
+            lane += 128
+
+
+def pack_kernel(
+    gate_ref, up_ref, down_ref, own_ref, other_ref, first_ref, second_ref, first_held, second_held, sems
+):
+    share = down_ref.shape[0]
+    half, part = share // 2, 3 * share // 2
+    copies = [
+        pltpu.make_async_copy(gate_ref, first_held.at[pl.ds(0, share)], sems.at[0]),
+        pltpu.make_async_copy(up_ref.at[pl.ds(0, half)], first_held.at[pl.ds(share, half)], sems.at[1]),
+        pltpu.make_async_copy(up_ref.at[pl.ds(half, half)], second_held.at[pl.ds(0, half)], sems.at[2]),
+        pltpu.make_async_copy(down_ref, second_held.at[pl.ds(half, share)], sems.at[3]),
+    ]
+    for copy in copies:
+        copy.start()
+    lay_beside(first_held, part, own_ref, other_ref)
+    for copy in copies:
+        copy.wait()
+    copies = [
+        pltpu.make_async_copy(first_held, first_ref, sems.at[4]),
+        pltpu.make_async_copy(second_held, second_ref, sems.at[5]),
+    ]
     for copy in copies:
         copy.start()
     for copy in copies:
@@ -89,35 +113,103 @@
     out_ref[:, width:] = dot(table, patches, ((0,), (0,))).astype(BF)
 
 
-def expert_kernel(at_ref, rows_ref, router_ref, w0_ref, w1_ref, w2_ref, w3_ref, out_ref, embed_ref):
-    held = (w0_ref, w1_ref, w2_ref, w3_ref)
+def swap_kernel(rows_ref, own_ref, other_ref, a0_ref, a1_ref, a2_ref, out_ref, held_ref, sems):
+    slots, (_, tall, width) = rows_ref.shape[0], held_ref.shape
+    part = a0_ref.shape[0] - tall
+    copies = [
+        pltpu.make_async_copy(ref.at[pl.ds(part, tall)], held_ref.at[i], sems.at[i])
+        for i, ref in enumerate((a0_ref, a1_ref, a2_ref))
+    ]
+    for copy in copies:
+        copy.start()
+    out_ref[:slots] = rows_ref[...]
+    out_ref[slots:, width:] = jnp.zeros((out_ref.shape[0] - slots, out_ref.shape[1] - width), BF)
+    lay_beside(out_ref, slots + 3 * tall, own_ref, other_ref)
+    for i, copy in enumerate(copies):
+        copy.wait()
+        out_ref[slots + i * tall : slots + (i + 1) * tall, :width] = held_ref[i]
+
+
+def near_kernel(
+    at_ref,
+    mine_ref,
+    theirs_ref,
+    router_ref,
+    a0_ref,
+    b0_ref,
+    a1_ref,
+    b1_ref,
+    a2_ref,
+    b2_ref,
+    tokens_ref,
+    score_ref,
+    total_ref,
+    held_ref,
+    embed_ref,
+    sems,
+):
     yh, x, c = at_ref[0], at_ref[1], at_ref[2]
-    width = out_ref.shape[1]
-    size = embed_ref.shape[1]
-    share = (w0_ref.shape[0] - 4 * size * 128 // width) // 3
-    tall = 4 * size * 128 // width
-    for i, ref in enumerate(held):
-        for m in range(4):
-            shard = (yh ^ m % 2) * 8 + (x ^ i // 2 ^ m // 2 * 3) * 2 + (c ^ i % 2)
-            for j in range(size // tall):
-                lane = (m * (size // tall) + j) * 128
-                embed_ref[shard, j * tall : (j + 1) * tall] = ref[3 * share :, lane : lane + 128]
+    rows, width = tokens_ref.shape[0] // 2, total_ref.shape[1]
+    part = b0_ref.shape[0]
+    share = part * 2 // 3
+    copies = [
+        pltpu.make_async_copy(ref.at[pl.ds(0, part)], held_ref.at[i // 2, pl.ds(i % 2 * part, part)], sems.at[i])
+        for i, ref in enumerate((a0_ref, b0_ref, a1_ref, b1_ref, a2_ref, b2_ref))
+    ]
+    for copy in copies:
+        copy.start()
+    tall = (mine_ref.shape[0] - rows) // 4
+    tiles = embed_ref.shape[1] // tall
+    for core, ref in enumerate((mine_ref, theirs_ref)):
+        for i, turn in enumerate((0, 3, 1, 2)):
+            for j in range(2 * tiles):
+                shard = (yh ^ j // tiles) * 8 + lax.rem(x + turn, 4) * 2 + (c ^ core)
+                at = rows + i * tall
+                embed_ref[shard, j % tiles * tall : (j % tiles + 1) * tall] = ref[at : at + tall, j * 128 : (j + 1) * 128]
     embed = embed_ref[...].reshape(width, 128)
-    embedded = dot(rows_ref[:, width:], embed, ((1,), (1,))).astype(BF)
-    total = embedded.astype(F32) + rows_ref[:, :width].astype(F32)
-    meansq = jnp.mean(total * total, axis=1, keepdims=True)
-    tokens = (total * lax.rsqrt(meansq + 1e-06)).astype(BF)
     router = jnp.where(yh == 0, router_ref[:1], router_ref[1:]).astype(F32)
-    score = 1.0 / (1.0 + jnp.exp(-jnp.sum(tokens.astype(F32) * router, axis=1, keepdims=True)))
+    for half, ref in enumerate((theirs_ref, mine_ref)):
+        embedded = dot(ref[:rows, width:], embed, ((1,), (1,))).astype(BF)
+        total = embedded.astype(F32) + ref[:rows, :width].astype(F32)
+        meansq = jnp.mean(total * total, axis=1, keepdims=True)
+        tokens = (total * lax.rsqrt(meansq + 1e-06)).astype(BF)
+        logit = jnp.sum(tokens.astype(F32) * router, axis=1, keepdims=True)
+        at = slice(half * rows, (half + 1) * rows)
+        tokens_ref[at] = tokens
+        score_ref[at] = 1.0 / (1.0 + jnp.exp(-logit))
     hidden = []
-    for ref in held:
-        both = dot(tokens, ref[: 2 * share], ((1,), (1,)))
+    for i in range(3):
+        copies[2 * i].wait()
+        copies[2 * i + 1].wait()
+        both = dot(tokens_ref[...], held_ref[i, : 2 * share], ((1,), (1,)))
         hidden.append((silu(both[:, :share]) * both[:, share:]).astype(BF))
     hidden = jnp.concatenate(hidden, axis=1)
     tile = 512
     for at in range(0, width, tile):
-        down = jnp.concatenate([ref[2 * share : 3 * share, at : at + tile] for ref in held], axis=0)
-        out_ref[:, at : at + tile] = (dot(hidden, down) * score).astype(BF)
+        down = jnp.concatenate([held_ref[i, 2 * share :, at : at + tile] for i in range(3)], axis=0)
+        total_ref[:, at : at + tile] = dot(hidden, down)
+
+
+def last_kernel(tokens_ref, score_ref, total_ref, w0_ref, w1_ref, other_ref, own_ref, held_ref, sems):
+    rows, width = other_ref.shape
+    part, share = w1_ref.shape[0], held_ref.shape[0] // 3
+    copies = [
+        pltpu.make_async_copy(ref.at[pl.ds(0, part)], held_ref.at[pl.ds(i * part, part)], sems.at[i])
+        for i, ref in enumerate((w0_ref, w1_ref))
+    ]
+    for copy in copies:
+        copy.start()
+    for copy in copies:
+        copy.wait()
+    both = dot(tokens_ref[...], held_ref[: 2 * share], ((1,), (1,)))
+    hidden = (silu(both[:, :share]) * both[:, share:]).astype(BF)
+    tile = 512
+    for at in range(0, width, tile):
+        cut = slice(at, at + tile)
+        total = total_ref[:, cut] + dot(hidden, held_ref[2 * share :, cut])
+        total = (total * score_ref[...]).astype(BF)
+        other_ref[:, cut] = total[:rows]
+        own_ref[:, cut] = total[rows:]
 
 
 def local(
@@ -143,21 +235,28 @@
     params = pltpu.CompilerParams(vmem_limit_bytes=VMEM_BYTES)
 
     past = shifted(video, FRAME, 1)
-    parts = embed_weight.T
-    for axis, pairs in (("yh", SWAP), ("x", XOR3)):
-        parts = jnp.concatenate([parts, lax.ppermute(parts, axis, pairs)], axis=0)
-    tall = parts.shape[0] * parts.shape[1] // width
-    held = pl.pallas_call(
+    shard = embed_weight.T
+    paired = lax.ppermute(shard, "yh", SWAP)
+    opposite = ring(shard, 2)
+    crossed = lax.ppermute(shard, ("yh", "x"), [(i, (i + 4) % 8 // 4 * 4 + (i + 2) % 4) for i in range(8)])
+    part = 3 * share // 2
+    tall = 2 * shard.shape[0] * shard.shape[1] // width
+    first, second = pl.pallas_call(
         pack_kernel,
-        out_shape=jax.ShapeDtypeStruct((3 * share + tall, width), BF),
-        in_specs=[hbm] * 4,
-        out_specs=hbm,
-        scratch_shapes=[pltpu.SemaphoreType.DMA((3 + width // 128,))],
+        out_shape=[jax.ShapeDtypeStruct((part + tall, width), BF), jax.ShapeDtypeStruct((part, width), BF)],
+        in_specs=[hbm] * 3 + [vmem] * 2,
+        out_specs=[hbm] * 2,
+        scratch_shapes=[
+            pltpu.VMEM((part + tall, width), BF),
+            pltpu.VMEM((part, width), BF),
+            pltpu.SemaphoreType.DMA((6,)),
+        ],
         compiler_params=pltpu.CompilerParams(vmem_limit_bytes=PACK_BYTES),
-    )(gate_weight[0].T, up_weight[0].T, down_weight[0], parts)
-    held, past = lax.optimization_barrier((held, past))
-    across = lax.ppermute(held, "x", XOR1)
-    beside = lax.ppermute(held, "c", SWAP)
+    )(gate_weight[0].T, up_weight[0].T, down_weight[0], shard, paired)
+    first, second, past, opposite, crossed = lax.optimization_barrier((first, second, past, opposite, crossed))
+    first_behind, second_ahead = ring(first, -1), ring(second, 1)
+    first_ahead, second_behind = ring(first, 1), ring(second, -1)
+    first_opposite, second_opposite = ring(first_behind, -1), ring(second_ahead, 1)
 
     stacked = jnp.concatenate([past, video], axis=0)
     above = shifted(stacked[:, rows - 1 :], EXPERT, 1)
@@ -175,25 +274,42 @@
     )(padded, conv_weight.reshape(3, 3, 3 * chans, chans), jnp.tile(latent_weight, (1, 8)), context, routes)
 
     arrived = lax.all_to_all(outgoing.reshape(experts, capacity, raw), SOURCES, split_axis=0, concat_axis=0, tiled=True)
-    mine = arrived.reshape(slots, raw)
-    theirs = lax.ppermute(mine, "x", XOR3)
-    across, mine = lax.optimization_barrier((across, mine))
-    corner = lax.ppermute(across, "c", SWAP)
-    weights = (held, beside, across, corner)
+    arrived, first_ahead, second_behind = lax.optimization_barrier((arrived, first_ahead, second_behind))
+    mine = pl.pallas_call(
+        swap_kernel,
+        out_shape=jax.ShapeDtypeStruct((slots + 4 * tall, raw), BF),
+        in_specs=[vmem] * 3 + [hbm] * 3,
+        out_specs=vmem,
+        scratch_shapes=[pltpu.VMEM((3, tall, width), BF), pltpu.SemaphoreType.DMA((3,))],
+        compiler_params=params,
+    )(arrived.reshape(slots, raw), opposite, crossed, first, first_behind, first_ahead)
+    theirs = lax.ppermute(mine, "c", SWAP)
     place = jnp.stack([lax.axis_index(axis) for axis in FRAME]).astype(jnp.int32)
-
-    def expert(block):
-        return pl.pallas_call(
-            expert_kernel,
-            out_shape=jax.ShapeDtypeStruct((slots, width), BF),
-            in_specs=[smem] + [vmem] * 6,
-            out_specs=vmem,
-            scratch_shapes=[pltpu.VMEM((16, embed_weight.shape[1], 128), BF)],
-            compiler_params=params,
-        )(place, block, router_weight[:, :, 0], *weights)
-
-    back = lax.ppermute(expert(theirs), "x", XOR3)
-    own = expert(mine)
+    tokens, score, total = pl.pallas_call(
+        near_kernel,
+        out_shape=[
+            jax.ShapeDtypeStruct((2 * slots, width), BF),
+            jax.ShapeDtypeStruct((2 * slots, 1), F32),
+            jax.ShapeDtypeStruct((2 * slots, width), F32),
+        ],
+        in_specs=[smem] + [vmem] * 3 + [hbm] * 6,
+        out_specs=[vmem] * 3,
+        scratch_shapes=[
+            pltpu.VMEM((3, 3 * share, width), BF),
+            pltpu.VMEM((16, embed_weight.shape[1], 128), BF),
+            pltpu.SemaphoreType.DMA((6,)),
+        ],
+        compiler_params=params,
+    )(place, mine, theirs, router_weight[:, :, 0], first, second, first_behind, second_behind, first_ahead, second_ahead)
+    other, own = pl.pallas_call(
+        last_kernel,
+        out_shape=[jax.ShapeDtypeStruct((slots, width), BF)] * 2,
+        in_specs=[vmem] * 3 + [hbm] * 2,
+        out_specs=[vmem] * 2,
+        scratch_shapes=[pltpu.VMEM((3 * share, width), BF), pltpu.SemaphoreType.DMA((2,))],
+        compiler_params=params,
+    )(tokens, score, total, first_opposite, second_opposite)
+    back = lax.ppermute(other, "c", SWAP)
     summed = (back.astype(F32) + own.astype(F32)).astype(BF).reshape(experts, capacity, width)
     homeward = lax.all_to_all(summed, SOURCES, split_axis=0, concat_axis=0, tiled=True)
     return dot(table, homeward.reshape(slots, width)).astype(BF)

time: 192 us -> 131 us (0.68)
  Pallas kernels: 69.7 us -> 13.4 us
  waiting for transfers between devices: 41.4 us -> 21.2 us
  starting transfers between devices: 47 us -> 59 us
  local copies, waits for them, and re-layouts: 2.29 us -> 6.75 us
  blocking collectives: 25.8 us -> 28.5 us
  other arithmetic: 2.34 us -> 0.22 us
    pallas_call x3 -> x4, Pallas kernels: 67.8 us -> 11.6 us  [the longest x1 5.42 us: local(): pl.pallas_call(near_kernel, out_shape=[jax.ShapeDtypeStruct((2 * slots, w...]
    ppermute x7 -> x11, starting transfers between devices: 26.1 us -> 37.5 us  [the longest x7 22.3 us: ring(): return lax.ppermute(value, 'x', [(i, (i - step) % 4) for i in range(4)])]
    ppermute x7 -> x11, waiting for transfers between devices: 21.5 us -> 11.8 us  [the longest x1 4.85 us: local(): lax.ppermute(shard, ('yh', 'x'), [(i, (i + 4) % 8 // 4 * 4 + (i + 2) % 4)...]
    all_to_all x1, waiting for transfers between devices: 14.9 us -> 9.43 us  [local(): lax.all_to_all(outgoing.reshape(experts, capacity, raw), SOURCES, split_a...]
    ppermute x3, waiting for transfers between devices: 4.97 us -> 0.01 us  [shifted(): return lax.ppermute(value, axes, pairs)]
    unnamed x16 -> x22, local copies, waits for them, and re-layouts: 0.14 us -> 3.82 us
    ppermute x3, starting transfers between devices: 4.85 us -> 8.24 us  [shifted(): return lax.ppermute(value, axes, pairs)]
    all_to_all x1, starting transfers between devices: 16 us -> 13.3 us  [local(): lax.all_to_all(outgoing.reshape(experts, capacity, raw), SOURCES, split_a...]
  transfers between devices with their start and end apart: 11 -> 15, of which waited for: 7 -> 6; matrix products, arithmetic and copies ran while one was open for 2% -> 2% of each run, Pallas kernels for 34% -> 8%
where the time goes in v8:
time: 131 us; the launch traced here: 130 us
  starting transfers between devices  59 us (45%)
  blocking collectives  28.5 us (22%)
  waiting for transfers between devices  21.2 us (16%)
  Pallas kernels  13.4 us (10%)
  local copies, waits for them, and re-layouts  6.75 us (5%)
    all_to_all x1, blocking collectives, local(): lax.all_to_all(summed, SOURCES, split_axis=0, concat_axis=0, tiled=True)  28.5 us
    ppermute x7, starting transfers between devices, ring(): return lax.ppermute(value, 'x', [(i, (i - step) % 4) for i in range(4)])  22.3 us
    all_to_all x1, starting transfers between devices, local(): lax.all_to_all(outgoing.reshape(experts, capacity, raw), SOURCES, split_a...  13.3 us
    all_to_all x1, waiting for transfers between devices, local(): lax.all_to_all(outgoing.reshape(experts, capacity, raw), SOURCES, split_a...  9.43 us
    ppermute x3, starting transfers between devices, shifted(): return lax.ppermute(value, axes, pairs)  8.24 us
    ppermute x1, starting transfers between devices, local(): paired = lax.ppermute(shard, 'yh', SWAP)  7.73 us
    pallas_call x1, Pallas kernels, local(): pl.pallas_call(near_kernel, out_shape=[jax.ShapeDtypeStruct((2 * slots, w...  5.42 us
    ppermute x1, waiting for transfers between devices, local(): lax.ppermute(shard, ('yh', 'x'), [(i, (i + 4) % 8 // 4 * 4 + (i + 2) % 4)...  4.85 us
  transfers between devices with their start and end apart: 15, of which 6 were waited for; matrix products, arithmetic and copies ran while one was open for 2% of the time, Pallas kernels for 8%

profile of v8, /device:TPU:6, one launch (start us, length us, event | category | flops | bytes accessed | tf_op | source)
XLA Modules:
  0.0 130.4 jit_solution(8429702433136687809)
XLA Ops:
  0.0 2.1 %collective-permute-start.1 = (bf16[2,4,64,128]{3,2,1,0:T(8,128)(2,1)}, bf16[2,4,64,128]{3,2,1,0:T(8,128)(2,1)}, u32[]{:S(2)}, u32[]{:S(2)}) collective-permute-start(bf16[2,4,64,128]{3,2,1,0:T(8,128)(2,1)} %param.10), channel_id=1, source_target_pairs={{0,32},{32,64},{64,96},{96,128},{128,160},{160,192},{192,224},{224... | collective-permute-start | bytes 393224 | tf_op jit(solution)/shard_map/ppermute | solution.py:27
  2.1 7.7 %collective-permute-start = (bf16[96,128]{1,0:T(8,128)(2,1)}, bf16[96,128]{1,0:T(8,128)(2,1)S(1)}, u32[]{:S(2)}, u32[]{:S(2)}) collective-permute-start(bf16[96,128]{1,0:T(8,128)(2,1)} %bitcast.22), channel_id=1, source_target_pairs={{0,256},{256,0},{1,257},{257,1},{2,258},{258,2},{3,259},{259,3},{4... | collective-permute-start | bytes 73736 | tf_op jit(solution)/shard_map/ppermute | solution.py:239
  9.8 3.3 %collective-permute-start.2 = (bf16[96,128]{1,0:T(8,128)(2,1)}, bf16[96,128]{1,0:T(8,128)(2,1)S(1)}, u32[]{:S(2)}, u32[]{:S(2)}) collective-permute-start(bf16[96,128]{1,0:T(8,128)(2,1)} %bitcast.23), channel_id=1, source_target_pairs={{0,128},{64,192},{128,0},{192,64},{1,129},{65,193},{129,1},{193,65... | collective-permute-start | bytes 73736 | tf_op jit(solution)/shard_map/ppermute | solution.py:31
  13.1 3.6 %collective-permute-start.3 = (bf16[96,128]{1,0:T(8,128)(2,1)}, bf16[96,128]{1,0:T(8,128)(2,1)S(1)}, u32[]{:S(2)}, u32[]{:S(2)}) collective-permute-start(bf16[96,128]{1,0:T(8,128)(2,1)} %bitcast.24), channel_id=1, source_target_pairs={{0,384},{64,448},{128,256},{192,320},{256,128},{320,192},{384,0},{... | collective-permute-start | bytes 73736 | tf_op jit(solution)/shard_map/ppermute | solution.py:241
  17.3 3.5 %shard_map.100 = (bf16[304,1536]{1,0:T(8,128)(2,1)}, bf16[288,1536]{1,0:T(8,128)(2,1)}) custom-call(bf16[192,1536]{1,0:T(8,128)(2,1)} %bitcast.18, bf16[192,1536]{1,0:T(8,128)(2,1)} %bitcast.19, bf16[192,1536]{1,0:T(8,128)(2,1)} %bitcast.20, bf16[96,128]{1,0:T(8,128)(2,1)} %bitcast.25, bf16[96,128]{1,0:T(8,128)(2,1)} %copy-done.7), custom_call_target="tpu_custom_call" | custom-call | tf_op jit(solution)/shard_map/pallas_call | solution.py:244
  20.9 4.8 %collective-permute-done.3.other_ref = bf16[96,128]{1,0:T(8,128)(2,1)S(1)} collective-permute-done((bf16[96,128]{1,0:T(8,128)(2,1)}, bf16[96,128]{1,0:T(8,128)(2,1)S(1)}, u32[]{:S(2)}, u32[]{:S(2)}) %collective-permute-start.3) | collective-permute-done | bytes 24608 | tf_op jit(solution)/shard_map/ppermute | solution.py:241
  26.7 4.2 %collective-permute-start.8 = (bf16[304,1536]{1,0:T(8,128)(2,1)}, bf16[304,1536]{1,0:T(8,128)(2,1)S(1)}, u32[]{:S(2)}, u32[]{:S(2)}) collective-permute-start(bf16[304,1536]{1,0:T(8,128)(2,1)} %get-tuple-element.27.a0_ref), channel_id=1, source_target_pairs={{0,64},{64,128},{128,192},{192,0},{1,65},{65,129},{129,193},{193,1... | collective-permute-start | bytes 2801672 | tf_op jit(solution)/shard_map/ppermute | solution.py:31
  30.9 1.9 %collective-permute-start.10 = (bf16[288,1536]{1,0:T(8,128)(2,1)}, bf16[288,1536]{1,0:T(8,128)(2,1)}, u32[]{:S(2)}, u32[]{:S(2)}) collective-permute-start(bf16[288,1536]{1,0:T(8,128)(2,1)} %get-tuple-element.28.b0_ref), channel_id=1, source_target_pairs={{0,192},{64,0},{128,64},{192,128},{1,193},{65,1},{129,65},{193,129... | collective-permute-start | bytes 2654216 | tf_op jit(solution)/shard_map/ppermute | solution.py:31
  34.8 4.9 %collective-permute-start.4 = (bf16[4,1,64,128]{3,2,1,0:T(8,128)(2,1)}, bf16[4,1,64,128]{3,2,1,0:T(8,128)(2,1)S(1)}, u32[]{:S(2)}, u32[]{:S(2)}) collective-permute-start(bf16[4,1,64,128]{3,2,1,0:T(8,128)(2,1)} %get-tuple-element.39), channel_id=1, source_target_pairs={{0,1},{1,2},{2,3},{3,4},{4,5},{5,6},{6,7},{7,8},{8,9},{9,10},{10,1... | collective-permute-start | bytes 196616 | tf_op jit(solution)/shard_map/ppermute | solution.py:27
  39.9 1.9 %collective-permute-start.6 = (bf16[304,1536]{1,0:T(8,128)(2,1)}, bf16[304,1536]{1,0:T(8,128)(2,1)S(1)}, u32[]{:S(2)}, u32[]{:S(2)}) collective-permute-start(bf16[304,1536]{1,0:T(8,128)(2,1)} %get-tuple-element.27.a0_ref), channel_id=1, source_target_pairs={{0,192},{64,0},{128,64},{192,128},{1,193},{65,1},{129,65},{193,129... | collective-permute-start | bytes 2801672 | tf_op jit(solution)/shard_map/ppermute | solution.py:31
  41.9 5.1 %collective-permute-start.7 = (bf16[288,1536]{1,0:T(8,128)(2,1)}, bf16[288,1536]{1,0:T(8,128)(2,1)}, u32[]{:S(2)}, u32[]{:S(2)}) collective-permute-start(bf16[288,1536]{1,0:T(8,128)(2,1)} %get-tuple-element.28.b0_ref), channel_id=1, source_target_pairs={{0,64},{64,128},{128,192},{192,0},{1,65},{65,129},{129,193},{193,1... | collective-permute-start | bytes 2654216 | tf_op jit(solution)/shard_map/ppermute | solution.py:31
  47.1 1.9 %shard_map.101 = (bf16[128,1664]{1,0:T(8,128)(2,1)S(1)}, bf16[64,128]{1,0:T(8,128)(2,1)S(1)}) custom-call(bf16[4,6,64,128]{3,2,1,0:T(8,128)(2,1)S(1)} %pad_maximum_fusion.tall_ref, bf16[3,3,384,128]{3,2,1,0:T(8,128)(2,1)S(1)} %bitcast.16, bf16[128,128]{1,0:T(8,128)(2,1)S(1)} %copy.13.latent_ref, bf16[64,1536]{1,0:T(8,128)(2,1)S(1)} %copy-done.4, ...), custom_call_target="tpu_custom_call" | custom-call | tf_op jit(solution)/shard_map/pallas_call | solution.py:267
  49.9 13.3 %all-to-all-start = ((bf16[64,2,1664]{2,1,0:T(2,128)(2,1)}), bf16[64,2,1664]{2,1,0:T(2,128)(2,1)S(1)}, u32[]{:S(2)}, u32[]{:S(2)}) async-start(bf16[64,2,1664]{2,1,0:T(2,128)(2,1)} %reshape.20), calls=%async_computation | async-start | bytes 851968 | tf_op jit(solution)/shard_map/all_to_all | solution.py:276
  63.2 3.7 %collective-permute-start.11 = (bf16[304,1536]{1,0:T(8,128)(2,1)S(1)}, bf16[304,1536]{1,0:T(8,128)(2,1)}, u32[]{:S(2)}, u32[]{:S(2)}) collective-permute-start(bf16[304,1536]{1,0:T(8,128)(2,1)S(1)} %collective-permute-done.8.a1_ref), channel_id=1, source_target_pairs={{0,64},{64,128},{128,192},{192,0},{1,65},{65,129},{129,193},{193,1... | collective-permute-start | bytes 2801672 | tf_op jit(solution)/shard_map/ppermute | solution.py:31
  66.9 2.1 %collective-permute-start.12 = (bf16[288,1536]{1,0:T(8,128)(2,1)}, bf16[288,1536]{1,0:T(8,128)(2,1)}, u32[]{:S(2)}, u32[]{:S(2)}) collective-permute-start(bf16[288,1536]{1,0:T(8,128)(2,1)} %collective-permute-done.10.b2_ref), channel_id=1, source_target_pairs={{0,192},{64,0},{128,64},{192,128},{1,193},{65,1},{129,65},{193,129... | collective-permute-start | bytes 2654216 | tf_op jit(solution)/shard_map/ppermute | solution.py:31
  69.1 2.3 %collective-permute-done.7.b1_ref = bf16[288,1536]{1,0:T(8,128)(2,1)} collective-permute-done((bf16[288,1536]{1,0:T(8,128)(2,1)}, bf16[288,1536]{1,0:T(8,128)(2,1)}, u32[]{:S(2)}, u32[]{:S(2)}) %collective-permute-start.7) | collective-permute-done | bytes 884768 | tf_op jit(solution)/shard_map/ppermute | solution.py:31
  71.4 9.4 %all-to-all-done = bf16[64,2,1664]{2,1,0:T(2,128)(2,1)S(1)} async-done(((bf16[64,2,1664]{2,1,0:T(2,128)(2,1)}), bf16[64,2,1664]{2,1,0:T(2,128)(2,1)S(1)}, u32[]{:S(2)}, u32[]{:S(2)}) %all-to-all-start) | async-done | bytes 426016 | tf_op jit(solution)/shard_map/all_to_all | solution.py:276
  83.0 1.9 %collective-permute-start.9 = (bf16[192,1664]{1,0:T(8,128)(2,1)S(1)}, bf16[192,1664]{1,0:T(8,128)(2,1)}, u32[]{:S(2)}, u32[]{:S(2)}) collective-permute-start(bf16[192,1664]{1,0:T(8,128)(2,1)S(1)} %shard_map.102.mine_ref), channel_id=1, source_target_pairs={{0,32},{32,0},{1,33},{33,1},{2,34},{34,2},{3,35},{35,3},{4,36},{36... | collective-permute-start | bytes 1916936 | tf_op jit(solution)/shard_map/ppermute | solution.py:286
  85.0 2.1 %collective-permute-done.9.theirs_ref = bf16[192,1664]{1,0:T(8,128)(2,1)} collective-permute-done((bf16[192,1664]{1,0:T(8,128)(2,1)S(1)}, bf16[192,1664]{1,0:T(8,128)(2,1)}, u32[]{:S(2)}, u32[]{:S(2)}) %collective-permute-start.9) | collective-permute-done | bytes 639008 | tf_op jit(solution)/shard_map/ppermute | solution.py:286
  88.3 5.4 %shard_map.103 = (bf16[256,1536]{1,0:T(8,128)(2,1)S(1)}, f32[256,1]{1,0:T(8,128)S(1)}, f32[256,1536]{1,0:T(8,128)S(1)}) custom-call(s32[3]{0:T(128)S(1)} %pad_add_fusion.at_ref, bf16[192,1664]{1,0:T(8,128)(2,1)S(1)} %shard_map.102.mine_ref, bf16[192,1664]{1,0:T(8,128)(2,1)} %collective-permute-done.9.theirs_ref, bf16[2,1536]{1,0:T(2,128)(2,1)S(1)} %bitcast.17, ...), custom_call_target="tpu_custom_call" | custom-call | tf_op jit(solution)/shard_map/pallas_call | solution.py:288
  94.6 2.4 %shard_map.104 = (bf16[128,1536]{1,0:T(8,128)(2,1)S(1)}, bf16[128,1536]{1,0:T(8,128)(2,1)S(1)}) custom-call(bf16[256,1536]{1,0:T(8,128)(2,1)S(1)} %get-tuple-element.34.tokens_ref, f32[256,1]{1,0:T(8,128)S(1)} %get-tuple-element.35.score_ref, f32[256,1536]{1,0:T(8,128)S(1)} %get-tuple-element.36.total_ref, bf16[304,1536]{1,0:T(8,128)(2,1)} %collective-permute-done.11.w0_ref, ...), custom_call_target="tpu_custom_call" | custom-call | tf_op jit(solution)/shard_map/pallas_call | solution.py:304
  97.0 1.9 %collective-permute-start.13 = (bf16[128,1536]{1,0:T(8,128)(2,1)S(1)}, bf16[128,1536]{1,0:T(8,128)(2,1)S(1)}, u32[]{:S(2)}, u32[]{:S(2)}) collective-permute-start(bf16[128,1536]{1,0:T(8,128)(2,1)S(1)} %get-tuple-element.37), channel_id=1, source_target_pairs={{0,32},{32,0},{1,33},{33,1},{2,34},{34,2},{3,35},{35,3},{4,36},{36... | collective-permute-start | bytes 1179656 | tf_op jit(solution)/shard_map/ppermute | solution.py:312
  98.9 1.7 %collective-permute-done.13 = bf16[128,1536]{1,0:T(8,128)(2,1)S(1)} collective-permute-done((bf16[128,1536]{1,0:T(8,128)(2,1)S(1)}, bf16[128,1536]{1,0:T(8,128)(2,1)S(1)}, u32[]{:S(2)}, u32[]{:S(2)}) %collective-permute-start.13) | collective-permute-done | bytes 393248 | tf_op jit(solution)/shard_map/ppermute | solution.py:312
  100.8 28.5 %all_to_all.10 = bf16[64,2,1536]{2,1,0:T(2,128)(2,1)S(1)} all-to-all(bf16[64,2,1536]{2,1,0:T(2,128)(2,1)S(1)} %reshape.22), channel_id=1, replica_groups=mesh['yh'=2,'x'=4,'c'=2,'yl'=4,'z'=8] {'yh','yl','z'}, dimensions={0} | all-to-all | bytes 786432 | tf_op jit(solution)/shard_map/all_to_all | solution.py:314
  (46 shorter events, 10.3 us)
Async XLA Ops:
  0.0 26.6 %copy-start.6 = (bf16[2,4,64,128]{3,2,1,0:T(8,128)(2,1)S(1)}, bf16[2,4,64,128]{3,2,1,0:T(8,128)(2,1)}, u32[]{:S(2)}) copy-start(bf16[2,4,64,128]{3,2,1,0:T(8,128)(2,1)} %param.10) | copy-start | bytes 393220
  0.0 39.7 %copy-start.8 = (bf16[128,16]{0,1:T(8,128)(2,1)S(1)}, bf16[128,16]{0,1:T(8,128)(2,1)}, u32[]{:S(2)}) copy-start(bf16[128,16]{0,1:T(8,128)(2,1)} %param.12) | copy-start | bytes 12292
  0.0 39.8 %copy-start.9 = (s32[64,2]{0,1:T(2,128)S(1)}, s32[64,2]{0,1:T(2,128)}, u32[]{:S(2)}) copy-start(s32[64,2]{0,1:T(2,128)} %param.19) | copy-start | bytes 1540
  0.0 25.7 %collective-permute-start.1 = (bf16[2,4,64,128]{3,2,1,0:T(8,128)(2,1)}, bf16[2,4,64,128]{3,2,1,0:T(8,128)(2,1)}, u32[]{:S(2)}, u32[]{:S(2)}) collective-permute-start(bf16[2,4,64,128]{3,2,1,0:T(8,128)(2,1)} %param.10), channel_id=1, source_target_pairs={{0,32},{32,64},{64,96},{96,128},{128,160},{160,192},{192,224},{224... | collective-permute-start | bytes 393224 | tf_op jit(solution)/shard_map/ppermute | solution.py:27
  2.1 14.7 %collective-permute-start = (bf16[96,128]{1,0:T(8,128)(2,1)}, bf16[96,128]{1,0:T(8,128)(2,1)S(1)}, u32[]{:S(2)}, u32[]{:S(2)}) collective-permute-start(bf16[96,128]{1,0:T(8,128)(2,1)} %bitcast.22), channel_id=1, source_target_pairs={{0,256},{256,0},{1,257},{257,1},{2,258},{258,2},{3,259},{259,3},{4... | collective-permute-start | bytes 73736 | tf_op jit(solution)/shard_map/ppermute | solution.py:239
  9.8 11.0 %collective-permute-start.2 = (bf16[96,128]{1,0:T(8,128)(2,1)}, bf16[96,128]{1,0:T(8,128)(2,1)S(1)}, u32[]{:S(2)}, u32[]{:S(2)}) collective-permute-start(bf16[96,128]{1,0:T(8,128)(2,1)} %bitcast.23), channel_id=1, source_target_pairs={{0,128},{64,192},{128,0},{192,64},{1,129},{65,193},{129,1},{193,65... | collective-permute-start | bytes 73736 | tf_op jit(solution)/shard_map/ppermute | solution.py:31
  13.1 12.6 %collective-permute-start.3 = (bf16[96,128]{1,0:T(8,128)(2,1)}, bf16[96,128]{1,0:T(8,128)(2,1)S(1)}, u32[]{:S(2)}, u32[]{:S(2)}) collective-permute-start(bf16[96,128]{1,0:T(8,128)(2,1)} %bitcast.24), channel_id=1, source_target_pairs={{0,384},{64,448},{128,256},{192,320},{256,128},{320,192},{384,0},{... | collective-permute-start | bytes 73736 | tf_op jit(solution)/shard_map/ppermute | solution.py:241
  17.3 29.7 %copy-start.4 = (bf16[64,1536]{1,0:T(8,128)(2,1)S(1)}, bf16[64,1536]{1,0:T(8,128)(2,1)}, u32[]{:S(2)}) copy-start(bf16[64,1536]{1,0:T(8,128)(2,1)} %context_ref.1) | copy-start | bytes 589828
  20.8 26.2 %copy-start.2 = (bf16[3,3,3,128,128]{4,3,2,1,0:T(8,128)(2,1)S(1)}, bf16[3,3,3,128,128]{4,3,2,1,0:T(8,128)(2,1)}, u32[]{:S(2)}) copy-start(bf16[3,3,3,128,128]{4,3,2,1,0:T(8,128)(2,1)} %param.11) | copy-start | bytes 2654212
  26.7 36.5 %collective-permute-start.8 = (bf16[304,1536]{1,0:T(8,128)(2,1)}, bf16[304,1536]{1,0:T(8,128)(2,1)S(1)}, u32[]{:S(2)}, u32[]{:S(2)}) collective-permute-start(bf16[304,1536]{1,0:T(8,128)(2,1)} %get-tuple-element.27.a0_ref), channel_id=1, source_target_pairs={{0,64},{64,128},{128,192},{192,0},{1,65},{65,129},{129,193},{193,1... | collective-permute-start | bytes 2801672 | tf_op jit(solution)/shard_map/ppermute | solution.py:31
  30.9 36.1 %collective-permute-start.10 = (bf16[288,1536]{1,0:T(8,128)(2,1)}, bf16[288,1536]{1,0:T(8,128)(2,1)}, u32[]{:S(2)}, u32[]{:S(2)}) collective-permute-start(bf16[288,1536]{1,0:T(8,128)(2,1)} %get-tuple-element.28.b0_ref), channel_id=1, source_target_pairs={{0,192},{64,0},{128,64},{192,128},{1,193},{65,1},{129,65},{193,129... | collective-permute-start | bytes 2654216 | tf_op jit(solution)/shard_map/ppermute | solution.py:31
  33.5 8.4 %collective-permute-start.5 = (bf16[4,1,64,128]{3,2,1,0:T(8,128)(2,1)}, bf16[4,1,64,128]{3,2,1,0:T(8,128)(2,1)S(1)}, u32[]{:S(2)}, u32[]{:S(2)}) collective-permute-start(bf16[4,1,64,128]{3,2,1,0:T(8,128)(2,1)} %get-tuple-element.40), channel_id=1, source_target_pairs={{1,0},{2,1},{3,2},{4,3},{5,4},{6,5},{7,6},{8,7},{9,8},{10,9},{11,1... | collective-permute-start | bytes 196616 | tf_op jit(solution)/shard_map/ppermute | solution.py:27
  34.8 12.2 %collective-permute-start.4 = (bf16[4,1,64,128]{3,2,1,0:T(8,128)(2,1)}, bf16[4,1,64,128]{3,2,1,0:T(8,128)(2,1)S(1)}, u32[]{:S(2)}, u32[]{:S(2)}) collective-permute-start(bf16[4,1,64,128]{3,2,1,0:T(8,128)(2,1)} %get-tuple-element.39), channel_id=1, source_target_pairs={{0,1},{1,2},{2,3},{3,4},{4,5},{5,6},{6,7},{7,8},{8,9},{9,10},{10,1... | collective-permute-start | bytes 196616 | tf_op jit(solution)/shard_map/ppermute | solution.py:27
  39.9 40.9 %collective-permute-start.6 = (bf16[304,1536]{1,0:T(8,128)(2,1)}, bf16[304,1536]{1,0:T(8,128)(2,1)S(1)}, u32[]{:S(2)}, u32[]{:S(2)}) collective-permute-start(bf16[304,1536]{1,0:T(8,128)(2,1)} %get-tuple-element.27.a0_ref), channel_id=1, source_target_pairs={{0,192},{64,0},{128,64},{192,128},{1,193},{65,1},{129,65},{193,129... | collective-permute-start | bytes 2801672 | tf_op jit(solution)/shard_map/ppermute | solution.py:31
  41.9 29.5 %collective-permute-start.7 = (bf16[288,1536]{1,0:T(8,128)(2,1)}, bf16[288,1536]{1,0:T(8,128)(2,1)}, u32[]{:S(2)}, u32[]{:S(2)}) collective-permute-start(bf16[288,1536]{1,0:T(8,128)(2,1)} %get-tuple-element.28.b0_ref), channel_id=1, source_target_pairs={{0,64},{64,128},{128,192},{192,0},{1,65},{65,129},{129,193},{193,1... | collective-permute-start | bytes 2654216 | tf_op jit(solution)/shard_map/ppermute | solution.py:31
  49.0 32.8 %copy-start = (bf16[304,1536]{1,0:T(8,128)(2,1)S(1)}, bf16[304,1536]{1,0:T(8,128)(2,1)}, u32[]{:S(2)}) copy-start(bf16[304,1536]{1,0:T(8,128)(2,1)} %get-tuple-element.27.a0_ref) | copy-start | bytes 2801668
  49.9 30.9 %all-to-all-start = ((bf16[64,2,1664]{2,1,0:T(2,128)(2,1)}), bf16[64,2,1664]{2,1,0:T(2,128)(2,1)S(1)}, u32[]{:S(2)}, u32[]{:S(2)}) async-start(bf16[64,2,1664]{2,1,0:T(2,128)(2,1)} %reshape.20), calls=%async_computation | async-start | bytes 851968 | tf_op jit(solution)/shard_map/all_to_all | solution.py:276
  63.2 31.3 %collective-permute-start.11 = (bf16[304,1536]{1,0:T(8,128)(2,1)S(1)}, bf16[304,1536]{1,0:T(8,128)(2,1)}, u32[]{:S(2)}, u32[]{:S(2)}) collective-permute-start(bf16[304,1536]{1,0:T(8,128)(2,1)S(1)} %collective-permute-done.8.a1_ref), channel_id=1, source_target_pairs={{0,64},{64,128},{128,192},{192,0},{1,65},{65,129},{129,193},{193,1... | collective-permute-start | bytes 2801672 | tf_op jit(solution)/shard_map/ppermute | solution.py:31
  66.9 27.6 %collective-permute-start.12 = (bf16[288,1536]{1,0:T(8,128)(2,1)}, bf16[288,1536]{1,0:T(8,128)(2,1)}, u32[]{:S(2)}, u32[]{:S(2)}) collective-permute-start(bf16[288,1536]{1,0:T(8,128)(2,1)} %collective-permute-done.10.b2_ref), channel_id=1, source_target_pairs={{0,192},{64,0},{128,64},{192,128},{1,193},{65,1},{129,65},{193,129... | collective-permute-start | bytes 2654216 | tf_op jit(solution)/shard_map/ppermute | solution.py:31
  81.7 1.0 copy-start.1
  82.7 4.4 %copy-start.5 = (bf16[2,1536,1]{1,0,2:T(2,128)(2,1)S(1)}, bf16[2,1536,1]{1,0,2:T(2,128)(2,1)}, u32[]{:S(2)}) copy-start(bf16[2,1536,1]{1,0,2:T(2,128)(2,1)} %param.15) | copy-start | bytes 18436
  83.0 4.1 %collective-permute-start.9 = (bf16[192,1664]{1,0:T(8,128)(2,1)S(1)}, bf16[192,1664]{1,0:T(8,128)(2,1)}, u32[]{:S(2)}, u32[]{:S(2)}) collective-permute-start(bf16[192,1664]{1,0:T(8,128)(2,1)S(1)} %shard_map.102.mine_ref), channel_id=1, source_target_pairs={{0,32},{32,0},{1,33},{33,1},{2,34},{34,2},{3,35},{35,3},{4,36},{36... | collective-permute-start | bytes 1916936 | tf_op jit(solution)/shard_map/ppermute | solution.py:286
  87.1 1.2 copy-start.3
  97.0 3.6 %collective-permute-start.13 = (bf16[128,1536]{1,0:T(8,128)(2,1)S(1)}, bf16[128,1536]{1,0:T(8,128)(2,1)S(1)}, u32[]{:S(2)}, u32[]{:S(2)}) collective-permute-start(bf16[128,1536]{1,0:T(8,128)(2,1)S(1)} %get-tuple-element.37), channel_id=1, source_target_pairs={{0,32},{32,0},{1,33},{33,1},{2,34},{34,2},{3,35},{35,3},{4,36},{36... | collective-permute-start | bytes 1179656 | tf_op jit(solution)/shard_map/ppermute | solution.py:312
  (1 other events, 0.6 us)

commit v9 on v8

--- a/solution.py
+++ b/solution.py
@@ -15,6 +15,8 @@
 SWAP = [(0, 1), (1, 0)]
 VMEM_BYTES = 16 * 1024 * 1024
 PACK_BYTES = 66_400_000
+SWAP_BYTES = 65_600_000
+NEAR_BYTES = 62_500_000
 
 
 def dot(a, b, dims=((1,), (0,))):
@@ -44,29 +46,39 @@
             lane += 128
 
 
-def pack_kernel(
-    gate_ref, up_ref, down_ref, own_ref, other_ref, first_ref, second_ref, first_held, second_held, sems
-):
+def pack_kernel(gate_ref, up_ref, down_ref, own_ref, other_ref, out_ref, embed_ref, held_ref, sems):
     share = down_ref.shape[0]
-    half, part = share // 2, 3 * share // 2
-    copies = [
-        pltpu.make_async_copy(gate_ref, first_held.at[pl.ds(0, share)], sems.at[0]),
-        pltpu.make_async_copy(up_ref.at[pl.ds(0, half)], first_held.at[pl.ds(share, half)], sems.at[1]),
-        pltpu.make_async_copy(up_ref.at[pl.ds(half, half)], second_held.at[pl.ds(0, half)], sems.at[2]),
-        pltpu.make_async_copy(down_ref, second_held.at[pl.ds(half, share)], sems.at[3]),
-    ]
-    for copy in copies:
-        copy.start()
-    lay_beside(first_held, part, own_ref, other_ref)
-    for copy in copies:
-        copy.wait()
-    copies = [
-        pltpu.make_async_copy(first_held, first_ref, sems.at[4]),
-        pltpu.make_async_copy(second_held, second_ref, sems.at[5]),
-    ]
-    for copy in copies:
-        copy.start()
-    for copy in copies:
+    copies = [
+        pltpu.make_async_copy(ref, held_ref.at[pl.ds(i * share, share)], sems.at[i])
+        for i, ref in enumerate((gate_ref, up_ref, down_ref))
+    ]
+    for copy in copies:
+        copy.start()
+    lay_beside(embed_ref, 0, own_ref, other_ref)
+    held_ref[3 * share :] = embed_ref[...]
+    for copy in copies:
+        copy.wait()
+    copy = pltpu.make_async_copy(held_ref, out_ref, sems.at[3])
+    copy.start()
+    copy.wait()
+
+
+def halves_kernel(behind_ref, ahead_ref, first_ref, second_ref, first_held, second_held, sems):
+    part = first_ref.shape[0]
+    copies = [
+        pltpu.make_async_copy(behind_ref.at[pl.ds(0, part)], first_held, sems.at[0]),
+        pltpu.make_async_copy(ahead_ref.at[pl.ds(part, part)], second_held, sems.at[1]),
+    ]
+    back = [
+        pltpu.make_async_copy(first_held, first_ref, sems.at[2]),
+        pltpu.make_async_copy(second_held, second_ref, sems.at[3]),
+    ]
+    for copy in copies:
+        copy.start()
+    for copy, then in zip(copies, back):
+        copy.wait()
+        then.start()
+    for copy in back:
         copy.wait()
 
 
@@ -113,7 +125,7 @@
     out_ref[:, width:] = dot(table, patches, ((0,), (0,))).astype(BF)
 
 
-def swap_kernel(rows_ref, own_ref, other_ref, a0_ref, a1_ref, a2_ref, out_ref, held_ref, sems):
+def swap_kernel(rows_ref, embed_ref, a0_ref, a1_ref, a2_ref, out_ref, held_ref, sems):
     slots, (_, tall, width) = rows_ref.shape[0], held_ref.shape
     part = a0_ref.shape[0] - tall
     copies = [
@@ -124,7 +136,7 @@
         copy.start()
     out_ref[:slots] = rows_ref[...]
     out_ref[slots:, width:] = jnp.zeros((out_ref.shape[0] - slots, out_ref.shape[1] - width), BF)
-    lay_beside(out_ref, slots + 3 * tall, own_ref, other_ref)
+    out_ref[slots + 3 * tall :, :width] = embed_ref[...]
     for i, copy in enumerate(copies):
         copy.wait()
         out_ref[slots + i * tall : slots + (i + 1) * tall, :width] = held_ref[i]
@@ -135,12 +147,9 @@
     mine_ref,
     theirs_ref,
     router_ref,
-    a0_ref,
-    b0_ref,
-    a1_ref,
-    b1_ref,
-    a2_ref,
-    b2_ref,
+    w0_ref,
+    w1_ref,
+    w2_ref,
     tokens_ref,
     score_ref,
     total_ref,
@@ -150,11 +159,10 @@
 ):
     yh, x, c = at_ref[0], at_ref[1], at_ref[2]
     rows, width = tokens_ref.shape[0] // 2, total_ref.shape[1]
-    part = b0_ref.shape[0]
-    share = part * 2 // 3
-    copies = [
-        pltpu.make_async_copy(ref.at[pl.ds(0, part)], held_ref.at[i // 2, pl.ds(i % 2 * part, part)], sems.at[i])
-        for i, ref in enumerate((a0_ref, b0_ref, a1_ref, b1_ref, a2_ref, b2_ref))
+    share = held_ref.shape[1] // 3
+    copies = [
+        pltpu.make_async_copy(ref.at[pl.ds(0, 3 * share)], held_ref.at[i], sems.at[i])
+        for i, ref in enumerate((w0_ref, w1_ref, w2_ref))
     ]
     for copy in copies:
         copy.start()
@@ -178,9 +186,8 @@
         tokens_ref[at] = tokens
         score_ref[at] = 1.0 / (1.0 + jnp.exp(-logit))
     hidden = []
-    for i in range(3):
-        copies[2 * i].wait()
-        copies[2 * i + 1].wait()
+    for i, copy in enumerate(copies):
+        copy.wait()
         both = dot(tokens_ref[...], held_ref[i, : 2 * share], ((1,), (1,)))
         hidden.append((silu(both[:, :share]) * both[:, share:]).astype(BF))
     hidden = jnp.concatenate(hidden, axis=1)
@@ -192,9 +199,9 @@
 
 def last_kernel(tokens_ref, score_ref, total_ref, w0_ref, w1_ref, other_ref, own_ref, held_ref, sems):
     rows, width = other_ref.shape
-    part, share = w1_ref.shape[0], held_ref.shape[0] // 3
-    copies = [
-        pltpu.make_async_copy(ref.at[pl.ds(0, part)], held_ref.at[pl.ds(i * part, part)], sems.at[i])
+    part, share = w0_ref.shape[0], held_ref.shape[0] // 3
+    copies = [
+        pltpu.make_async_copy(ref, held_ref.at[pl.ds(i * part, part)], sems.at[i])
         for i, ref in enumerate((w0_ref, w1_ref))
     ]
     for copy in copies:
@@ -237,26 +244,29 @@
     past = shifted(video, FRAME, 1)
     shard = embed_weight.T
     paired = lax.ppermute(shard, "yh", SWAP)
-    opposite = ring(shard, 2)
-    crossed = lax.ppermute(shard, ("yh", "x"), [(i, (i + 4) % 8 // 4 * 4 + (i + 2) % 4) for i in range(8)])
     part = 3 * share // 2
     tall = 2 * shard.shape[0] * shard.shape[1] // width
-    first, second = pl.pallas_call(
+    held, embed = pl.pallas_call(
         pack_kernel,
-        out_shape=[jax.ShapeDtypeStruct((part + tall, width), BF), jax.ShapeDtypeStruct((part, width), BF)],
+        out_shape=[jax.ShapeDtypeStruct((3 * share + tall, width), BF), jax.ShapeDtypeStruct((tall, width), BF)],
         in_specs=[hbm] * 3 + [vmem] * 2,
-        out_specs=[hbm] * 2,
-        scratch_shapes=[
-            pltpu.VMEM((part + tall, width), BF),
-            pltpu.VMEM((part, width), BF),
-            pltpu.SemaphoreType.DMA((6,)),
-        ],
+        out_specs=[hbm, vmem],
+        scratch_shapes=[pltpu.VMEM((3 * share + tall, width), BF), pltpu.SemaphoreType.DMA((4,))],
         compiler_params=pltpu.CompilerParams(vmem_limit_bytes=PACK_BYTES),
     )(gate_weight[0].T, up_weight[0].T, down_weight[0], shard, paired)
-    first, second, past, opposite, crossed = lax.optimization_barrier((first, second, past, opposite, crossed))
-    first_behind, second_ahead = ring(first, -1), ring(second, 1)
-    first_ahead, second_behind = ring(first, 1), ring(second, -1)
-    first_opposite, second_opposite = ring(first_behind, -1), ring(second_ahead, 1)
+    held, embed, past = lax.optimization_barrier((held, embed, past))
+    behind, ahead = ring(held, -1), ring(held, 1)
+    opposite = ring(embed, 2)
+    first, second = pl.pallas_call(
+        halves_kernel,
+        out_shape=[jax.ShapeDtypeStruct((part, width), BF)] * 2,
+        in_specs=[hbm] * 2,
+        out_specs=[hbm] * 2,
+        scratch_shapes=[pltpu.VMEM((part, width), BF)] * 2 + [pltpu.SemaphoreType.DMA((4,))],
+        compiler_params=params,
+    )(behind, ahead)
+    first, second, opposite = lax.optimization_barrier((first, second, opposite))
+    first, second = ring(first, -1), ring(second, 1)
 
     stacked = jnp.concatenate([past, video], axis=0)
     above = shifted(stacked[:, rows - 1 :], EXPERT, 1)
@@ -274,15 +284,14 @@
     )(padded, conv_weight.reshape(3, 3, 3 * chans, chans), jnp.tile(latent_weight, (1, 8)), context, routes)
 
     arrived = lax.all_to_all(outgoing.reshape(experts, capacity, raw), SOURCES, split_axis=0, concat_axis=0, tiled=True)
-    arrived, first_ahead, second_behind = lax.optimization_barrier((arrived, first_ahead, second_behind))
     mine = pl.pallas_call(
         swap_kernel,
         out_shape=jax.ShapeDtypeStruct((slots + 4 * tall, raw), BF),
-        in_specs=[vmem] * 3 + [hbm] * 3,
+        in_specs=[vmem] * 2 + [hbm] * 3,
         out_specs=vmem,
         scratch_shapes=[pltpu.VMEM((3, tall, width), BF), pltpu.SemaphoreType.DMA((3,))],
-        compiler_params=params,
-    )(arrived.reshape(slots, raw), opposite, crossed, first, first_behind, first_ahead)
+        compiler_params=pltpu.CompilerParams(vmem_limit_bytes=SWAP_BYTES),
+    )(arrived.reshape(slots, raw), opposite, held, behind, ahead)
     theirs = lax.ppermute(mine, "c", SWAP)
     place = jnp.stack([lax.axis_index(axis) for axis in FRAME]).astype(jnp.int32)
     tokens, score, total = pl.pallas_call(
@@ -292,15 +301,15 @@
             jax.ShapeDtypeStruct((2 * slots, 1), F32),
             jax.ShapeDtypeStruct((2 * slots, width), F32),
         ],
-        in_specs=[smem] + [vmem] * 3 + [hbm] * 6,
+        in_specs=[smem] + [vmem] * 3 + [hbm] * 3,
         out_specs=[vmem] * 3,
         scratch_shapes=[
             pltpu.VMEM((3, 3 * share, width), BF),
             pltpu.VMEM((16, embed_weight.shape[1], 128), BF),
-            pltpu.SemaphoreType.DMA((6,)),
+            pltpu.SemaphoreType.DMA((3,)),
         ],
-        compiler_params=params,
-    )(place, mine, theirs, router_weight[:, :, 0], first, second, first_behind, second_behind, first_ahead, second_ahead)
+        compiler_params=pltpu.CompilerParams(vmem_limit_bytes=NEAR_BYTES),
+    )(place, mine, theirs, router_weight[:, :, 0], held, behind, ahead)
     other, own = pl.pallas_call(
         last_kernel,
         out_shape=[jax.ShapeDtypeStruct((slots, width), BF)] * 2,
@@ -308,7 +317,7 @@
         out_specs=[vmem] * 2,
         scratch_shapes=[pltpu.VMEM((3 * share, width), BF), pltpu.SemaphoreType.DMA((2,))],
         compiler_params=params,
-    )(tokens, score, total, first_opposite, second_opposite)
+    )(tokens, score, total, first, second)
     back = lax.ppermute(other, "c", SWAP)
     summed = (back.astype(F32) + own.astype(F32)).astype(BF).reshape(experts, capacity, width)
     homeward = lax.all_to_all(summed, SOURCES, split_axis=0, concat_axis=0, tiled=True)

time: 131 us -> 141 us (1.076)
  waiting for transfers between devices: 21.2 us -> 28.4 us
  Pallas kernels: 13.4 us -> 20.2 us
  starting transfers between devices: 59 us -> 52.4 us
  local copies, waits for them, and re-layouts: 6.75 us -> 8.22 us
    ppermute x7 -> x5, waiting for transfers between devices: 3.15 us -> 18.4 us  [ring(): return lax.ppermute(value, 'x', [(i, (i - step) % 4) for i in range(4)])]
    all_to_all x1, waiting for transfers between devices: 9.43 us -> 0.01 us  [local(): lax.all_to_all(outgoing.reshape(experts, capacity, raw), SOURCES, split_a...]
    ppermute x3, waiting for transfers between devices: 0.01 us -> 4.97 us  [shifted(): return lax.ppermute(value, axes, pairs)]
    ppermute x1 -> x0, waiting for transfers between devices: 4.85 us -> none  [local(): lax.ppermute(shard, ('yh', 'x'), [(i, (i + 4) % 8 // 4 * 4 + (i + 2) % 4)...]
    ppermute x1 -> x0, starting transfers between devices: 3.58 us -> none  [local(): lax.ppermute(shard, ('yh', 'x'), [(i, (i + 4) % 8 // 4 * 4 + (i + 2) % 4)...]
    ppermute x3, starting transfers between devices: 8.24 us -> 5 us  [shifted(): return lax.ppermute(value, axes, pairs)]
    pallas_call x1 -> x2, Pallas kernels: 3.48 us -> 6.55 us  [the longest x1 4.08 us: local(): pl.pallas_call(pack_kernel, out_shape=[jax.ShapeDtypeStruct((3 * share +...]
    ppermute x7 -> x5, starting transfers between devices: 22.3 us -> 19.4 us  [ring(): return lax.ppermute(value, 'x', [(i, (i - step) % 4) for i in range(4)])]
  transfers between devices with their start and end apart: 15 -> 12, of which waited for: 6 -> 9; matrix products, arithmetic and copies ran while one was open for 2% -> 3% of each run, Pallas kernels for 8% -> 13%
where the time goes in v9:
time: 141 us; the launch traced here: 140 us
  starting transfers between devices  52.4 us (37%)
  blocking collectives  29 us (21%)
  waiting for transfers between devices  28.4 us (20%)
  Pallas kernels  20.2 us (14%)
  local copies, waits for them, and re-layouts  8.22 us (6%)
    all_to_all x1, blocking collectives, local(): lax.all_to_all(summed, SOURCES, split_axis=0, concat_axis=0, tiled=True)  29 us
    ppermute x5, starting transfers between devices, ring(): return lax.ppermute(value, 'x', [(i, (i - step) % 4) for i in range(4)])  19.4 us
    ppermute x5, waiting for transfers between devices, ring(): return lax.ppermute(value, 'x', [(i, (i - step) % 4) for i in range(4)])  18.4 us
    all_to_all x1, starting transfers between devices, local(): lax.all_to_all(outgoing.reshape(experts, capacity, raw), SOURCES, split_a...  16 us
    ppermute x1, starting transfers between devices, local(): paired = lax.ppermute(shard, 'yh', SWAP)  7.73 us
    pallas_call x1, Pallas kernels, local(): pl.pallas_call(near_kernel, out_shape=[jax.ShapeDtypeStruct((2 * slots, w...  6.66 us
    unnamed x28, local copies, waits for them, and re-layouts  5.94 us
    ppermute x3, starting transfers between devices, shifted(): return lax.ppermute(value, axes, pairs)  5 us
  transfers between devices with their start and end apart: 12, of which 9 were waited for; matrix products, arithmetic and copies ran while one was open for 3% of the time, Pallas kernels for 13%

profile of v9, /device:TPU:6, one launch (start us, length us, event | category | flops | bytes accessed | tf_op | source)
XLA Modules:
  0.0 140.2 jit_solution(13045060007641375660)
XLA Ops:
  0.0 2.1 %collective-permute-start.1 = (bf16[2,4,64,128]{3,2,1,0:T(8,128)(2,1)}, bf16[2,4,64,128]{3,2,1,0:T(8,128)(2,1)}, u32[]{:S(2)}, u32[]{:S(2)}) collective-permute-start(bf16[2,4,64,128]{3,2,1,0:T(8,128)(2,1)} %param.10), channel_id=1, source_target_pairs={{0,32},{32,64},{64,96},{96,128},{128,160},{160,192},{192,224},{224... | collective-permute-start | bytes 393224 | tf_op jit(solution)/shard_map/ppermute | solution.py:29
  2.1 7.7 %collective-permute-start = (bf16[96,128]{1,0:T(8,128)(2,1)}, bf16[96,128]{1,0:T(8,128)(2,1)S(1)}, u32[]{:S(2)}, u32[]{:S(2)}) collective-permute-start(bf16[96,128]{1,0:T(8,128)(2,1)} %bitcast.21), channel_id=1, source_target_pairs={{0,256},{256,0},{1,257},{257,1},{2,258},{258,2},{3,259},{259,3},{4... | collective-permute-start | bytes 73736 | tf_op jit(solution)/shard_map/ppermute | solution.py:246
  9.8 2.1 %collective-permute-done.other_ref = bf16[96,128]{1,0:T(8,128)(2,1)S(1)} collective-permute-done((bf16[96,128]{1,0:T(8,128)(2,1)}, bf16[96,128]{1,0:T(8,128)(2,1)S(1)}, u32[]{:S(2)}, u32[]{:S(2)}) %collective-permute-start) | collective-permute-done | bytes 24608 | tf_op jit(solution)/shard_map/ppermute | solution.py:246
  12.5 4.1 %shard_map.100 = (bf16[592,1536]{1,0:T(8,128)(2,1)}, bf16[16,1536]{1,0:T(8,128)(2,1)}) custom-call(bf16[192,1536]{1,0:T(8,128)(2,1)} %bitcast.17, bf16[192,1536]{1,0:T(8,128)(2,1)} %bitcast.18, bf16[192,1536]{1,0:T(8,128)(2,1)} %bitcast.19, bf16[96,128]{1,0:T(8,128)(2,1)} %bitcast.22, bf16[96,128]{1,0:T(8,128)(2,1)} %copy-done.9), custom_call_target="tpu_custom_call" | custom-call | tf_op jit(solution)/shard_map/pallas_call | solution.py:249
  16.6 2.9 %collective-permute-start.5 = (bf16[592,1536]{1,0:T(8,128)(2,1)}, bf16[592,1536]{1,0:T(8,128)(2,1)S(1)}, u32[]{:S(2)}, u32[]{:S(2)}) collective-permute-start(bf16[592,1536]{1,0:T(8,128)(2,1)} %get-tuple-element.27.a0_ref.w0_ref), channel_id=1, source_target_pairs={{0,192},{64,0},{128,64},{192,128},{1,193},{65,1},{129,65},{193,129... | collective-permute-start | bytes 5455880 | tf_op jit(solution)/shard_map/ppermute | solution.py:33
  19.5 6.9 %collective-permute-start.4 = (bf16[592,1536]{1,0:T(8,128)(2,1)}, bf16[592,1536]{1,0:T(8,128)(2,1)}, u32[]{:S(2)}, u32[]{:S(2)}) collective-permute-start(bf16[592,1536]{1,0:T(8,128)(2,1)} %get-tuple-element.27.a0_ref.w0_ref), channel_id=1, source_target_pairs={{0,64},{64,128},{128,192},{192,0},{1,65},{65,129},{129,193},{193,1... | collective-permute-start | bytes 5455880 | tf_op jit(solution)/shard_map/ppermute | solution.py:33
  31.0 4.6 %collective-permute-done.3 = bf16[4,1,64,128]{3,2,1,0:T(8,128)(2,1)S(1)} collective-permute-done((bf16[4,1,64,128]{3,2,1,0:T(8,128)(2,1)S(1)}, bf16[4,1,64,128]{3,2,1,0:T(8,128)(2,1)S(1)}, u32[]{:S(2)}, u32[]{:S(2)}) %collective-permute-start.3) | collective-permute-done | bytes 65568 | tf_op jit(solution)/shard_map/ppermute | solution.py:29
  35.7 1.9 %shard_map.101 = (bf16[128,1664]{1,0:T(8,128)(2,1)S(1)}, bf16[64,128]{1,0:T(8,128)(2,1)S(1)}) custom-call(bf16[4,6,64,128]{3,2,1,0:T(8,128)(2,1)S(1)} %pad_maximum_fusion.tall_ref, bf16[3,3,384,128]{3,2,1,0:T(8,128)(2,1)S(1)} %bitcast.16, bf16[128,128]{1,0:T(8,128)(2,1)S(1)} %copy.13.latent_ref, bf16[64,1536]{1,0:T(8,128)(2,1)S(1)} %copy-done.4, ...), custom_call_target="tpu_custom_call" | custom-call | tf_op jit(solution)/shard_map/pallas_call | solution.py:277
  38.5 16.0 %all-to-all-start = ((bf16[64,2,1664]{2,1,0:T(2,128)(2,1)}), bf16[64,2,1664]{2,1,0:T(2,128)(2,1)S(1)}, u32[]{:S(2)}, u32[]{:S(2)}) async-start(bf16[64,2,1664]{2,1,0:T(2,128)(2,1)} %reshape.20), calls=%async_computation | async-start | bytes 851968 | tf_op jit(solution)/shard_map/all_to_all | solution.py:286
  54.6 2.1 %collective-permute-start.6 = (bf16[16,1536]{1,0:T(8,128)(2,1)S(1)}, bf16[16,1536]{1,0:T(8,128)(2,1)S(1)}, u32[]{:S(2)}, u32[]{:S(2)}) collective-permute-start(bf16[16,1536]{1,0:T(8,128)(2,1)S(1)} %copy-done.12), channel_id=1, source_target_pairs={{0,128},{64,192},{128,0},{192,64},{1,129},{65,193},{129,1},{193,65... | collective-permute-start | bytes 147464 | tf_op jit(solution)/shard_map/ppermute | solution.py:33
  56.7 8.5 %collective-permute-done.5.ahead_ref.a2_ref.w2_ref = bf16[592,1536]{1,0:T(8,128)(2,1)S(1)} collective-permute-done((bf16[592,1536]{1,0:T(8,128)(2,1)}, bf16[592,1536]{1,0:T(8,128)(2,1)S(1)}, u32[]{:S(2)}, u32[]{:S(2)}) %collective-permute-start.5) | collective-permute-done | bytes 1818656 | tf_op jit(solution)/shard_map/ppermute | solution.py:33
  65.2 1.9 %collective-permute-done.4.behind_ref.a1_ref.w1_ref = bf16[592,1536]{1,0:T(8,128)(2,1)} collective-permute-done((bf16[592,1536]{1,0:T(8,128)(2,1)}, bf16[592,1536]{1,0:T(8,128)(2,1)}, u32[]{:S(2)}, u32[]{:S(2)}) %collective-permute-start.4) | collective-permute-done | bytes 1818656 | tf_op jit(solution)/shard_map/ppermute | solution.py:33
  67.1 2.5 %shard_map.102 = (bf16[288,1536]{1,0:T(8,128)(2,1)}, bf16[288,1536]{1,0:T(8,128)(2,1)}) custom-call(bf16[592,1536]{1,0:T(8,128)(2,1)} %collective-permute-done.4.behind_ref.a1_ref.w1_ref, bf16[592,1536]{1,0:T(8,128)(2,1)S(1)} %collective-permute-done.5.ahead_ref.a2_ref.w2_ref), custom_call_target="tpu_custom_call" | custom-call | tf_op jit(solution)/shard_map/pallas_call | solution.py:260
  69.6 5.6 %collective-permute-start.8 = (bf16[288,1536]{1,0:T(8,128)(2,1)}, bf16[288,1536]{1,0:T(8,128)(2,1)S(1)}, u32[]{:S(2)}, u32[]{:S(2)}) collective-permute-start(bf16[288,1536]{1,0:T(8,128)(2,1)} %get-tuple-element.35), channel_id=1, source_target_pairs={{0,64},{64,128},{128,192},{192,0},{1,65},{65,129},{129,193},{193,1... | collective-permute-start | bytes 2654216 | tf_op jit(solution)/shard_map/ppermute | solution.py:33
  75.2 1.9 %collective-permute-start.9 = (bf16[288,1536]{1,0:T(8,128)(2,1)}, bf16[288,1536]{1,0:T(8,128)(2,1)}, u32[]{:S(2)}, u32[]{:S(2)}) collective-permute-start(bf16[288,1536]{1,0:T(8,128)(2,1)} %get-tuple-element.36), channel_id=1, source_target_pairs={{0,192},{64,0},{128,64},{192,128},{1,193},{65,1},{129,65},{193,129... | collective-permute-start | bytes 2654216 | tf_op jit(solution)/shard_map/ppermute | solution.py:33
  78.1 2.7 %shard_map.103.mine_ref = bf16[192,1664]{1,0:T(8,128)(2,1)} custom-call(bf16[128,1664]{1,0:T(8,128)(2,1)} %reshape.21.rows_ref, bf16[16,1536]{1,0:T(8,128)(2,1)} %copy-done.8, bf16[592,1536]{1,0:T(8,128)(2,1)} %get-tuple-element.27.a0_ref.w0_ref, bf16[592,1536]{1,0:T(8,128)(2,1)} %collective-permute-done.4.behind_ref.a1_ref.w1_ref, bf16[592,1536]{1,0:T(8,128)(2,1)} %copy-done), custom_call_target="tpu_custom_call" | custom-call | tf_op jit(solution)/shard_map/pallas_call | solution.py:287
  80.8 2.2 %collective-permute-start.7 = (bf16[192,1664]{1,0:T(8,128)(2,1)}, bf16[192,1664]{1,0:T(8,128)(2,1)S(1)}, u32[]{:S(2)}, u32[]{:S(2)}) collective-permute-start(bf16[192,1664]{1,0:T(8,128)(2,1)} %shard_map.103.mine_ref), channel_id=1, source_target_pairs={{0,32},{32,0},{1,33},{33,1},{2,34},{34,2},{3,35},{35,3},{4,36},{36... | collective-permute-start | bytes 1916936 | tf_op jit(solution)/shard_map/ppermute | solution.py:295
  85.8 6.7 %shard_map.104 = (bf16[256,1536]{1,0:T(8,128)(2,1)}, f32[256,1]{1,0:T(8,128)}, f32[256,1536]{1,0:T(8,128)}) custom-call(s32[3]{0:T(128)} %pad_add_fusion.at_ref, bf16[192,1664]{1,0:T(8,128)(2,1)} %shard_map.103.mine_ref, bf16[192,1664]{1,0:T(8,128)(2,1)} %copy-done.6, bf16[2,1536]{1,0:T(2,128)(2,1)} %bitcast.23, ...), custom_call_target="tpu_custom_call" | custom-call | tf_op jit(solution)/shard_map/pallas_call | solution.py:297
  92.5 2.7 %collective-permute-done.8.w0_ref = bf16[288,1536]{1,0:T(8,128)(2,1)S(1)} collective-permute-done((bf16[288,1536]{1,0:T(8,128)(2,1)}, bf16[288,1536]{1,0:T(8,128)(2,1)S(1)}, u32[]{:S(2)}, u32[]{:S(2)}) %collective-permute-start.8) | collective-permute-done | bytes 884768 | tf_op jit(solution)/shard_map/ppermute | solution.py:33
  95.2 5.3 %collective-permute-done.9.w1_ref = bf16[288,1536]{1,0:T(8,128)(2,1)} collective-permute-done((bf16[288,1536]{1,0:T(8,128)(2,1)}, bf16[288,1536]{1,0:T(8,128)(2,1)}, u32[]{:S(2)}, u32[]{:S(2)}) %collective-permute-start.9) | collective-permute-done | bytes 884768 | tf_op jit(solution)/shard_map/ppermute | solution.py:33
  104.0 2.3 %shard_map.105 = (bf16[128,1536]{1,0:T(8,128)(2,1)S(1)}, bf16[128,1536]{1,0:T(8,128)(2,1)S(1)}) custom-call(bf16[256,1536]{1,0:T(8,128)(2,1)S(1)} %copy-done.3, f32[256,1]{1,0:T(8,128)S(1)} %copy-done.5, f32[256,1536]{1,0:T(8,128)S(1)} %copy-done.1, bf16[288,1536]{1,0:T(8,128)(2,1)S(1)} %collective-permute-done.8.w0_ref, ...), custom_call_target="tpu_custom_call" | custom-call | tf_op jit(solution)/shard_map/pallas_call | solution.py:313
  106.3 1.9 %collective-permute-start.10 = (bf16[128,1536]{1,0:T(8,128)(2,1)S(1)}, bf16[128,1536]{1,0:T(8,128)(2,1)S(1)}, u32[]{:S(2)}, u32[]{:S(2)}) collective-permute-start(bf16[128,1536]{1,0:T(8,128)(2,1)S(1)} %get-tuple-element.37), channel_id=1, source_target_pairs={{0,32},{32,0},{1,33},{33,1},{2,34},{34,2},{3,35},{35,3},{4,36},{36... | collective-permute-start | bytes 1179656 | tf_op jit(solution)/shard_map/ppermute | solution.py:321
  108.2 1.7 %collective-permute-done.10 = bf16[128,1536]{1,0:T(8,128)(2,1)S(1)} collective-permute-done((bf16[128,1536]{1,0:T(8,128)(2,1)S(1)}, bf16[128,1536]{1,0:T(8,128)(2,1)S(1)}, u32[]{:S(2)}, u32[]{:S(2)}) %collective-permute-start.10) | collective-permute-done | bytes 393248 | tf_op jit(solution)/shard_map/ppermute | solution.py:321
  110.2 29.0 %all_to_all.10 = bf16[64,2,1536]{2,1,0:T(2,128)(2,1)S(1)} all-to-all(bf16[64,2,1536]{2,1,0:T(2,128)(2,1)S(1)} %reshape.22), channel_id=1, replica_groups=mesh['yh'=2,'x'=4,'c'=2,'yl'=4,'z'=8] {'yh','yl','z'}, dimensions={0} | all-to-all | bytes 786432 | tf_op jit(solution)/shard_map/all_to_all | solution.py:323
  (47 shorter events, 14.5 us)
Async XLA Ops:
  0.0 27.4 %copy-start.7 = (bf16[2,4,64,128]{3,2,1,0:T(8,128)(2,1)S(1)}, bf16[2,4,64,128]{3,2,1,0:T(8,128)(2,1)}, u32[]{:S(2)}) copy-start(bf16[2,4,64,128]{3,2,1,0:T(8,128)(2,1)} %param.10) | copy-start | bytes 393220
  0.0 30.4 %copy-start.10 = (bf16[128,16]{0,1:T(8,128)(2,1)S(1)}, bf16[128,16]{0,1:T(8,128)(2,1)}, u32[]{:S(2)}) copy-start(bf16[128,16]{0,1:T(8,128)(2,1)} %param.12) | copy-start | bytes 12292
  0.0 30.5 %copy-start.11 = (s32[64,2]{0,1:T(2,128)S(1)}, s32[64,2]{0,1:T(2,128)}, u32[]{:S(2)}) copy-start(s32[64,2]{0,1:T(2,128)} %param.19) | copy-start | bytes 1540
  0.0 35.7 %copy-start.4 = (bf16[64,1536]{1,0:T(8,128)(2,1)S(1)}, bf16[64,1536]{1,0:T(8,128)(2,1)}, u32[]{:S(2)}) copy-start(bf16[64,1536]{1,0:T(8,128)(2,1)} %context_ref.1) | copy-start | bytes 589828
  0.0 16.6 %collective-permute-start.1 = (bf16[2,4,64,128]{3,2,1,0:T(8,128)(2,1)}, bf16[2,4,64,128]{3,2,1,0:T(8,128)(2,1)}, u32[]{:S(2)}, u32[]{:S(2)}) collective-permute-start(bf16[2,4,64,128]{3,2,1,0:T(8,128)(2,1)} %param.10), channel_id=1, source_target_pairs={{0,32},{32,64},{64,96},{96,128},{128,160},{160,192},{192,224},{224... | collective-permute-start | bytes 393224 | tf_op jit(solution)/shard_map/ppermute | solution.py:29
  2.1 9.8 %collective-permute-start = (bf16[96,128]{1,0:T(8,128)(2,1)}, bf16[96,128]{1,0:T(8,128)(2,1)S(1)}, u32[]{:S(2)}, u32[]{:S(2)}) collective-permute-start(bf16[96,128]{1,0:T(8,128)(2,1)} %bitcast.21), channel_id=1, source_target_pairs={{0,256},{256,0},{1,257},{257,1},{2,258},{258,2},{3,259},{259,3},{4... | collective-permute-start | bytes 73736 | tf_op jit(solution)/shard_map/ppermute | solution.py:246
  16.6 19.1 %copy-start.2 = (bf16[3,3,3,128,128]{4,3,2,1,0:T(8,128)(2,1)S(1)}, bf16[3,3,3,128,128]{4,3,2,1,0:T(8,128)(2,1)}, u32[]{:S(2)}) copy-start(bf16[3,3,3,128,128]{4,3,2,1,0:T(8,128)(2,1)} %param.11) | copy-start | bytes 2654212
  16.6 48.5 %collective-permute-start.5 = (bf16[592,1536]{1,0:T(8,128)(2,1)}, bf16[592,1536]{1,0:T(8,128)(2,1)S(1)}, u32[]{:S(2)}, u32[]{:S(2)}) collective-permute-start(bf16[592,1536]{1,0:T(8,128)(2,1)} %get-tuple-element.27.a0_ref.w0_ref), channel_id=1, source_target_pairs={{0,192},{64,0},{128,64},{192,128},{1,193},{65,1},{129,65},{193,129... | collective-permute-start | bytes 5455880 | tf_op jit(solution)/shard_map/ppermute | solution.py:33
  19.5 47.6 %collective-permute-start.4 = (bf16[592,1536]{1,0:T(8,128)(2,1)}, bf16[592,1536]{1,0:T(8,128)(2,1)}, u32[]{:S(2)}, u32[]{:S(2)}) collective-permute-start(bf16[592,1536]{1,0:T(8,128)(2,1)} %get-tuple-element.27.a0_ref.w0_ref), channel_id=1, source_target_pairs={{0,64},{64,128},{128,192},{192,0},{1,65},{65,129},{129,193},{193,1... | collective-permute-start | bytes 5455880 | tf_op jit(solution)/shard_map/ppermute | solution.py:33
  27.4 3.5 %collective-permute-start.2 = (bf16[4,1,64,128]{3,2,1,0:T(8,128)(2,1)S(1)}, bf16[4,1,64,128]{3,2,1,0:T(8,128)(2,1)S(1)}, u32[]{:S(2)}, u32[]{:S(2)}) collective-permute-start(bf16[4,1,64,128]{3,2,1,0:T(8,128)(2,1)S(1)} %get-tuple-element.39), channel_id=1, source_target_pairs={{0,1},{1,2},{2,3},{3,4},{4,5},{5,6},{6,7},{7,8},{8,9},{9,10},{10,1... | collective-permute-start | bytes 196616 | tf_op jit(solution)/shard_map/ppermute | solution.py:29
  29.1 6.5 %collective-permute-start.3 = (bf16[4,1,64,128]{3,2,1,0:T(8,128)(2,1)S(1)}, bf16[4,1,64,128]{3,2,1,0:T(8,128)(2,1)S(1)}, u32[]{:S(2)}, u32[]{:S(2)}) collective-permute-start(bf16[4,1,64,128]{3,2,1,0:T(8,128)(2,1)S(1)} %get-tuple-element.40), channel_id=1, source_target_pairs={{1,0},{2,1},{3,2},{4,3},{5,4},{6,5},{7,6},{8,7},{9,8},{10,9},{11,1... | collective-permute-start | bytes 196616 | tf_op jit(solution)/shard_map/ppermute | solution.py:29
  35.7 18.9 %copy-start.12 = (bf16[16,1536]{1,0:T(8,128)(2,1)S(1)}, bf16[16,1536]{1,0:T(8,128)(2,1)}, u32[]{:S(2)}) copy-start(bf16[16,1536]{1,0:T(8,128)(2,1)} %get-tuple-element.30) | copy-start | bytes 147460
  38.5 38.6 %all-to-all-start = ((bf16[64,2,1664]{2,1,0:T(2,128)(2,1)}), bf16[64,2,1664]{2,1,0:T(2,128)(2,1)S(1)}, u32[]{:S(2)}, u32[]{:S(2)}) async-start(bf16[64,2,1664]{2,1,0:T(2,128)(2,1)} %reshape.20), calls=%async_computation | async-start | bytes 851968 | tf_op jit(solution)/shard_map/all_to_all | solution.py:286
  54.6 15.0 %collective-permute-start.6 = (bf16[16,1536]{1,0:T(8,128)(2,1)S(1)}, bf16[16,1536]{1,0:T(8,128)(2,1)S(1)}, u32[]{:S(2)}, u32[]{:S(2)}) collective-permute-start(bf16[16,1536]{1,0:T(8,128)(2,1)S(1)} %copy-done.12), channel_id=1, source_target_pairs={{0,128},{64,192},{128,0},{192,64},{1,129},{65,193},{129,1},{193,65... | collective-permute-start | bytes 147464 | tf_op jit(solution)/shard_map/ppermute | solution.py:33
  65.2 4.4 %copy-start = (bf16[592,1536]{1,0:T(8,128)(2,1)}, bf16[592,1536]{1,0:T(8,128)(2,1)S(1)}, u32[]{:S(2)}) copy-start(bf16[592,1536]{1,0:T(8,128)(2,1)S(1)} %collective-permute-done.5.ahead_ref.a2_ref.w2_ref) | copy-start | bytes 5455876
  69.6 8.5 %copy-start.8 = (bf16[16,1536]{1,0:T(8,128)(2,1)}, bf16[16,1536]{1,0:T(8,128)(2,1)S(1)}, u32[]{:S(2)}) copy-start(bf16[16,1536]{1,0:T(8,128)(2,1)S(1)} %collective-permute-done.6.embed_ref) | copy-start | bytes 147460
  69.6 25.6 %collective-permute-start.8 = (bf16[288,1536]{1,0:T(8,128)(2,1)}, bf16[288,1536]{1,0:T(8,128)(2,1)S(1)}, u32[]{:S(2)}, u32[]{:S(2)}) collective-permute-start(bf16[288,1536]{1,0:T(8,128)(2,1)} %get-tuple-element.35), channel_id=1, source_target_pairs={{0,64},{64,128},{128,192},{192,0},{1,65},{65,129},{129,193},{193,1... | collective-permute-start | bytes 2654216 | tf_op jit(solution)/shard_map/ppermute | solution.py:33
  75.2 25.3 %collective-permute-start.9 = (bf16[288,1536]{1,0:T(8,128)(2,1)}, bf16[288,1536]{1,0:T(8,128)(2,1)}, u32[]{:S(2)}, u32[]{:S(2)}) collective-permute-start(bf16[288,1536]{1,0:T(8,128)(2,1)} %get-tuple-element.36), channel_id=1, source_target_pairs={{0,192},{64,0},{128,64},{192,128},{1,193},{65,1},{129,65},{193,129... | collective-permute-start | bytes 2654216 | tf_op jit(solution)/shard_map/ppermute | solution.py:33
  80.8 4.2 %collective-permute-start.7 = (bf16[192,1664]{1,0:T(8,128)(2,1)}, bf16[192,1664]{1,0:T(8,128)(2,1)S(1)}, u32[]{:S(2)}, u32[]{:S(2)}) collective-permute-start(bf16[192,1664]{1,0:T(8,128)(2,1)} %shard_map.103.mine_ref), channel_id=1, source_target_pairs={{0,32},{32,0},{1,33},{33,1},{2,34},{34,2},{3,35},{35,3},{4,36},{36... | collective-permute-start | bytes 1916936 | tf_op jit(solution)/shard_map/ppermute | solution.py:295
  85.0 0.8 copy-start.6
  100.5 1.4 %copy-start.1 = (f32[256,1536]{1,0:T(8,128)S(1)}, f32[256,1536]{1,0:T(8,128)}, u32[]{:S(2)}) copy-start(f32[256,1536]{1,0:T(8,128)} %get-tuple-element.34.total_ref) | copy-start | bytes 4718596
  101.9 1.1 copy-start.3
  103.0 0.9 copy-start.5
  106.3 3.6 %collective-permute-start.10 = (bf16[128,1536]{1,0:T(8,128)(2,1)S(1)}, bf16[128,1536]{1,0:T(8,128)(2,1)S(1)}, u32[]{:S(2)}, u32[]{:S(2)}) collective-permute-start(bf16[128,1536]{1,0:T(8,128)(2,1)S(1)} %get-tuple-element.37), channel_id=1, source_target_pairs={{0,32},{32,0},{1,33},{33,1},{2,34},{34,2},{3,35},{35,3},{4,36},{36... | collective-permute-start | bytes 1179656 | tf_op jit(solution)/shard_map/ppermute | solution.py:321
  (1 other events, 0.6 us)

commit v10 on v8

--- a/solution.py
+++ b/solution.py
@@ -35,18 +35,14 @@
     return value / (1.0 + jnp.exp(-value))
 
 
-def lay_beside(out_ref, at, *refs):
-    tall = len(refs) * refs[0].shape[0] * 128 // 1536
-    lane = 0
-    for ref in refs:
-        for row in range(0, ref.shape[0], tall):
-            out_ref[at : at + tall, lane : lane + 128] = ref[row : row + tall]
-            lane += 128
-
-
-def pack_kernel(
-    gate_ref, up_ref, down_ref, own_ref, other_ref, first_ref, second_ref, first_held, second_held, sems
-):
+def lay_beside(out_ref, at, ref, lane=0):
+    tall = 16
+    for i in range(ref.shape[0] // tall):
+        lanes = slice(lane + i * 128, lane + (i + 1) * 128)
+        out_ref[at : at + tall, lanes] = ref[i * tall : (i + 1) * tall]
+
+
+def pack_kernel(gate_ref, up_ref, down_ref, shard_ref, first_ref, second_ref, first_held, second_held, sems):
     share = down_ref.shape[0]
     half, part = share // 2, 3 * share // 2
     copies = [
@@ -57,7 +53,9 @@
     ]
     for copy in copies:
         copy.start()
-    lay_beside(first_held, part, own_ref, other_ref)
+    tall, width = first_held.shape[0] - part, first_held.shape[1]
+    first_held[part:] = jnp.zeros((tall, width), BF)
+    lay_beside(first_held, part, shard_ref)
     for copy in copies:
         copy.wait()
     copies = [
@@ -68,6 +66,21 @@
         copy.start()
     for copy in copies:
         copy.wait()
+
+
+def shards_kernel(opposite_ref, a0_ref, a1_ref, a2_ref, out_ref, held_ref, sems):
+    tall, lanes = held_ref.shape[1], out_ref.shape[1]
+    part = a0_ref.shape[0] - tall
+    copies = [
+        pltpu.make_async_copy(ref.at[pl.ds(part, tall)], held_ref.at[i], sems.at[i])
+        for i, ref in enumerate((a0_ref, a1_ref, a2_ref))
+    ]
+    for copy in copies:
+        copy.start()
+    lay_beside(out_ref, 3 * tall, opposite_ref)
+    for i, copy in enumerate(copies):
+        copy.wait()
+        out_ref[i * tall : (i + 1) * tall] = held_ref[i, :, :lanes]
 
 
 def front_kernel(tall_ref, conv_ref, latent_ref, context_ref, routes_ref, out_ref, table_ref, wide_ref):
@@ -113,21 +126,12 @@
     out_ref[:, width:] = dot(table, patches, ((0,), (0,))).astype(BF)
 
 
-def swap_kernel(rows_ref, own_ref, other_ref, a0_ref, a1_ref, a2_ref, out_ref, held_ref, sems):
-    slots, (_, tall, width) = rows_ref.shape[0], held_ref.shape
-    part = a0_ref.shape[0] - tall
-    copies = [
-        pltpu.make_async_copy(ref.at[pl.ds(part, tall)], held_ref.at[i], sems.at[i])
-        for i, ref in enumerate((a0_ref, a1_ref, a2_ref))
-    ]
-    for copy in copies:
-        copy.start()
+def swap_kernel(rows_ref, near_ref, far_ref, out_ref):
+    slots, lanes = rows_ref.shape[0], near_ref.shape[1]
     out_ref[:slots] = rows_ref[...]
-    out_ref[slots:, width:] = jnp.zeros((out_ref.shape[0] - slots, out_ref.shape[1] - width), BF)
-    lay_beside(out_ref, slots + 3 * tall, own_ref, other_ref)
-    for i, copy in enumerate(copies):
-        copy.wait()
-        out_ref[slots + i * tall : slots + (i + 1) * tall, :width] = held_ref[i]
+    out_ref[slots:, :lanes] = near_ref[...]
+    out_ref[slots:, lanes : 2 * lanes] = far_ref[...]
+    out_ref[slots:, 2 * lanes :] = jnp.zeros((near_ref.shape[0], out_ref.shape[1] - 2 * lanes), BF)
 
 
 def near_kernel(
@@ -236,15 +240,11 @@
 
     past = shifted(video, FRAME, 1)
     shard = embed_weight.T
-    paired = lax.ppermute(shard, "yh", SWAP)
-    opposite = ring(shard, 2)
-    crossed = lax.ppermute(shard, ("yh", "x"), [(i, (i + 4) % 8 // 4 * 4 + (i + 2) % 4) for i in range(8)])
-    part = 3 * share // 2
-    tall = 2 * shard.shape[0] * shard.shape[1] // width
+    part, tall = 3 * share // 2, 16
     first, second = pl.pallas_call(
         pack_kernel,
         out_shape=[jax.ShapeDtypeStruct((part + tall, width), BF), jax.ShapeDtypeStruct((part, width), BF)],
-        in_specs=[hbm] * 3 + [vmem] * 2,
+        in_specs=[hbm] * 3 + [vmem],
         out_specs=[hbm] * 2,
         scratch_shapes=[
             pltpu.VMEM((part + tall, width), BF),
@@ -252,11 +252,12 @@
             pltpu.SemaphoreType.DMA((6,)),
         ],
         compiler_params=pltpu.CompilerParams(vmem_limit_bytes=PACK_BYTES),
-    )(gate_weight[0].T, up_weight[0].T, down_weight[0], shard, paired)
-    first, second, past, opposite, crossed = lax.optimization_barrier((first, second, past, opposite, crossed))
+    )(gate_weight[0].T, up_weight[0].T, down_weight[0], shard)
     first_behind, second_ahead = ring(first, -1), ring(second, 1)
     first_ahead, second_behind = ring(first, 1), ring(second, -1)
-    first_opposite, second_opposite = ring(first_behind, -1), ring(second_ahead, 1)
+    opposite = ring(shard, 2)
+    from_behind, from_ahead, opposite = lax.optimization_barrier((first_behind, second_ahead, opposite))
+    first_opposite, second_opposite = ring(from_behind, -1), ring(from_ahead, 1)
 
     stacked = jnp.concatenate([past, video], axis=0)
     above = shifted(stacked[:, rows - 1 :], EXPERT, 1)
@@ -274,15 +275,24 @@
     )(padded, conv_weight.reshape(3, 3, 3 * chans, chans), jnp.tile(latent_weight, (1, 8)), context, routes)
 
     arrived = lax.all_to_all(outgoing.reshape(experts, capacity, raw), SOURCES, split_axis=0, concat_axis=0, tiled=True)
-    arrived, first_ahead, second_behind = lax.optimization_barrier((arrived, first_ahead, second_behind))
+    lanes = shard.shape[0] // tall * 128
+    shards = pl.pallas_call(
+        shards_kernel,
+        out_shape=jax.ShapeDtypeStruct((4 * tall, lanes), BF),
+        in_specs=[vmem] + [hbm] * 3,
+        out_specs=vmem,
+        scratch_shapes=[pltpu.VMEM((3, tall, width), BF), pltpu.SemaphoreType.DMA((3,))],
+        compiler_params=params,
+    )(opposite, first, first_behind, first_ahead)
+    beyond = lax.ppermute(shards, "yh", SWAP)
+    arrived, beyond, second_behind = lax.optimization_barrier((arrived, beyond, second_behind))
     mine = pl.pallas_call(
         swap_kernel,
         out_shape=jax.ShapeDtypeStruct((slots + 4 * tall, raw), BF),
-        in_specs=[vmem] * 3 + [hbm] * 3,
+        in_specs=[vmem] * 3,
         out_specs=vmem,
-        scratch_shapes=[pltpu.VMEM((3, tall, width), BF), pltpu.SemaphoreType.DMA((3,))],
-        compiler_params=params,
-    )(arrived.reshape(slots, raw), opposite, crossed, first, first_behind, first_ahead)
+        compiler_params=params,
+    )(arrived.reshape(slots, raw), shards, beyond)
     theirs = lax.ppermute(mine, "c", SWAP)
     place = jnp.stack([lax.axis_index(axis) for axis in FRAME]).astype(jnp.int32)
     tokens, score, total = pl.pallas_call(

time: 131 us -> 131 us (level)
  the two profiles are of different devices: /device:TPU:6 before, /device:TPU:16 now
where the time goes in v10:
time: 131 us; the launch traced here: 130 us
  starting transfers between devices  59.6 us (45%)
  blocking collectives  32.3 us (25%)
  waiting for transfers between devices  14.3 us (11%)
  Pallas kernels  13.5 us (10%)
  local copies, waits for them, and re-layouts  9.36 us (7%)
    all_to_all x1, blocking collectives, local(): lax.all_to_all(summed, SOURCES, split_axis=0, concat_axis=0, tiled=True)  32.3 us
    ppermute x7, starting transfers between devices, ring(): return lax.ppermute(value, 'x', [(i, (i - step) % 4) for i in range(4)])  24.2 us
    ppermute x3, starting transfers between devices, shifted(): return lax.ppermute(value, axes, pairs)  14.6 us
    all_to_all x1, starting transfers between devices, local(): lax.all_to_all(outgoing.reshape(experts, capacity, raw), SOURCES, split_a...  10.7 us
    ppermute x1, waiting for transfers between devices, local(): beyond = lax.ppermute(shards, 'yh', SWAP)  6.46 us
    unnamed x22, local copies, waits for them, and re-layouts  6.36 us
    ppermute x1, starting transfers between devices, local(): beyond = lax.ppermute(shards, 'yh', SWAP)  6 us
    pallas_call x1, Pallas kernels, local(): pl.pallas_call(near_kernel, out_shape=[jax.ShapeDtypeStruct((2 * slots, w...  5.42 us
  transfers between devices with their start and end apart: 14, of which 4 were waited for; matrix products, arithmetic and copies ran while one was open for 3% of the time, Pallas kernels for 8%

profile of v10, /device:TPU:16, one launch (start us, length us, event | category | flops | bytes accessed | tf_op | source)
XLA Modules:
  0.0 130.4 jit_solution(4513450305458018557)
XLA Ops:
  0.0 1.9 %collective-permute-start = (bf16[2,4,64,128]{3,2,1,0:T(8,128)(2,1)}, bf16[2,4,64,128]{3,2,1,0:T(8,128)(2,1)S(1)}, u32[]{:S(2)}, u32[]{:S(2)}) collective-permute-start(bf16[2,4,64,128]{3,2,1,0:T(8,128)(2,1)} %param.10), channel_id=1, source_target_pairs={{0,32},{32,64},{64,96},{96,128},{128,160},{160,192},{192,224},{224... | collective-permute-start | bytes 393224 | tf_op jit(solution)/shard_map/ppermute | solution.py:27
  1.9 3.5 %shard_map.101 = (bf16[304,1536]{1,0:T(8,128)(2,1)}, bf16[288,1536]{1,0:T(8,128)(2,1)}) custom-call(bf16[192,1536]{1,0:T(8,128)(2,1)} %bitcast.18, bf16[192,1536]{1,0:T(8,128)(2,1)} %bitcast.19, bf16[192,1536]{1,0:T(8,128)(2,1)} %bitcast.20, bf16[96,128]{1,0:T(8,128)(2,1)} %bitcast.22), custom_call_target="tpu_custom_call" | custom-call | tf_op jit(solution)/shard_map/pallas_call | solution.py:244
  5.3 4.8 %collective-permute-start.6 = (bf16[304,1536]{1,0:T(8,128)(2,1)}, bf16[304,1536]{1,0:T(8,128)(2,1)S(1)}, u32[]{:S(2)}, u32[]{:S(2)}) collective-permute-start(bf16[304,1536]{1,0:T(8,128)(2,1)} %get-tuple-element.22.a0_ref), channel_id=1, source_target_pairs={{0,192},{64,0},{128,64},{192,128},{1,193},{65,1},{129,65},{193,129... | collective-permute-start | bytes 2801672 | tf_op jit(solution)/shard_map/ppermute | solution.py:31
  10.2 1.9 %collective-permute-start.3 = (bf16[304,1536]{1,0:T(8,128)(2,1)}, bf16[304,1536]{1,0:T(8,128)(2,1)S(1)}, u32[]{:S(2)}, u32[]{:S(2)}) collective-permute-start(bf16[304,1536]{1,0:T(8,128)(2,1)} %get-tuple-element.22.a0_ref), channel_id=1, source_target_pairs={{0,64},{64,128},{128,192},{192,0},{1,65},{65,129},{129,193},{193,1... | collective-permute-start | bytes 2801672 | tf_op jit(solution)/shard_map/ppermute | solution.py:31
  12.1 5.1 %collective-permute-start.4 = (bf16[288,1536]{1,0:T(8,128)(2,1)}, bf16[288,1536]{1,0:T(8,128)(2,1)}, u32[]{:S(2)}, u32[]{:S(2)}) collective-permute-start(bf16[288,1536]{1,0:T(8,128)(2,1)} %get-tuple-element.23.b0_ref), channel_id=1, source_target_pairs={{0,192},{64,0},{128,64},{192,128},{1,193},{65,1},{129,65},{193,129... | collective-permute-start | bytes 2654216 | tf_op jit(solution)/shard_map/ppermute | solution.py:31
  17.3 4.3 %collective-permute-start.1 = (bf16[4,1,64,128]{3,2,1,0:T(8,128)(2,1)S(1)}, bf16[4,1,64,128]{3,2,1,0:T(8,128)(2,1)S(1)}, u32[]{:S(2)}, u32[]{:S(2)}) collective-permute-start(bf16[4,1,64,128]{3,2,1,0:T(8,128)(2,1)S(1)} %get-tuple-element.35), channel_id=1, source_target_pairs={{0,1},{1,2},{2,3},{3,4},{4,5},{5,6},{6,7},{7,8},{8,9},{9,10},{10,1... | collective-permute-start | bytes 196616 | tf_op jit(solution)/shard_map/ppermute | solution.py:27
  21.6 8.5 %collective-permute-start.2 = (bf16[4,1,64,128]{3,2,1,0:T(8,128)(2,1)S(1)}, bf16[4,1,64,128]{3,2,1,0:T(8,128)(2,1)S(1)}, u32[]{:S(2)}, u32[]{:S(2)}) collective-permute-start(bf16[4,1,64,128]{3,2,1,0:T(8,128)(2,1)S(1)} %get-tuple-element.36), channel_id=1, source_target_pairs={{1,0},{2,1},{3,2},{4,3},{5,4},{6,5},{7,6},{8,7},{9,8},{10,9},{11,1... | collective-permute-start | bytes 196616 | tf_op jit(solution)/shard_map/ppermute | solution.py:27
  31.7 1.9 %collective-permute-start.8 = (bf16[288,1536]{1,0:T(8,128)(2,1)}, bf16[288,1536]{1,0:T(8,128)(2,1)}, u32[]{:S(2)}, u32[]{:S(2)}) collective-permute-start(bf16[288,1536]{1,0:T(8,128)(2,1)} %get-tuple-element.23.b0_ref), channel_id=1, source_target_pairs={{0,64},{64,128},{128,192},{192,0},{1,65},{65,129},{129,193},{193,1... | collective-permute-start | bytes 2654216 | tf_op jit(solution)/shard_map/ppermute | solution.py:31
  34.9 1.9 %shard_map.100 = (bf16[128,1664]{1,0:T(8,128)(2,1)S(1)}, bf16[64,128]{1,0:T(8,128)(2,1)S(1)}) custom-call(bf16[4,6,64,128]{3,2,1,0:T(8,128)(2,1)S(1)} %pad_maximum_fusion.tall_ref, bf16[3,3,384,128]{3,2,1,0:T(8,128)(2,1)S(1)} %bitcast.16, bf16[128,128]{1,0:T(8,128)(2,1)S(1)} %copy.13.latent_ref, bf16[64,1536]{1,0:T(8,128)(2,1)S(1)} %copy-done.4, ...), custom_call_target="tpu_custom_call" | custom-call | tf_op jit(solution)/shard_map/pallas_call | solution.py:268
  37.7 10.7 %all-to-all-start = ((bf16[64,2,1664]{2,1,0:T(2,128)(2,1)}), bf16[64,2,1664]{2,1,0:T(2,128)(2,1)S(1)}, u32[]{:S(2)}, u32[]{:S(2)}) async-start(bf16[64,2,1664]{2,1,0:T(2,128)(2,1)} %reshape.20), calls=%async_computation | async-start | bytes 851968 | tf_op jit(solution)/shard_map/all_to_all | solution.py:277
  48.5 3.4 %collective-permute-start.5 = (bf16[96,128]{1,0:T(8,128)(2,1)S(1)}, bf16[96,128]{1,0:T(8,128)(2,1)S(1)}, u32[]{:S(2)}, u32[]{:S(2)}) collective-permute-start(bf16[96,128]{1,0:T(8,128)(2,1)S(1)} %bitcast.23), channel_id=1, source_target_pairs={{0,128},{64,192},{128,0},{192,64},{1,129},{65,193},{129,1},{193,65... | collective-permute-start | bytes 73736 | tf_op jit(solution)/shard_map/ppermute | solution.py:31
  51.9 4.2 %collective-permute-done.5.opposite_ref = bf16[96,128]{1,0:T(8,128)(2,1)S(1)} collective-permute-done((bf16[96,128]{1,0:T(8,128)(2,1)S(1)}, bf16[96,128]{1,0:T(8,128)(2,1)S(1)}, u32[]{:S(2)}, u32[]{:S(2)}) %collective-permute-start.5) | collective-permute-done | bytes 24608 | tf_op jit(solution)/shard_map/ppermute | solution.py:31
  56.0 2.1 %collective-permute-start.10 = (bf16[304,1536]{1,0:T(8,128)(2,1)S(1)}, bf16[304,1536]{1,0:T(8,128)(2,1)}, u32[]{:S(2)}, u32[]{:S(2)}) collective-permute-start(bf16[304,1536]{1,0:T(8,128)(2,1)S(1)} %collective-permute-done.3.a1_ref), channel_id=1, source_target_pairs={{0,64},{64,128},{128,192},{192,0},{1,65},{65,129},{129,193},{193,1... | collective-permute-start | bytes 2801672 | tf_op jit(solution)/shard_map/ppermute | solution.py:31
  58.2 4.9 %collective-permute-start.11 = (bf16[288,1536]{1,0:T(8,128)(2,1)}, bf16[288,1536]{1,0:T(8,128)(2,1)}, u32[]{:S(2)}, u32[]{:S(2)}) collective-permute-start(bf16[288,1536]{1,0:T(8,128)(2,1)} %collective-permute-done.4.b2_ref), channel_id=1, source_target_pairs={{0,192},{64,0},{128,64},{192,128},{1,193},{65,1},{129,65},{193,129... | collective-permute-start | bytes 2654216 | tf_op jit(solution)/shard_map/ppermute | solution.py:31
  63.4 6.0 %collective-permute-start.7 = (bf16[64,768]{1,0:T(8,128)(2,1)S(1)}, bf16[64,768]{1,0:T(8,128)(2,1)S(1)}, u32[]{:S(2)}, u32[]{:S(2)}) collective-permute-start(bf16[64,768]{1,0:T(8,128)(2,1)S(1)} %shard_map.102.near_ref), channel_id=1, source_target_pairs={{0,256},{256,0},{1,257},{257,1},{2,258},{258,2},{3,259},{259,3},{4... | collective-permute-start | bytes 294920 | tf_op jit(solution)/shard_map/ppermute | solution.py:287
  69.4 6.5 %collective-permute-done.7.far_ref = bf16[64,768]{1,0:T(8,128)(2,1)S(1)} collective-permute-done((bf16[64,768]{1,0:T(8,128)(2,1)S(1)}, bf16[64,768]{1,0:T(8,128)(2,1)S(1)}, u32[]{:S(2)}, u32[]{:S(2)}) %collective-permute-start.7) | collective-permute-done | bytes 98336 | tf_op jit(solution)/shard_map/ppermute | solution.py:287
  79.4 1.9 %collective-permute-start.9 = (bf16[192,1664]{1,0:T(8,128)(2,1)S(1)}, bf16[192,1664]{1,0:T(8,128)(2,1)}, u32[]{:S(2)}, u32[]{:S(2)}) collective-permute-start(bf16[192,1664]{1,0:T(8,128)(2,1)S(1)} %shard_map.103.mine_ref), channel_id=1, source_target_pairs={{0,32},{32,0},{1,33},{33,1},{2,34},{34,2},{3,35},{35,3},{4,36},{36... | collective-permute-start | bytes 1916936 | tf_op jit(solution)/shard_map/ppermute | solution.py:296
  81.4 2.1 %collective-permute-done.9.theirs_ref = bf16[192,1664]{1,0:T(8,128)(2,1)} collective-permute-done((bf16[192,1664]{1,0:T(8,128)(2,1)S(1)}, bf16[192,1664]{1,0:T(8,128)(2,1)}, u32[]{:S(2)}, u32[]{:S(2)}) %collective-permute-start.9) | collective-permute-done | bytes 639008 | tf_op jit(solution)/shard_map/ppermute | solution.py:296
  83.5 1.2 copy-done.3
  85.3 5.4 %shard_map.104 = (bf16[256,1536]{1,0:T(8,128)(2,1)S(1)}, f32[256,1]{1,0:T(8,128)S(1)}, f32[256,1536]{1,0:T(8,128)S(1)}) custom-call(s32[3]{0:T(128)S(1)} %pad_add_fusion.at_ref, bf16[192,1664]{1,0:T(8,128)(2,1)S(1)} %shard_map.103.mine_ref, bf16[192,1664]{1,0:T(8,128)(2,1)} %collective-permute-done.9.theirs_ref, bf16[2,1536]{1,0:T(2,128)(2,1)S(1)} %bitcast.17, ...), custom_call_target="tpu_custom_call" | custom-call | tf_op jit(solution)/shard_map/pallas_call | solution.py:298
  90.8 2.4 %shard_map.105 = (bf16[128,1536]{1,0:T(8,128)(2,1)S(1)}, bf16[128,1536]{1,0:T(8,128)(2,1)S(1)}) custom-call(bf16[256,1536]{1,0:T(8,128)(2,1)S(1)} %get-tuple-element.28.tokens_ref, f32[256,1]{1,0:T(8,128)S(1)} %get-tuple-element.29.score_ref, f32[256,1536]{1,0:T(8,128)S(1)} %get-tuple-element.30.total_ref, bf16[304,1536]{1,0:T(8,128)(2,1)} %collective-permute-done.10.w0_ref, ...), custom_call_target="tpu_custom_call" | custom-call | tf_op jit(solution)/shard_map/pallas_call | solution.py:314
  93.2 2.0 %collective-permute-start.12 = (bf16[128,1536]{1,0:T(8,128)(2,1)S(1)}, bf16[128,1536]{1,0:T(8,128)(2,1)S(1)}, u32[]{:S(2)}, u32[]{:S(2)}) collective-permute-start(bf16[128,1536]{1,0:T(8,128)(2,1)S(1)} %get-tuple-element.33), channel_id=1, source_target_pairs={{0,32},{32,0},{1,33},{33,1},{2,34},{34,2},{3,35},{35,3},{4,36},{36... | collective-permute-start | bytes 1179656 | tf_op jit(solution)/shard_map/ppermute | solution.py:322
  95.2 1.6 %collective-permute-done.12 = bf16[128,1536]{1,0:T(8,128)(2,1)S(1)} collective-permute-done((bf16[128,1536]{1,0:T(8,128)(2,1)S(1)}, bf16[128,1536]{1,0:T(8,128)(2,1)S(1)}, u32[]{:S(2)}, u32[]{:S(2)}) %collective-permute-start.12) | collective-permute-done | bytes 393248 | tf_op jit(solution)/shard_map/ppermute | solution.py:322
  97.1 32.3 %all_to_all.10 = bf16[64,2,1536]{2,1,0:T(2,128)(2,1)S(1)} all-to-all(bf16[64,2,1536]{2,1,0:T(2,128)(2,1)S(1)} %reshape.22), channel_id=1, replica_groups=mesh['yh'=2,'x'=4,'c'=2,'yl'=4,'z'=8] {'yh','yl','z'}, dimensions={0} | all-to-all | bytes 786432 | tf_op jit(solution)/shard_map/all_to_all | solution.py:324
  (45 shorter events, 9.6 us)
Async XLA Ops:
  0.0 17.3 %copy-start.8 = (bf16[2,4,64,128]{3,2,1,0:T(8,128)(2,1)S(1)}, bf16[2,4,64,128]{3,2,1,0:T(8,128)(2,1)}, u32[]{:S(2)}) copy-start(bf16[2,4,64,128]{3,2,1,0:T(8,128)(2,1)} %param.10) | copy-start | bytes 393220
  0.0 17.3 %collective-permute-start = (bf16[2,4,64,128]{3,2,1,0:T(8,128)(2,1)}, bf16[2,4,64,128]{3,2,1,0:T(8,128)(2,1)S(1)}, u32[]{:S(2)}, u32[]{:S(2)}) collective-permute-start(bf16[2,4,64,128]{3,2,1,0:T(8,128)(2,1)} %param.10), channel_id=1, source_target_pairs={{0,32},{32,64},{64,96},{96,128},{128,160},{160,192},{192,224},{224... | collective-permute-start | bytes 393224 | tf_op jit(solution)/shard_map/ppermute | solution.py:27
  1.9 31.8 %copy-start.4 = (bf16[64,1536]{1,0:T(8,128)(2,1)S(1)}, bf16[64,1536]{1,0:T(8,128)(2,1)}, u32[]{:S(2)}) copy-start(bf16[64,1536]{1,0:T(8,128)(2,1)} %context_ref.1) | copy-start | bytes 589828
  5.3 57.7 %collective-permute-start.6 = (bf16[304,1536]{1,0:T(8,128)(2,1)}, bf16[304,1536]{1,0:T(8,128)(2,1)S(1)}, u32[]{:S(2)}, u32[]{:S(2)}) collective-permute-start(bf16[304,1536]{1,0:T(8,128)(2,1)} %get-tuple-element.22.a0_ref), channel_id=1, source_target_pairs={{0,192},{64,0},{128,64},{192,128},{1,193},{65,1},{129,65},{193,129... | collective-permute-start | bytes 2801672 | tf_op jit(solution)/shard_map/ppermute | solution.py:31
  10.2 45.8 %collective-permute-start.3 = (bf16[304,1536]{1,0:T(8,128)(2,1)}, bf16[304,1536]{1,0:T(8,128)(2,1)S(1)}, u32[]{:S(2)}, u32[]{:S(2)}) collective-permute-start(bf16[304,1536]{1,0:T(8,128)(2,1)} %get-tuple-element.22.a0_ref), channel_id=1, source_target_pairs={{0,64},{64,128},{128,192},{192,0},{1,65},{65,129},{129,193},{193,1... | collective-permute-start | bytes 2801672 | tf_op jit(solution)/shard_map/ppermute | solution.py:31
  12.1 43.9 %collective-permute-start.4 = (bf16[288,1536]{1,0:T(8,128)(2,1)}, bf16[288,1536]{1,0:T(8,128)(2,1)}, u32[]{:S(2)}, u32[]{:S(2)}) collective-permute-start(bf16[288,1536]{1,0:T(8,128)(2,1)} %get-tuple-element.23.b0_ref), channel_id=1, source_target_pairs={{0,192},{64,0},{128,64},{192,128},{1,193},{65,1},{129,65},{193,129... | collective-permute-start | bytes 2654216 | tf_op jit(solution)/shard_map/ppermute | solution.py:31
  17.3 14.4 %collective-permute-start.1 = (bf16[4,1,64,128]{3,2,1,0:T(8,128)(2,1)S(1)}, bf16[4,1,64,128]{3,2,1,0:T(8,128)(2,1)S(1)}, u32[]{:S(2)}, u32[]{:S(2)}) collective-permute-start(bf16[4,1,64,128]{3,2,1,0:T(8,128)(2,1)S(1)} %get-tuple-element.35), channel_id=1, source_target_pairs={{0,1},{1,2},{2,3},{3,4},{4,5},{5,6},{6,7},{7,8},{8,9},{9,10},{10,1... | collective-permute-start | bytes 196616 | tf_op jit(solution)/shard_map/ppermute | solution.py:27
  21.6 12.0 %collective-permute-start.2 = (bf16[4,1,64,128]{3,2,1,0:T(8,128)(2,1)S(1)}, bf16[4,1,64,128]{3,2,1,0:T(8,128)(2,1)S(1)}, u32[]{:S(2)}, u32[]{:S(2)}) collective-permute-start(bf16[4,1,64,128]{3,2,1,0:T(8,128)(2,1)S(1)} %get-tuple-element.36), channel_id=1, source_target_pairs={{1,0},{2,1},{3,2},{4,3},{5,4},{6,5},{7,6},{8,7},{9,8},{10,9},{11,1... | collective-permute-start | bytes 196616 | tf_op jit(solution)/shard_map/ppermute | solution.py:27
  31.7 37.7 %collective-permute-start.8 = (bf16[288,1536]{1,0:T(8,128)(2,1)}, bf16[288,1536]{1,0:T(8,128)(2,1)}, u32[]{:S(2)}, u32[]{:S(2)}) collective-permute-start(bf16[288,1536]{1,0:T(8,128)(2,1)} %get-tuple-element.23.b0_ref), channel_id=1, source_target_pairs={{0,64},{64,128},{128,192},{192,0},{1,65},{65,129},{129,193},{193,1... | collective-permute-start | bytes 2654216 | tf_op jit(solution)/shard_map/ppermute | solution.py:31
  33.7 1.2 copy-start.2
  34.9 13.6 %copy-start.9 = (bf16[128,96]{0,1:T(8,128)(2,1)S(1)}, bf16[128,96]{0,1:T(8,128)(2,1)}, u32[]{:S(2)}) copy-start(bf16[128,96]{0,1:T(8,128)(2,1)} %param.13) | copy-start | bytes 73732
  34.9 28.2 %copy-start = (bf16[304,1536]{1,0:T(8,128)(2,1)S(1)}, bf16[304,1536]{1,0:T(8,128)(2,1)}, u32[]{:S(2)}) copy-start(bf16[304,1536]{1,0:T(8,128)(2,1)} %get-tuple-element.22.a0_ref) | copy-start | bytes 2801668
  37.7 38.8 %all-to-all-start = ((bf16[64,2,1664]{2,1,0:T(2,128)(2,1)}), bf16[64,2,1664]{2,1,0:T(2,128)(2,1)S(1)}, u32[]{:S(2)}, u32[]{:S(2)}) async-start(bf16[64,2,1664]{2,1,0:T(2,128)(2,1)} %reshape.20), calls=%async_computation | async-start | bytes 851968 | tf_op jit(solution)/shard_map/all_to_all | solution.py:277
  48.5 7.6 %collective-permute-start.5 = (bf16[96,128]{1,0:T(8,128)(2,1)S(1)}, bf16[96,128]{1,0:T(8,128)(2,1)S(1)}, u32[]{:S(2)}, u32[]{:S(2)}) collective-permute-start(bf16[96,128]{1,0:T(8,128)(2,1)S(1)} %bitcast.23), channel_id=1, source_target_pairs={{0,128},{64,192},{128,0},{192,64},{1,129},{65,193},{129,1},{193,65... | collective-permute-start | bytes 73736 | tf_op jit(solution)/shard_map/ppermute | solution.py:31
  56.0 34.7 %collective-permute-start.10 = (bf16[304,1536]{1,0:T(8,128)(2,1)S(1)}, bf16[304,1536]{1,0:T(8,128)(2,1)}, u32[]{:S(2)}, u32[]{:S(2)}) collective-permute-start(bf16[304,1536]{1,0:T(8,128)(2,1)S(1)} %collective-permute-done.3.a1_ref), channel_id=1, source_target_pairs={{0,64},{64,128},{128,192},{192,0},{1,65},{65,129},{129,193},{193,1... | collective-permute-start | bytes 2801672 | tf_op jit(solution)/shard_map/ppermute | solution.py:31
  58.2 32.6 %collective-permute-start.11 = (bf16[288,1536]{1,0:T(8,128)(2,1)}, bf16[288,1536]{1,0:T(8,128)(2,1)}, u32[]{:S(2)}, u32[]{:S(2)}) collective-permute-start(bf16[288,1536]{1,0:T(8,128)(2,1)} %collective-permute-done.4.b2_ref), channel_id=1, source_target_pairs={{0,192},{64,0},{128,64},{192,128},{1,193},{65,1},{129,65},{193,129... | collective-permute-start | bytes 2654216 | tf_op jit(solution)/shard_map/ppermute | solution.py:31
  63.4 12.5 %collective-permute-start.7 = (bf16[64,768]{1,0:T(8,128)(2,1)S(1)}, bf16[64,768]{1,0:T(8,128)(2,1)S(1)}, u32[]{:S(2)}, u32[]{:S(2)}) collective-permute-start(bf16[64,768]{1,0:T(8,128)(2,1)S(1)} %shard_map.102.near_ref), channel_id=1, source_target_pairs={{0,256},{256,0},{1,257},{257,1},{2,258},{258,2},{3,259},{259,3},{4... | collective-permute-start | bytes 294920 | tf_op jit(solution)/shard_map/ppermute | solution.py:287
  75.8 0.6 copy-start.5
  77.4 1.0 copy-start.1
  78.4 0.9 copy-start.6
  79.4 4.1 %collective-permute-start.9 = (bf16[192,1664]{1,0:T(8,128)(2,1)S(1)}, bf16[192,1664]{1,0:T(8,128)(2,1)}, u32[]{:S(2)}, u32[]{:S(2)}) collective-permute-start(bf16[192,1664]{1,0:T(8,128)(2,1)S(1)} %shard_map.103.mine_ref), channel_id=1, source_target_pairs={{0,32},{32,0},{1,33},{33,1},{2,34},{34,2},{3,35},{35,3},{4,36},{36... | collective-permute-start | bytes 1916936 | tf_op jit(solution)/shard_map/ppermute | solution.py:296
  83.5 1.2 copy-start.3
  84.6 0.7 copy-start.7
  93.2 3.6 %collective-permute-start.12 = (bf16[128,1536]{1,0:T(8,128)(2,1)S(1)}, bf16[128,1536]{1,0:T(8,128)(2,1)S(1)}, u32[]{:S(2)}, u32[]{:S(2)}) collective-permute-start(bf16[128,1536]{1,0:T(8,128)(2,1)S(1)} %get-tuple-element.33), channel_id=1, source_target_pairs={{0,32},{32,0},{1,33},{33,1},{2,34},{34,2},{3,35},{35,3},{4,36},{36... | collective-permute-start | bytes 1179656 | tf_op jit(solution)/shard_map/ppermute | solution.py:322

commit v11 on v8

--- a/solution.py
+++ b/solution.py
@@ -44,29 +44,31 @@
             lane += 128
 
 
-def pack_kernel(
-    gate_ref, up_ref, down_ref, own_ref, other_ref, first_ref, second_ref, first_held, second_held, sems
-):
+def bring(pairs, sems):
+    copies = [pltpu.make_async_copy(source, target, sems.at[i]) for i, (source, target) in enumerate(pairs)]
+    for copy in copies:
+        copy.start()
+    return copies
+
+
+def pack_first_kernel(gate_ref, up_ref, out_ref, held_ref, sems):
+    share, part = gate_ref.shape[0], out_ref.shape[0]
+    pairs = [(gate_ref, held_ref.at[pl.ds(0, share)]), (up_ref.at[pl.ds(0, part - share)], held_ref.at[pl.ds(share, part - share)])]
+    for copy in bring(pairs, sems):
+        copy.wait()
+    for copy in bring([(held_ref, out_ref)], sems):
+        copy.wait()
+
+
+def pack_second_kernel(up_ref, down_ref, own_ref, other_ref, out_ref, held_ref, sems):
     share = down_ref.shape[0]
-    half, part = share // 2, 3 * share // 2
-    copies = [
-        pltpu.make_async_copy(gate_ref, first_held.at[pl.ds(0, share)], sems.at[0]),
-        pltpu.make_async_copy(up_ref.at[pl.ds(0, half)], first_held.at[pl.ds(share, half)], sems.at[1]),
-        pltpu.make_async_copy(up_ref.at[pl.ds(half, half)], second_held.at[pl.ds(0, half)], sems.at[2]),
-        pltpu.make_async_copy(down_ref, second_held.at[pl.ds(half, share)], sems.at[3]),
-    ]
-    for copy in copies:
-        copy.start()
-    lay_beside(first_held, part, own_ref, other_ref)
-    for copy in copies:
-        copy.wait()
-    copies = [
-        pltpu.make_async_copy(first_held, first_ref, sems.at[4]),
-        pltpu.make_async_copy(second_held, second_ref, sems.at[5]),
-    ]
-    for copy in copies:
-        copy.start()
-    for copy in copies:
+    half = share // 2
+    pairs = [(up_ref.at[pl.ds(half, half)], held_ref.at[pl.ds(0, half)]), (down_ref, held_ref.at[pl.ds(half, share)])]
+    copies = bring(pairs, sems)
+    lay_beside(held_ref, half + share, own_ref, other_ref)
+    for copy in copies:
+        copy.wait()
+    for copy in bring([(held_ref, out_ref)], sems):
         copy.wait()
 
 
@@ -150,7 +152,7 @@
 ):
     yh, x, c = at_ref[0], at_ref[1], at_ref[2]
     rows, width = tokens_ref.shape[0] // 2, total_ref.shape[1]
-    part = b0_ref.shape[0]
+    part = a0_ref.shape[0]
     share = part * 2 // 3
     copies = [
         pltpu.make_async_copy(ref.at[pl.ds(0, part)], held_ref.at[i // 2, pl.ds(i % 2 * part, part)], sems.at[i])
@@ -192,7 +194,7 @@
 
 def last_kernel(tokens_ref, score_ref, total_ref, w0_ref, w1_ref, other_ref, own_ref, held_ref, sems):
     rows, width = other_ref.shape
-    part, share = w1_ref.shape[0], held_ref.shape[0] // 3
+    part, share = w0_ref.shape[0], held_ref.shape[0] // 3
     copies = [
         pltpu.make_async_copy(ref.at[pl.ds(0, part)], held_ref.at[pl.ds(i * part, part)], sems.at[i])
         for i, ref in enumerate((w0_ref, w1_ref))
@@ -241,21 +243,27 @@
     crossed = lax.ppermute(shard, ("yh", "x"), [(i, (i + 4) % 8 // 4 * 4 + (i + 2) % 4) for i in range(8)])
     part = 3 * share // 2
     tall = 2 * shard.shape[0] * shard.shape[1] // width
-    first, second = pl.pallas_call(
-        pack_kernel,
-        out_shape=[jax.ShapeDtypeStruct((part + tall, width), BF), jax.ShapeDtypeStruct((part, width), BF)],
-        in_specs=[hbm] * 3 + [vmem] * 2,
-        out_specs=[hbm] * 2,
-        scratch_shapes=[
-            pltpu.VMEM((part + tall, width), BF),
-            pltpu.VMEM((part, width), BF),
-            pltpu.SemaphoreType.DMA((6,)),
-        ],
-        compiler_params=pltpu.CompilerParams(vmem_limit_bytes=PACK_BYTES),
-    )(gate_weight[0].T, up_weight[0].T, down_weight[0], shard, paired)
-    first, second, past, opposite, crossed = lax.optimization_barrier((first, second, past, opposite, crossed))
-    first_behind, second_ahead = ring(first, -1), ring(second, 1)
-    first_ahead, second_behind = ring(first, 1), ring(second, -1)
+    wide = pltpu.CompilerParams(vmem_limit_bytes=PACK_BYTES)
+    gate, up, down = gate_weight[0].T, up_weight[0].T, down_weight[0]
+    first = pl.pallas_call(
+        pack_first_kernel,
+        out_shape=jax.ShapeDtypeStruct((part, width), BF),
+        in_specs=[hbm] * 2,
+        out_specs=hbm,
+        scratch_shapes=[pltpu.VMEM((part, width), BF), pltpu.SemaphoreType.DMA((2,))],
+        compiler_params=wide,
+    )(gate, up)
+    second = pl.pallas_call(
+        pack_second_kernel,
+        out_shape=jax.ShapeDtypeStruct((part + tall, width), BF),
+        in_specs=[hbm] * 2 + [vmem] * 2,
+        out_specs=hbm,
+        scratch_shapes=[pltpu.VMEM((part + tall, width), BF), pltpu.SemaphoreType.DMA((2,))],
+        compiler_params=wide,
+    )(up, down, shard, paired)
+    first_behind, first_ahead = ring(first, -1), ring(first, 1)
+    second, opposite, crossed = lax.optimization_barrier((second, opposite, crossed))
+    second_ahead, second_behind = ring(second, 1), ring(second, -1)
     first_opposite, second_opposite = ring(first_behind, -1), ring(second_ahead, 1)
 
     stacked = jnp.concatenate([past, video], axis=0)
@@ -282,7 +290,7 @@
         out_specs=vmem,
         scratch_shapes=[pltpu.VMEM((3, tall, width), BF), pltpu.SemaphoreType.DMA((3,))],
         compiler_params=params,
-    )(arrived.reshape(slots, raw), opposite, crossed, first, first_behind, first_ahead)
+    )(arrived.reshape(slots, raw), opposite, crossed, second, second_behind, second_ahead)
     theirs = lax.ppermute(mine, "c", SWAP)
     place = jnp.stack([lax.axis_index(axis) for axis in FRAME]).astype(jnp.int32)
     tokens, score, total = pl.pallas_call(

time: 131 us -> 132 us (level)
  waiting for transfers between devices: 21.2 us -> 13.5 us
  starting transfers between devices: 59 us -> 65.1 us
  Pallas kernels: 13.4 us -> 14.9 us
    ppermute x7, starting transfers between devices: 22.3 us -> 27.4 us  [ring(): return lax.ppermute(value, 'x', [(i, (i - step) % 4) for i in range(4)])]
    ppermute x1, waiting for transfers between devices: 4.85 us -> 0.01 us  [local(): lax.ppermute(shard, ('yh', 'x'), [(i, (i + 4) % 8 // 4 * 4 + (i + 2) % 4)...]
    all_to_all x1, waiting for transfers between devices: 9.43 us -> 4.84 us  [local(): lax.all_to_all(outgoing.reshape(experts, capacity, raw), SOURCES, split_a...]
    ppermute x7, waiting for transfers between devices: 3.15 us -> 4.86 us  [ring(): return lax.ppermute(value, 'x', [(i, (i - step) % 4) for i in range(4)])]
    all_to_all x1, starting transfers between devices: 13.3 us -> 14.9 us  [local(): lax.all_to_all(outgoing.reshape(experts, capacity, raw), SOURCES, split_a...]
    pallas_call x1 -> x2, Pallas kernels: 3.48 us -> 4.98 us  [the longest x1 2.9 us: local(): pl.pallas_call(pack_second_kernel, out_shape=jax.ShapeDtypeStruct((part +...]
  transfers between devices with their start and end apart: 15 -> 15, of which waited for: 6 -> 5; matrix products, arithmetic and copies ran while one was open for 2% -> 3% of each run, Pallas kernels for 8% -> 10%
where the time goes in v11:
time: 132 us; the launch traced here: 131 us
  starting transfers between devices  65.1 us (49%)
  blocking collectives  29.5 us (22%)
  Pallas kernels  14.9 us (11%)
  waiting for transfers between devices  13.5 us (10%)
  local copies, waits for them, and re-layouts  6.75 us (5%)
    all_to_all x1, blocking collectives, local(): lax.all_to_all(summed, SOURCES, split_axis=0, concat_axis=0, tiled=True)  29.5 us
    ppermute x7, starting transfers between devices, ring(): return lax.ppermute(value, 'x', [(i, (i - step) % 4) for i in range(4)])  27.4 us
    all_to_all x1, starting transfers between devices, local(): lax.all_to_all(outgoing.reshape(experts, capacity, raw), SOURCES, split_a...  14.9 us
    ppermute x3, starting transfers between devices, shifted(): return lax.ppermute(value, axes, pairs)  7.74 us
    ppermute x1, starting transfers between devices, local(): paired = lax.ppermute(shard, 'yh', SWAP)  7.74 us
    pallas_call x1, Pallas kernels, local(): pl.pallas_call(near_kernel, out_shape=[jax.ShapeDtypeStruct((2 * slots, w...  5.41 us
    ppermute x7, waiting for transfers between devices, ring(): return lax.ppermute(value, 'x', [(i, (i - step) % 4) for i in range(4)])  4.86 us
    all_to_all x1, waiting for transfers between devices, local(): lax.all_to_all(outgoing.reshape(experts, capacity, raw), SOURCES, split_a...  4.84 us
  transfers between devices with their start and end apart: 15, of which 5 were waited for; matrix products, arithmetic and copies ran while one was open for 3% of the time, Pallas kernels for 10%

profile of v11, /device:TPU:6, one launch (start us, length us, event | category | flops | bytes accessed | tf_op | source)
XLA Modules:
  0.0 131.3 jit_solution(10292421151499587245)
XLA Ops:
  0.0 1.9 %collective-permute-start = (bf16[2,4,64,128]{3,2,1,0:T(8,128)(2,1)}, bf16[2,4,64,128]{3,2,1,0:T(8,128)(2,1)}, u32[]{:S(2)}, u32[]{:S(2)}) collective-permute-start(bf16[2,4,64,128]{3,2,1,0:T(8,128)(2,1)} %param.10), channel_id=1, source_target_pairs={{0,32},{32,64},{64,96},{96,128},{128,160},{160,192},{192,224},{224... | collective-permute-start | bytes 393224 | tf_op jit(solution)/shard_map/ppermute | solution.py:27
  1.9 7.7 %collective-permute-start.4 = (bf16[96,128]{1,0:T(8,128)(2,1)}, bf16[96,128]{1,0:T(8,128)(2,1)S(1)}, u32[]{:S(2)}, u32[]{:S(2)}) collective-permute-start(bf16[96,128]{1,0:T(8,128)(2,1)} %bitcast.23), channel_id=1, source_target_pairs={{0,256},{256,0},{1,257},{257,1},{2,258},{258,2},{3,259},{259,3},{4... | collective-permute-start | bytes 73736 | tf_op jit(solution)/shard_map/ppermute | solution.py:241
  9.7 3.3 %collective-permute-start.5 = (bf16[96,128]{1,0:T(8,128)(2,1)}, bf16[96,128]{1,0:T(8,128)(2,1)S(1)}, u32[]{:S(2)}, u32[]{:S(2)}) collective-permute-start(bf16[96,128]{1,0:T(8,128)(2,1)} %bitcast.24), channel_id=1, source_target_pairs={{0,128},{64,192},{128,0},{192,64},{1,129},{65,193},{129,1},{193,65... | collective-permute-start | bytes 73736 | tf_op jit(solution)/shard_map/ppermute | solution.py:31
  13.0 3.6 %collective-permute-start.6 = (bf16[96,128]{1,0:T(8,128)(2,1)}, bf16[96,128]{1,0:T(8,128)(2,1)S(1)}, u32[]{:S(2)}, u32[]{:S(2)}) collective-permute-start(bf16[96,128]{1,0:T(8,128)(2,1)} %bitcast.25), channel_id=1, source_target_pairs={{0,384},{64,448},{128,256},{192,320},{256,128},{320,192},{384,0},{... | collective-permute-start | bytes 73736 | tf_op jit(solution)/shard_map/ppermute | solution.py:243
  16.6 2.1 %shard_map.101.a0_ref = bf16[288,1536]{1,0:T(8,128)(2,1)} custom-call(bf16[192,1536]{1,0:T(8,128)(2,1)} %bitcast.20, bf16[192,1536]{1,0:T(8,128)(2,1)} %bitcast.18), custom_call_target="tpu_custom_call" | custom-call | tf_op jit(solution)/shard_map/pallas_call | solution.py:248
  18.7 7.9 %collective-permute-start.10 = (bf16[288,1536]{1,0:T(8,128)(2,1)}, bf16[288,1536]{1,0:T(8,128)(2,1)}, u32[]{:S(2)}, u32[]{:S(2)}) collective-permute-start(bf16[288,1536]{1,0:T(8,128)(2,1)} %shard_map.101.a0_ref), channel_id=1, source_target_pairs={{0,64},{64,128},{128,192},{192,0},{1,65},{65,129},{129,193},{193,1... | collective-permute-start | bytes 2654216 | tf_op jit(solution)/shard_map/ppermute | solution.py:31
  27.2 2.9 %shard_map.102.a0_ref.b0_ref = bf16[304,1536]{1,0:T(8,128)(2,1)} custom-call(bf16[192,1536]{1,0:T(8,128)(2,1)} %bitcast.19, bf16[192,1536]{1,0:T(8,128)(2,1)} %bitcast.21, bf16[96,128]{1,0:T(8,128)(2,1)} %bitcast.26, bf16[96,128]{1,0:T(8,128)(2,1)} %copy-done.7), custom_call_target="tpu_custom_call" | custom-call | tf_op jit(solution)/shard_map/pallas_call | solution.py:256
  30.2 2.1 %collective-permute-start.8 = (bf16[304,1536]{1,0:T(8,128)(2,1)}, bf16[304,1536]{1,0:T(8,128)(2,1)S(1)}, u32[]{:S(2)}, u32[]{:S(2)}) collective-permute-start(bf16[304,1536]{1,0:T(8,128)(2,1)} %shard_map.102.a0_ref.b0_ref), channel_id=1, source_target_pairs={{0,192},{64,0},{128,64},{192,128},{1,193},{65,1},{129,65},{193,129... | collective-permute-start | bytes 2801672 | tf_op jit(solution)/shard_map/ppermute | solution.py:31
  35.1 4.5 %collective-permute-start.1 = (bf16[4,1,64,128]{3,2,1,0:T(8,128)(2,1)}, bf16[4,1,64,128]{3,2,1,0:T(8,128)(2,1)S(1)}, u32[]{:S(2)}, u32[]{:S(2)}) collective-permute-start(bf16[4,1,64,128]{3,2,1,0:T(8,128)(2,1)} %get-tuple-element.31), channel_id=1, source_target_pairs={{0,1},{1,2},{2,3},{3,4},{4,5},{5,6},{6,7},{7,8},{8,9},{9,10},{10,1... | collective-permute-start | bytes 196616 | tf_op jit(solution)/shard_map/ppermute | solution.py:27
  39.7 1.9 %collective-permute-start.3 = (bf16[288,1536]{1,0:T(8,128)(2,1)}, bf16[288,1536]{1,0:T(8,128)(2,1)}, u32[]{:S(2)}, u32[]{:S(2)}) collective-permute-start(bf16[288,1536]{1,0:T(8,128)(2,1)} %shard_map.101.a0_ref), channel_id=1, source_target_pairs={{0,192},{64,0},{128,64},{192,128},{1,193},{65,1},{129,65},{193,129... | collective-permute-start | bytes 2654216 | tf_op jit(solution)/shard_map/ppermute | solution.py:31
  41.9 5.1 %collective-permute-start.7 = (bf16[304,1536]{1,0:T(8,128)(2,1)}, bf16[304,1536]{1,0:T(8,128)(2,1)S(1)}, u32[]{:S(2)}, u32[]{:S(2)}) collective-permute-start(bf16[304,1536]{1,0:T(8,128)(2,1)} %shard_map.102.a0_ref.b0_ref), channel_id=1, source_target_pairs={{0,64},{64,128},{128,192},{192,0},{1,65},{65,129},{129,193},{193,1... | collective-permute-start | bytes 2801672 | tf_op jit(solution)/shard_map/ppermute | solution.py:31
  47.1 1.9 %shard_map.100 = (bf16[128,1664]{1,0:T(8,128)(2,1)S(1)}, bf16[64,128]{1,0:T(8,128)(2,1)S(1)}) custom-call(bf16[4,6,64,128]{3,2,1,0:T(8,128)(2,1)S(1)} %pad_maximum_fusion.tall_ref, bf16[3,3,384,128]{3,2,1,0:T(8,128)(2,1)S(1)} %bitcast.16, bf16[128,128]{1,0:T(8,128)(2,1)S(1)} %copy.13.latent_ref, bf16[64,1536]{1,0:T(8,128)(2,1)S(1)} %copy-done.4, ...), custom_call_target="tpu_custom_call" | custom-call | tf_op jit(solution)/shard_map/pallas_call | solution.py:275
  49.9 14.9 %all-to-all-start = ((bf16[64,2,1664]{2,1,0:T(2,128)(2,1)}), bf16[64,2,1664]{2,1,0:T(2,128)(2,1)S(1)}, u32[]{:S(2)}, u32[]{:S(2)}) async-start(bf16[64,2,1664]{2,1,0:T(2,128)(2,1)} %reshape.20), calls=%async_computation | async-start | bytes 851968 | tf_op jit(solution)/shard_map/all_to_all | solution.py:284
  64.8 1.9 %collective-permute-start.12 = (bf16[304,1536]{1,0:T(8,128)(2,1)S(1)}, bf16[304,1536]{1,0:T(8,128)(2,1)}, u32[]{:S(2)}, u32[]{:S(2)}) collective-permute-start(bf16[304,1536]{1,0:T(8,128)(2,1)S(1)} %collective-permute-done.8.a2_ref.b2_ref), channel_id=1, source_target_pairs={{0,192},{64,0},{128,64},{192,128},{1,193},{65,1},{129,65},{193,129... | collective-permute-start | bytes 2801672 | tf_op jit(solution)/shard_map/ppermute | solution.py:31
  66.7 5.1 %collective-permute-start.11 = (bf16[288,1536]{1,0:T(8,128)(2,1)}, bf16[288,1536]{1,0:T(8,128)(2,1)}, u32[]{:S(2)}, u32[]{:S(2)}) collective-permute-start(bf16[288,1536]{1,0:T(8,128)(2,1)} %collective-permute-done.10.a1_ref), channel_id=1, source_target_pairs={{0,64},{64,128},{128,192},{192,0},{1,65},{65,129},{129,193},{193,1... | collective-permute-start | bytes 2654216 | tf_op jit(solution)/shard_map/ppermute | solution.py:31
  71.9 4.4 %collective-permute-done.3.a2_ref = bf16[288,1536]{1,0:T(8,128)(2,1)} collective-permute-done((bf16[288,1536]{1,0:T(8,128)(2,1)}, bf16[288,1536]{1,0:T(8,128)(2,1)}, u32[]{:S(2)}, u32[]{:S(2)}) %collective-permute-start.3) | collective-permute-done | bytes 884768 | tf_op jit(solution)/shard_map/ppermute | solution.py:31
  76.3 4.8 %all-to-all-done = bf16[64,2,1664]{2,1,0:T(2,128)(2,1)S(1)} async-done(((bf16[64,2,1664]{2,1,0:T(2,128)(2,1)}), bf16[64,2,1664]{2,1,0:T(2,128)(2,1)S(1)}, u32[]{:S(2)}, u32[]{:S(2)}) %all-to-all-start) | async-done | bytes 426016 | tf_op jit(solution)/shard_map/all_to_all | solution.py:284
  83.3 1.9 %collective-permute-start.9 = (bf16[192,1664]{1,0:T(8,128)(2,1)S(1)}, bf16[192,1664]{1,0:T(8,128)(2,1)}, u32[]{:S(2)}, u32[]{:S(2)}) collective-permute-start(bf16[192,1664]{1,0:T(8,128)(2,1)S(1)} %shard_map.103.mine_ref), channel_id=1, source_target_pairs={{0,32},{32,0},{1,33},{33,1},{2,34},{34,2},{3,35},{35,3},{4,36},{36... | collective-permute-start | bytes 1916936 | tf_op jit(solution)/shard_map/ppermute | solution.py:294
  85.4 2.1 %collective-permute-done.9.theirs_ref = bf16[192,1664]{1,0:T(8,128)(2,1)} collective-permute-done((bf16[192,1664]{1,0:T(8,128)(2,1)S(1)}, bf16[192,1664]{1,0:T(8,128)(2,1)}, u32[]{:S(2)}, u32[]{:S(2)}) %collective-permute-start.9) | collective-permute-done | bytes 639008 | tf_op jit(solution)/shard_map/ppermute | solution.py:294
  88.6 5.4 %shard_map.104 = (bf16[256,1536]{1,0:T(8,128)(2,1)S(1)}, f32[256,1]{1,0:T(8,128)S(1)}, f32[256,1536]{1,0:T(8,128)S(1)}) custom-call(s32[3]{0:T(128)S(1)} %pad_add_fusion.at_ref, bf16[192,1664]{1,0:T(8,128)(2,1)S(1)} %shard_map.103.mine_ref, bf16[192,1664]{1,0:T(8,128)(2,1)} %collective-permute-done.9.theirs_ref, bf16[2,1536]{1,0:T(2,128)(2,1)S(1)} %bitcast.17, ...), custom_call_target="tpu_custom_call" | custom-call | tf_op jit(solution)/shard_map/pallas_call | solution.py:296
  94.5 2.4 %shard_map.105 = (bf16[128,1536]{1,0:T(8,128)(2,1)S(1)}, bf16[128,1536]{1,0:T(8,128)(2,1)S(1)}) custom-call(bf16[256,1536]{1,0:T(8,128)(2,1)S(1)} %get-tuple-element.26.tokens_ref, f32[256,1]{1,0:T(8,128)S(1)} %get-tuple-element.27.score_ref, f32[256,1536]{1,0:T(8,128)S(1)} %get-tuple-element.28.total_ref, bf16[288,1536]{1,0:T(8,128)(2,1)} %collective-permute-done.11.w0_ref, ...), custom_call_target="tpu_custom_call" | custom-call | tf_op jit(solution)/shard_map/pallas_call | solution.py:312
  96.9 1.9 %collective-permute-start.13 = (bf16[128,1536]{1,0:T(8,128)(2,1)S(1)}, bf16[128,1536]{1,0:T(8,128)(2,1)S(1)}, u32[]{:S(2)}, u32[]{:S(2)}) collective-permute-start(bf16[128,1536]{1,0:T(8,128)(2,1)S(1)} %get-tuple-element.29), channel_id=1, source_target_pairs={{0,32},{32,0},{1,33},{33,1},{2,34},{34,2},{3,35},{35,3},{4,36},{36... | collective-permute-start | bytes 1179656 | tf_op jit(solution)/shard_map/ppermute | solution.py:320
  98.8 1.7 %collective-permute-done.13 = bf16[128,1536]{1,0:T(8,128)(2,1)S(1)} collective-permute-done((bf16[128,1536]{1,0:T(8,128)(2,1)S(1)}, bf16[128,1536]{1,0:T(8,128)(2,1)S(1)}, u32[]{:S(2)}, u32[]{:S(2)}) %collective-permute-start.13) | collective-permute-done | bytes 393248 | tf_op jit(solution)/shard_map/ppermute | solution.py:320
  100.7 29.5 %all_to_all.10 = bf16[64,2,1536]{2,1,0:T(2,128)(2,1)S(1)} all-to-all(bf16[64,2,1536]{2,1,0:T(2,128)(2,1)S(1)} %reshape.22), channel_id=1, replica_groups=mesh['yh'=2,'x'=4,'c'=2,'yl'=4,'z'=8] {'yh','yl','z'}, dimensions={0} | all-to-all | bytes 786432 | tf_op jit(solution)/shard_map/all_to_all | solution.py:322
  (47 shorter events, 9.8 us)
Async XLA Ops:
  0.0 32.2 %collective-permute-start = (bf16[2,4,64,128]{3,2,1,0:T(8,128)(2,1)}, bf16[2,4,64,128]{3,2,1,0:T(8,128)(2,1)}, u32[]{:S(2)}, u32[]{:S(2)}) collective-permute-start(bf16[2,4,64,128]{3,2,1,0:T(8,128)(2,1)} %param.10), channel_id=1, source_target_pairs={{0,32},{32,64},{64,96},{96,128},{128,160},{160,192},{192,224},{224... | collective-permute-start | bytes 393224 | tf_op jit(solution)/shard_map/ppermute | solution.py:27
  1.9 24.7 %collective-permute-start.4 = (bf16[96,128]{1,0:T(8,128)(2,1)}, bf16[96,128]{1,0:T(8,128)(2,1)S(1)}, u32[]{:S(2)}, u32[]{:S(2)}) collective-permute-start(bf16[96,128]{1,0:T(8,128)(2,1)} %bitcast.23), channel_id=1, source_target_pairs={{0,256},{256,0},{1,257},{257,1},{2,258},{258,2},{3,259},{259,3},{4... | collective-permute-start | bytes 73736 | tf_op jit(solution)/shard_map/ppermute | solution.py:241
  9.7 20.5 %collective-permute-start.5 = (bf16[96,128]{1,0:T(8,128)(2,1)}, bf16[96,128]{1,0:T(8,128)(2,1)S(1)}, u32[]{:S(2)}, u32[]{:S(2)}) collective-permute-start(bf16[96,128]{1,0:T(8,128)(2,1)} %bitcast.24), channel_id=1, source_target_pairs={{0,128},{64,192},{128,0},{192,64},{1,129},{65,193},{129,1},{193,65... | collective-permute-start | bytes 73736 | tf_op jit(solution)/shard_map/ppermute | solution.py:31
  13.0 17.2 %collective-permute-start.6 = (bf16[96,128]{1,0:T(8,128)(2,1)}, bf16[96,128]{1,0:T(8,128)(2,1)S(1)}, u32[]{:S(2)}, u32[]{:S(2)}) collective-permute-start(bf16[96,128]{1,0:T(8,128)(2,1)} %bitcast.25), channel_id=1, source_target_pairs={{0,384},{64,448},{128,256},{192,320},{256,128},{320,192},{384,0},{... | collective-permute-start | bytes 73736 | tf_op jit(solution)/shard_map/ppermute | solution.py:243
  18.7 14.5 %copy-start.6 = (bf16[2,4,64,128]{3,2,1,0:T(8,128)(2,1)S(1)}, bf16[2,4,64,128]{3,2,1,0:T(8,128)(2,1)}, u32[]{:S(2)}) copy-start(bf16[2,4,64,128]{3,2,1,0:T(8,128)(2,1)} %param.10) | copy-start | bytes 393220
  18.7 22.9 %copy-start.8 = (bf16[128,16]{0,1:T(8,128)(2,1)S(1)}, bf16[128,16]{0,1:T(8,128)(2,1)}, u32[]{:S(2)}) copy-start(bf16[128,16]{0,1:T(8,128)(2,1)} %param.12) | copy-start | bytes 12292
  18.7 23.1 %copy-start.9 = (s32[64,2]{0,1:T(2,128)S(1)}, s32[64,2]{0,1:T(2,128)}, u32[]{:S(2)}) copy-start(s32[64,2]{0,1:T(2,128)} %param.19) | copy-start | bytes 1540
  18.7 48.0 %collective-permute-start.10 = (bf16[288,1536]{1,0:T(8,128)(2,1)}, bf16[288,1536]{1,0:T(8,128)(2,1)}, u32[]{:S(2)}, u32[]{:S(2)}) collective-permute-start(bf16[288,1536]{1,0:T(8,128)(2,1)} %shard_map.101.a0_ref), channel_id=1, source_target_pairs={{0,64},{64,128},{128,192},{192,0},{1,65},{65,129},{129,193},{193,1... | collective-permute-start | bytes 2654216 | tf_op jit(solution)/shard_map/ppermute | solution.py:31
  27.2 19.8 %copy-start.4 = (bf16[64,1536]{1,0:T(8,128)(2,1)S(1)}, bf16[64,1536]{1,0:T(8,128)(2,1)}, u32[]{:S(2)}) copy-start(bf16[64,1536]{1,0:T(8,128)(2,1)} %context_ref.1) | copy-start | bytes 589828
  30.1 16.9 %copy-start.3 = (bf16[3,3,3,128,128]{4,3,2,1,0:T(8,128)(2,1)S(1)}, bf16[3,3,3,128,128]{4,3,2,1,0:T(8,128)(2,1)}, u32[]{:S(2)}) copy-start(bf16[3,3,3,128,128]{4,3,2,1,0:T(8,128)(2,1)} %param.11) | copy-start | bytes 2654212
  30.2 34.6 %collective-permute-start.8 = (bf16[304,1536]{1,0:T(8,128)(2,1)}, bf16[304,1536]{1,0:T(8,128)(2,1)S(1)}, u32[]{:S(2)}, u32[]{:S(2)}) collective-permute-start(bf16[304,1536]{1,0:T(8,128)(2,1)} %shard_map.102.a0_ref.b0_ref), channel_id=1, source_target_pairs={{0,192},{64,0},{128,64},{192,128},{1,193},{65,1},{129,65},{193,129... | collective-permute-start | bytes 2801672 | tf_op jit(solution)/shard_map/ppermute | solution.py:31
  33.8 8.0 %collective-permute-start.2 = (bf16[4,1,64,128]{3,2,1,0:T(8,128)(2,1)S(1)}, bf16[4,1,64,128]{3,2,1,0:T(8,128)(2,1)S(1)}, u32[]{:S(2)}, u32[]{:S(2)}) collective-permute-start(bf16[4,1,64,128]{3,2,1,0:T(8,128)(2,1)S(1)} %get-tuple-element.32), channel_id=1, source_target_pairs={{1,0},{2,1},{3,2},{4,3},{5,4},{6,5},{7,6},{8,7},{9,8},{10,9},{11,1... | collective-permute-start | bytes 196616 | tf_op jit(solution)/shard_map/ppermute | solution.py:27
  35.1 11.9 %collective-permute-start.1 = (bf16[4,1,64,128]{3,2,1,0:T(8,128)(2,1)}, bf16[4,1,64,128]{3,2,1,0:T(8,128)(2,1)S(1)}, u32[]{:S(2)}, u32[]{:S(2)}) collective-permute-start(bf16[4,1,64,128]{3,2,1,0:T(8,128)(2,1)} %get-tuple-element.31), channel_id=1, source_target_pairs={{0,1},{1,2},{2,3},{3,4},{4,5},{5,6},{6,7},{7,8},{8,9},{9,10},{10,1... | collective-permute-start | bytes 196616 | tf_op jit(solution)/shard_map/ppermute | solution.py:27
  39.7 36.6 %collective-permute-start.3 = (bf16[288,1536]{1,0:T(8,128)(2,1)}, bf16[288,1536]{1,0:T(8,128)(2,1)}, u32[]{:S(2)}, u32[]{:S(2)}) collective-permute-start(bf16[288,1536]{1,0:T(8,128)(2,1)} %shard_map.101.a0_ref), channel_id=1, source_target_pairs={{0,192},{64,0},{128,64},{192,128},{1,193},{65,1},{129,65},{193,129... | collective-permute-start | bytes 2654216 | tf_op jit(solution)/shard_map/ppermute | solution.py:31
  41.9 34.5 %collective-permute-start.7 = (bf16[304,1536]{1,0:T(8,128)(2,1)}, bf16[304,1536]{1,0:T(8,128)(2,1)S(1)}, u32[]{:S(2)}, u32[]{:S(2)}) collective-permute-start(bf16[304,1536]{1,0:T(8,128)(2,1)} %shard_map.102.a0_ref.b0_ref), channel_id=1, source_target_pairs={{0,64},{64,128},{128,192},{192,0},{1,65},{65,129},{129,193},{193,1... | collective-permute-start | bytes 2801672 | tf_op jit(solution)/shard_map/ppermute | solution.py:31
  49.0 33.1 %copy-start = (bf16[304,1536]{1,0:T(8,128)(2,1)S(1)}, bf16[304,1536]{1,0:T(8,128)(2,1)}, u32[]{:S(2)}) copy-start(bf16[304,1536]{1,0:T(8,128)(2,1)} %shard_map.102.a0_ref.b0_ref) | copy-start | bytes 2801668
  49.9 31.2 %all-to-all-start = ((bf16[64,2,1664]{2,1,0:T(2,128)(2,1)}), bf16[64,2,1664]{2,1,0:T(2,128)(2,1)S(1)}, u32[]{:S(2)}, u32[]{:S(2)}) async-start(bf16[64,2,1664]{2,1,0:T(2,128)(2,1)} %reshape.20), calls=%async_computation | async-start | bytes 851968 | tf_op jit(solution)/shard_map/all_to_all | solution.py:284
  64.8 29.7 %collective-permute-start.12 = (bf16[304,1536]{1,0:T(8,128)(2,1)S(1)}, bf16[304,1536]{1,0:T(8,128)(2,1)}, u32[]{:S(2)}, u32[]{:S(2)}) collective-permute-start(bf16[304,1536]{1,0:T(8,128)(2,1)S(1)} %collective-permute-done.8.a2_ref.b2_ref), channel_id=1, source_target_pairs={{0,192},{64,0},{128,64},{192,128},{1,193},{65,1},{129,65},{193,129... | collective-permute-start | bytes 2801672 | tf_op jit(solution)/shard_map/ppermute | solution.py:31
  66.7 27.3 %collective-permute-start.11 = (bf16[288,1536]{1,0:T(8,128)(2,1)}, bf16[288,1536]{1,0:T(8,128)(2,1)}, u32[]{:S(2)}, u32[]{:S(2)}) collective-permute-start(bf16[288,1536]{1,0:T(8,128)(2,1)} %collective-permute-done.10.a1_ref), channel_id=1, source_target_pairs={{0,64},{64,128},{128,192},{192,0},{1,65},{65,129},{129,193},{193,1... | collective-permute-start | bytes 2654216 | tf_op jit(solution)/shard_map/ppermute | solution.py:31
  82.1 1.0 copy-start.2
  83.1 4.4 %copy-start.5 = (bf16[2,1536,1]{1,0,2:T(2,128)(2,1)S(1)}, bf16[2,1536,1]{1,0,2:T(2,128)(2,1)}, u32[]{:S(2)}) copy-start(bf16[2,1536,1]{1,0,2:T(2,128)(2,1)} %param.15) | copy-start | bytes 18436
  83.3 4.1 %collective-permute-start.9 = (bf16[192,1664]{1,0:T(8,128)(2,1)S(1)}, bf16[192,1664]{1,0:T(8,128)(2,1)}, u32[]{:S(2)}, u32[]{:S(2)}) collective-permute-start(bf16[192,1664]{1,0:T(8,128)(2,1)S(1)} %shard_map.103.mine_ref), channel_id=1, source_target_pairs={{0,32},{32,0},{1,33},{33,1},{2,34},{34,2},{3,35},{35,3},{4,36},{36... | collective-permute-start | bytes 1916936 | tf_op jit(solution)/shard_map/ppermute | solution.py:294
  87.5 1.2 copy-start.1
  96.9 3.6 %collective-permute-start.13 = (bf16[128,1536]{1,0:T(8,128)(2,1)S(1)}, bf16[128,1536]{1,0:T(8,128)(2,1)S(1)}, u32[]{:S(2)}, u32[]{:S(2)}) collective-permute-start(bf16[128,1536]{1,0:T(8,128)(2,1)S(1)} %get-tuple-element.29), channel_id=1, source_target_pairs={{0,32},{32,0},{1,33},{33,1},{2,34},{34,2},{3,35},{35,3},{4,36},{36... | collective-permute-start | bytes 1179656 | tf_op jit(solution)/shard_map/ppermute | solution.py:320
  (1 other events, 0.6 us)

commit v12 on v10

--- a/solution.py
+++ b/solution.py
@@ -240,6 +240,8 @@
 
     past = shifted(video, FRAME, 1)
     shard = embed_weight.T
+    opposite = ring(shard, 2)
+    past, opposite = lax.optimization_barrier((past, opposite))
     part, tall = 3 * share // 2, 16
     first, second = pl.pallas_call(
         pack_kernel,
@@ -255,9 +257,7 @@
     )(gate_weight[0].T, up_weight[0].T, down_weight[0], shard)
     first_behind, second_ahead = ring(first, -1), ring(second, 1)
     first_ahead, second_behind = ring(first, 1), ring(second, -1)
-    opposite = ring(shard, 2)
-    from_behind, from_ahead, opposite = lax.optimization_barrier((first_behind, second_ahead, opposite))
-    first_opposite, second_opposite = ring(from_behind, -1), ring(from_ahead, 1)
+    first_opposite, second_opposite = ring(first_behind, -1), ring(second_ahead, 1)
 
     stacked = jnp.concatenate([past, video], axis=0)
     above = shifted(stacked[:, rows - 1 :], EXPERT, 1)
@@ -282,7 +282,7 @@
         in_specs=[vmem] + [hbm] * 3,
         out_specs=vmem,
         scratch_shapes=[pltpu.VMEM((3, tall, width), BF), pltpu.SemaphoreType.DMA((3,))],
-        compiler_params=params,
+        compiler_params=pltpu.CompilerParams(vmem_limit_bytes=PACK_BYTES),
     )(opposite, first, first_behind, first_ahead)
     beyond = lax.ppermute(shards, "yh", SWAP)
     arrived, beyond, second_behind = lax.optimization_barrier((arrived, beyond, second_behind))

time: 131 us -> 130 us (level)
  local copies, waits for them, and re-layouts: 9.36 us -> 2.56 us
  waiting for transfers between devices: 14.3 us -> 16.3 us
    unnamed x22, local copies, waits for them, and re-layouts: 6.36 us -> 1.04 us
    ppermute x3, waiting for transfers between devices: 0.01 us -> 2.16 us  [shifted(): return lax.ppermute(value, axes, pairs)]
    pallas_call x1, Pallas kernels: 0.23 us -> 2.26 us  [local(): pl.pallas_call(shards_kernel, out_shape=jax.ShapeDtypeStruct((4 * tall, l...]
    ppermute x7, starting transfers between devices: 24.2 us -> 26.2 us  [ring(): return lax.ppermute(value, 'x', [(i, (i - step) % 4) for i in range(4)])]
  transfers between devices with their start and end apart: 14 -> 14, of which waited for: 4 -> 5; matrix products, arithmetic and copies ran while one was open for 3% -> 1% of each run, Pallas kernels for 8% -> 10%
where the time goes in v12:
time: 130 us; the launch traced here: 129 us
  starting transfers between devices  60.4 us (46%)
  blocking collectives  33.3 us (26%)
  waiting for transfers between devices  16.3 us (13%)
  Pallas kernels  14.8 us (11%)
  local copies, waits for them, and re-layouts  2.56 us (2%)
    all_to_all x1, blocking collectives, local(): lax.all_to_all(summed, SOURCES, split_axis=0, concat_axis=0, tiled=True)  33.3 us
    ppermute x7, starting transfers between devices, ring(): return lax.ppermute(value, 'x', [(i, (i - step) % 4) for i in range(4)])  26.2 us
    ppermute x3, starting transfers between devices, shifted(): return lax.ppermute(value, axes, pairs)  14.6 us
    all_to_all x1, starting transfers between devices, local(): lax.all_to_all(outgoing.reshape(experts, capacity, raw), SOURCES, split_a...  9.57 us
    ppermute x1, waiting for transfers between devices, local(): beyond = lax.ppermute(shards, 'yh', SWAP)  6.55 us
    ppermute x1, starting transfers between devices, local(): beyond = lax.ppermute(shards, 'yh', SWAP)  6 us
    pallas_call x1, Pallas kernels, local(): pl.pallas_call(near_kernel, out_shape=[jax.ShapeDtypeStruct((2 * slots, w...  4.7 us
    ppermute x7, waiting for transfers between devices, ring(): return lax.ppermute(value, 'x', [(i, (i - step) % 4) for i in range(4)])  4.08 us
  transfers between devices with their start and end apart: 14, of which 5 were waited for; matrix products, arithmetic and copies ran while one was open for 1% of the time, Pallas kernels for 10%

profile of v12, /device:TPU:16, one launch (start us, length us, event | category | flops | bytes accessed | tf_op | source)
XLA Modules:
  0.0 128.9 jit_solution(6317760732501501695)
XLA Ops:
  0.0 1.9 %collective-permute-start = (bf16[2,4,64,128]{3,2,1,0:T(8,128)(2,1)}, bf16[2,4,64,128]{3,2,1,0:T(8,128)(2,1)S(1)}, u32[]{:S(2)}, u32[]{:S(2)}) collective-permute-start(bf16[2,4,64,128]{3,2,1,0:T(8,128)(2,1)} %param.10), channel_id=1, source_target_pairs={{0,32},{32,64},{64,96},{96,128},{128,160},{160,192},{192,224},{224... | collective-permute-start | bytes 393224 | tf_op jit(solution)/shard_map/ppermute | solution.py:27
  1.9 5.1 %collective-permute-start.1 = (bf16[96,128]{1,0:T(8,128)(2,1)}, bf16[96,128]{1,0:T(8,128)(2,1)S(1)}, u32[]{:S(2)}, u32[]{:S(2)}) collective-permute-start(bf16[96,128]{1,0:T(8,128)(2,1)} %bitcast.22), channel_id=1, source_target_pairs={{0,128},{64,192},{128,0},{192,64},{1,129},{65,193},{129,1},{193,65... | collective-permute-start | bytes 73736 | tf_op jit(solution)/shard_map/ppermute | solution.py:31
  7.0 3.5 %shard_map.101 = (bf16[304,1536]{1,0:T(8,128)(2,1)}, bf16[288,1536]{1,0:T(8,128)(2,1)}) custom-call(bf16[192,1536]{1,0:T(8,128)(2,1)} %bitcast.18, bf16[192,1536]{1,0:T(8,128)(2,1)} %bitcast.19, bf16[192,1536]{1,0:T(8,128)(2,1)} %bitcast.20, bf16[96,128]{1,0:T(8,128)(2,1)} %bitcast.23), custom_call_target="tpu_custom_call" | custom-call | tf_op jit(solution)/shard_map/pallas_call | solution.py:246
  10.6 2.6 %collective-permute-start.4 = (bf16[304,1536]{1,0:T(8,128)(2,1)}, bf16[304,1536]{1,0:T(8,128)(2,1)}, u32[]{:S(2)}, u32[]{:S(2)}) collective-permute-start(bf16[304,1536]{1,0:T(8,128)(2,1)} %get-tuple-element.23.a0_ref), channel_id=1, source_target_pairs={{0,64},{64,128},{128,192},{192,0},{1,65},{65,129},{129,193},{193,1... | collective-permute-start | bytes 2801672 | tf_op jit(solution)/shard_map/ppermute | solution.py:31
  13.2 4.6 %collective-permute-start.5 = (bf16[304,1536]{1,0:T(8,128)(2,1)}, bf16[304,1536]{1,0:T(8,128)(2,1)}, u32[]{:S(2)}, u32[]{:S(2)}) collective-permute-start(bf16[304,1536]{1,0:T(8,128)(2,1)} %get-tuple-element.23.a0_ref), channel_id=1, source_target_pairs={{0,192},{64,0},{128,64},{192,128},{1,193},{65,1},{129,65},{193,129... | collective-permute-start | bytes 2801672 | tf_op jit(solution)/shard_map/ppermute | solution.py:31
  17.8 1.9 %collective-permute-start.9 = (bf16[288,1536]{1,0:T(8,128)(2,1)}, bf16[288,1536]{1,0:T(8,128)(2,1)}, u32[]{:S(2)}, u32[]{:S(2)}) collective-permute-start(bf16[288,1536]{1,0:T(8,128)(2,1)} %get-tuple-element.24.b0_ref), channel_id=1, source_target_pairs={{0,192},{64,0},{128,64},{192,128},{1,193},{65,1},{129,65},{193,129... | collective-permute-start | bytes 2654216 | tf_op jit(solution)/shard_map/ppermute | solution.py:31
  19.8 10.8 %collective-permute-start.3 = (bf16[4,1,64,128]{3,2,1,0:T(8,128)(2,1)S(1)}, bf16[4,1,64,128]{3,2,1,0:T(8,128)(2,1)S(1)}, u32[]{:S(2)}, u32[]{:S(2)}) collective-permute-start(bf16[4,1,64,128]{3,2,1,0:T(8,128)(2,1)S(1)} %get-tuple-element.34), channel_id=1, source_target_pairs={{1,0},{2,1},{3,2},{4,3},{5,4},{6,5},{7,6},{8,7},{9,8},{10,9},{11,1... | collective-permute-start | bytes 196616 | tf_op jit(solution)/shard_map/ppermute | solution.py:27
  30.6 1.9 %collective-permute-start.2 = (bf16[4,1,64,128]{3,2,1,0:T(8,128)(2,1)S(1)}, bf16[4,1,64,128]{3,2,1,0:T(8,128)(2,1)S(1)}, u32[]{:S(2)}, u32[]{:S(2)}) collective-permute-start(bf16[4,1,64,128]{3,2,1,0:T(8,128)(2,1)S(1)} %get-tuple-element.33), channel_id=1, source_target_pairs={{0,1},{1,2},{2,3},{3,4},{4,5},{5,6},{6,7},{7,8},{8,9},{9,10},{10,1... | collective-permute-start | bytes 196616 | tf_op jit(solution)/shard_map/ppermute | solution.py:27
  32.8 3.9 %collective-permute-start.7 = (bf16[288,1536]{1,0:T(8,128)(2,1)}, bf16[288,1536]{1,0:T(8,128)(2,1)}, u32[]{:S(2)}, u32[]{:S(2)}) collective-permute-start(bf16[288,1536]{1,0:T(8,128)(2,1)} %get-tuple-element.24.b0_ref), channel_id=1, source_target_pairs={{0,64},{64,128},{128,192},{192,0},{1,65},{65,129},{129,193},{193,1... | collective-permute-start | bytes 2654216 | tf_op jit(solution)/shard_map/ppermute | solution.py:31
  36.8 2.2 %collective-permute-done.2 = bf16[4,1,64,128]{3,2,1,0:T(8,128)(2,1)S(1)} collective-permute-done((bf16[4,1,64,128]{3,2,1,0:T(8,128)(2,1)S(1)}, bf16[4,1,64,128]{3,2,1,0:T(8,128)(2,1)S(1)}, u32[]{:S(2)}, u32[]{:S(2)}) %collective-permute-start.2) | collective-permute-done | bytes 65568 | tf_op jit(solution)/shard_map/ppermute | solution.py:27
  39.0 1.9 %shard_map.100 = (bf16[128,1664]{1,0:T(8,128)(2,1)S(1)}, bf16[64,128]{1,0:T(8,128)(2,1)S(1)}) custom-call(bf16[4,6,64,128]{3,2,1,0:T(8,128)(2,1)S(1)} %pad_maximum_fusion.tall_ref, bf16[3,3,384,128]{3,2,1,0:T(8,128)(2,1)S(1)} %bitcast.16, bf16[128,128]{1,0:T(8,128)(2,1)S(1)} %copy.13.latent_ref, bf16[64,1536]{1,0:T(8,128)(2,1)S(1)} %copy-done.4, ...), custom_call_target="tpu_custom_call" | custom-call | tf_op jit(solution)/shard_map/pallas_call | solution.py:268
  41.8 9.6 %all-to-all-start = ((bf16[64,2,1664]{2,1,0:T(2,128)(2,1)}), bf16[64,2,1664]{2,1,0:T(2,128)(2,1)S(1)}, u32[]{:S(2)}, u32[]{:S(2)}) async-start(bf16[64,2,1664]{2,1,0:T(2,128)(2,1)} %reshape.20), calls=%async_computation | async-start | bytes 851968 | tf_op jit(solution)/shard_map/all_to_all | solution.py:277
  51.4 2.5 %collective-permute-start.10 = (bf16[304,1536]{1,0:T(8,128)(2,1)}, bf16[304,1536]{1,0:T(8,128)(2,1)}, u32[]{:S(2)}, u32[]{:S(2)}) collective-permute-start(bf16[304,1536]{1,0:T(8,128)(2,1)} %collective-permute-done.4.a1_ref), channel_id=1, source_target_pairs={{0,64},{64,128},{128,192},{192,0},{1,65},{65,129},{129,193},{193,1... | collective-permute-start | bytes 2801672 | tf_op jit(solution)/shard_map/ppermute | solution.py:31
  53.9 4.1 %collective-permute-done.9.b2_ref = bf16[288,1536]{1,0:T(8,128)(2,1)} collective-permute-done((bf16[288,1536]{1,0:T(8,128)(2,1)}, bf16[288,1536]{1,0:T(8,128)(2,1)}, u32[]{:S(2)}, u32[]{:S(2)}) %collective-permute-start.9) | collective-permute-done | bytes 884768 | tf_op jit(solution)/shard_map/ppermute | solution.py:31
  57.9 5.6 %collective-permute-start.11 = (bf16[288,1536]{1,0:T(8,128)(2,1)}, bf16[288,1536]{1,0:T(8,128)(2,1)}, u32[]{:S(2)}, u32[]{:S(2)}) collective-permute-start(bf16[288,1536]{1,0:T(8,128)(2,1)} %collective-permute-done.9.b2_ref), channel_id=1, source_target_pairs={{0,192},{64,0},{128,64},{192,128},{1,193},{65,1},{129,65},{193,129... | collective-permute-start | bytes 2654216 | tf_op jit(solution)/shard_map/ppermute | solution.py:31
  63.6 2.3 %shard_map.102.near_ref = bf16[64,768]{1,0:T(8,128)(2,1)} custom-call(bf16[96,128]{1,0:T(8,128)(2,1)} %copy-done.7, bf16[304,1536]{1,0:T(8,128)(2,1)} %get-tuple-element.23.a0_ref, bf16[304,1536]{1,0:T(8,128)(2,1)} %collective-permute-done.4.a1_ref, bf16[304,1536]{1,0:T(8,128)(2,1)} %collective-permute-done.5.a2_ref), custom_call_target="tpu_custom_call" | custom-call | tf_op jit(solution)/shard_map/pallas_call | solution.py:279
  65.9 6.0 %collective-permute-start.6 = (bf16[64,768]{1,0:T(8,128)(2,1)}, bf16[64,768]{1,0:T(8,128)(2,1)S(1)}, u32[]{:S(2)}, u32[]{:S(2)}) collective-permute-start(bf16[64,768]{1,0:T(8,128)(2,1)} %shard_map.102.near_ref), channel_id=1, source_target_pairs={{0,256},{256,0},{1,257},{257,1},{2,258},{258,2},{3,259},{259,3},{4... | collective-permute-start | bytes 294920 | tf_op jit(solution)/shard_map/ppermute | solution.py:287
  71.9 6.6 %collective-permute-done.6.far_ref = bf16[64,768]{1,0:T(8,128)(2,1)S(1)} collective-permute-done((bf16[64,768]{1,0:T(8,128)(2,1)}, bf16[64,768]{1,0:T(8,128)(2,1)S(1)}, u32[]{:S(2)}, u32[]{:S(2)}) %collective-permute-start.6) | collective-permute-done | bytes 98336 | tf_op jit(solution)/shard_map/ppermute | solution.py:287
  79.5 1.9 %collective-permute-start.8 = (bf16[192,1664]{1,0:T(8,128)(2,1)S(1)}, bf16[192,1664]{1,0:T(8,128)(2,1)S(1)}, u32[]{:S(2)}, u32[]{:S(2)}) collective-permute-start(bf16[192,1664]{1,0:T(8,128)(2,1)S(1)} %shard_map.103.mine_ref), channel_id=1, source_target_pairs={{0,32},{32,0},{1,33},{33,1},{2,34},{34,2},{3,35},{35,3},{4,36},{36... | collective-permute-start | bytes 1916936 | tf_op jit(solution)/shard_map/ppermute | solution.py:296
  81.6 2.0 %collective-permute-done.8.theirs_ref = bf16[192,1664]{1,0:T(8,128)(2,1)S(1)} collective-permute-done((bf16[192,1664]{1,0:T(8,128)(2,1)S(1)}, bf16[192,1664]{1,0:T(8,128)(2,1)S(1)}, u32[]{:S(2)}, u32[]{:S(2)}) %collective-permute-start.8) | collective-permute-done | bytes 639008 | tf_op jit(solution)/shard_map/ppermute | solution.py:296
  83.5 4.7 %shard_map.104 = (bf16[256,1536]{1,0:T(8,128)(2,1)S(1)}, f32[256,1]{1,0:T(8,128)S(1)}, f32[256,1536]{1,0:T(8,128)S(1)}) custom-call(s32[3]{0:T(128)S(1)} %pad_add_fusion.at_ref, bf16[192,1664]{1,0:T(8,128)(2,1)S(1)} %shard_map.103.mine_ref, bf16[192,1664]{1,0:T(8,128)(2,1)S(1)} %collective-permute-done.8.theirs_ref, bf16[2,1536]{1,0:T(2,128)(2,1)S(1)} %bitcast.17, ...), custom_call_target="tpu_custom_call" | custom-call | tf_op jit(solution)/shard_map/pallas_call | solution.py:298
  88.2 2.4 %shard_map.105 = (bf16[128,1536]{1,0:T(8,128)(2,1)S(1)}, bf16[128,1536]{1,0:T(8,128)(2,1)S(1)}) custom-call(bf16[256,1536]{1,0:T(8,128)(2,1)S(1)} %get-tuple-element.28.tokens_ref, f32[256,1]{1,0:T(8,128)S(1)} %get-tuple-element.29.score_ref, f32[256,1536]{1,0:T(8,128)S(1)} %get-tuple-element.30.total_ref, bf16[304,1536]{1,0:T(8,128)(2,1)} %collective-permute-done.10.w0_ref, ...), custom_call_target="tpu_custom_call" | custom-call | tf_op jit(solution)/shard_map/pallas_call | solution.py:314
  90.7 2.0 %collective-permute-start.12 = (bf16[128,1536]{1,0:T(8,128)(2,1)S(1)}, bf16[128,1536]{1,0:T(8,128)(2,1)S(1)}, u32[]{:S(2)}, u32[]{:S(2)}) collective-permute-start(bf16[128,1536]{1,0:T(8,128)(2,1)S(1)} %get-tuple-element.31), channel_id=1, source_target_pairs={{0,32},{32,0},{1,33},{33,1},{2,34},{34,2},{3,35},{35,3},{4,36},{36... | collective-permute-start | bytes 1179656 | tf_op jit(solution)/shard_map/ppermute | solution.py:322
  94.5 33.3 %all_to_all.10 = bf16[64,2,1536]{2,1,0:T(2,128)(2,1)S(1)} all-to-all(bf16[64,2,1536]{2,1,0:T(2,128)(2,1)S(1)} %reshape.22), channel_id=1, replica_groups=mesh['yh'=2,'x'=4,'c'=2,'yl'=4,'z'=8] {'yh','yl','z'}, dimensions={0} | all-to-all | bytes 786432 | tf_op jit(solution)/shard_map/all_to_all | solution.py:324
  (45 shorter events, 5.3 us)
Async XLA Ops:
  0.0 19.7 %copy-start.6 = (bf16[2,4,64,128]{3,2,1,0:T(8,128)(2,1)S(1)}, bf16[2,4,64,128]{3,2,1,0:T(8,128)(2,1)}, u32[]{:S(2)}) copy-start(bf16[2,4,64,128]{3,2,1,0:T(8,128)(2,1)} %param.10) | copy-start | bytes 393220
  0.0 32.6 %copy-start.8 = (bf16[128,16]{0,1:T(8,128)(2,1)S(1)}, bf16[128,16]{0,1:T(8,128)(2,1)}, u32[]{:S(2)}) copy-start(bf16[128,16]{0,1:T(8,128)(2,1)} %param.12) | copy-start | bytes 12292
  0.0 32.7 %copy-start.9 = (s32[64,2]{0,1:T(2,128)S(1)}, s32[64,2]{0,1:T(2,128)}, u32[]{:S(2)}) copy-start(s32[64,2]{0,1:T(2,128)} %param.19) | copy-start | bytes 1540
  0.0 19.7 %collective-permute-start = (bf16[2,4,64,128]{3,2,1,0:T(8,128)(2,1)}, bf16[2,4,64,128]{3,2,1,0:T(8,128)(2,1)S(1)}, u32[]{:S(2)}, u32[]{:S(2)}) collective-permute-start(bf16[2,4,64,128]{3,2,1,0:T(8,128)(2,1)} %param.10), channel_id=1, source_target_pairs={{0,32},{32,64},{64,96},{96,128},{128,160},{160,192},{192,224},{224... | collective-permute-start | bytes 393224 | tf_op jit(solution)/shard_map/ppermute | solution.py:27
  1.9 17.8 %collective-permute-start.1 = (bf16[96,128]{1,0:T(8,128)(2,1)}, bf16[96,128]{1,0:T(8,128)(2,1)S(1)}, u32[]{:S(2)}, u32[]{:S(2)}) collective-permute-start(bf16[96,128]{1,0:T(8,128)(2,1)} %bitcast.22), channel_id=1, source_target_pairs={{0,128},{64,192},{128,0},{192,64},{1,129},{65,193},{129,1},{193,65... | collective-permute-start | bytes 73736 | tf_op jit(solution)/shard_map/ppermute | solution.py:31
  7.0 32.0 %copy-start.4 = (bf16[64,1536]{1,0:T(8,128)(2,1)S(1)}, bf16[64,1536]{1,0:T(8,128)(2,1)}, u32[]{:S(2)}) copy-start(bf16[64,1536]{1,0:T(8,128)(2,1)} %context_ref.1) | copy-start | bytes 589828
  10.5 28.4 %copy-start.1 = (bf16[3,3,3,128,128]{4,3,2,1,0:T(8,128)(2,1)S(1)}, bf16[3,3,3,128,128]{4,3,2,1,0:T(8,128)(2,1)}, u32[]{:S(2)}) copy-start(bf16[3,3,3,128,128]{4,3,2,1,0:T(8,128)(2,1)} %param.11) | copy-start | bytes 2654212
  10.6 40.8 %collective-permute-start.4 = (bf16[304,1536]{1,0:T(8,128)(2,1)}, bf16[304,1536]{1,0:T(8,128)(2,1)}, u32[]{:S(2)}, u32[]{:S(2)}) collective-permute-start(bf16[304,1536]{1,0:T(8,128)(2,1)} %get-tuple-element.23.a0_ref), channel_id=1, source_target_pairs={{0,64},{64,128},{128,192},{192,0},{1,65},{65,129},{129,193},{193,1... | collective-permute-start | bytes 2801672 | tf_op jit(solution)/shard_map/ppermute | solution.py:31
  13.2 50.3 %collective-permute-start.5 = (bf16[304,1536]{1,0:T(8,128)(2,1)}, bf16[304,1536]{1,0:T(8,128)(2,1)}, u32[]{:S(2)}, u32[]{:S(2)}) collective-permute-start(bf16[304,1536]{1,0:T(8,128)(2,1)} %get-tuple-element.23.a0_ref), channel_id=1, source_target_pairs={{0,192},{64,0},{128,64},{192,128},{1,193},{65,1},{129,65},{193,129... | collective-permute-start | bytes 2801672 | tf_op jit(solution)/shard_map/ppermute | solution.py:31
  17.8 40.2 %collective-permute-start.9 = (bf16[288,1536]{1,0:T(8,128)(2,1)}, bf16[288,1536]{1,0:T(8,128)(2,1)}, u32[]{:S(2)}, u32[]{:S(2)}) collective-permute-start(bf16[288,1536]{1,0:T(8,128)(2,1)} %get-tuple-element.24.b0_ref), channel_id=1, source_target_pairs={{0,192},{64,0},{128,64},{192,128},{1,193},{65,1},{129,65},{193,129... | collective-permute-start | bytes 2654216 | tf_op jit(solution)/shard_map/ppermute | solution.py:31
  19.7 21.2 %copy-start.7 = (bf16[96,128]{1,0:T(8,128)(2,1)}, bf16[96,128]{1,0:T(8,128)(2,1)S(1)}, u32[]{:S(2)}) copy-start(bf16[96,128]{1,0:T(8,128)(2,1)S(1)} %collective-permute-done.1.opposite_ref) | copy-start | bytes 73732
  19.8 13.0 %collective-permute-start.3 = (bf16[4,1,64,128]{3,2,1,0:T(8,128)(2,1)S(1)}, bf16[4,1,64,128]{3,2,1,0:T(8,128)(2,1)S(1)}, u32[]{:S(2)}, u32[]{:S(2)}) collective-permute-start(bf16[4,1,64,128]{3,2,1,0:T(8,128)(2,1)S(1)} %get-tuple-element.34), channel_id=1, source_target_pairs={{1,0},{2,1},{3,2},{4,3},{5,4},{6,5},{7,6},{8,7},{9,8},{10,9},{11,1... | collective-permute-start | bytes 196616 | tf_op jit(solution)/shard_map/ppermute | solution.py:27
  30.6 8.3 %collective-permute-start.2 = (bf16[4,1,64,128]{3,2,1,0:T(8,128)(2,1)S(1)}, bf16[4,1,64,128]{3,2,1,0:T(8,128)(2,1)S(1)}, u32[]{:S(2)}, u32[]{:S(2)}) collective-permute-start(bf16[4,1,64,128]{3,2,1,0:T(8,128)(2,1)S(1)} %get-tuple-element.33), channel_id=1, source_target_pairs={{0,1},{1,2},{2,3},{3,4},{4,5},{5,6},{6,7},{7,8},{8,9},{9,10},{10,1... | collective-permute-start | bytes 196616 | tf_op jit(solution)/shard_map/ppermute | solution.py:27
  32.8 39.0 %collective-permute-start.7 = (bf16[288,1536]{1,0:T(8,128)(2,1)}, bf16[288,1536]{1,0:T(8,128)(2,1)}, u32[]{:S(2)}, u32[]{:S(2)}) collective-permute-start(bf16[288,1536]{1,0:T(8,128)(2,1)} %get-tuple-element.24.b0_ref), channel_id=1, source_target_pairs={{0,64},{64,128},{128,192},{192,0},{1,65},{65,129},{129,193},{193,1... | collective-permute-start | bytes 2654216 | tf_op jit(solution)/shard_map/ppermute | solution.py:31
  41.8 36.6 %all-to-all-start = ((bf16[64,2,1664]{2,1,0:T(2,128)(2,1)}), bf16[64,2,1664]{2,1,0:T(2,128)(2,1)S(1)}, u32[]{:S(2)}, u32[]{:S(2)}) async-start(bf16[64,2,1664]{2,1,0:T(2,128)(2,1)} %reshape.20), calls=%async_computation | async-start | bytes 851968 | tf_op jit(solution)/shard_map/all_to_all | solution.py:277
  51.4 36.8 %collective-permute-start.10 = (bf16[304,1536]{1,0:T(8,128)(2,1)}, bf16[304,1536]{1,0:T(8,128)(2,1)}, u32[]{:S(2)}, u32[]{:S(2)}) collective-permute-start(bf16[304,1536]{1,0:T(8,128)(2,1)} %collective-permute-done.4.a1_ref), channel_id=1, source_target_pairs={{0,64},{64,128},{128,192},{192,0},{1,65},{65,129},{129,193},{193,1... | collective-permute-start | bytes 2801672 | tf_op jit(solution)/shard_map/ppermute | solution.py:31
  57.9 30.3 %collective-permute-start.11 = (bf16[288,1536]{1,0:T(8,128)(2,1)}, bf16[288,1536]{1,0:T(8,128)(2,1)}, u32[]{:S(2)}, u32[]{:S(2)}) collective-permute-start(bf16[288,1536]{1,0:T(8,128)(2,1)} %collective-permute-done.9.b2_ref), channel_id=1, source_target_pairs={{0,192},{64,0},{128,64},{192,128},{1,193},{65,1},{129,65},{193,129... | collective-permute-start | bytes 2654216 | tf_op jit(solution)/shard_map/ppermute | solution.py:31
  63.6 20.0 %copy-start.5 = (bf16[2,1536,1]{1,0,2:T(2,128)(2,1)S(1)}, bf16[2,1536,1]{1,0,2:T(2,128)(2,1)}, u32[]{:S(2)}) copy-start(bf16[2,1536,1]{1,0,2:T(2,128)(2,1)} %param.15) | copy-start | bytes 18436
  65.8 17.7 %copy-start = (bf16[304,1536]{1,0:T(8,128)(2,1)S(1)}, bf16[304,1536]{1,0:T(8,128)(2,1)}, u32[]{:S(2)}) copy-start(bf16[304,1536]{1,0:T(8,128)(2,1)} %get-tuple-element.23.a0_ref) | copy-start | bytes 2801668
  65.8 17.7 %copy-start.2 = (bf16[288,1536]{1,0:T(8,128)(2,1)S(1)}, bf16[288,1536]{1,0:T(8,128)(2,1)}, u32[]{:S(2)}) copy-start(bf16[288,1536]{1,0:T(8,128)(2,1)} %get-tuple-element.24.b0_ref) | copy-start | bytes 2654212
  65.9 12.6 %collective-permute-start.6 = (bf16[64,768]{1,0:T(8,128)(2,1)}, bf16[64,768]{1,0:T(8,128)(2,1)S(1)}, u32[]{:S(2)}, u32[]{:S(2)}) collective-permute-start(bf16[64,768]{1,0:T(8,128)(2,1)} %shard_map.102.near_ref), channel_id=1, source_target_pairs={{0,256},{256,0},{1,257},{257,1},{2,258},{258,2},{3,259},{259,3},{4... | collective-permute-start | bytes 294920 | tf_op jit(solution)/shard_map/ppermute | solution.py:287
  78.6 0.9 copy-start.3
  79.5 4.0 %collective-permute-start.8 = (bf16[192,1664]{1,0:T(8,128)(2,1)S(1)}, bf16[192,1664]{1,0:T(8,128)(2,1)S(1)}, u32[]{:S(2)}, u32[]{:S(2)}) collective-permute-start(bf16[192,1664]{1,0:T(8,128)(2,1)S(1)} %shard_map.103.mine_ref), channel_id=1, source_target_pairs={{0,32},{32,0},{1,33},{33,1},{2,34},{34,2},{3,35},{35,3},{4,36},{36... | collective-permute-start | bytes 1916936 | tf_op jit(solution)/shard_map/ppermute | solution.py:296
  90.7 3.6 %collective-permute-start.12 = (bf16[128,1536]{1,0:T(8,128)(2,1)S(1)}, bf16[128,1536]{1,0:T(8,128)(2,1)S(1)}, u32[]{:S(2)}, u32[]{:S(2)}) collective-permute-start(bf16[128,1536]{1,0:T(8,128)(2,1)S(1)} %get-tuple-element.31), channel_id=1, source_target_pairs={{0,32},{32,0},{1,33},{33,1},{2,34},{34,2},{3,35},{35,3},{4,36},{36... | collective-permute-start | bytes 1179656 | tf_op jit(solution)/shard_map/ppermute | solution.py:322

commit v13 on v12

--- a/solution.py
+++ b/solution.py
@@ -54,8 +54,9 @@
     for copy in copies:
         copy.start()
     tall, width = first_held.shape[0] - part, first_held.shape[1]
-    first_held[part:] = jnp.zeros((tall, width), BF)
-    lay_beside(first_held, part, shard_ref)
+    for ref in (first_held, second_held):
+        ref[part:] = jnp.zeros((tall, width), BF)
+        lay_beside(ref, part, shard_ref)
     for copy in copies:
         copy.wait()
     copies = [
@@ -154,8 +155,7 @@
 ):
     yh, x, c = at_ref[0], at_ref[1], at_ref[2]
     rows, width = tokens_ref.shape[0] // 2, total_ref.shape[1]
-    part = b0_ref.shape[0]
-    share = part * 2 // 3
+    part, share = held_ref.shape[1] // 2, held_ref.shape[1] // 3
     copies = [
         pltpu.make_async_copy(ref.at[pl.ds(0, part)], held_ref.at[i // 2, pl.ds(i % 2 * part, part)], sems.at[i])
         for i, ref in enumerate((a0_ref, b0_ref, a1_ref, b1_ref, a2_ref, b2_ref))
@@ -196,7 +196,7 @@
 
 def last_kernel(tokens_ref, score_ref, total_ref, w0_ref, w1_ref, other_ref, own_ref, held_ref, sems):
     rows, width = other_ref.shape
-    part, share = w1_ref.shape[0], held_ref.shape[0] // 3
+    part, share = held_ref.shape[0] // 2, held_ref.shape[0] // 3
     copies = [
         pltpu.make_async_copy(ref.at[pl.ds(0, part)], held_ref.at[pl.ds(i * part, part)], sems.at[i])
         for i, ref in enumerate((w0_ref, w1_ref))
@@ -245,14 +245,10 @@
     part, tall = 3 * share // 2, 16
     first, second = pl.pallas_call(
         pack_kernel,
-        out_shape=[jax.ShapeDtypeStruct((part + tall, width), BF), jax.ShapeDtypeStruct((part, width), BF)],
+        out_shape=[jax.ShapeDtypeStruct((part + tall, width), BF)] * 2,
         in_specs=[hbm] * 3 + [vmem],
         out_specs=[hbm] * 2,
-        scratch_shapes=[
-            pltpu.VMEM((part + tall, width), BF),
-            pltpu.VMEM((part, width), BF),
-            pltpu.SemaphoreType.DMA((6,)),
-        ],
+        scratch_shapes=[pltpu.VMEM((part + tall, width), BF)] * 2 + [pltpu.SemaphoreType.DMA((6,))],
         compiler_params=pltpu.CompilerParams(vmem_limit_bytes=PACK_BYTES),
     )(gate_weight[0].T, up_weight[0].T, down_weight[0], shard)
     first_behind, second_ahead = ring(first, -1), ring(second, 1)
@@ -283,9 +279,11 @@
         out_specs=vmem,
         scratch_shapes=[pltpu.VMEM((3, tall, width), BF), pltpu.SemaphoreType.DMA((3,))],
         compiler_params=pltpu.CompilerParams(vmem_limit_bytes=PACK_BYTES),
-    )(opposite, first, first_behind, first_ahead)
+    )(opposite, first, first_behind, second_ahead)
     beyond = lax.ppermute(shards, "yh", SWAP)
-    arrived, beyond, second_behind = lax.optimization_barrier((arrived, beyond, second_behind))
+    arrived, beyond, first_ahead, second_behind = lax.optimization_barrier(
+        (arrived, beyond, first_ahead, second_behind)
+    )
     mine = pl.pallas_call(
         swap_kernel,
         out_shape=jax.ShapeDtypeStruct((slots + 4 * tall, raw), BF),

time: 130 us -> 122 us (0.938)
  the two profiles are of different devices: /device:TPU:16 before, /device:TPU:6 now
where the time goes in v13:
time: 122 us; the launch traced here: 121 us
  starting transfers between devices  60.4 us (50%)
  blocking collectives  31.9 us (26%)
  Pallas kernels  15.1 us (12%)
  waiting for transfers between devices  9.2 us (8%)
  local copies, waits for them, and re-layouts  2.58 us (2%)
    all_to_all x1, blocking collectives, local(): lax.all_to_all(summed, SOURCES, split_axis=0, concat_axis=0, tiled=True)  31.9 us
    ppermute x7, starting transfers between devices, ring(): return lax.ppermute(value, 'x', [(i, (i - step) % 4) for i in range(4)])  24.8 us
    all_to_all x1, starting transfers between devices, local(): lax.all_to_all(outgoing.reshape(experts, capacity, raw), SOURCES, split_a...  16.1 us
    ppermute x3, starting transfers between devices, shifted(): return lax.ppermute(value, axes, pairs)  7.89 us
    ppermute x1, starting transfers between devices, local(): beyond = lax.ppermute(shards, 'yh', SWAP)  7.62 us
    pallas_call x1, Pallas kernels, local(): pl.pallas_call(near_kernel, out_shape=[jax.ShapeDtypeStruct((2 * slots, w...  5.07 us
    ppermute x1, waiting for transfers between devices, local(): beyond = lax.ppermute(shards, 'yh', SWAP)  4.17 us
    pallas_call x1, Pallas kernels, local(): pl.pallas_call(pack_kernel, out_shape=[jax.ShapeDtypeStruct((part + tall,...  3.47 us
  transfers between devices with their start and end apart: 14, of which 4 were waited for; matrix products, arithmetic and copies ran while one was open for 1% of the time, Pallas kernels for 11%

profile of v13, /device:TPU:6, one launch (start us, length us, event | category | flops | bytes accessed | tf_op | source)
XLA Modules:
  0.0 120.7 jit_solution(5097269710873879432)
XLA Ops:
  0.0 2.1 %collective-permute-start = (bf16[2,4,64,128]{3,2,1,0:T(8,128)(2,1)}, bf16[2,4,64,128]{3,2,1,0:T(8,128)(2,1)S(1)}, u32[]{:S(2)}, u32[]{:S(2)}) collective-permute-start(bf16[2,4,64,128]{3,2,1,0:T(8,128)(2,1)} %param.10), channel_id=1, source_target_pairs={{0,32},{32,64},{64,96},{96,128},{128,160},{160,192},{192,224},{224... | collective-permute-start | bytes 393224 | tf_op jit(solution)/shard_map/ppermute | solution.py:27
  2.1 3.3 %collective-permute-start.1 = (bf16[96,128]{1,0:T(8,128)(2,1)}, bf16[96,128]{1,0:T(8,128)(2,1)S(1)}, u32[]{:S(2)}, u32[]{:S(2)}) collective-permute-start(bf16[96,128]{1,0:T(8,128)(2,1)} %bitcast.22), channel_id=1, source_target_pairs={{0,128},{64,192},{128,0},{192,64},{1,129},{65,193},{129,1},{193,65... | collective-permute-start | bytes 73736 | tf_op jit(solution)/shard_map/ppermute | solution.py:31
  5.4 3.5 %shard_map.101 = (bf16[304,1536]{1,0:T(8,128)(2,1)}, bf16[304,1536]{1,0:T(8,128)(2,1)}) custom-call(bf16[192,1536]{1,0:T(8,128)(2,1)} %bitcast.18, bf16[192,1536]{1,0:T(8,128)(2,1)} %bitcast.19, bf16[192,1536]{1,0:T(8,128)(2,1)} %bitcast.20, bf16[96,128]{1,0:T(8,128)(2,1)} %bitcast.23), custom_call_target="tpu_custom_call" | custom-call | tf_op jit(solution)/shard_map/pallas_call | solution.py:246
  8.9 5.9 %collective-permute-start.4 = (bf16[304,1536]{1,0:T(8,128)(2,1)}, bf16[304,1536]{1,0:T(8,128)(2,1)}, u32[]{:S(2)}, u32[]{:S(2)}) collective-permute-start(bf16[304,1536]{1,0:T(8,128)(2,1)} %get-tuple-element.24.a0_ref), channel_id=1, source_target_pairs={{0,64},{64,128},{128,192},{192,0},{1,65},{65,129},{129,193},{193,1... | collective-permute-start | bytes 2801672 | tf_op jit(solution)/shard_map/ppermute | solution.py:31
  14.8 2.8 %collective-permute-start.5 = (bf16[304,1536]{1,0:T(8,128)(2,1)}, bf16[304,1536]{1,0:T(8,128)(2,1)}, u32[]{:S(2)}, u32[]{:S(2)}) collective-permute-start(bf16[304,1536]{1,0:T(8,128)(2,1)} %get-tuple-element.25.b0_ref), channel_id=1, source_target_pairs={{0,192},{64,0},{128,64},{192,128},{1,193},{65,1},{129,65},{193,129... | collective-permute-start | bytes 2801672 | tf_op jit(solution)/shard_map/ppermute | solution.py:31
  17.6 1.3 %collective-permute-start.3 = (bf16[4,1,64,128]{3,2,1,0:T(8,128)(2,1)S(1)}, bf16[4,1,64,128]{3,2,1,0:T(8,128)(2,1)S(1)}, u32[]{:S(2)}, u32[]{:S(2)}) collective-permute-start(bf16[4,1,64,128]{3,2,1,0:T(8,128)(2,1)S(1)} %get-tuple-element.36), channel_id=1, source_target_pairs={{1,0},{2,1},{3,2},{4,3},{5,4},{6,5},{7,6},{8,7},{9,8},{10,9},{11,1... | collective-permute-start | bytes 196616 | tf_op jit(solution)/shard_map/ppermute | solution.py:27
  18.9 4.5 %collective-permute-start.2 = (bf16[4,1,64,128]{3,2,1,0:T(8,128)(2,1)S(1)}, bf16[4,1,64,128]{3,2,1,0:T(8,128)(2,1)S(1)}, u32[]{:S(2)}, u32[]{:S(2)}) collective-permute-start(bf16[4,1,64,128]{3,2,1,0:T(8,128)(2,1)S(1)} %get-tuple-element.35), channel_id=1, source_target_pairs={{0,1},{1,2},{2,3},{3,4},{4,5},{5,6},{6,7},{7,8},{8,9},{9,10},{10,1... | collective-permute-start | bytes 196616 | tf_op jit(solution)/shard_map/ppermute | solution.py:27
  23.5 3.9 %collective-permute-start.7 = (bf16[304,1536]{1,0:T(8,128)(2,1)}, bf16[304,1536]{1,0:T(8,128)(2,1)}, u32[]{:S(2)}, u32[]{:S(2)}) collective-permute-start(bf16[304,1536]{1,0:T(8,128)(2,1)} %get-tuple-element.24.a0_ref), channel_id=1, source_target_pairs={{0,192},{64,0},{128,64},{192,128},{1,193},{65,1},{129,65},{193,129... | collective-permute-start | bytes 2801672 | tf_op jit(solution)/shard_map/ppermute | solution.py:31
  27.7 3.1 %collective-permute-start.8 = (bf16[304,1536]{1,0:T(8,128)(2,1)}, bf16[304,1536]{1,0:T(8,128)(2,1)}, u32[]{:S(2)}, u32[]{:S(2)}) collective-permute-start(bf16[304,1536]{1,0:T(8,128)(2,1)} %get-tuple-element.25.b0_ref), channel_id=1, source_target_pairs={{0,64},{64,128},{128,192},{192,0},{1,65},{65,129},{129,193},{193,1... | collective-permute-start | bytes 2801672 | tf_op jit(solution)/shard_map/ppermute | solution.py:31
  30.9 1.9 %shard_map.100 = (bf16[128,1664]{1,0:T(8,128)(2,1)S(1)}, bf16[64,128]{1,0:T(8,128)(2,1)S(1)}) custom-call(bf16[4,6,64,128]{3,2,1,0:T(8,128)(2,1)S(1)} %pad_maximum_fusion.tall_ref, bf16[3,3,384,128]{3,2,1,0:T(8,128)(2,1)S(1)} %bitcast.16, bf16[128,128]{1,0:T(8,128)(2,1)S(1)} %copy.13.latent_ref, bf16[64,1536]{1,0:T(8,128)(2,1)S(1)} %copy-done.4, ...), custom_call_target="tpu_custom_call" | custom-call | tf_op jit(solution)/shard_map/pallas_call | solution.py:264
  33.8 16.1 %all-to-all-start = ((bf16[64,2,1664]{2,1,0:T(2,128)(2,1)}), bf16[64,2,1664]{2,1,0:T(2,128)(2,1)S(1)}, u32[]{:S(2)}, u32[]{:S(2)}) async-start(bf16[64,2,1664]{2,1,0:T(2,128)(2,1)} %reshape.20), calls=%async_computation | async-start | bytes 851968 | tf_op jit(solution)/shard_map/all_to_all | solution.py:273
  49.9 3.9 %collective-permute-start.10 = (bf16[304,1536]{1,0:T(8,128)(2,1)}, bf16[304,1536]{1,0:T(8,128)(2,1)}, u32[]{:S(2)}, u32[]{:S(2)}) collective-permute-start(bf16[304,1536]{1,0:T(8,128)(2,1)} %collective-permute-done.4.a1_ref), channel_id=1, source_target_pairs={{0,64},{64,128},{128,192},{192,0},{1,65},{65,129},{129,193},{193,1... | collective-permute-start | bytes 2801672 | tf_op jit(solution)/shard_map/ppermute | solution.py:31
  53.9 1.9 %collective-permute-start.11 = (bf16[304,1536]{1,0:T(8,128)(2,1)}, bf16[304,1536]{1,0:T(8,128)(2,1)}, u32[]{:S(2)}, u32[]{:S(2)}) collective-permute-start(bf16[304,1536]{1,0:T(8,128)(2,1)} %collective-permute-done.5.a2_ref.b2_ref), channel_id=1, source_target_pairs={{0,192},{64,0},{128,64},{192,128},{1,193},{65,1},{129,65},{193,129... | collective-permute-start | bytes 2801672 | tf_op jit(solution)/shard_map/ppermute | solution.py:31
  55.8 2.3 %shard_map.102.near_ref = bf16[64,768]{1,0:T(8,128)(2,1)} custom-call(bf16[96,128]{1,0:T(8,128)(2,1)} %copy-done.7, bf16[304,1536]{1,0:T(8,128)(2,1)} %get-tuple-element.24.a0_ref, bf16[304,1536]{1,0:T(8,128)(2,1)} %collective-permute-done.4.a1_ref, bf16[304,1536]{1,0:T(8,128)(2,1)} %collective-permute-done.5.a2_ref.b2_ref), custom_call_target="tpu_custom_call" | custom-call | tf_op jit(solution)/shard_map/pallas_call | solution.py:275
  58.1 7.6 %collective-permute-start.6 = (bf16[64,768]{1,0:T(8,128)(2,1)}, bf16[64,768]{1,0:T(8,128)(2,1)S(1)}, u32[]{:S(2)}, u32[]{:S(2)}) collective-permute-start(bf16[64,768]{1,0:T(8,128)(2,1)} %shard_map.102.near_ref), channel_id=1, source_target_pairs={{0,256},{256,0},{1,257},{257,1},{2,258},{258,2},{3,259},{259,3},{4... | collective-permute-start | bytes 294920 | tf_op jit(solution)/shard_map/ppermute | solution.py:283
  65.7 4.2 %collective-permute-done.6.far_ref = bf16[64,768]{1,0:T(8,128)(2,1)S(1)} collective-permute-done((bf16[64,768]{1,0:T(8,128)(2,1)}, bf16[64,768]{1,0:T(8,128)(2,1)S(1)}, u32[]{:S(2)}, u32[]{:S(2)}) %collective-permute-start.6) | collective-permute-done | bytes 98336 | tf_op jit(solution)/shard_map/ppermute | solution.py:283
  71.0 1.9 %collective-permute-start.9 = (bf16[192,1664]{1,0:T(8,128)(2,1)S(1)}, bf16[192,1664]{1,0:T(8,128)(2,1)}, u32[]{:S(2)}, u32[]{:S(2)}) collective-permute-start(bf16[192,1664]{1,0:T(8,128)(2,1)S(1)} %shard_map.103.mine_ref), channel_id=1, source_target_pairs={{0,32},{32,0},{1,33},{33,1},{2,34},{34,2},{3,35},{35,3},{4,36},{36... | collective-permute-start | bytes 1916936 | tf_op jit(solution)/shard_map/ppermute | solution.py:294
  73.0 2.1 %collective-permute-done.9.theirs_ref = bf16[192,1664]{1,0:T(8,128)(2,1)} collective-permute-done((bf16[192,1664]{1,0:T(8,128)(2,1)S(1)}, bf16[192,1664]{1,0:T(8,128)(2,1)}, u32[]{:S(2)}, u32[]{:S(2)}) %collective-permute-start.9) | collective-permute-done | bytes 639008 | tf_op jit(solution)/shard_map/ppermute | solution.py:294
  75.1 5.1 %shard_map.104 = (bf16[256,1536]{1,0:T(8,128)(2,1)S(1)}, f32[256,1]{1,0:T(8,128)S(1)}, f32[256,1536]{1,0:T(8,128)S(1)}) custom-call(s32[3]{0:T(128)S(1)} %pad_add_fusion.at_ref, bf16[192,1664]{1,0:T(8,128)(2,1)S(1)} %shard_map.103.mine_ref, bf16[192,1664]{1,0:T(8,128)(2,1)} %collective-permute-done.9.theirs_ref, bf16[2,1536]{1,0:T(2,128)(2,1)S(1)} %bitcast.17, ...), custom_call_target="tpu_custom_call" | custom-call | tf_op jit(solution)/shard_map/pallas_call | solution.py:296
  80.2 1.3 %collective-permute-done.11.w1_ref = bf16[304,1536]{1,0:T(8,128)(2,1)} collective-permute-done((bf16[304,1536]{1,0:T(8,128)(2,1)}, bf16[304,1536]{1,0:T(8,128)(2,1)}, u32[]{:S(2)}, u32[]{:S(2)}) %collective-permute-start.11) | collective-permute-done | bytes 933920 | tf_op jit(solution)/shard_map/ppermute | solution.py:31
  81.5 2.4 %shard_map.105 = (bf16[128,1536]{1,0:T(8,128)(2,1)S(1)}, bf16[128,1536]{1,0:T(8,128)(2,1)S(1)}) custom-call(bf16[256,1536]{1,0:T(8,128)(2,1)S(1)} %get-tuple-element.30.tokens_ref, f32[256,1]{1,0:T(8,128)S(1)} %get-tuple-element.31.score_ref, f32[256,1536]{1,0:T(8,128)S(1)} %get-tuple-element.32.total_ref, bf16[304,1536]{1,0:T(8,128)(2,1)} %collective-permute-done.10.w0_ref, ...), custom_call_target="tpu_custom_call" | custom-call | tf_op jit(solution)/shard_map/pallas_call | solution.py:312
  84.0 2.0 %collective-permute-start.12 = (bf16[128,1536]{1,0:T(8,128)(2,1)S(1)}, bf16[128,1536]{1,0:T(8,128)(2,1)S(1)}, u32[]{:S(2)}, u32[]{:S(2)}) collective-permute-start(bf16[128,1536]{1,0:T(8,128)(2,1)S(1)} %get-tuple-element.33), channel_id=1, source_target_pairs={{0,32},{32,0},{1,33},{33,1},{2,34},{34,2},{3,35},{35,3},{4,36},{36... | collective-permute-start | bytes 1179656 | tf_op jit(solution)/shard_map/ppermute | solution.py:320
  86.0 1.6 %collective-permute-done.12 = bf16[128,1536]{1,0:T(8,128)(2,1)S(1)} collective-permute-done((bf16[128,1536]{1,0:T(8,128)(2,1)S(1)}, bf16[128,1536]{1,0:T(8,128)(2,1)S(1)}, u32[]{:S(2)}, u32[]{:S(2)}) %collective-permute-start.12) | collective-permute-done | bytes 393248 | tf_op jit(solution)/shard_map/ppermute | solution.py:320
  87.8 31.9 %all_to_all.10 = bf16[64,2,1536]{2,1,0:T(2,128)(2,1)S(1)} all-to-all(bf16[64,2,1536]{2,1,0:T(2,128)(2,1)S(1)} %reshape.22), channel_id=1, replica_groups=mesh['yh'=2,'x'=4,'c'=2,'yl'=4,'z'=8] {'yh','yl','z'}, dimensions={0} | all-to-all | bytes 786432 | tf_op jit(solution)/shard_map/all_to_all | solution.py:322
  (45 shorter events, 3.8 us)
Async XLA Ops:
  0.0 17.6 %copy-start.6 = (bf16[2,4,64,128]{3,2,1,0:T(8,128)(2,1)S(1)}, bf16[2,4,64,128]{3,2,1,0:T(8,128)(2,1)}, u32[]{:S(2)}) copy-start(bf16[2,4,64,128]{3,2,1,0:T(8,128)(2,1)} %param.10) | copy-start | bytes 393220
  0.0 27.4 %copy-start.8 = (bf16[128,16]{0,1:T(8,128)(2,1)S(1)}, bf16[128,16]{0,1:T(8,128)(2,1)}, u32[]{:S(2)}) copy-start(bf16[128,16]{0,1:T(8,128)(2,1)} %param.12) | copy-start | bytes 12292
  0.0 27.6 %copy-start.9 = (s32[64,2]{0,1:T(2,128)S(1)}, s32[64,2]{0,1:T(2,128)}, u32[]{:S(2)}) copy-start(s32[64,2]{0,1:T(2,128)} %param.19) | copy-start | bytes 1540
  0.0 17.6 %collective-permute-start = (bf16[2,4,64,128]{3,2,1,0:T(8,128)(2,1)}, bf16[2,4,64,128]{3,2,1,0:T(8,128)(2,1)S(1)}, u32[]{:S(2)}, u32[]{:S(2)}) collective-permute-start(bf16[2,4,64,128]{3,2,1,0:T(8,128)(2,1)} %param.10), channel_id=1, source_target_pairs={{0,32},{32,64},{64,96},{96,128},{128,160},{160,192},{192,224},{224... | collective-permute-start | bytes 393224 | tf_op jit(solution)/shard_map/ppermute | solution.py:27
  2.1 15.5 %collective-permute-start.1 = (bf16[96,128]{1,0:T(8,128)(2,1)}, bf16[96,128]{1,0:T(8,128)(2,1)S(1)}, u32[]{:S(2)}, u32[]{:S(2)}) collective-permute-start(bf16[96,128]{1,0:T(8,128)(2,1)} %bitcast.22), channel_id=1, source_target_pairs={{0,128},{64,192},{128,0},{192,64},{1,129},{65,193},{129,1},{193,65... | collective-permute-start | bytes 73736 | tf_op jit(solution)/shard_map/ppermute | solution.py:31
  5.4 25.5 %copy-start.4 = (bf16[64,1536]{1,0:T(8,128)(2,1)S(1)}, bf16[64,1536]{1,0:T(8,128)(2,1)}, u32[]{:S(2)}) copy-start(bf16[64,1536]{1,0:T(8,128)(2,1)} %context_ref.1) | copy-start | bytes 589828
  8.9 22.0 %copy-start.2 = (bf16[3,3,3,128,128]{4,3,2,1,0:T(8,128)(2,1)S(1)}, bf16[3,3,3,128,128]{4,3,2,1,0:T(8,128)(2,1)}, u32[]{:S(2)}) copy-start(bf16[3,3,3,128,128]{4,3,2,1,0:T(8,128)(2,1)} %param.11) | copy-start | bytes 2654212
  8.9 41.0 %collective-permute-start.4 = (bf16[304,1536]{1,0:T(8,128)(2,1)}, bf16[304,1536]{1,0:T(8,128)(2,1)}, u32[]{:S(2)}, u32[]{:S(2)}) collective-permute-start(bf16[304,1536]{1,0:T(8,128)(2,1)} %get-tuple-element.24.a0_ref), channel_id=1, source_target_pairs={{0,64},{64,128},{128,192},{192,0},{1,65},{65,129},{129,193},{193,1... | collective-permute-start | bytes 2801672 | tf_op jit(solution)/shard_map/ppermute | solution.py:31
  14.8 39.1 %collective-permute-start.5 = (bf16[304,1536]{1,0:T(8,128)(2,1)}, bf16[304,1536]{1,0:T(8,128)(2,1)}, u32[]{:S(2)}, u32[]{:S(2)}) collective-permute-start(bf16[304,1536]{1,0:T(8,128)(2,1)} %get-tuple-element.25.b0_ref), channel_id=1, source_target_pairs={{0,192},{64,0},{128,64},{192,128},{1,193},{65,1},{129,65},{193,129... | collective-permute-start | bytes 2801672 | tf_op jit(solution)/shard_map/ppermute | solution.py:31
  17.5 15.3 %copy-start.7 = (bf16[96,128]{1,0:T(8,128)(2,1)}, bf16[96,128]{1,0:T(8,128)(2,1)S(1)}, u32[]{:S(2)}) copy-start(bf16[96,128]{1,0:T(8,128)(2,1)S(1)} %collective-permute-done.1.opposite_ref) | copy-start | bytes 73732
  17.6 10.0 %collective-permute-start.3 = (bf16[4,1,64,128]{3,2,1,0:T(8,128)(2,1)S(1)}, bf16[4,1,64,128]{3,2,1,0:T(8,128)(2,1)S(1)}, u32[]{:S(2)}, u32[]{:S(2)}) collective-permute-start(bf16[4,1,64,128]{3,2,1,0:T(8,128)(2,1)S(1)} %get-tuple-element.36), channel_id=1, source_target_pairs={{1,0},{2,1},{3,2},{4,3},{5,4},{6,5},{7,6},{8,7},{9,8},{10,9},{11,1... | collective-permute-start | bytes 196616 | tf_op jit(solution)/shard_map/ppermute | solution.py:27
  18.9 11.9 %collective-permute-start.2 = (bf16[4,1,64,128]{3,2,1,0:T(8,128)(2,1)S(1)}, bf16[4,1,64,128]{3,2,1,0:T(8,128)(2,1)S(1)}, u32[]{:S(2)}, u32[]{:S(2)}) collective-permute-start(bf16[4,1,64,128]{3,2,1,0:T(8,128)(2,1)S(1)} %get-tuple-element.35), channel_id=1, source_target_pairs={{0,1},{1,2},{2,3},{3,4},{4,5},{5,6},{6,7},{7,8},{8,9},{9,10},{10,1... | collective-permute-start | bytes 196616 | tf_op jit(solution)/shard_map/ppermute | solution.py:27
  23.5 42.2 %collective-permute-start.7 = (bf16[304,1536]{1,0:T(8,128)(2,1)}, bf16[304,1536]{1,0:T(8,128)(2,1)}, u32[]{:S(2)}, u32[]{:S(2)}) collective-permute-start(bf16[304,1536]{1,0:T(8,128)(2,1)} %get-tuple-element.24.a0_ref), channel_id=1, source_target_pairs={{0,192},{64,0},{128,64},{192,128},{1,193},{65,1},{129,65},{193,129... | collective-permute-start | bytes 2801672 | tf_op jit(solution)/shard_map/ppermute | solution.py:31
  27.7 38.0 %collective-permute-start.8 = (bf16[304,1536]{1,0:T(8,128)(2,1)}, bf16[304,1536]{1,0:T(8,128)(2,1)}, u32[]{:S(2)}, u32[]{:S(2)}) collective-permute-start(bf16[304,1536]{1,0:T(8,128)(2,1)} %get-tuple-element.25.b0_ref), channel_id=1, source_target_pairs={{0,64},{64,128},{128,192},{192,0},{1,65},{65,129},{129,193},{193,1... | collective-permute-start | bytes 2801672 | tf_op jit(solution)/shard_map/ppermute | solution.py:31
  33.8 36.1 %all-to-all-start = ((bf16[64,2,1664]{2,1,0:T(2,128)(2,1)}), bf16[64,2,1664]{2,1,0:T(2,128)(2,1)S(1)}, u32[]{:S(2)}, u32[]{:S(2)}) async-start(bf16[64,2,1664]{2,1,0:T(2,128)(2,1)} %reshape.20), calls=%async_computation | async-start | bytes 851968 | tf_op jit(solution)/shard_map/all_to_all | solution.py:273
  49.9 30.3 %collective-permute-start.10 = (bf16[304,1536]{1,0:T(8,128)(2,1)}, bf16[304,1536]{1,0:T(8,128)(2,1)}, u32[]{:S(2)}, u32[]{:S(2)}) collective-permute-start(bf16[304,1536]{1,0:T(8,128)(2,1)} %collective-permute-done.4.a1_ref), channel_id=1, source_target_pairs={{0,64},{64,128},{128,192},{192,0},{1,65},{65,129},{129,193},{193,1... | collective-permute-start | bytes 2801672 | tf_op jit(solution)/shard_map/ppermute | solution.py:31
  53.9 27.7 %collective-permute-start.11 = (bf16[304,1536]{1,0:T(8,128)(2,1)}, bf16[304,1536]{1,0:T(8,128)(2,1)}, u32[]{:S(2)}, u32[]{:S(2)}) collective-permute-start(bf16[304,1536]{1,0:T(8,128)(2,1)} %collective-permute-done.5.a2_ref.b2_ref), channel_id=1, source_target_pairs={{0,192},{64,0},{128,64},{192,128},{1,193},{65,1},{129,65},{193,129... | collective-permute-start | bytes 2801672 | tf_op jit(solution)/shard_map/ppermute | solution.py:31
  55.8 19.3 %copy-start.5 = (bf16[2,1536,1]{1,0,2:T(2,128)(2,1)S(1)}, bf16[2,1536,1]{1,0,2:T(2,128)(2,1)}, u32[]{:S(2)}) copy-start(bf16[2,1536,1]{1,0,2:T(2,128)(2,1)} %param.15) | copy-start | bytes 18436
  58.1 17.1 %copy-start = (bf16[304,1536]{1,0:T(8,128)(2,1)S(1)}, bf16[304,1536]{1,0:T(8,128)(2,1)}, u32[]{:S(2)}) copy-start(bf16[304,1536]{1,0:T(8,128)(2,1)} %get-tuple-element.24.a0_ref) | copy-start | bytes 2801668
  58.1 17.0 %copy-start.1 = (bf16[304,1536]{1,0:T(8,128)(2,1)S(1)}, bf16[304,1536]{1,0:T(8,128)(2,1)}, u32[]{:S(2)}) copy-start(bf16[304,1536]{1,0:T(8,128)(2,1)} %get-tuple-element.25.b0_ref) | copy-start | bytes 2801668
  58.1 11.8 %collective-permute-start.6 = (bf16[64,768]{1,0:T(8,128)(2,1)}, bf16[64,768]{1,0:T(8,128)(2,1)S(1)}, u32[]{:S(2)}, u32[]{:S(2)}) collective-permute-start(bf16[64,768]{1,0:T(8,128)(2,1)} %shard_map.102.near_ref), channel_id=1, source_target_pairs={{0,256},{256,0},{1,257},{257,1},{2,258},{258,2},{3,259},{259,3},{4... | collective-permute-start | bytes 294920 | tf_op jit(solution)/shard_map/ppermute | solution.py:283
  70.1 0.9 copy-start.3
  71.0 4.1 %collective-permute-start.9 = (bf16[192,1664]{1,0:T(8,128)(2,1)S(1)}, bf16[192,1664]{1,0:T(8,128)(2,1)}, u32[]{:S(2)}, u32[]{:S(2)}) collective-permute-start(bf16[192,1664]{1,0:T(8,128)(2,1)S(1)} %shard_map.103.mine_ref), channel_id=1, source_target_pairs={{0,32},{32,0},{1,33},{33,1},{2,34},{34,2},{3,35},{35,3},{4,36},{36... | collective-permute-start | bytes 1916936 | tf_op jit(solution)/shard_map/ppermute | solution.py:294
  84.0 3.6 %collective-permute-start.12 = (bf16[128,1536]{1,0:T(8,128)(2,1)S(1)}, bf16[128,1536]{1,0:T(8,128)(2,1)S(1)}, u32[]{:S(2)}, u32[]{:S(2)}) collective-permute-start(bf16[128,1536]{1,0:T(8,128)(2,1)S(1)} %get-tuple-element.33), channel_id=1, source_target_pairs={{0,32},{32,0},{1,33},{33,1},{2,34},{34,2},{3,35},{35,3},{4,36},{36... | collective-permute-start | bytes 1179656 | tf_op jit(solution)/shard_map/ppermute | solution.py:320
